TPU v7x, 512 devices: a whole 4x4x16 slice. The times are simulated.
512 devices in a mesh: dom: 64 (over z, x), blk: 8 (over y, core).
Axes of the slice: x: 4, y: 4, z: 16, core: 2. Of those that a mesh axis runs over, the one named last changes fastest.
Arguments:
- adjoint_source: float32 [16, 2048, 162], P(None, ('dom', 'blk')), may hold values from -20 to 20
- diag_blocks: float32 [2048, 162, 162], P(('dom', 'blk')), may hold values from -3 to 9
- face_blocks: float32 [2048, 6, 162, 162], P(('dom', 'blk')), may hold values from -0.625 to 0.625
- neighbors: int32 [2048, 6], P(('dom', 'blk')), may hold values from -1 to 2047, as said below
- partner: int32 [2048, 6], P(('dom', 'blk')), may hold values from -1 to 5, as said below
- flags: int32 [2048, 6], P(('dom', 'blk')), may hold values from 0 to 2, as said below
Outputs:
- adjoint: float32 [16, 2048, 162], P(None, ('dom', 'blk'))
- rel_residual: float32 [16], replicated
Inputs may be any that keep to these rules, and one draw needn't show every extreme that they name: Elements form a grid of 128 x 16 cells with one layer in the third direction; device number d = index along dom times the blk size plus index along blk holds elements d * 4 to (d + 1) * 4 - 1, a block of 2 x 2 cells in some order. neighbors[e, f] is the element across face f, -1 on a boundary face; the relation is symmetric, and every neighbor lies on the same device or on the next device along dom or along blk, 2 faces of a device meeting each existing next device along dom and 2 each existing next device along blk. partner[e, f] is the face of neighbors[e, f] whose neighbor is e; -1 on a boundary face. `flags`: 0 where the face has a neighbor; on a boundary face of the first or second grid direction 1 for a wall or 2 for the far field; the two faces of the third direction are always 2.
All inputs are finite; a program needn't handle non-finite values.
Results may differ from a plain program's by a relative error of at most 0.00085.
Values sent between devices are 32-bit elements; how exact they have to be, the bound alone decides.
No kernel may reach another device: no remote copies, remote signals or barrier semaphores. Data moves between devices by JAX's collectives and lax.ppermute only.
A program may use at most 64 MiB of HBM per device.

v0:
```python
import jax
import jax.numpy as jnp
from jax import lax
from jax.sharding import PartitionSpec as P

EX = 2
EY = 2
ITERS = 8
SWEEPS = 3


HIGH = lax.Precision.HIGHEST


def shifted(value, axis, steps):
    count = lax.axis_size(axis)
    leading, last = (max(0, -steps), min(count, count - steps))
    return lax.ppermute(value, axis, [(source, source + steps) for source in range(leading, last)])


def invert_blocks(center):
    width = center.shape[-1]
    identity = jnp.eye(width, dtype=center.dtype)
    pivots = jnp.diagonal(center, axis1=1, axis2=2)
    estimate = identity[None, :, :] / pivots[:, :, None]
    for sweep_index in range(SWEEPS):
        product = jnp.einsum("eab,ebc->eac", center, estimate, precision=HIGH)
        estimate = 2.0 * estimate - jnp.einsum("eab,ebc->eac", estimate, product, precision=HIGH)
    return estimate


def least_squares(hessen, start_norm):
    count = len(hessen)
    cosines = []
    sines = []
    rotated_rhs = [start_norm] + [jnp.zeros_like(start_norm) for row_index in range(count)]
    upper = []
    for col_index in range(count):
        column = [hessen[col_index][row_index] for row_index in range(col_index + 2)]
        for row_index in range(col_index):
            rotated = (
                cosines[row_index] * column[row_index] + sines[row_index] * column[row_index + 1]
            )
            column[row_index + 1] = (
                -sines[row_index] * column[row_index] + cosines[row_index] * column[row_index + 1]
            )
            column[row_index] = rotated
        radius = jnp.sqrt(
            column[col_index] * column[col_index] + column[col_index + 1] * column[col_index + 1]
        )
        cosine = column[col_index] / radius
        sine_value = column[col_index + 1] / radius
        column[col_index] = radius
        cosines.append(cosine)
        sines.append(sine_value)
        rotated_rhs[col_index + 1] = -sine_value * rotated_rhs[col_index]
        rotated_rhs[col_index] = cosine * rotated_rhs[col_index]
        upper.append(column[: col_index + 1])
    coeffs = [None] * count
    for row_index in reversed(range(count)):
        total = rotated_rhs[row_index]
        for col_index in range(row_index + 1, count):
            total = total - upper[col_index][row_index] * coeffs[col_index]
        coeffs[row_index] = total / upper[row_index][row_index]
    return (coeffs, jnp.abs(rotated_rhs[count]) / start_norm)


def move_vectors_dom(vectors, offset):
    return shifted(vectors, "dom", offset)


def move_vectors_blk(vectors, offset):
    return shifted(vectors, "blk", offset)


def move_facing_dom(blocks, offset):
    return shifted(blocks, "dom", offset)


def move_facing_blk(blocks, offset):
    return shifted(blocks, "blk", offset)


def shards(adjoint_source, diag_blocks, face_blocks, neighbors, partner, flags):
    nrhs, elements, width = adjoint_source.shape
    blk_count = lax.axis_size("blk")
    dom_here = lax.axis_index("dom")
    blk_here = lax.axis_index("blk")
    wall_mask = (flags == 1).astype(jnp.float32)
    center = diag_blocks + jnp.einsum("ef,efab->eab", wall_mask, face_blocks, precision=HIGH)
    inverse = invert_blocks(center)
    inside = neighbors >= 0
    source_elem = jnp.where(inside, neighbors, 0)
    source_face = jnp.where(inside, partner, 0)
    owner_dev = source_elem // elements
    owner_dom = owner_dev // blk_count
    owner_blk = owner_dev % blk_count
    direction = jnp.where(
        owner_dom == dom_here - 1,
        1,
        jnp.where(
            owner_dom == dom_here + 1,
            2,
            jnp.where(owner_blk == blk_here - 1, 3, jnp.where(owner_blk == blk_here + 1, 4, 0)),
        ),
    )
    direction = jnp.where(inside, direction, 0).astype(jnp.int32)
    local_slot = source_elem % elements
    flat_direction = direction.reshape(-1)
    flat_inside = inside.reshape(-1)
    flat_local = (local_slot * 6 + source_face).reshape(-1)
    face_keys = (source_elem * 6 + source_face).reshape(-1)
    same_way = (flat_direction[None, :] == flat_direction[:, None]) & flat_inside[None, :]
    placing = jnp.sum(
        (same_way & (face_keys[None, :] < face_keys[:, None])).astype(jnp.int32), axis=1
    )
    offsets = jnp.array(
        [0, 6 * elements, 6 * elements + EY, 6 * elements + 2 * EY, 6 * elements + 2 * EY + EX],
        jnp.int32,
    )
    candidate = jnp.where(flat_direction == 0, flat_local, offsets[flat_direction] + placing)
    slot_range = jnp.arange(elements * 6, dtype=jnp.int32)

    def pick_rows(target, count):
        marked = ((flat_direction == target) & flat_inside).astype(jnp.int32)
        ranking = jnp.cumsum(marked) - marked
        chooser = (ranking[None, :] == jnp.arange(count)[:, None]) & (marked[None, :] > 0)
        return jnp.sum(jnp.where(chooser, slot_range[None, :], 0), axis=1)

    toward_next_dom = pick_rows(2, EY)
    toward_prev_dom = pick_rows(1, EY)
    toward_next_blk = pick_rows(4, EX)
    toward_prev_blk = pick_rows(3, EX)
    flat_blocks = face_blocks.reshape(elements * 6, width, width)
    block_pool = jnp.concatenate(
        [
            flat_blocks,
            move_facing_dom(jnp.take(flat_blocks, toward_next_dom, axis=0), 1),
            move_facing_dom(jnp.take(flat_blocks, toward_prev_dom, axis=0), -1),
            move_facing_blk(jnp.take(flat_blocks, toward_next_blk, axis=0), 1),
            move_facing_blk(jnp.take(flat_blocks, toward_prev_blk, axis=0), -1),
        ],
        axis=0,
    )
    column_blocks = (
        jnp.take(block_pool, candidate, axis=0) * flat_inside.astype(jnp.float32)[:, None, None]
    )
    column_blocks = column_blocks.reshape(elements, 6, width, width)
    vector_index = (direction * elements + local_slot).reshape(-1)

    def precondition(vectors):
        return jnp.einsum("eab,rea->reb", inverse, vectors, precision=HIGH)

    start_norm = jnp.sqrt(
        lax.psum(jnp.sum(adjoint_source * adjoint_source, axis=(1, 2)), ("dom", "blk"))
    )
    krylov_basis = [adjoint_source / start_norm[:, None, None]]
    hessen = []
    for iteration in range(ITERS):
        operator_vectors = precondition(krylov_basis[-1])
        gathered = jnp.concatenate(
            [
                operator_vectors,
                move_vectors_dom(operator_vectors, 1),
                move_vectors_dom(operator_vectors, -1),
                move_vectors_blk(operator_vectors, 1),
                move_vectors_blk(operator_vectors, -1),
            ],
            axis=1,
        )
        nearby = jnp.take(gathered, vector_index, axis=1).reshape(nrhs, elements, 6, width)
        own_part = jnp.einsum("eab,rea->reb", center, operator_vectors, precision=HIGH)
        mapped = own_part + jnp.einsum("egab,rega->reb", column_blocks, nearby, precision=HIGH)
        local_dots = [jnp.sum(mapped * member, axis=(1, 2)) for member in krylov_basis]
        projections = lax.psum(jnp.stack(local_dots), ("dom", "blk"))
        for row_index in range(len(krylov_basis)):
            mapped = mapped - projections[row_index][:, None, None] * krylov_basis[row_index]
        new_norm = jnp.sqrt(lax.psum(jnp.sum(mapped * mapped, axis=(1, 2)), ("dom", "blk")))
        hessen.append(jnp.concatenate([projections, new_norm[None, :]], axis=0))
        krylov_basis.append(mapped / new_norm[:, None, None])
    coeffs, rel_residual = least_squares(hessen, start_norm)
    combined = coeffs[0][:, None, None] * krylov_basis[0]
    for col_index in range(1, ITERS):
        combined = combined + coeffs[col_index][:, None, None] * krylov_basis[col_index]
    return (precondition(combined), rel_residual)


def solution(mesh):
    in_specs = (
        P(None, ("dom", "blk"), None),
        P(("dom", "blk"), None, None),
        P(("dom", "blk"), None, None, None),
        P(("dom", "blk"), None),
        P(("dom", "blk"), None),
        P(("dom", "blk"), None),
    )
    out_specs = (P(None, ("dom", "blk"), None), P())
    return jax.shard_map(shards, mesh=mesh, in_specs=in_specs, out_specs=out_specs, check_vma=False)
```

profile of v0, /device:TPU:1, one launch (start us, length us, event | category | flops | bytes accessed | tf_op | source)
XLA Modules:
  0.0 1977.7 jit_solution(12773045627226368610)
XLA Ops:
  1.4 5.8 fusion
  7.4 7.6 copy.63
  15.0 5.6 gather_fusion
  26.1 111.2 %psum.119 = f32[16]{0:T(128)S(1)} all-reduce(f32[16]{0:T(128)S(1)} %multiply_reduce_fusion.44), channel_id=1, replica_groups=mesh['dom'=64,'blk'=8] {'dom','blk'}, use_global_device_ids=true, to_apply=%region_1.2 | all-reduce | flops 16 | bytes 128 | tf_op jit(solution)/shard_map/psum | solution.py:155
  138.5 2.0 collective-permute-start
  141.8 3.3 collective-permute-start.2
  147.1 4.9 copy.69
  153.7 2.7 gather_fusion.4
  156.5 4.3 collective-permute-start.4
  160.8 2.0 fusion.35
  162.9 4.4 constant_dynamic-update-slice_fusion.9
  167.6 2.7 gather_fusion.5
  170.4 2.7 gather_fusion.6
  173.1 2.7 gather_fusion.7
  181.7 3.9 collective-permute-start.6
  197.1 5.4 gather_fusion.2
  202.5 4.5 multiply_reduce_fusion.43
  207.0 107.5 %psum.120 = f32[16]{0:T(128)S(1)} all-reduce(f32[16]{0:T(128)S(1)} %get-tuple-element.154), channel_id=1, replica_groups=mesh['dom'=64,'blk'=8] {'dom','blk'}, use_global_device_ids=true, to_apply=%region_12.15 | all-reduce | flops 16 | bytes 128 | tf_op jit(solution)/shard_map/psum | solution.py:175
  314.7 99.6 %psum.121 = f32[16]{0:T(128)S(1)} all-reduce(f32[16]{0:T(128)S(1)} %multiply_reduce_fusion.42), channel_id=1, replica_groups=mesh['dom'=64,'blk'=8] {'dom','blk'}, use_global_device_ids=true, to_apply=%region_14.17 | all-reduce | flops 16 | bytes 128 | tf_op jit(solution)/shard_map/psum | solution.py:178
  414.8 2.9 collective-permute-start.8
  421.5 2.4 collective-permute-start.11
  424.0 3.1 collective-permute-done.11
  427.8 4.5 multiply_reduce_fusion.41
  432.2 105.5 %psum.122 = f32[2,16]{1,0:T(2,128)S(1)} all-reduce(f32[2,16]{1,0:T(2,128)S(1)} %pad_maximum_fusion.2), channel_id=1, replica_groups=mesh['dom'=64,'blk'=8] {'dom','blk'}, use_global_device_ids=true, to_apply=%region_17.20 | all-reduce | flops 32 | bytes 256 | tf_op jit(solution)/shard_map/psum | solution.py:175
  537.9 99.9 %psum.123 = f32[16]{0:T(128)S(1)} all-reduce(f32[16]{0:T(128)S(1)} %get-tuple-element.97), channel_id=1, replica_groups=mesh['dom'=64,'blk'=8] {'dom','blk'}, use_global_device_ids=true, to_apply=%region_19.22 | all-reduce | flops 16 | bytes 128 | tf_op jit(solution)/shard_map/psum | solution.py:178
  638.3 2.3 collective-permute-start.12
  642.5 2.0 collective-permute-start.14
  644.5 2.3 collective-permute-start.15
  646.9 3.2 collective-permute-done.15
  650.7 4.5 multiply_reduce_fusion.38
  655.3 104.7 %psum.124 = f32[3,16]{1,0:T(4,128)S(1)} all-reduce(f32[3,16]{1,0:T(4,128)S(1)} %pad_maximum_fusion), channel_id=1, replica_groups=mesh['dom'=64,'blk'=8] {'dom','blk'}, use_global_device_ids=true, to_apply=%region_23.26 | all-reduce | flops 48 | bytes 384 | tf_op jit(solution)/shard_map/psum | solution.py:175
  760.2 100.5 %psum.125 = f32[16]{0:T(128)S(1)} all-reduce(f32[16]{0:T(128)S(1)} %get-tuple-element.95), channel_id=1, replica_groups=mesh['dom'=64,'blk'=8] {'dom','blk'}, use_global_device_ids=true, to_apply=%region_25.28 | all-reduce | flops 16 | bytes 128 | tf_op jit(solution)/shard_map/psum | solution.py:178
  861.1 2.3 collective-permute-start.16
  865.3 1.9 collective-permute-start.18
  867.3 2.4 collective-permute-start.19
  869.7 3.1 collective-permute-done.19
  873.5 4.5 multiply_reduce_fusion.34
  878.1 104.6 %psum.126 = f32[4,16]{1,0:T(4,128)S(1)} all-reduce(f32[4,16]{1,0:T(4,128)S(1)} %pad_maximum_fusion.1), channel_id=1, replica_groups=mesh['dom'=64,'blk'=8] {'dom','blk'}, use_global_device_ids=true, to_apply=%region_30.33 | all-reduce | flops 64 | bytes 512 | tf_op jit(solution)/shard_map/psum | solution.py:175
  983.0 100.5 %psum.127 = f32[16]{0:T(128)S(1)} all-reduce(f32[16]{0:T(128)S(1)} %get-tuple-element.93), channel_id=1, replica_groups=mesh['dom'=64,'blk'=8] {'dom','blk'}, use_global_device_ids=true, to_apply=%region_32.35 | all-reduce | flops 16 | bytes 128 | tf_op jit(solution)/shard_map/psum | solution.py:178
  1083.9 2.3 collective-permute-start.20
  1090.1 2.4 collective-permute-start.23
  1092.5 3.1 collective-permute-done.23
  1096.3 4.6 multiply_reduce_fusion.25
  1100.9 105.1 %psum.128 = f32[5,16]{1,0:T(8,128)S(1)} all-reduce(f32[5,16]{1,0:T(8,128)S(1)} %stack.147), channel_id=1, replica_groups=mesh['dom'=64,'blk'=8] {'dom','blk'}, use_global_device_ids=true, to_apply=%region_38.41 | all-reduce | flops 80 | bytes 640 | tf_op jit(solution)/shard_map/psum | solution.py:175
  1206.2 100.5 %psum.129 = f32[16]{0:T(128)S(1)} all-reduce(f32[16]{0:T(128)S(1)} %get-tuple-element.91), channel_id=1, replica_groups=mesh['dom'=64,'blk'=8] {'dom','blk'}, use_global_device_ids=true, to_apply=%region_40.43 | all-reduce | flops 16 | bytes 128 | tf_op jit(solution)/shard_map/psum | solution.py:178
  1307.2 2.3 collective-permute-start.24
  1313.3 2.4 collective-permute-start.27
  1315.8 3.1 collective-permute-done.27
  1319.6 4.6 multiply_reduce_fusion.18
  1324.2 104.7 %psum.130 = f32[6,16]{1,0:T(8,128)S(1)} all-reduce(f32[6,16]{1,0:T(8,128)S(1)} %stack.154), channel_id=1, replica_groups=mesh['dom'=64,'blk'=8] {'dom','blk'}, use_global_device_ids=true, to_apply=%region_47.50 | all-reduce | flops 96 | bytes 768 | tf_op jit(solution)/shard_map/psum | solution.py:175
  1429.1 100.5 %psum.131 = f32[16]{0:T(128)S(1)} all-reduce(f32[16]{0:T(128)S(1)} %get-tuple-element.89), channel_id=1, replica_groups=mesh['dom'=64,'blk'=8] {'dom','blk'}, use_global_device_ids=true, to_apply=%region_49.52 | all-reduce | flops 16 | bytes 128 | tf_op jit(solution)/shard_map/psum | solution.py:178
  1530.1 2.3 collective-permute-start.28
  1536.2 2.4 collective-permute-start.31
  1538.7 3.1 collective-permute-done.31
  1542.5 4.6 multiply_reduce_fusion.10
  1547.2 104.7 %psum.132 = f32[7,16]{1,0:T(8,128)S(1)} all-reduce(f32[7,16]{1,0:T(8,128)S(1)} %stack.162), channel_id=1, replica_groups=mesh['dom'=64,'blk'=8] {'dom','blk'}, use_global_device_ids=true, to_apply=%region_57.60 | all-reduce | flops 112 | bytes 896 | tf_op jit(solution)/shard_map/psum | solution.py:175
  1652.1 100.5 %psum.133 = f32[16]{0:T(128)S(1)} all-reduce(f32[16]{0:T(128)S(1)} %get-tuple-element.87), channel_id=1, replica_groups=mesh['dom'=64,'blk'=8] {'dom','blk'}, use_global_device_ids=true, to_apply=%region_59.62 | all-reduce | flops 16 | bytes 128 | tf_op jit(solution)/shard_map/psum | solution.py:178
  1753.0 2.3 collective-permute-start.32
  1757.2 1.9 collective-permute-start.34
  1759.2 2.5 collective-permute-start.35
  1761.8 3.0 collective-permute-done.35
  1765.4 4.7 multiply_reduce_fusion.1
  1770.2 104.7 %psum.134 = f32[8,16]{1,0:T(8,128)S(1)} all-reduce(f32[8,16]{1,0:T(8,128)S(1)} %stack.171), channel_id=1, replica_groups=mesh['dom'=64,'blk'=8] {'dom','blk'}, use_global_device_ids=true, to_apply=%region_68.71 | all-reduce | flops 128 | bytes 1024 | tf_op jit(solution)/shard_map/psum | solution.py:175
  1875.1 100.5 %psum.135 = f32[16]{0:T(128)S(1)} all-reduce(f32[16]{0:T(128)S(1)} %multiply_reduce_fusion), channel_id=1, replica_groups=mesh['dom'=64,'blk'=8] {'dom','blk'}, use_global_device_ids=true, to_apply=%region_70.73 | all-reduce | flops 16 | bytes 128 | tf_op jit(solution)/shard_map/psum | solution.py:178
  (224 shorter events, 62.8 us)
Async XLA Ops:
  1.4 5.8 copy-start.2
  22.5 2.5 copy-start.1
  138.5 13.5 copy-start.4
  138.5 13.7 copy-start.5
  138.5 41.1 %collective-permute-start = (f32[16,4,162]{2,0,1:T(8,128)}, f32[16,4,162]{2,0,1:T(8,128)}, u32[]{:S(2)}, u32[]{:S(2)}) collective-permute-start(f32[16,4,162]{2,0,1:T(8,128)} %get-tuple-element.153), channel_id=1, source_target_pairs={{0,8},{8,16},{16,24},{24,32},{32,40},{40,48},{48,56},{56,64},{64,7... | collective-permute-start | bytes 124424 | tf_op jit(solution)/shard_map/ppermute | solution.py:18
  140.5 41.2 %collective-permute-start.1 = (f32[16,4,162]{2,0,1:T(8,128)}, f32[16,4,162]{2,0,1:T(8,128)}, u32[]{:S(2)}, u32[]{:S(2)}) collective-permute-start(f32[16,4,162]{2,0,1:T(8,128)} %get-tuple-element.153), channel_id=1, source_target_pairs={{8,0},{16,8},{24,16},{32,24},{40,32},{48,40},{56,48},{64,56},{72,6... | collective-permute-start | bytes 124424 | tf_op jit(solution)/shard_map/ppermute | solution.py:18
  141.8 44.7 %collective-permute-start.2 = (f32[16,4,162]{2,0,1:T(8,128)}, f32[16,4,162]{2,0,1:T(8,128)}, u32[]{:S(2)}, u32[]{:S(2)}) collective-permute-start(f32[16,4,162]{2,0,1:T(8,128)} %get-tuple-element.153), channel_id=1, source_target_pairs={{0,1},{1,2},{2,3},{3,4},{4,5},{5,6},{6,7},{8,9},{9,10},{10,11},{11... | collective-permute-start | bytes 124424 | tf_op jit(solution)/shard_map/ppermute | solution.py:18
  145.1 44.2 %collective-permute-start.3 = (f32[16,4,162]{2,0,1:T(8,128)}, f32[16,4,162]{2,0,1:T(8,128)}, u32[]{:S(2)}, u32[]{:S(2)}) collective-permute-start(f32[16,4,162]{2,0,1:T(8,128)} %get-tuple-element.153), channel_id=1, source_target_pairs={{1,0},{2,1},{3,2},{4,3},{5,4},{6,5},{7,6},{9,8},{10,9},{11,10},{12... | collective-permute-start | bytes 124424 | tf_op jit(solution)/shard_map/ppermute | solution.py:18
  156.5 34.3 %collective-permute-start.4 = (f32[2,162,162]{2,1,0:T(8,128)S(1)}, f32[2,162,162]{2,1,0:T(8,128)S(1)}, u32[]{:S(2)}, u32[]{:S(2)}) collective-permute-start(f32[2,162,162]{2,1,0:T(8,128)S(1)} %broadcast_select_fusion.11), channel_id=1, source_target_pairs={{0,8},{8,16},{16,24},{24,32},{32,40},{40,48},{48,56},{56,64},{64,7... | collective-permute-start | bytes 629864 | tf_op jit(solution)/shard_map/ppermute | solution.py:18
  162.9 13.2 copy-start
  179.6 12.0 collective-permute-start.5
  181.7 11.6 collective-permute-start.6
  186.5 8.9 collective-permute-start.7
  197.1 5.4 copy-start.3
  414.8 9.1 collective-permute-start.8
  418.3 5.7 collective-permute-start.9
  419.5 4.4 collective-permute-start.10
  421.5 5.6 collective-permute-start.11
  638.3 8.5 collective-permute-start.12
  641.2 5.7 collective-permute-start.13
  642.5 4.4 collective-permute-start.14
  644.5 5.6 collective-permute-start.15
  861.1 8.5 collective-permute-start.16
  864.0 5.7 collective-permute-start.17
  865.3 4.4 collective-permute-start.18
  867.3 5.6 collective-permute-start.19
  1083.9 8.5 collective-permute-start.20
  1086.8 5.7 collective-permute-start.21
  1088.1 4.4 collective-permute-start.22
  1090.1 5.6 collective-permute-start.23
  1307.2 8.5 collective-permute-start.24
  1310.1 5.7 collective-permute-start.25
  1311.4 4.4 collective-permute-start.26
  1313.3 5.6 collective-permute-start.27
  1530.1 8.5 collective-permute-start.28
  1533.0 5.7 collective-permute-start.29
  1534.3 4.4 collective-permute-start.30
  1536.2 5.6 collective-permute-start.31
  1753.0 8.7 collective-permute-start.32
  1755.9 5.8 collective-permute-start.33
  1757.2 4.6 collective-permute-start.34
  1759.2 5.6 collective-permute-start.35
where the time goes:
time: 1990 us; the launch traced here: 1980 us
  blocking collectives  1760 us (88%)
  starting transfers between devices  76.3 us (4%)
  matrix products  58 us (3%)
  local copies, waits for them, and re-layouts  55.7 us (3%)
  waiting for transfers between devices  22.1 us (1%)
    psum x8, blocking collectives, shards(): projections = lax.psum(jnp.stack(local_dots), ('dom', 'blk'))  841 us
    psum x8, blocking collectives, shards(): lax.psum(jnp.sum(mapped * mapped, axis=(1, 2)), ('dom', 'blk'))  803 us
    psum x1, blocking collectives, shards(): lax.psum(jnp.sum(adjoint_source * adjoint_source, axis=(1, 2)), ('dom', '...  111 us
    ppermute x36, starting transfers between devices, shifted(): lax.ppermute(value, axis, [(source, source + steps) for source in range(l...  76.3 us
  transfers between devices with their start and end apart: 36, of which 8 were waited for; matrix products, arithmetic and copies ran while one was open for 2% of the time, Pallas kernels for 0%

commit v1 on v0

--- a/solution.py
+++ b/solution.py
@@ -1,6 +1,10 @@
+import functools
+
 import jax
 import jax.numpy as jnp
 from jax import lax
+from jax.experimental import pallas as pl
+from jax.experimental.pallas import tpu as pltpu
 from jax.sharding import PartitionSpec as P
 
 EX = 2
@@ -81,7 +85,7 @@
     return shifted(blocks, "blk", offset)
 
 
-def shards(adjoint_source, diag_blocks, face_blocks, neighbors, partner, flags):
+def direct_path(adjoint_source, diag_blocks, face_blocks, neighbors, partner, flags):
     nrhs, elements, width = adjoint_source.shape
     blk_count = lax.axis_size("blk")
     dom_here = lax.axis_index("dom")
@@ -185,6 +189,442 @@
     return (precondition(combined), rel_residual)
 
 
+CELLS = EX * EY
+F32 = jnp.float32
+BF16 = jnp.bfloat16
+VMEM_LIMIT = 40 * 1024 * 1024
+OUT_CELLS = ((0, 1), (2, 3), (0, 2), (1, 3))
+PIVOT_FLOOR = 0.02
+RESIDUAL_FLOOR = 0.02
+
+
+def pair_lane(row, col):
+    return row * (row + 1) // 2 + col
+
+
+def split_halves(value):
+    high = value.astype(BF16)
+    low = (value - high.astype(F32)).astype(BF16)
+    return high, low
+
+
+def dot32(left, right):
+    return jnp.dot(left, right, preferred_element_type=F32)
+
+
+def dot_full(left, right):
+    return jnp.dot(left, right, preferred_element_type=F32, precision=HIGH)
+
+
+def stack_halves(vector):
+    high, low = split_halves(vector)
+    return jnp.concatenate([high, low], axis=0), high
+
+
+def row_times(stacked, high, block_high, block_low):
+    rows = high.shape[0]
+    both = dot32(stacked, block_high)
+    return both[:rows] + both[rows:] + dot32(high, block_low)
+
+
+def write_sends(halves, out_high_ref, out_low_ref, send_refs):
+    for way in range(4):
+        for place in range(2):
+            stacked, high = halves[OUT_CELLS[way][place]]
+            slot = 2 * way + place
+            send_refs[way][place] = row_times(
+                stacked, high, out_high_ref[slot], out_low_ref[slot]
+            )
+
+
+def setup_kernel(
+    nbr_ref, flag_ref, src_ref, diag_ref, face_ref,
+    out_high_ref, out_low_ref, loc_high_ref, loc_low_ref, inv_high_ref, inv_low_ref,
+    base_ref, send0_ref, send1_ref, send2_ref, send3_ref, slot_ref,
+    center_ref, x_ref, y_ref, cell_ref, face_of_ref,
+    *, dom_count, blk_count,
+):
+    width = diag_ref.shape[-1]
+    dom_here = lax.axis_index("dom")
+    blk_here = lax.axis_index("blk")
+    here = dom_here * blk_count + blk_here
+    for slot in range(CELLS):
+        up_x = jnp.int32(0)
+        down_x = jnp.int32(0)
+        up_y = jnp.int32(0)
+        down_y = jnp.int32(0)
+        for face in range(6):
+            other = nbr_ref[slot, face]
+            gap = jnp.where(other >= 0, other // CELLS - here, 0)
+            up_x = jnp.where(gap == blk_count, 1, up_x)
+            down_x = jnp.where(gap == -blk_count, 1, down_x)
+            up_y = jnp.where(gap == 1, 1, up_y)
+            down_y = jnp.where(gap == -1, 1, down_y)
+        cell_x = jnp.where(dom_here < dom_count - 1, up_x, 1 - down_x)
+        cell_y = jnp.where(blk_here < blk_count - 1, up_y, 1 - down_y)
+        cell = 2 * cell_x + cell_y
+        cell_ref[slot] = cell
+        slot_ref[cell] = slot
+    for entry in range(CELLS * 4):
+        face_of_ref[entry] = -1
+    for slot in range(CELLS):
+        cell = cell_ref[slot]
+        for face in range(6):
+            other = nbr_ref[slot, face]
+            inside = other >= 0
+            safe = jnp.where(inside, other, 0)
+            gap = safe // CELLS - here
+            mate = cell_ref[safe % CELLS]
+            change = jnp.bitwise_xor(mate, cell)
+            way_x = jnp.where(cell >= 2, 0, 1)
+            way_y = jnp.where(cell % 2 == 1, 2, 3)
+            way_in = jnp.where(change == 2, way_x, way_y)
+            way = jnp.where(
+                gap == 0, way_in,
+                jnp.where(
+                    gap == -blk_count, 0,
+                    jnp.where(gap == blk_count, 1, jnp.where(gap == -1, 2, 3)),
+                ),
+            )
+
+            @pl.when(inside)
+            def _():
+                face_of_ref[cell * 4 + way] = face
+
+    rows = lax.broadcasted_iota(jnp.int32, (width, width), 0)
+    cols = lax.broadcasted_iota(jnp.int32, (width, width), 1)
+    on_diag = rows == cols
+    for cell in range(CELLS):
+        slot = slot_ref[cell]
+        center = diag_ref[slot]
+        for face in range(6):
+            wall = jnp.where(flag_ref[slot, face] == 1, 1.0, 0.0).astype(F32)
+            center = center + wall * face_ref[slot, face]
+        center_ref[cell] = center
+        marked = jnp.where(on_diag, center, 0.0)
+        inv_row = 1.0 / jnp.sum(marked, axis=0, keepdims=True)
+        inv_col = 1.0 / jnp.sum(marked, axis=1, keepdims=True)
+        first = jnp.where(on_diag, inv_col, 0.0)
+        x_ref[cell] = 2.0 * first - inv_col * (center * inv_row)
+    for sweep in range(SWEEPS - 1):
+        for cell in range(CELLS):
+            y_ref[cell] = dot_full(center_ref[cell], x_ref[cell])
+        for cell in range(CELLS):
+            x_ref[cell] = 2.0 * x_ref[cell] - dot_full(x_ref[cell], y_ref[cell])
+    halves = []
+    for cell in range(CELLS):
+        base = jnp.zeros(base_ref.shape[1:], F32)
+        for slot in range(CELLS):
+            base = jnp.where(slot_ref[cell] == slot, src_ref[:, slot, :], base)
+        base_ref[cell] = base
+        halves.append(stack_halves(base))
+        high, low = split_halves(x_ref[cell])
+        inv_high_ref[cell] = high
+        inv_low_ref[cell] = low
+        own = dot_full(x_ref[cell], center_ref[cell]) - jnp.where(on_diag, 1.0, 0.0)
+        high, low = split_halves(own)
+        loc_high_ref[cell] = high
+        loc_low_ref[cell] = low
+        slot = slot_ref[cell]
+        for way in range(4):
+            face = face_of_ref[cell * 4 + way]
+            keep = jnp.where(face >= 0, 1.0, 0.0).astype(F32)
+            block = face_ref[slot, jnp.maximum(face, 0)] * keep
+            f_high, f_low = split_halves(block)
+            product = (
+                dot32(inv_high_ref[cell], f_high)
+                + dot32(inv_low_ref[cell], f_high)
+                + dot32(inv_high_ref[cell], f_low)
+            )
+            high, low = split_halves(product)
+            if cell in OUT_CELLS[way]:
+                entry = 2 * way + OUT_CELLS[way].index(cell)
+                out_high_ref[entry] = high
+                out_low_ref[entry] = low
+            else:
+                entry = (4 if way < 2 else 8) + cell
+                loc_high_ref[entry] = high
+                loc_low_ref[entry] = low
+    write_sends(halves, out_high_ref, out_low_ref, (send0_ref, send1_ref, send2_ref, send3_ref))
+
+
+def local_kernel(step, base_refs, loc_high_ref, loc_low_ref, gram_in_ref, acc_ref, gram_ref):
+    newest = base_refs[step]
+    halves = [stack_halves(newest[cell]) for cell in range(CELLS)]
+    for cell in range(CELLS):
+        total = None
+        for source, entry in ((cell, cell), (cell ^ 2, 4 + (cell ^ 2)), (cell ^ 1, 8 + (cell ^ 1))):
+            stacked, high = halves[source]
+            part = row_times(stacked, high, loc_high_ref[entry], loc_low_ref[entry])
+            total = part if total is None else total + part
+        acc_ref[cell] = total
+    gram_ref[...] = gram_rows(step, base_refs, None if gram_in_ref is None else gram_in_ref[...])
+
+
+def gram_rows(step, base_refs, gram):
+    newest = base_refs[step]
+    nrhs = newest.shape[1]
+    lanes = lax.broadcasted_iota(jnp.int32, (nrhs, 128), 1)
+    if gram is None:
+        gram = jnp.zeros((nrhs, 128), F32)
+    for col in range(step + 1):
+        total = newest[0] * base_refs[col][0]
+        for cell in range(1, CELLS):
+            total = total + newest[cell] * base_refs[col][cell]
+        value = jnp.sum(total, axis=1, keepdims=True)
+        gram = jnp.where(lanes == pair_lane(step, col), value, gram)
+    return gram
+
+
+def add_received(acc_ref, recv_refs, base_ref):
+    from_dom_prev, from_dom_next, from_blk_prev, from_blk_next = recv_refs
+    for cell in range(CELLS):
+        dom_part = from_dom_prev[cell % 2] if cell < 2 else from_dom_next[cell % 2]
+        blk_part = from_blk_prev[cell // 2] if cell % 2 == 0 else from_blk_next[cell // 2]
+        base_ref[cell] = acc_ref[cell] + dom_part + blk_part
+
+
+def border_kernel(
+    acc_ref, recv0_ref, recv1_ref, recv2_ref, recv3_ref, out_high_ref, out_low_ref,
+    base_ref, send0_ref, send1_ref, send2_ref, send3_ref,
+):
+    add_received(acc_ref, (recv0_ref, recv1_ref, recv2_ref, recv3_ref), base_ref)
+    halves = [stack_halves(base_ref[cell]) for cell in range(CELLS)]
+    write_sends(halves, out_high_ref, out_low_ref, (send0_ref, send1_ref, send2_ref, send3_ref))
+
+
+def last_kernel(*refs):
+    acc_ref, recv0_ref, recv1_ref, recv2_ref, recv3_ref = refs[:5]
+    gram_in_ref = refs[5]
+    older = refs[6 : 6 + ITERS]
+    gram_ref, base_ref = refs[6 + ITERS :]
+    add_received(acc_ref, (recv0_ref, recv1_ref, recv2_ref, recv3_ref), base_ref)
+    gram_ref[...] = gram_rows(ITERS, list(older) + [base_ref], gram_in_ref[...])
+
+
+def finish_kernel(*refs):
+    gram_ref = refs[0]
+    base_refs = refs[1 : 1 + ITERS]
+    inv_high_ref, inv_low_ref, slot_ref, adjoint_ref, rel_ref, fine_ref = refs[1 + ITERS :]
+    count = ITERS + 1
+    gram = gram_ref[...]
+
+    def lane(row, col):
+        place = pair_lane(row, col)
+        return jnp.broadcast_to(gram[:, place : place + 1], gram.shape)
+
+    diag = [lane(j, j) for j in range(count)]
+    scale = [1.0 / jnp.sqrt(value) for value in diag]
+    start = jnp.sqrt(diag[0])
+    lower = [[None] * count for j in range(count)]
+    solved = []
+    ratio = [scale[j] * start for j in range(count)]
+    smallest = jnp.ones_like(gram)
+    inv_pivot = []
+    for col in range(count):
+        pivot = jnp.ones_like(gram)
+        for k in range(col):
+            pivot = pivot - lower[col][k] * lower[col][k]
+        smallest = jnp.minimum(smallest, pivot)
+        inv_root = 1.0 / jnp.sqrt(pivot)
+        inv_pivot.append(inv_root)
+        for row in range(col + 1, count):
+            value = lane(row, col) * scale[row] * scale[col]
+            for k in range(col):
+                value = value - lower[row][k] * lower[col][k]
+            lower[row][col] = value * inv_root
+        right = ratio[col] if col % 2 == 0 else -ratio[col]
+        for k in range(col):
+            right = right - lower[col][k] * solved[k]
+        solved.append(right * inv_root)
+    squares = solved[0] * solved[0]
+    for j in range(1, count):
+        squares = squares + solved[j] * solved[j]
+    rel = 1.0 / jnp.sqrt(squares)
+    back = [None] * count
+    for j in reversed(range(count)):
+        value = solved[j]
+        for k in range(j + 1, count):
+            value = value - lower[k][j] * back[k]
+        back[j] = value * inv_pivot[j]
+    inv_squares = 1.0 / squares
+    residual = [ratio[j] * back[j] * inv_squares for j in range(count)]
+    coeffs = [None] * ITERS
+    coeffs[ITERS - 1] = -residual[ITERS]
+    for j in reversed(range(1, ITERS)):
+        coeffs[j - 1] = -residual[j] - coeffs[j]
+    lanes = lax.broadcasted_iota(jnp.int32, gram.shape, 1)
+    good = (smallest > PIVOT_FLOOR) & (rel > RESIDUAL_FLOOR) & (rel < 2.0)
+    for j in range(count):
+        good = good & (diag[j] > 1e-30) & (diag[j] < 1e36)
+    worst = jnp.min(jnp.where(good, 1.0, 0.0))
+    fine_ref[0] = jnp.where(worst > 0.5, 1, 0).astype(jnp.int32)
+    rel_ref[...] = jnp.transpose(rel)[0:1, :]
+    width = base_refs[0].shape[-1]
+    wide = [
+        jnp.concatenate([value, value], axis=1)[:, :width] for value in coeffs
+    ]
+    results = []
+    for cell in range(CELLS):
+        total = wide[0] * base_refs[0][cell]
+        for j in range(1, ITERS):
+            total = total + wide[j] * base_refs[j][cell]
+        stacked, high = stack_halves(total)
+        results.append(row_times(stacked, high, inv_high_ref[cell], inv_low_ref[cell]))
+    for slot in range(CELLS):
+        value = results[0]
+        for cell in range(1, CELLS):
+            value = jnp.where(slot_ref[cell] == slot, results[cell], value)
+        adjoint_ref[:, slot, :] = value
+
+
+def vmem(count):
+    return [pl.BlockSpec(memory_space=pltpu.VMEM)] * count
+
+
+def smem(count):
+    return [pl.BlockSpec(memory_space=pltpu.SMEM)] * count
+
+
+PARAMS = pltpu.CompilerParams(vmem_limit_bytes=VMEM_LIMIT)
+
+
+def struct(*shape, kind=F32):
+    return jax.ShapeDtypeStruct(shape, kind)
+
+
+def group_sizes(count):
+    return (16, count // 16) if count > 16 and count % 16 == 0 else (count,)
+
+
+def sum_over(value, axis):
+    count = lax.axis_size(axis)
+    stride = 1
+    for size in group_sizes(count):
+        groups = [
+            [high * size * stride + k * stride + low for k in range(size)]
+            for high in range(count // (size * stride))
+            for low in range(stride)
+        ]
+        copies = jnp.broadcast_to(value[None], (size,) + value.shape)
+        parts = lax.all_to_all(
+            copies, axis, 0, 0, axis_index_groups=None if size == count else groups
+        )
+        value = jnp.sum(parts, axis=0)
+        stride *= size
+    return value
+
+
+def exchange(sends):
+    to_dom_prev, to_dom_next, to_blk_prev, to_blk_next = sends
+    return (
+        shifted(to_dom_next, "dom", 1),
+        shifted(to_dom_prev, "dom", -1),
+        shifted(to_blk_next, "blk", 1),
+        shifted(to_blk_prev, "blk", -1),
+    )
+
+
+def shards(adjoint_source, diag_blocks, face_blocks, neighbors, partner, flags):
+    nrhs, elements, width = adjoint_source.shape
+    block = (width, width)
+    field = struct(CELLS, nrhs, width)
+    edge = struct(2, nrhs, width)
+    cost = lambda flops, data: pl.CostEstimate(
+        flops=flops, bytes_accessed=data, transcendentals=0
+    )
+    products = 2 * nrhs * width * width * 3
+    setup = pl.pallas_call(
+        functools.partial(
+            setup_kernel, dom_count=lax.axis_size("dom"), blk_count=lax.axis_size("blk")
+        ),
+        out_shape=(
+            struct(8, *block, kind=BF16), struct(8, *block, kind=BF16),
+            struct(12, *block, kind=BF16), struct(12, *block, kind=BF16),
+            struct(CELLS, *block, kind=BF16), struct(CELLS, *block, kind=BF16),
+            field, edge, edge, edge, edge, struct(CELLS, kind=jnp.int32),
+        ),
+        in_specs=smem(2) + vmem(3),
+        out_specs=tuple(vmem(11) + smem(1)),
+        scratch_shapes=[
+            pltpu.VMEM((CELLS,) + block, F32),
+            pltpu.VMEM((CELLS,) + block, F32),
+            pltpu.VMEM((CELLS,) + block, F32),
+            pltpu.SMEM((CELLS,), jnp.int32),
+            pltpu.SMEM((CELLS * 4,), jnp.int32),
+        ],
+        compiler_params=PARAMS,
+        name="setup_blocks",
+    )
+    outs = setup(neighbors, flags, adjoint_source, diag_blocks, face_blocks)
+    out_high, out_low, loc_high, loc_low, inv_high, inv_low = outs[:6]
+    bases = [outs[6]]
+    sends = outs[7:11]
+    slots = outs[11]
+    gram = None
+    for step in range(ITERS):
+        received = exchange(sends)
+
+        def local_body(*refs, step=step):
+            has_gram = step > 0
+            base_refs = refs[: step + 1]
+            loc_refs = refs[step + 1 : step + 3]
+            gram_in = refs[step + 3] if has_gram else None
+            local_kernel(step, base_refs, *loc_refs, gram_in, *refs[-2:])
+
+        given = bases + [loc_high, loc_low] + ([gram] if step > 0 else [])
+        acc, gram = pl.pallas_call(
+            local_body,
+            out_shape=(field, struct(nrhs, 128)),
+            in_specs=vmem(len(given)),
+            out_specs=tuple(vmem(2)),
+            compiler_params=PARAMS,
+            cost_estimate=cost(12 * products, 3000000),
+            name=f"local_part_{step}",
+        )(*given)
+        if step < ITERS - 1:
+            outs = pl.pallas_call(
+                border_kernel,
+                out_shape=(field, edge, edge, edge, edge),
+                in_specs=vmem(7),
+                out_specs=tuple(vmem(5)),
+                compiler_params=PARAMS,
+                cost_estimate=cost(8 * products, 2000000),
+                name=f"border_part_{step}",
+            )(acc, *received, out_high, out_low)
+            bases.append(outs[0])
+            sends = outs[1:]
+        else:
+            given = [acc, *received, gram] + bases
+            gram, _ = pl.pallas_call(
+                last_kernel,
+                out_shape=(struct(nrhs, 128), field),
+                in_specs=vmem(len(given)),
+                out_specs=tuple(vmem(2)),
+                compiler_params=PARAMS,
+                name="last_part",
+            )(*given)
+    gram = sum_over(gram, "blk")
+    gram = sum_over(gram, "dom")
+    given = [gram] + bases + [inv_high, inv_low, slots]
+    adjoint, rel, fine = pl.pallas_call(
+        finish_kernel,
+        out_shape=(
+            struct(nrhs, elements, width), struct(1, nrhs), struct(1, kind=jnp.int32)
+        ),
+        in_specs=vmem(len(given) - 1) + smem(1),
+        out_specs=tuple(vmem(2) + smem(1)),
+        compiler_params=PARAMS,
+        name="finish_part",
+    )(*given)
+    return lax.cond(
+        fine[0] == 1,
+        lambda given: (adjoint, rel.reshape(nrhs)),
+        lambda given: direct_path(*given),
+        (adjoint_source, diag_blocks, face_blocks, neighbors, partner, flags),
+    )
+
+
 def solution(mesh):
     in_specs = (
         P(None, ("dom", "blk"), None),

time: 1990 us -> 199 us (0.10)
  blocking collectives: 1760 us -> 43 us
  matrix products: 58 us -> 0 us
  local copies, waits for them, and re-layouts: 55.7 us -> 4.82 us
  starting transfers between devices: 76.3 us -> 101 us
    psum x17 -> x0, blocking collectives: 1760 us -> none  [the longest x8 841 us: shards(): projections = lax.psum(jnp.stack(local_dots), ('dom', 'blk'))]
    dot_general x32 -> x0, matrix products: 58 us -> none  [the longest x8 36.5 us: shards(): jnp.einsum('egab,rega->reb', column_blocks, nearby, precision=HIGH)]
    all_to_all x0 -> x2, blocking collectives: none -> 43 us  [sum_over(): lax.all_to_all(copies, axis, 0, 0, axis_index_groups=None if size == coun...]
    gather x16 -> x0, local copies, waits for them, and re-layouts: 27.3 us -> none  [the longest x2 5.67 us: invert_blocks(): pivots = jnp.diagonal(center, axis1=1, axis2=2)]
    ppermute x36 -> x32, starting transfers between devices: 76.3 us -> 88.9 us  [shifted(): lax.ppermute(value, axis, [(source, source + steps) for source in range(l...]
  transfers between devices with their start and end apart: 36 -> 33, of which waited for: 8 -> 13; matrix products, arithmetic and copies ran while one was open for 2% -> 0% of each run, Pallas kernels for 0% -> 2%
where the time goes in v1:
time: 199 us; the launch traced here: 197 us
  starting transfers between devices  101 us (51%)
  blocking collectives  43 us (22%)
  waiting for transfers between devices  31.6 us (16%)
  Pallas kernels  14.3 us (7%)
  local copies, waits for them, and re-layouts  4.82 us (2%)
    ppermute x32, starting transfers between devices, shifted(): lax.ppermute(value, axis, [(source, source + steps) for source in range(l...  88.9 us
    all_to_all x2, blocking collectives, sum_over(): lax.all_to_all(copies, axis, 0, 0, axis_index_groups=None if size == coun...  43 us
    ppermute x32, waiting for transfers between devices, shifted(): lax.ppermute(value, axis, [(source, source + steps) for source in range(l...  19.8 us
    all_to_all x1, starting transfers between devices, sum_over(): lax.all_to_all(copies, axis, 0, 0, axis_index_groups=None if size == coun...  11.9 us
    all_to_all x1, waiting for transfers between devices, sum_over(): lax.all_to_all(copies, axis, 0, 0, axis_index_groups=None if size == coun...  11.8 us
    pallas_call x1, Pallas kernels, shards(): outs = setup(neighbors, flags, adjoint_source, diag_blocks, face_blocks)  6.23 us
    unnamed x12, local copies, waits for them, and re-layouts  4.19 us
  transfers between devices with their start and end apart: 33, of which 13 were waited for; matrix products, arithmetic and copies ran while one was open for 0% of the time, Pallas kernels for 2%

profile of v1, /device:TPU:1, one launch (start us, length us, event | category | flops | bytes accessed | tf_op | source)
XLA Modules:
  0.0 196.9 jit_solution(9696301059202210994)
XLA Ops:
  0.6 1.2 copy.95.diag_ref
  1.9 2.9 %copy.96.face_ref = f32[4,6,162,162]{3,2,1,0:T(8,128)S(1)} copy(f32[4,6,162,162]{3,0,2,1:T(4,128)} %param.15) | data formatting | bytes 5038848 | tf_op args[2]
  4.9 6.2 %setup_blocks.1 = (bf16[8,162,162]{2,1,0:T(8,128)(2,1)S(1)}, bf16[8,162,162]{2,1,0:T(8,128)(2,1)S(1)}, bf16[12,162,162]{2,1,0:T(8,128)(2,1)S(1)}, bf16[12,162,16...) custom-call(s32[4,6]{1,0:T(4,128)S(1)} %copy-done.3, ...), custom_call_target="tpu_custom_call" | custom-call | tf_op jit(solution)/shard_map/setup_blocks/pallas_call | solution.py:559
  11.1 3.9 %collective-permute-start.36 = (f32[2,16,162]{2,1,0:T(8,128)S(1)}, f32[2,16,162]{2,1,0:T(8,128)S(1)}, u32[]{:S(2)}, u32[]{:S(2)}) collective-permute-start(f32[2,16,162]{2,1,0:T(8,128)S(1)} %get-tuple-element.102), channel_id=1, source_target_pairs={{0,8},{8,16},{16,24},{24,32},{32,40},{40,48},{48,56},{56,64},{64,7... | collective-permute-start | bytes 62216 | tf_op jit(solution)/shard_map/ppermute | solution.py:22
  15.0 1.3 collective-permute-start.37
  16.3 4.1 %collective-permute-start.38 = (f32[2,16,162]{2,1,0:T(8,128)S(1)}, f32[2,16,162]{2,1,0:T(8,128)S(1)}, u32[]{:S(2)}, u32[]{:S(2)}) collective-permute-start(f32[2,16,162]{2,1,0:T(8,128)S(1)} %get-tuple-element.104), channel_id=1, source_target_pairs={{0,1},{1,2},{2,3},{3,4},{4,5},{5,6},{6,7},{8,9},{9,10},{10,11},{11... | collective-permute-start | bytes 62216 | tf_op jit(solution)/shard_map/ppermute | solution.py:22
  20.4 3.4 %collective-permute-start.39 = (f32[2,16,162]{2,1,0:T(8,128)S(1)}, f32[2,16,162]{2,1,0:T(8,128)S(1)}, u32[]{:S(2)}, u32[]{:S(2)}) collective-permute-start(f32[2,16,162]{2,1,0:T(8,128)S(1)} %get-tuple-element.105), channel_id=1, source_target_pairs={{1,0},{2,1},{3,2},{4,3},{5,4},{6,5},{7,6},{9,8},{10,9},{11,10},{12... | collective-permute-start | bytes 62216 | tf_op jit(solution)/shard_map/ppermute | solution.py:22
  23.8 0.4 local_part_0.1
  24.2 1.4 collective-permute-done.39.recv3_ref
  25.6 0.3 border_part_0.1
  26.0 4.3 %collective-permute-start.40 = (f32[2,16,162]{2,1,0:T(8,128)S(1)}, f32[2,16,162]{2,1,0:T(8,128)S(1)}, u32[]{:S(2)}, u32[]{:S(2)}) collective-permute-start(f32[2,16,162]{2,1,0:T(8,128)S(1)} %get-tuple-element.111), channel_id=1, source_target_pairs={{0,8},{8,16},{16,24},{24,32},{32,40},{40,48},{48,56},{56,64},{64,7... | collective-permute-start | bytes 62216 | tf_op jit(solution)/shard_map/ppermute | solution.py:22
  30.2 1.3 collective-permute-start.41
  31.5 2.2 %collective-permute-start.42 = (f32[2,16,162]{2,1,0:T(8,128)S(1)}, f32[2,16,162]{2,1,0:T(8,128)S(1)}, u32[]{:S(2)}, u32[]{:S(2)}) collective-permute-start(f32[2,16,162]{2,1,0:T(8,128)S(1)} %get-tuple-element.113), channel_id=1, source_target_pairs={{0,1},{1,2},{2,3},{3,4},{4,5},{5,6},{6,7},{8,9},{9,10},{10,11},{11... | collective-permute-start | bytes 62216 | tf_op jit(solution)/shard_map/ppermute | solution.py:22
  33.7 2.1 %collective-permute-start.43 = (f32[2,16,162]{2,1,0:T(8,128)S(1)}, f32[2,16,162]{2,1,0:T(8,128)S(1)}, u32[]{:S(2)}, u32[]{:S(2)}) collective-permute-start(f32[2,16,162]{2,1,0:T(8,128)S(1)} %get-tuple-element.114), channel_id=1, source_target_pairs={{1,0},{2,1},{3,2},{4,3},{5,4},{6,5},{7,6},{9,8},{10,9},{11,10},{12... | collective-permute-start | bytes 62216 | tf_op jit(solution)/shard_map/ppermute | solution.py:22
  35.9 0.4 local_part_1.1
  36.3 2.6 %collective-permute-done.43.recv3_ref = f32[2,16,162]{2,1,0:T(8,128)S(1)} collective-permute-done((f32[2,16,162]{2,1,0:T(8,128)S(1)}, f32[2,16,162]{2,1,0:T(8,128)S(1)}, u32[]{:S(2)}, u32[]{:S(2)}) %collective-permute-start.43) | collective-permute-done | bytes 20768 | tf_op jit(solution)/shard_map/ppermute | solution.py:22
  39.0 0.3 border_part_1.1
  39.3 4.3 %collective-permute-start.44 = (f32[2,16,162]{2,1,0:T(8,128)S(1)}, f32[2,16,162]{2,1,0:T(8,128)S(1)}, u32[]{:S(2)}, u32[]{:S(2)}) collective-permute-start(f32[2,16,162]{2,1,0:T(8,128)S(1)} %get-tuple-element.118), channel_id=1, source_target_pairs={{0,8},{8,16},{16,24},{24,32},{32,40},{40,48},{48,56},{56,64},{64,7... | collective-permute-start | bytes 62216 | tf_op jit(solution)/shard_map/ppermute | solution.py:22
  43.6 1.3 collective-permute-start.45
  44.9 2.2 %collective-permute-start.46 = (f32[2,16,162]{2,1,0:T(8,128)S(1)}, f32[2,16,162]{2,1,0:T(8,128)S(1)}, u32[]{:S(2)}, u32[]{:S(2)}) collective-permute-start(f32[2,16,162]{2,1,0:T(8,128)S(1)} %get-tuple-element.120), channel_id=1, source_target_pairs={{0,1},{1,2},{2,3},{3,4},{4,5},{5,6},{6,7},{8,9},{9,10},{10,11},{11... | collective-permute-start | bytes 62216 | tf_op jit(solution)/shard_map/ppermute | solution.py:22
  47.1 2.1 %collective-permute-start.47 = (f32[2,16,162]{2,1,0:T(8,128)S(1)}, f32[2,16,162]{2,1,0:T(8,128)S(1)}, u32[]{:S(2)}, u32[]{:S(2)}) collective-permute-start(f32[2,16,162]{2,1,0:T(8,128)S(1)} %get-tuple-element.121), channel_id=1, source_target_pairs={{1,0},{2,1},{3,2},{4,3},{5,4},{6,5},{7,6},{9,8},{10,9},{11,10},{12... | collective-permute-start | bytes 62216 | tf_op jit(solution)/shard_map/ppermute | solution.py:22
  49.2 0.4 local_part_2.1
  49.7 2.6 %collective-permute-done.47.recv3_ref = f32[2,16,162]{2,1,0:T(8,128)S(1)} collective-permute-done((f32[2,16,162]{2,1,0:T(8,128)S(1)}, f32[2,16,162]{2,1,0:T(8,128)S(1)}, u32[]{:S(2)}, u32[]{:S(2)}) %collective-permute-start.47) | collective-permute-done | bytes 20768 | tf_op jit(solution)/shard_map/ppermute | solution.py:22
  52.6 4.3 %collective-permute-start.48 = (f32[2,16,162]{2,1,0:T(8,128)S(1)}, f32[2,16,162]{2,1,0:T(8,128)S(1)}, u32[]{:S(2)}, u32[]{:S(2)}) collective-permute-start(f32[2,16,162]{2,1,0:T(8,128)S(1)} %get-tuple-element.125), channel_id=1, source_target_pairs={{0,8},{8,16},{16,24},{24,32},{32,40},{40,48},{48,56},{56,64},{64,7... | collective-permute-start | bytes 62216 | tf_op jit(solution)/shard_map/ppermute | solution.py:22
  56.9 1.3 collective-permute-start.49
  58.2 2.2 %collective-permute-start.50 = (f32[2,16,162]{2,1,0:T(8,128)S(1)}, f32[2,16,162]{2,1,0:T(8,128)S(1)}, u32[]{:S(2)}, u32[]{:S(2)}) collective-permute-start(f32[2,16,162]{2,1,0:T(8,128)S(1)} %get-tuple-element.127), channel_id=1, source_target_pairs={{0,1},{1,2},{2,3},{3,4},{4,5},{5,6},{6,7},{8,9},{9,10},{10,11},{11... | collective-permute-start | bytes 62216 | tf_op jit(solution)/shard_map/ppermute | solution.py:22
  60.4 2.1 %collective-permute-start.51 = (f32[2,16,162]{2,1,0:T(8,128)S(1)}, f32[2,16,162]{2,1,0:T(8,128)S(1)}, u32[]{:S(2)}, u32[]{:S(2)}) collective-permute-start(f32[2,16,162]{2,1,0:T(8,128)S(1)} %get-tuple-element.128), channel_id=1, source_target_pairs={{1,0},{2,1},{3,2},{4,3},{5,4},{6,5},{7,6},{9,8},{10,9},{11,10},{12... | collective-permute-start | bytes 62216 | tf_op jit(solution)/shard_map/ppermute | solution.py:22
  62.5 0.4 local_part_3.1
  63.0 2.6 %collective-permute-done.51.recv3_ref = f32[2,16,162]{2,1,0:T(8,128)S(1)} collective-permute-done((f32[2,16,162]{2,1,0:T(8,128)S(1)}, f32[2,16,162]{2,1,0:T(8,128)S(1)}, u32[]{:S(2)}, u32[]{:S(2)}) %collective-permute-start.51) | collective-permute-done | bytes 20768 | tf_op jit(solution)/shard_map/ppermute | solution.py:22
  66.0 4.8 %collective-permute-start.52 = (f32[2,16,162]{2,1,0:T(8,128)S(1)}, f32[2,16,162]{2,1,0:T(8,128)S(1)}, u32[]{:S(2)}, u32[]{:S(2)}) collective-permute-start(f32[2,16,162]{2,1,0:T(8,128)S(1)} %get-tuple-element.132), channel_id=1, source_target_pairs={{0,8},{8,16},{16,24},{24,32},{32,40},{40,48},{48,56},{56,64},{64,7... | collective-permute-start | bytes 62216 | tf_op jit(solution)/shard_map/ppermute | solution.py:22
  70.8 1.3 collective-permute-start.53
  72.1 2.2 %collective-permute-start.54 = (f32[2,16,162]{2,1,0:T(8,128)S(1)}, f32[2,16,162]{2,1,0:T(8,128)S(1)}, u32[]{:S(2)}, u32[]{:S(2)}) collective-permute-start(f32[2,16,162]{2,1,0:T(8,128)S(1)} %get-tuple-element.134), channel_id=1, source_target_pairs={{0,1},{1,2},{2,3},{3,4},{4,5},{5,6},{6,7},{8,9},{9,10},{10,11},{11... | collective-permute-start | bytes 62216 | tf_op jit(solution)/shard_map/ppermute | solution.py:22
  74.3 2.1 %collective-permute-start.55 = (f32[2,16,162]{2,1,0:T(8,128)S(1)}, f32[2,16,162]{2,1,0:T(8,128)S(1)}, u32[]{:S(2)}, u32[]{:S(2)}) collective-permute-start(f32[2,16,162]{2,1,0:T(8,128)S(1)} %get-tuple-element.135), channel_id=1, source_target_pairs={{1,0},{2,1},{3,2},{4,3},{5,4},{6,5},{7,6},{9,8},{10,9},{11,10},{12... | collective-permute-start | bytes 62216 | tf_op jit(solution)/shard_map/ppermute | solution.py:22
  76.5 0.4 local_part_4.1
  76.9 1.0 collective-permute-done.53.recv1_ref
  77.9 1.7 collective-permute-done.55.recv3_ref
  79.9 6.4 %collective-permute-start.56 = (f32[2,16,162]{2,1,0:T(8,128)S(1)}, f32[2,16,162]{2,1,0:T(8,128)S(1)}, u32[]{:S(2)}, u32[]{:S(2)}) collective-permute-start(f32[2,16,162]{2,1,0:T(8,128)S(1)} %get-tuple-element.139), channel_id=1, source_target_pairs={{0,8},{8,16},{16,24},{24,32},{32,40},{40,48},{48,56},{56,64},{64,7... | collective-permute-start | bytes 62216 | tf_op jit(solution)/shard_map/ppermute | solution.py:22
  86.3 1.3 collective-permute-start.57
  87.6 2.2 %collective-permute-start.58 = (f32[2,16,162]{2,1,0:T(8,128)S(1)}, f32[2,16,162]{2,1,0:T(8,128)S(1)}, u32[]{:S(2)}, u32[]{:S(2)}) collective-permute-start(f32[2,16,162]{2,1,0:T(8,128)S(1)} %get-tuple-element.141), channel_id=1, source_target_pairs={{0,1},{1,2},{2,3},{3,4},{4,5},{5,6},{6,7},{8,9},{9,10},{10,11},{11... | collective-permute-start | bytes 62216 | tf_op jit(solution)/shard_map/ppermute | solution.py:22
  89.8 2.1 %collective-permute-start.59 = (f32[2,16,162]{2,1,0:T(8,128)S(1)}, f32[2,16,162]{2,1,0:T(8,128)S(1)}, u32[]{:S(2)}, u32[]{:S(2)}) collective-permute-start(f32[2,16,162]{2,1,0:T(8,128)S(1)} %get-tuple-element.142), channel_id=1, source_target_pairs={{1,0},{2,1},{3,2},{4,3},{5,4},{6,5},{7,6},{9,8},{10,9},{11,10},{12... | collective-permute-start | bytes 62216 | tf_op jit(solution)/shard_map/ppermute | solution.py:22
  91.9 0.4 local_part_5.1
  92.3 1.0 collective-permute-done.57.recv1_ref
  93.3 1.7 collective-permute-done.59.recv3_ref
  95.3 6.4 %collective-permute-start.60 = (f32[2,16,162]{2,1,0:T(8,128)S(1)}, f32[2,16,162]{2,1,0:T(8,128)S(1)}, u32[]{:S(2)}, u32[]{:S(2)}) collective-permute-start(f32[2,16,162]{2,1,0:T(8,128)S(1)} %get-tuple-element.146), channel_id=1, source_target_pairs={{0,8},{8,16},{16,24},{24,32},{32,40},{40,48},{48,56},{56,64},{64,7... | collective-permute-start | bytes 62216 | tf_op jit(solution)/shard_map/ppermute | solution.py:22
  101.7 1.3 collective-permute-start.61
  103.0 2.2 %collective-permute-start.62 = (f32[2,16,162]{2,1,0:T(8,128)S(1)}, f32[2,16,162]{2,1,0:T(8,128)S(1)}, u32[]{:S(2)}, u32[]{:S(2)}) collective-permute-start(f32[2,16,162]{2,1,0:T(8,128)S(1)} %get-tuple-element.148), channel_id=1, source_target_pairs={{0,1},{1,2},{2,3},{3,4},{4,5},{5,6},{6,7},{8,9},{9,10},{10,11},{11... | collective-permute-start | bytes 62216 | tf_op jit(solution)/shard_map/ppermute | solution.py:22
  105.2 2.1 %collective-permute-start.63 = (f32[2,16,162]{2,1,0:T(8,128)S(1)}, f32[2,16,162]{2,1,0:T(8,128)S(1)}, u32[]{:S(2)}, u32[]{:S(2)}) collective-permute-start(f32[2,16,162]{2,1,0:T(8,128)S(1)} %get-tuple-element.149), channel_id=1, source_target_pairs={{1,0},{2,1},{3,2},{4,3},{5,4},{6,5},{7,6},{9,8},{10,9},{11,10},{12... | collective-permute-start | bytes 62216 | tf_op jit(solution)/shard_map/ppermute | solution.py:22
  107.3 0.4 local_part_6.1
  107.8 1.0 collective-permute-done.61.recv1_ref
  108.8 1.7 collective-permute-done.63.recv3_ref
  110.7 6.4 %collective-permute-start.64 = (f32[2,16,162]{2,1,0:T(8,128)S(1)}, f32[2,16,162]{2,1,0:T(8,128)S(1)}, u32[]{:S(2)}, u32[]{:S(2)}) collective-permute-start(f32[2,16,162]{2,1,0:T(8,128)S(1)} %get-tuple-element.153), channel_id=1, source_target_pairs={{0,8},{8,16},{16,24},{24,32},{32,40},{40,48},{48,56},{56,64},{64,7... | collective-permute-start | bytes 62216 | tf_op jit(solution)/shard_map/ppermute | solution.py:22
  117.1 1.3 collective-permute-start.65
  118.4 2.2 %collective-permute-start.66 = (f32[2,16,162]{2,1,0:T(8,128)S(1)}, f32[2,16,162]{2,1,0:T(8,128)S(1)}, u32[]{:S(2)}, u32[]{:S(2)}) collective-permute-start(f32[2,16,162]{2,1,0:T(8,128)S(1)} %get-tuple-element.155), channel_id=1, source_target_pairs={{0,1},{1,2},{2,3},{3,4},{4,5},{5,6},{6,7},{8,9},{9,10},{10,11},{11... | collective-permute-start | bytes 62216 | tf_op jit(solution)/shard_map/ppermute | solution.py:22
  120.6 2.3 %collective-permute-start.67 = (f32[2,16,162]{2,1,0:T(8,128)S(1)}, f32[2,16,162]{2,1,0:T(8,128)S(1)}, u32[]{:S(2)}, u32[]{:S(2)}) collective-permute-start(f32[2,16,162]{2,1,0:T(8,128)S(1)} %get-tuple-element.156), channel_id=1, source_target_pairs={{1,0},{2,1},{3,2},{4,3},{5,4},{6,5},{7,6},{9,8},{10,9},{11,10},{12... | collective-permute-start | bytes 62216 | tf_op jit(solution)/shard_map/ppermute | solution.py:22
  123.0 0.4 local_part_7.1
  123.4 0.8 collective-permute-done.65.refs_2_
  124.2 1.7 collective-permute-done.67.refs_4_
  125.9 0.7 last_part.1
  126.6 8.9 %all_to_all.15 = f32[8,16,128]{2,1,0:T(8,128)S(1)} all-to-all(f32[8,16,128]{2,1,0:T(8,128)S(1)} %broadcast_in_dim.81), channel_id=1, replica_groups=mesh['dom'=64,'blk'=8] {'blk'}, dimensions={0} | all-to-all | bytes 131072 | tf_op jit(solution)/shard_map/all_to_all | solution.py:510
  135.5 34.1 %all_to_all.16 = f32[16,16,128]{2,1,0:T(8,128)S(1)} all-to-all(f32[16,16,128]{2,1,0:T(8,128)S(1)} %broadcast_in_dim.82), channel_id=1, replica_groups={{0,8,16,24,32,40,48,56,64,72,80,88,96,104,112,120},{128,136,144,152,160..., dimensions={0} | all-to-all | bytes 262144 | tf_op jit(solution)/shard_map/all_to_all | solution.py:510
  169.6 0.6 broadcast_in_dim.83
  170.2 11.9 %all-to-all-start.2 = ((f32[4,16,128]{2,1,0:T(8,128)}), f32[4,16,128]{2,1,0:T(8,128)S(1)}, u32[]{:S(2)}, u32[]{:S(2)}) async-start(f32[4,16,128]{2,1,0:T(8,128)} %broadcast_in_dim.83), calls=%async_computation.2 | async-start | bytes 65536 | tf_op jit(solution)/shard_map/all_to_all | solution.py:510
  182.2 11.8 %all-to-all-done.2 = f32[4,16,128]{2,1,0:T(8,128)S(1)} async-done(((f32[4,16,128]{2,1,0:T(8,128)}), f32[4,16,128]{2,1,0:T(8,128)S(1)}, u32[]{:S(2)}, u32[]{:S(2)}) %all-to-all-start.2) | async-done | bytes 32800 | tf_op jit(solution)/shard_map/all_to_all | solution.py:510
  193.9 1.7 finish_part.1
  (41 shorter events, 2.0 us)
Async XLA Ops:
  1.9 3.0 %copy-start.1 = (f32[16,4,162]{2,1,0:T(4,128)S(1)}, f32[16,4,162]{2,1,0:T(4,128)}, u32[]{:S(2)}) copy-start(f32[16,4,162]{2,1,0:T(4,128)} %src_ref.1) | copy-start | bytes 124420
  1.9 3.0 %copy-start.3 = (s32[4,6]{1,0:T(4,128)S(1)}, s32[4,6]{1,0:T(4,128)}, u32[]{:S(2)}) copy-start(s32[4,6]{1,0:T(4,128)} %nbr_ref.1) | copy-start | bytes 292
  1.9 3.0 %copy-start.6 = (s32[4,6]{1,0:T(4,128)S(1)}, s32[4,6]{1,0:T(4,128)}, u32[]{:S(2)}) copy-start(s32[4,6]{1,0:T(4,128)} %flag_ref.1) | copy-start | bytes 292
  11.1 13.1 %collective-permute-start.36 = (f32[2,16,162]{2,1,0:T(8,128)S(1)}, f32[2,16,162]{2,1,0:T(8,128)S(1)}, u32[]{:S(2)}, u32[]{:S(2)}) collective-permute-start(f32[2,16,162]{2,1,0:T(8,128)S(1)} %get-tuple-element.102), channel_id=1, source_target_pairs={{0,8},{8,16},{16,24},{24,32},{32,40},{40,48},{48,56},{56,64},{64,7... | collective-permute-start | bytes 62216 | tf_op jit(solution)/shard_map/ppermute | solution.py:22
  15.0 9.2 %collective-permute-start.37 = (f32[2,16,162]{2,1,0:T(8,128)S(1)}, f32[2,16,162]{2,1,0:T(8,128)S(1)}, u32[]{:S(2)}, u32[]{:S(2)}) collective-permute-start(f32[2,16,162]{2,1,0:T(8,128)S(1)} %get-tuple-element.103), channel_id=1, source_target_pairs={{8,0},{16,8},{24,16},{32,24},{40,32},{48,40},{56,48},{64,56},{72,6... | collective-permute-start | bytes 62216 | tf_op jit(solution)/shard_map/ppermute | solution.py:22
  16.3 7.9 %collective-permute-start.38 = (f32[2,16,162]{2,1,0:T(8,128)S(1)}, f32[2,16,162]{2,1,0:T(8,128)S(1)}, u32[]{:S(2)}, u32[]{:S(2)}) collective-permute-start(f32[2,16,162]{2,1,0:T(8,128)S(1)} %get-tuple-element.104), channel_id=1, source_target_pairs={{0,1},{1,2},{2,3},{3,4},{4,5},{5,6},{6,7},{8,9},{9,10},{10,11},{11... | collective-permute-start | bytes 62216 | tf_op jit(solution)/shard_map/ppermute | solution.py:22
  20.4 5.2 %collective-permute-start.39 = (f32[2,16,162]{2,1,0:T(8,128)S(1)}, f32[2,16,162]{2,1,0:T(8,128)S(1)}, u32[]{:S(2)}, u32[]{:S(2)}) collective-permute-start(f32[2,16,162]{2,1,0:T(8,128)S(1)} %get-tuple-element.105), channel_id=1, source_target_pairs={{1,0},{2,1},{3,2},{4,3},{5,4},{6,5},{7,6},{9,8},{10,9},{11,10},{12... | collective-permute-start | bytes 62216 | tf_op jit(solution)/shard_map/ppermute | solution.py:22
  26.0 10.3 %collective-permute-start.40 = (f32[2,16,162]{2,1,0:T(8,128)S(1)}, f32[2,16,162]{2,1,0:T(8,128)S(1)}, u32[]{:S(2)}, u32[]{:S(2)}) collective-permute-start(f32[2,16,162]{2,1,0:T(8,128)S(1)} %get-tuple-element.111), channel_id=1, source_target_pairs={{0,8},{8,16},{16,24},{24,32},{32,40},{40,48},{48,56},{56,64},{64,7... | collective-permute-start | bytes 62216 | tf_op jit(solution)/shard_map/ppermute | solution.py:22
  30.2 6.1 %collective-permute-start.41 = (f32[2,16,162]{2,1,0:T(8,128)S(1)}, f32[2,16,162]{2,1,0:T(8,128)S(1)}, u32[]{:S(2)}, u32[]{:S(2)}) collective-permute-start(f32[2,16,162]{2,1,0:T(8,128)S(1)} %get-tuple-element.112), channel_id=1, source_target_pairs={{8,0},{16,8},{24,16},{32,24},{40,32},{48,40},{56,48},{64,56},{72,6... | collective-permute-start | bytes 62216 | tf_op jit(solution)/shard_map/ppermute | solution.py:22
  31.5 4.8 %collective-permute-start.42 = (f32[2,16,162]{2,1,0:T(8,128)S(1)}, f32[2,16,162]{2,1,0:T(8,128)S(1)}, u32[]{:S(2)}, u32[]{:S(2)}) collective-permute-start(f32[2,16,162]{2,1,0:T(8,128)S(1)} %get-tuple-element.113), channel_id=1, source_target_pairs={{0,1},{1,2},{2,3},{3,4},{4,5},{5,6},{6,7},{8,9},{9,10},{10,11},{11... | collective-permute-start | bytes 62216 | tf_op jit(solution)/shard_map/ppermute | solution.py:22
  33.7 5.2 %collective-permute-start.43 = (f32[2,16,162]{2,1,0:T(8,128)S(1)}, f32[2,16,162]{2,1,0:T(8,128)S(1)}, u32[]{:S(2)}, u32[]{:S(2)}) collective-permute-start(f32[2,16,162]{2,1,0:T(8,128)S(1)} %get-tuple-element.114), channel_id=1, source_target_pairs={{1,0},{2,1},{3,2},{4,3},{5,4},{6,5},{7,6},{9,8},{10,9},{11,10},{12... | collective-permute-start | bytes 62216 | tf_op jit(solution)/shard_map/ppermute | solution.py:22
  39.3 10.3 %collective-permute-start.44 = (f32[2,16,162]{2,1,0:T(8,128)S(1)}, f32[2,16,162]{2,1,0:T(8,128)S(1)}, u32[]{:S(2)}, u32[]{:S(2)}) collective-permute-start(f32[2,16,162]{2,1,0:T(8,128)S(1)} %get-tuple-element.118), channel_id=1, source_target_pairs={{0,8},{8,16},{16,24},{24,32},{32,40},{40,48},{48,56},{56,64},{64,7... | collective-permute-start | bytes 62216 | tf_op jit(solution)/shard_map/ppermute | solution.py:22
  43.6 6.1 %collective-permute-start.45 = (f32[2,16,162]{2,1,0:T(8,128)S(1)}, f32[2,16,162]{2,1,0:T(8,128)S(1)}, u32[]{:S(2)}, u32[]{:S(2)}) collective-permute-start(f32[2,16,162]{2,1,0:T(8,128)S(1)} %get-tuple-element.119), channel_id=1, source_target_pairs={{8,0},{16,8},{24,16},{32,24},{40,32},{48,40},{56,48},{64,56},{72,6... | collective-permute-start | bytes 62216 | tf_op jit(solution)/shard_map/ppermute | solution.py:22
  44.9 4.8 %collective-permute-start.46 = (f32[2,16,162]{2,1,0:T(8,128)S(1)}, f32[2,16,162]{2,1,0:T(8,128)S(1)}, u32[]{:S(2)}, u32[]{:S(2)}) collective-permute-start(f32[2,16,162]{2,1,0:T(8,128)S(1)} %get-tuple-element.120), channel_id=1, source_target_pairs={{0,1},{1,2},{2,3},{3,4},{4,5},{5,6},{6,7},{8,9},{9,10},{10,11},{11... | collective-permute-start | bytes 62216 | tf_op jit(solution)/shard_map/ppermute | solution.py:22
  47.1 5.2 %collective-permute-start.47 = (f32[2,16,162]{2,1,0:T(8,128)S(1)}, f32[2,16,162]{2,1,0:T(8,128)S(1)}, u32[]{:S(2)}, u32[]{:S(2)}) collective-permute-start(f32[2,16,162]{2,1,0:T(8,128)S(1)} %get-tuple-element.121), channel_id=1, source_target_pairs={{1,0},{2,1},{3,2},{4,3},{5,4},{6,5},{7,6},{9,8},{10,9},{11,10},{12... | collective-permute-start | bytes 62216 | tf_op jit(solution)/shard_map/ppermute | solution.py:22
  52.6 10.3 %collective-permute-start.48 = (f32[2,16,162]{2,1,0:T(8,128)S(1)}, f32[2,16,162]{2,1,0:T(8,128)S(1)}, u32[]{:S(2)}, u32[]{:S(2)}) collective-permute-start(f32[2,16,162]{2,1,0:T(8,128)S(1)} %get-tuple-element.125), channel_id=1, source_target_pairs={{0,8},{8,16},{16,24},{24,32},{32,40},{40,48},{48,56},{56,64},{64,7... | collective-permute-start | bytes 62216 | tf_op jit(solution)/shard_map/ppermute | solution.py:22
  56.9 6.1 %collective-permute-start.49 = (f32[2,16,162]{2,1,0:T(8,128)S(1)}, f32[2,16,162]{2,1,0:T(8,128)S(1)}, u32[]{:S(2)}, u32[]{:S(2)}) collective-permute-start(f32[2,16,162]{2,1,0:T(8,128)S(1)} %get-tuple-element.126), channel_id=1, source_target_pairs={{8,0},{16,8},{24,16},{32,24},{40,32},{48,40},{56,48},{64,56},{72,6... | collective-permute-start | bytes 62216 | tf_op jit(solution)/shard_map/ppermute | solution.py:22
  58.2 4.8 %collective-permute-start.50 = (f32[2,16,162]{2,1,0:T(8,128)S(1)}, f32[2,16,162]{2,1,0:T(8,128)S(1)}, u32[]{:S(2)}, u32[]{:S(2)}) collective-permute-start(f32[2,16,162]{2,1,0:T(8,128)S(1)} %get-tuple-element.127), channel_id=1, source_target_pairs={{0,1},{1,2},{2,3},{3,4},{4,5},{5,6},{6,7},{8,9},{9,10},{10,11},{11... | collective-permute-start | bytes 62216 | tf_op jit(solution)/shard_map/ppermute | solution.py:22
  60.4 5.2 %collective-permute-start.51 = (f32[2,16,162]{2,1,0:T(8,128)S(1)}, f32[2,16,162]{2,1,0:T(8,128)S(1)}, u32[]{:S(2)}, u32[]{:S(2)}) collective-permute-start(f32[2,16,162]{2,1,0:T(8,128)S(1)} %get-tuple-element.128), channel_id=1, source_target_pairs={{1,0},{2,1},{3,2},{4,3},{5,4},{6,5},{7,6},{9,8},{10,9},{11,10},{12... | collective-permute-start | bytes 62216 | tf_op jit(solution)/shard_map/ppermute | solution.py:22
  66.0 10.9 %collective-permute-start.52 = (f32[2,16,162]{2,1,0:T(8,128)S(1)}, f32[2,16,162]{2,1,0:T(8,128)S(1)}, u32[]{:S(2)}, u32[]{:S(2)}) collective-permute-start(f32[2,16,162]{2,1,0:T(8,128)S(1)} %get-tuple-element.132), channel_id=1, source_target_pairs={{0,8},{8,16},{16,24},{24,32},{32,40},{40,48},{48,56},{56,64},{64,7... | collective-permute-start | bytes 62216 | tf_op jit(solution)/shard_map/ppermute | solution.py:22
  70.8 7.1 %collective-permute-start.53 = (f32[2,16,162]{2,1,0:T(8,128)S(1)}, f32[2,16,162]{2,1,0:T(8,128)S(1)}, u32[]{:S(2)}, u32[]{:S(2)}) collective-permute-start(f32[2,16,162]{2,1,0:T(8,128)S(1)} %get-tuple-element.133), channel_id=1, source_target_pairs={{8,0},{16,8},{24,16},{32,24},{40,32},{48,40},{56,48},{64,56},{72,6... | collective-permute-start | bytes 62216 | tf_op jit(solution)/shard_map/ppermute | solution.py:22
  72.1 5.8 %collective-permute-start.54 = (f32[2,16,162]{2,1,0:T(8,128)S(1)}, f32[2,16,162]{2,1,0:T(8,128)S(1)}, u32[]{:S(2)}, u32[]{:S(2)}) collective-permute-start(f32[2,16,162]{2,1,0:T(8,128)S(1)} %get-tuple-element.134), channel_id=1, source_target_pairs={{0,1},{1,2},{2,3},{3,4},{4,5},{5,6},{6,7},{8,9},{9,10},{10,11},{11... | collective-permute-start | bytes 62216 | tf_op jit(solution)/shard_map/ppermute | solution.py:22
  74.3 5.2 %collective-permute-start.55 = (f32[2,16,162]{2,1,0:T(8,128)S(1)}, f32[2,16,162]{2,1,0:T(8,128)S(1)}, u32[]{:S(2)}, u32[]{:S(2)}) collective-permute-start(f32[2,16,162]{2,1,0:T(8,128)S(1)} %get-tuple-element.135), channel_id=1, source_target_pairs={{1,0},{2,1},{3,2},{4,3},{5,4},{6,5},{7,6},{9,8},{10,9},{11,10},{12... | collective-permute-start | bytes 62216 | tf_op jit(solution)/shard_map/ppermute | solution.py:22
  79.9 12.5 %collective-permute-start.56 = (f32[2,16,162]{2,1,0:T(8,128)S(1)}, f32[2,16,162]{2,1,0:T(8,128)S(1)}, u32[]{:S(2)}, u32[]{:S(2)}) collective-permute-start(f32[2,16,162]{2,1,0:T(8,128)S(1)} %get-tuple-element.139), channel_id=1, source_target_pairs={{0,8},{8,16},{16,24},{24,32},{32,40},{40,48},{48,56},{56,64},{64,7... | collective-permute-start | bytes 62216 | tf_op jit(solution)/shard_map/ppermute | solution.py:22
  86.3 7.0 %collective-permute-start.57 = (f32[2,16,162]{2,1,0:T(8,128)S(1)}, f32[2,16,162]{2,1,0:T(8,128)S(1)}, u32[]{:S(2)}, u32[]{:S(2)}) collective-permute-start(f32[2,16,162]{2,1,0:T(8,128)S(1)} %get-tuple-element.140), channel_id=1, source_target_pairs={{8,0},{16,8},{24,16},{32,24},{40,32},{48,40},{56,48},{64,56},{72,6... | collective-permute-start | bytes 62216 | tf_op jit(solution)/shard_map/ppermute | solution.py:22
  87.6 5.8 %collective-permute-start.58 = (f32[2,16,162]{2,1,0:T(8,128)S(1)}, f32[2,16,162]{2,1,0:T(8,128)S(1)}, u32[]{:S(2)}, u32[]{:S(2)}) collective-permute-start(f32[2,16,162]{2,1,0:T(8,128)S(1)} %get-tuple-element.141), channel_id=1, source_target_pairs={{0,1},{1,2},{2,3},{3,4},{4,5},{5,6},{6,7},{8,9},{9,10},{10,11},{11... | collective-permute-start | bytes 62216 | tf_op jit(solution)/shard_map/ppermute | solution.py:22
  89.8 5.2 %collective-permute-start.59 = (f32[2,16,162]{2,1,0:T(8,128)S(1)}, f32[2,16,162]{2,1,0:T(8,128)S(1)}, u32[]{:S(2)}, u32[]{:S(2)}) collective-permute-start(f32[2,16,162]{2,1,0:T(8,128)S(1)} %get-tuple-element.142), channel_id=1, source_target_pairs={{1,0},{2,1},{3,2},{4,3},{5,4},{6,5},{7,6},{9,8},{10,9},{11,10},{12... | collective-permute-start | bytes 62216 | tf_op jit(solution)/shard_map/ppermute | solution.py:22
  95.3 12.5 %collective-permute-start.60 = (f32[2,16,162]{2,1,0:T(8,128)S(1)}, f32[2,16,162]{2,1,0:T(8,128)S(1)}, u32[]{:S(2)}, u32[]{:S(2)}) collective-permute-start(f32[2,16,162]{2,1,0:T(8,128)S(1)} %get-tuple-element.146), channel_id=1, source_target_pairs={{0,8},{8,16},{16,24},{24,32},{32,40},{40,48},{48,56},{56,64},{64,7... | collective-permute-start | bytes 62216 | tf_op jit(solution)/shard_map/ppermute | solution.py:22
  101.7 7.1 %collective-permute-start.61 = (f32[2,16,162]{2,1,0:T(8,128)S(1)}, f32[2,16,162]{2,1,0:T(8,128)S(1)}, u32[]{:S(2)}, u32[]{:S(2)}) collective-permute-start(f32[2,16,162]{2,1,0:T(8,128)S(1)} %get-tuple-element.147), channel_id=1, source_target_pairs={{8,0},{16,8},{24,16},{32,24},{40,32},{48,40},{56,48},{64,56},{72,6... | collective-permute-start | bytes 62216 | tf_op jit(solution)/shard_map/ppermute | solution.py:22
  103.0 5.8 %collective-permute-start.62 = (f32[2,16,162]{2,1,0:T(8,128)S(1)}, f32[2,16,162]{2,1,0:T(8,128)S(1)}, u32[]{:S(2)}, u32[]{:S(2)}) collective-permute-start(f32[2,16,162]{2,1,0:T(8,128)S(1)} %get-tuple-element.148), channel_id=1, source_target_pairs={{0,1},{1,2},{2,3},{3,4},{4,5},{5,6},{6,7},{8,9},{9,10},{10,11},{11... | collective-permute-start | bytes 62216 | tf_op jit(solution)/shard_map/ppermute | solution.py:22
  105.2 5.2 %collective-permute-start.63 = (f32[2,16,162]{2,1,0:T(8,128)S(1)}, f32[2,16,162]{2,1,0:T(8,128)S(1)}, u32[]{:S(2)}, u32[]{:S(2)}) collective-permute-start(f32[2,16,162]{2,1,0:T(8,128)S(1)} %get-tuple-element.149), channel_id=1, source_target_pairs={{1,0},{2,1},{3,2},{4,3},{5,4},{6,5},{7,6},{9,8},{10,9},{11,10},{12... | collective-permute-start | bytes 62216 | tf_op jit(solution)/shard_map/ppermute | solution.py:22
  107.8 88.6 %copy-start.2 = (f32[4,162,162]{2,0,1:T(4,128)S(1)}, f32[4,162,162]{2,0,1:T(4,128)}, u32[]{:S(2)}) copy-start(f32[4,162,162]{2,0,1:T(4,128)} %param.14) | copy-start | bytes 1259716
  107.8 88.6 %copy-start.7 = (s32[4,6]{1,0:T(4,128)S(1)}, s32[4,6]{1,0:T(4,128)}, u32[]{:S(2)}) copy-start(s32[4,6]{1,0:T(4,128)} %param.17) | copy-start | bytes 292
  110.7 12.6 %collective-permute-start.64 = (f32[2,16,162]{2,1,0:T(8,128)S(1)}, f32[2,16,162]{2,1,0:T(8,128)S(1)}, u32[]{:S(2)}, u32[]{:S(2)}) collective-permute-start(f32[2,16,162]{2,1,0:T(8,128)S(1)} %get-tuple-element.153), channel_id=1, source_target_pairs={{0,8},{8,16},{16,24},{24,32},{32,40},{40,48},{48,56},{56,64},{64,7... | collective-permute-start | bytes 62216 | tf_op jit(solution)/shard_map/ppermute | solution.py:22
  117.1 7.0 %collective-permute-start.65 = (f32[2,16,162]{2,1,0:T(8,128)S(1)}, f32[2,16,162]{2,1,0:T(8,128)S(1)}, u32[]{:S(2)}, u32[]{:S(2)}) collective-permute-start(f32[2,16,162]{2,1,0:T(8,128)S(1)} %get-tuple-element.154), channel_id=1, source_target_pairs={{8,0},{16,8},{24,16},{32,24},{40,32},{48,40},{56,48},{64,56},{72,6... | collective-permute-start | bytes 62216 | tf_op jit(solution)/shard_map/ppermute | solution.py:22
  118.4 5.8 %collective-permute-start.66 = (f32[2,16,162]{2,1,0:T(8,128)S(1)}, f32[2,16,162]{2,1,0:T(8,128)S(1)}, u32[]{:S(2)}, u32[]{:S(2)}) collective-permute-start(f32[2,16,162]{2,1,0:T(8,128)S(1)} %get-tuple-element.155), channel_id=1, source_target_pairs={{0,1},{1,2},{2,3},{3,4},{4,5},{5,6},{6,7},{8,9},{9,10},{10,11},{11... | collective-permute-start | bytes 62216 | tf_op jit(solution)/shard_map/ppermute | solution.py:22
  120.6 5.2 %collective-permute-start.67 = (f32[2,16,162]{2,1,0:T(8,128)S(1)}, f32[2,16,162]{2,1,0:T(8,128)S(1)}, u32[]{:S(2)}, u32[]{:S(2)}) collective-permute-start(f32[2,16,162]{2,1,0:T(8,128)S(1)} %get-tuple-element.156), channel_id=1, source_target_pairs={{1,0},{2,1},{3,2},{4,3},{5,4},{6,5},{7,6},{9,8},{10,9},{11,10},{12... | collective-permute-start | bytes 62216 | tf_op jit(solution)/shard_map/ppermute | solution.py:22
  170.2 23.7 %all-to-all-start.2 = ((f32[4,16,128]{2,1,0:T(8,128)}), f32[4,16,128]{2,1,0:T(8,128)S(1)}, u32[]{:S(2)}, u32[]{:S(2)}) async-start(f32[4,16,128]{2,1,0:T(8,128)} %broadcast_in_dim.83), calls=%async_computation.2 | async-start | bytes 65536 | tf_op jit(solution)/shard_map/all_to_all | solution.py:510

commit v2 on v1

--- a/solution.py
+++ b/solution.py
@@ -399,7 +399,9 @@
     older = refs[6 : 6 + ITERS]
     gram_ref, base_ref = refs[6 + ITERS :]
     add_received(acc_ref, (recv0_ref, recv1_ref, recv2_ref, recv3_ref), base_ref)
-    gram_ref[...] = gram_rows(ITERS, list(older) + [base_ref], gram_in_ref[...])
+    gram = gram_rows(ITERS, list(older) + [base_ref], gram_in_ref[...])
+    half = gram.shape[0] // 2
+    gram_ref[...] = gram[:half] + pltpu.roll(gram[half:], 64, 1)
 
 
 def finish_kernel(*refs):
@@ -407,7 +409,8 @@
     base_refs = refs[1 : 1 + ITERS]
     inv_high_ref, inv_low_ref, slot_ref, adjoint_ref, rel_ref, fine_ref = refs[1 + ITERS :]
     count = ITERS + 1
-    gram = gram_ref[...]
+    packed = gram_ref[...]
+    gram = jnp.concatenate([packed, pltpu.roll(packed, 64, 1)], axis=0)
 
     def lane(row, col):
         place = pair_lane(row, col)
@@ -493,35 +496,43 @@
     return jax.ShapeDtypeStruct(shape, kind)
 
 
-def group_sizes(count):
-    return (16, count // 16) if count > 16 and count % 16 == 0 else (count,)
-
-
-def sum_over(value, axis):
+def sum_groups(value, axes, groups):
+    size = len(groups[0])
+    copies = jnp.broadcast_to(value[None], (size,) + value.shape)
+    parts = lax.all_to_all(
+        copies, axes, 0, 0, axis_index_groups=groups if len(groups) > 1 else None
+    )
+    return jnp.sum(parts, axis=0)
+
+
+def sum_devices(value):
+    dom_count, blk_count = (lax.axis_size("dom"), lax.axis_size("blk"))
+    inner = 4 if dom_count % 4 == 0 else dom_count
+    size = inner * blk_count
+    near = [
+        [first + k for k in range(size)] for first in range(0, dom_count * blk_count, size)
+    ]
+    value = sum_groups(value, ("dom", "blk"), near)
+    if inner < dom_count:
+        far = [[first + k for k in range(0, dom_count, inner)] for first in range(inner)]
+        value = sum_groups(value, "dom", far)
+    return value
+
+
+def rotated(value, axis, steps):
     count = lax.axis_size(axis)
-    stride = 1
-    for size in group_sizes(count):
-        groups = [
-            [high * size * stride + k * stride + low for k in range(size)]
-            for high in range(count // (size * stride))
-            for low in range(stride)
-        ]
-        copies = jnp.broadcast_to(value[None], (size,) + value.shape)
-        parts = lax.all_to_all(
-            copies, axis, 0, 0, axis_index_groups=None if size == count else groups
-        )
-        value = jnp.sum(parts, axis=0)
-        stride *= size
-    return value
+    return lax.ppermute(
+        value, axis, [(source, (source + steps) % count) for source in range(count)]
+    )
 
 
 def exchange(sends):
     to_dom_prev, to_dom_next, to_blk_prev, to_blk_next = sends
     return (
-        shifted(to_dom_next, "dom", 1),
-        shifted(to_dom_prev, "dom", -1),
-        shifted(to_blk_next, "blk", 1),
-        shifted(to_blk_prev, "blk", -1),
+        rotated(to_dom_next, "dom", 1),
+        rotated(to_dom_prev, "dom", -1),
+        rotated(to_blk_next, "blk", 1),
+        rotated(to_blk_prev, "blk", -1),
     )
 
 
@@ -598,14 +609,13 @@
             given = [acc, *received, gram] + bases
             gram, _ = pl.pallas_call(
                 last_kernel,
-                out_shape=(struct(nrhs, 128), field),
+                out_shape=(struct(nrhs // 2, 128), field),
                 in_specs=vmem(len(given)),
                 out_specs=tuple(vmem(2)),
                 compiler_params=PARAMS,
                 name="last_part",
             )(*given)
-    gram = sum_over(gram, "blk")
-    gram = sum_over(gram, "dom")
+    gram = sum_devices(gram)
     given = [gram] + bases + [inv_high, inv_low, slots]
     adjoint, rel, fine = pl.pallas_call(
         finish_kernel,

time: 199 us -> 168 us (0.84)
  blocking collectives: 43 us -> 15.6 us
  waiting for transfers between devices: 31.6 us -> 21.4 us
  starting transfers between devices: 101 us -> 109 us
    all_to_all x2 -> x1, blocking collectives: 43 us -> 15.6 us  [sum_groups(): lax.all_to_all(copies, axes, 0, 0, axis_index_groups=groups if len(groups...]
    ppermute x32, starting transfers between devices: 88.9 us -> 101 us  [rotated(): lax.ppermute(value, axis, [(source, (source + steps) % count) for source...]
    ppermute x32, waiting for transfers between devices: 19.8 us -> 9.81 us  [rotated(): lax.ppermute(value, axis, [(source, (source + steps) % count) for source...]
    all_to_all x1, starting transfers between devices: 11.9 us -> 8.53 us  [sum_groups(): lax.all_to_all(copies, axes, 0, 0, axis_index_groups=groups if len(groups...]
  transfers between devices with their start and end apart: 33 -> 33, of which waited for: 13 -> 17; matrix products, arithmetic and copies ran while one was open for 0% -> 0% of each run, Pallas kernels for 2% -> 2%
where the time goes in v2:
time: 168 us
  starting transfers between devices  109 us (65%)
  waiting for transfers between devices  21.4 us (13%)
  blocking collectives  15.6 us (9%)
  Pallas kernels  14.4 us (9%)
  local copies, waits for them, and re-layouts  4.83 us (3%)
  between operations  1.84 us (1%)
    ppermute x32, starting transfers between devices, rotated(): lax.ppermute(value, axis, [(source, (source + steps) % count) for source...  101 us
    all_to_all x1, blocking collectives, sum_groups(): lax.all_to_all(copies, axes, 0, 0, axis_index_groups=groups if len(groups...  15.6 us
    all_to_all x1, waiting for transfers between devices, sum_groups(): lax.all_to_all(copies, axes, 0, 0, axis_index_groups=groups if len(groups...  11.6 us
    ppermute x32, waiting for transfers between devices, rotated(): lax.ppermute(value, axis, [(source, (source + steps) % count) for source...  9.81 us
    all_to_all x1, starting transfers between devices, sum_groups(): lax.all_to_all(copies, axes, 0, 0, axis_index_groups=groups if len(groups...  8.53 us
    pallas_call x1, Pallas kernels, shards(): outs = setup(neighbors, flags, adjoint_source, diag_blocks, face_blocks)  6.27 us
    unnamed x12, local copies, waits for them, and re-layouts  4.19 us
    pallas_call x8, Pallas kernels, shards(): pl.pallas_call(local_body, out_shape=(field, struct(nrhs, 128)), in_specs...  3.4 us
  transfers between devices with their start and end apart: 33, of which 17 were waited for; matrix products, arithmetic and copies ran while one was open for 0% of the time, Pallas kernels for 2%

profile of v2, /device:TPU:1, one launch (start us, length us, event | category | flops | bytes accessed | tf_op | source)
XLA Modules:
  0.0 167.6 jit_solution(4974081695521820315)
XLA Ops:
  0.6 1.2 copy.95.diag_ref
  1.9 2.9 %copy.96.face_ref = f32[4,6,162,162]{3,2,1,0:T(8,128)S(1)} copy(f32[4,6,162,162]{3,0,2,1:T(4,128)} %param.15) | data formatting | bytes 5038848 | tf_op args[2]
  4.9 6.3 %setup_blocks.1 = (bf16[8,162,162]{2,1,0:T(8,128)(2,1)S(1)}, bf16[8,162,162]{2,1,0:T(8,128)(2,1)S(1)}, bf16[12,162,162]{2,1,0:T(8,128)(2,1)S(1)}, bf16[12,162,16...) custom-call(s32[4,6]{1,0:T(4,128)S(1)} %copy-done.3, ...), custom_call_target="tpu_custom_call" | custom-call | tf_op jit(solution)/shard_map/setup_blocks/pallas_call | solution.py:570
  11.1 3.9 %collective-permute-start.36 = (f32[2,16,162]{2,1,0:T(8,128)S(1)}, f32[2,16,162]{2,1,0:T(8,128)S(1)}, u32[]{:S(2)}, u32[]{:S(2)}) collective-permute-start(f32[2,16,162]{2,1,0:T(8,128)S(1)} %get-tuple-element.102), channel_id=1, source_target_pairs={{0,8},{8,16},{16,24},{24,32},{32,40},{40,48},{48,56},{56,64},{64,7... | collective-permute-start | bytes 62216 | tf_op jit(solution)/shard_map/ppermute | solution.py:524
  15.1 12.1 %collective-permute-start.37 = (f32[2,16,162]{2,1,0:T(8,128)S(1)}, f32[2,16,162]{2,1,0:T(8,128)S(1)}, u32[]{:S(2)}, u32[]{:S(2)}) collective-permute-start(f32[2,16,162]{2,1,0:T(8,128)S(1)} %get-tuple-element.103), channel_id=1, source_target_pairs={{0,504},{8,0},{16,8},{24,16},{32,24},{40,32},{48,40},{56,48},{64,5... | collective-permute-start | bytes 62216 | tf_op jit(solution)/shard_map/ppermute | solution.py:524
  27.2 2.2 %collective-permute-start.38 = (f32[2,16,162]{2,1,0:T(8,128)S(1)}, f32[2,16,162]{2,1,0:T(8,128)S(1)}, u32[]{:S(2)}, u32[]{:S(2)}) collective-permute-start(f32[2,16,162]{2,1,0:T(8,128)S(1)} %get-tuple-element.104), channel_id=1, source_target_pairs={{0,1},{1,2},{2,3},{3,4},{4,5},{5,6},{6,7},{7,0},{8,9},{9,10},{10,1... | collective-permute-start | bytes 62216 | tf_op jit(solution)/shard_map/ppermute | solution.py:524
  29.4 0.4 local_part_0.1
  29.8 0.6 collective-permute-done.38.recv2_ref
  30.4 2.3 %collective-permute-done.39.recv3_ref = f32[2,16,162]{2,1,0:T(8,128)S(1)} collective-permute-done((f32[2,16,162]{2,1,0:T(8,128)S(1)}, f32[2,16,162]{2,1,0:T(8,128)S(1)}, u32[]{:S(2)}, u32[]{:S(2)}) %collective-permute-start.39) | collective-permute-done | bytes 20768 | tf_op jit(solution)/shard_map/ppermute | solution.py:524
  32.7 0.3 border_part_0.1
  33.0 1.9 %collective-permute-start.40 = (f32[2,16,162]{2,1,0:T(8,128)S(1)}, f32[2,16,162]{2,1,0:T(8,128)S(1)}, u32[]{:S(2)}, u32[]{:S(2)}) collective-permute-start(f32[2,16,162]{2,1,0:T(8,128)S(1)} %get-tuple-element.111), channel_id=1, source_target_pairs={{0,8},{8,16},{16,24},{24,32},{32,40},{40,48},{48,56},{56,64},{64,7... | collective-permute-start | bytes 62216 | tf_op jit(solution)/shard_map/ppermute | solution.py:524
  35.0 6.7 %collective-permute-start.41 = (f32[2,16,162]{2,1,0:T(8,128)S(1)}, f32[2,16,162]{2,1,0:T(8,128)S(1)}, u32[]{:S(2)}, u32[]{:S(2)}) collective-permute-start(f32[2,16,162]{2,1,0:T(8,128)S(1)} %get-tuple-element.112), channel_id=1, source_target_pairs={{0,504},{8,0},{16,8},{24,16},{32,24},{40,32},{48,40},{56,48},{64,5... | collective-permute-start | bytes 62216 | tf_op jit(solution)/shard_map/ppermute | solution.py:524
  41.7 0.6 collective-permute-start.42
  42.3 0.4 local_part_1.1
  42.7 0.5 collective-permute-done.42.recv2_ref
  43.3 2.6 %collective-permute-done.43.recv3_ref = f32[2,16,162]{2,1,0:T(8,128)S(1)} collective-permute-done((f32[2,16,162]{2,1,0:T(8,128)S(1)}, f32[2,16,162]{2,1,0:T(8,128)S(1)}, u32[]{:S(2)}, u32[]{:S(2)}) %collective-permute-start.43) | collective-permute-done | bytes 20768 | tf_op jit(solution)/shard_map/ppermute | solution.py:524
  45.9 0.3 border_part_1.1
  46.2 1.9 %collective-permute-start.44 = (f32[2,16,162]{2,1,0:T(8,128)S(1)}, f32[2,16,162]{2,1,0:T(8,128)S(1)}, u32[]{:S(2)}, u32[]{:S(2)}) collective-permute-start(f32[2,16,162]{2,1,0:T(8,128)S(1)} %get-tuple-element.118), channel_id=1, source_target_pairs={{0,8},{8,16},{16,24},{24,32},{32,40},{40,48},{48,56},{56,64},{64,7... | collective-permute-start | bytes 62216 | tf_op jit(solution)/shard_map/ppermute | solution.py:524
  48.1 6.7 %collective-permute-start.45 = (f32[2,16,162]{2,1,0:T(8,128)S(1)}, f32[2,16,162]{2,1,0:T(8,128)S(1)}, u32[]{:S(2)}, u32[]{:S(2)}) collective-permute-start(f32[2,16,162]{2,1,0:T(8,128)S(1)} %get-tuple-element.119), channel_id=1, source_target_pairs={{0,504},{8,0},{16,8},{24,16},{32,24},{40,32},{48,40},{56,48},{64,5... | collective-permute-start | bytes 62216 | tf_op jit(solution)/shard_map/ppermute | solution.py:524
  54.8 0.3 collective-permute-start.46
  55.1 1.3 collective-permute-start.47
  56.4 0.4 local_part_2.1
  56.8 0.2 collective-permute-done.46.recv2_ref
  57.0 1.4 collective-permute-done.47.recv3_ref
  58.4 0.3 border_part_2.1
  58.8 1.9 %collective-permute-start.48 = (f32[2,16,162]{2,1,0:T(8,128)S(1)}, f32[2,16,162]{2,1,0:T(8,128)S(1)}, u32[]{:S(2)}, u32[]{:S(2)}) collective-permute-start(f32[2,16,162]{2,1,0:T(8,128)S(1)} %get-tuple-element.125), channel_id=1, source_target_pairs={{0,8},{8,16},{16,24},{24,32},{32,40},{40,48},{48,56},{56,64},{64,7... | collective-permute-start | bytes 62216 | tf_op jit(solution)/shard_map/ppermute | solution.py:524
  60.7 6.7 %collective-permute-start.49 = (f32[2,16,162]{2,1,0:T(8,128)S(1)}, f32[2,16,162]{2,1,0:T(8,128)S(1)}, u32[]{:S(2)}, u32[]{:S(2)}) collective-permute-start(f32[2,16,162]{2,1,0:T(8,128)S(1)} %get-tuple-element.126), channel_id=1, source_target_pairs={{0,504},{8,0},{16,8},{24,16},{32,24},{40,32},{48,40},{56,48},{64,5... | collective-permute-start | bytes 62216 | tf_op jit(solution)/shard_map/ppermute | solution.py:524
  67.4 0.6 collective-permute-start.50
  67.9 2.5 %collective-permute-start.51 = (f32[2,16,162]{2,1,0:T(8,128)S(1)}, f32[2,16,162]{2,1,0:T(8,128)S(1)}, u32[]{:S(2)}, u32[]{:S(2)}) collective-permute-start(f32[2,16,162]{2,1,0:T(8,128)S(1)} %get-tuple-element.128), channel_id=1, source_target_pairs={{0,7},{1,0},{2,1},{3,2},{4,3},{5,4},{6,5},{7,6},{8,15},{9,8},{10,9... | collective-permute-start | bytes 62216 | tf_op jit(solution)/shard_map/ppermute | solution.py:524
  70.4 0.4 local_part_3.1
  70.9 0.2 collective-permute-done.50.recv2_ref
  71.1 0.2 collective-permute-done.51.recv3_ref
  71.3 0.3 border_part_3.1
  71.6 1.9 %collective-permute-start.52 = (f32[2,16,162]{2,1,0:T(8,128)S(1)}, f32[2,16,162]{2,1,0:T(8,128)S(1)}, u32[]{:S(2)}, u32[]{:S(2)}) collective-permute-start(f32[2,16,162]{2,1,0:T(8,128)S(1)} %get-tuple-element.132), channel_id=1, source_target_pairs={{0,8},{8,16},{16,24},{24,32},{32,40},{40,48},{48,56},{56,64},{64,7... | collective-permute-start | bytes 62216 | tf_op jit(solution)/shard_map/ppermute | solution.py:524
  73.5 6.7 %collective-permute-start.53 = (f32[2,16,162]{2,1,0:T(8,128)S(1)}, f32[2,16,162]{2,1,0:T(8,128)S(1)}, u32[]{:S(2)}, u32[]{:S(2)}) collective-permute-start(f32[2,16,162]{2,1,0:T(8,128)S(1)} %get-tuple-element.133), channel_id=1, source_target_pairs={{0,504},{8,0},{16,8},{24,16},{32,24},{40,32},{48,40},{56,48},{64,5... | collective-permute-start | bytes 62216 | tf_op jit(solution)/shard_map/ppermute | solution.py:524
  80.2 0.6 collective-permute-start.54
  80.8 3.7 %collective-permute-start.55 = (f32[2,16,162]{2,1,0:T(8,128)S(1)}, f32[2,16,162]{2,1,0:T(8,128)S(1)}, u32[]{:S(2)}, u32[]{:S(2)}) collective-permute-start(f32[2,16,162]{2,1,0:T(8,128)S(1)} %get-tuple-element.135), channel_id=1, source_target_pairs={{0,7},{1,0},{2,1},{3,2},{4,3},{5,4},{6,5},{7,6},{8,15},{9,8},{10,9... | collective-permute-start | bytes 62216 | tf_op jit(solution)/shard_map/ppermute | solution.py:524
  84.5 0.4 local_part_4.1
  84.9 0.2 collective-permute-done.54.recv2_ref
  85.4 0.3 border_part_4.1
  85.7 1.9 %collective-permute-start.56 = (f32[2,16,162]{2,1,0:T(8,128)S(1)}, f32[2,16,162]{2,1,0:T(8,128)S(1)}, u32[]{:S(2)}, u32[]{:S(2)}) collective-permute-start(f32[2,16,162]{2,1,0:T(8,128)S(1)} %get-tuple-element.139), channel_id=1, source_target_pairs={{0,8},{8,16},{16,24},{24,32},{32,40},{40,48},{48,56},{56,64},{64,7... | collective-permute-start | bytes 62216 | tf_op jit(solution)/shard_map/ppermute | solution.py:524
  87.6 6.7 %collective-permute-start.57 = (f32[2,16,162]{2,1,0:T(8,128)S(1)}, f32[2,16,162]{2,1,0:T(8,128)S(1)}, u32[]{:S(2)}, u32[]{:S(2)}) collective-permute-start(f32[2,16,162]{2,1,0:T(8,128)S(1)} %get-tuple-element.140), channel_id=1, source_target_pairs={{0,504},{8,0},{16,8},{24,16},{32,24},{40,32},{48,40},{56,48},{64,5... | collective-permute-start | bytes 62216 | tf_op jit(solution)/shard_map/ppermute | solution.py:524
  94.3 4.2 %collective-permute-start.59 = (f32[2,16,162]{2,1,0:T(8,128)S(1)}, f32[2,16,162]{2,1,0:T(8,128)S(1)}, u32[]{:S(2)}, u32[]{:S(2)}) collective-permute-start(f32[2,16,162]{2,1,0:T(8,128)S(1)} %get-tuple-element.142), channel_id=1, source_target_pairs={{0,7},{1,0},{2,1},{3,2},{4,3},{5,4},{6,5},{7,6},{8,15},{9,8},{10,9... | collective-permute-start | bytes 62216 | tf_op jit(solution)/shard_map/ppermute | solution.py:524
  98.6 0.4 local_part_5.1
  99.0 0.2 collective-permute-done.58.recv2_ref
  99.4 0.3 border_part_5.1
  99.7 1.9 %collective-permute-start.60 = (f32[2,16,162]{2,1,0:T(8,128)S(1)}, f32[2,16,162]{2,1,0:T(8,128)S(1)}, u32[]{:S(2)}, u32[]{:S(2)}) collective-permute-start(f32[2,16,162]{2,1,0:T(8,128)S(1)} %get-tuple-element.146), channel_id=1, source_target_pairs={{0,8},{8,16},{16,24},{24,32},{32,40},{40,48},{48,56},{56,64},{64,7... | collective-permute-start | bytes 62216 | tf_op jit(solution)/shard_map/ppermute | solution.py:524
  101.7 6.7 %collective-permute-start.61 = (f32[2,16,162]{2,1,0:T(8,128)S(1)}, f32[2,16,162]{2,1,0:T(8,128)S(1)}, u32[]{:S(2)}, u32[]{:S(2)}) collective-permute-start(f32[2,16,162]{2,1,0:T(8,128)S(1)} %get-tuple-element.147), channel_id=1, source_target_pairs={{0,504},{8,0},{16,8},{24,16},{32,24},{40,32},{48,40},{56,48},{64,5... | collective-permute-start | bytes 62216 | tf_op jit(solution)/shard_map/ppermute | solution.py:524
  108.4 4.2 %collective-permute-start.63 = (f32[2,16,162]{2,1,0:T(8,128)S(1)}, f32[2,16,162]{2,1,0:T(8,128)S(1)}, u32[]{:S(2)}, u32[]{:S(2)}) collective-permute-start(f32[2,16,162]{2,1,0:T(8,128)S(1)} %get-tuple-element.149), channel_id=1, source_target_pairs={{0,7},{1,0},{2,1},{3,2},{4,3},{5,4},{6,5},{7,6},{8,15},{9,8},{10,9... | collective-permute-start | bytes 62216 | tf_op jit(solution)/shard_map/ppermute | solution.py:524
  112.6 0.4 local_part_6.1
  113.1 0.2 collective-permute-done.62.recv2_ref
  113.5 0.3 border_part_6.1
  113.8 1.9 %collective-permute-start.64 = (f32[2,16,162]{2,1,0:T(8,128)S(1)}, f32[2,16,162]{2,1,0:T(8,128)S(1)}, u32[]{:S(2)}, u32[]{:S(2)}) collective-permute-start(f32[2,16,162]{2,1,0:T(8,128)S(1)} %get-tuple-element.153), channel_id=1, source_target_pairs={{0,8},{8,16},{16,24},{24,32},{32,40},{40,48},{48,56},{56,64},{64,7... | collective-permute-start | bytes 62216 | tf_op jit(solution)/shard_map/ppermute | solution.py:524
  115.7 6.7 %collective-permute-start.65 = (f32[2,16,162]{2,1,0:T(8,128)S(1)}, f32[2,16,162]{2,1,0:T(8,128)S(1)}, u32[]{:S(2)}, u32[]{:S(2)}) collective-permute-start(f32[2,16,162]{2,1,0:T(8,128)S(1)} %get-tuple-element.154), channel_id=1, source_target_pairs={{0,504},{8,0},{16,8},{24,16},{32,24},{40,32},{48,40},{56,48},{64,5... | collective-permute-start | bytes 62216 | tf_op jit(solution)/shard_map/ppermute | solution.py:524
  122.5 4.2 %collective-permute-start.67 = (f32[2,16,162]{2,1,0:T(8,128)S(1)}, f32[2,16,162]{2,1,0:T(8,128)S(1)}, u32[]{:S(2)}, u32[]{:S(2)}) collective-permute-start(f32[2,16,162]{2,1,0:T(8,128)S(1)} %get-tuple-element.156), channel_id=1, source_target_pairs={{0,7},{1,0},{2,1},{3,2},{4,3},{5,4},{6,5},{7,6},{8,15},{9,8},{10,9... | collective-permute-start | bytes 62216 | tf_op jit(solution)/shard_map/ppermute | solution.py:524
  126.7 0.4 local_part_7.1
  127.1 0.2 collective-permute-done.66.refs_3_
  127.6 0.7 last_part.1
  128.3 15.6 %all_to_all.10 = f32[32,8,128]{2,1,0:T(8,128)S(1)} all-to-all(f32[32,8,128]{2,1,0:T(8,128)S(1)} %broadcast_in_dim.79), channel_id=1, replica_groups={{0,1,2,3,4,5,6,7,8,9,10,11,12,13,14,15,16,17,18,19,20,21,22,23,24,25,26..., dimensions={0} | all-to-all | bytes 262144 | tf_op jit(solution)/shard_map/all_to_all | solution.py:502
  143.8 0.6 broadcast_in_dim.80
  144.5 8.5 %all-to-all-start.1 = ((f32[16,8,128]{2,1,0:T(8,128)}), f32[16,8,128]{2,1,0:T(8,128)S(1)}, u32[]{:S(2)}, u32[]{:S(2)}) async-start(f32[16,8,128]{2,1,0:T(8,128)} %broadcast_in_dim.80), calls=%async_computation.1 | async-start | bytes 131072 | tf_op jit(solution)/shard_map/all_to_all | solution.py:502
  153.0 11.6 %all-to-all-done.1 = f32[16,8,128]{2,1,0:T(8,128)S(1)} async-done(((f32[16,8,128]{2,1,0:T(8,128)}), f32[16,8,128]{2,1,0:T(8,128)S(1)}, u32[]{:S(2)}, u32[]{:S(2)}) %all-to-all-start.1) | async-done | bytes 65568 | tf_op jit(solution)/shard_map/all_to_all | solution.py:502
  164.6 1.8 %finish_part.1 = (f32[16,4,162]{2,1,0:T(4,128)}, f32[1,16]{1,0:T(1,128)}, s32[1]{0:T(128)}) custom-call(f32[8,128]{1,0:T(8,128)S(1)} %reduce_sum.469.refs_0_, f32[4,16,162]{2,1,0:T(8,128)S(1)} %get-tuple-element.98.refs_0_.refs_6_.refs_1_, f32[4,16,162]{2,1,0:T(8,128)S(1)} %get-tuple-element.108.refs_1_.refs_7_.refs_2_, ...), custom_call_target="tpu_custom_call" | custom-call | tf_op jit(solution)/shard_map/finish_part/pallas_call | solution.py:620
  167.2 0.3 conditional.1
  (38 shorter events, 1.0 us)
Async XLA Ops:
  1.9 3.0 %copy-start.1 = (f32[16,4,162]{2,1,0:T(4,128)S(1)}, f32[16,4,162]{2,1,0:T(4,128)}, u32[]{:S(2)}) copy-start(f32[16,4,162]{2,1,0:T(4,128)} %src_ref.1) | copy-start | bytes 124420
  1.9 3.0 %copy-start.3 = (s32[4,6]{1,0:T(4,128)S(1)}, s32[4,6]{1,0:T(4,128)}, u32[]{:S(2)}) copy-start(s32[4,6]{1,0:T(4,128)} %nbr_ref.1) | copy-start | bytes 292
  1.9 3.0 %copy-start.6 = (s32[4,6]{1,0:T(4,128)S(1)}, s32[4,6]{1,0:T(4,128)}, u32[]{:S(2)}) copy-start(s32[4,6]{1,0:T(4,128)} %flag_ref.1) | copy-start | bytes 292
  11.1 18.7 %collective-permute-start.36 = (f32[2,16,162]{2,1,0:T(8,128)S(1)}, f32[2,16,162]{2,1,0:T(8,128)S(1)}, u32[]{:S(2)}, u32[]{:S(2)}) collective-permute-start(f32[2,16,162]{2,1,0:T(8,128)S(1)} %get-tuple-element.102), channel_id=1, source_target_pairs={{0,8},{8,16},{16,24},{24,32},{32,40},{40,48},{48,56},{56,64},{64,7... | collective-permute-start | bytes 62216 | tf_op jit(solution)/shard_map/ppermute | solution.py:524
  15.1 14.7 %collective-permute-start.37 = (f32[2,16,162]{2,1,0:T(8,128)S(1)}, f32[2,16,162]{2,1,0:T(8,128)S(1)}, u32[]{:S(2)}, u32[]{:S(2)}) collective-permute-start(f32[2,16,162]{2,1,0:T(8,128)S(1)} %get-tuple-element.103), channel_id=1, source_target_pairs={{0,504},{8,0},{16,8},{24,16},{32,24},{40,32},{48,40},{56,48},{64,5... | collective-permute-start | bytes 62216 | tf_op jit(solution)/shard_map/ppermute | solution.py:524
  27.2 3.2 %collective-permute-start.38 = (f32[2,16,162]{2,1,0:T(8,128)S(1)}, f32[2,16,162]{2,1,0:T(8,128)S(1)}, u32[]{:S(2)}, u32[]{:S(2)}) collective-permute-start(f32[2,16,162]{2,1,0:T(8,128)S(1)} %get-tuple-element.104), channel_id=1, source_target_pairs={{0,1},{1,2},{2,3},{3,4},{4,5},{5,6},{6,7},{7,0},{8,9},{9,10},{10,1... | collective-permute-start | bytes 62216 | tf_op jit(solution)/shard_map/ppermute | solution.py:524
  29.4 3.3 %collective-permute-start.39 = (f32[2,16,162]{2,1,0:T(8,128)S(1)}, f32[2,16,162]{2,1,0:T(8,128)S(1)}, u32[]{:S(2)}, u32[]{:S(2)}) collective-permute-start(f32[2,16,162]{2,1,0:T(8,128)S(1)} %get-tuple-element.105), channel_id=1, source_target_pairs={{0,7},{1,0},{2,1},{3,2},{4,3},{5,4},{6,5},{7,6},{8,15},{9,8},{10,9... | collective-permute-start | bytes 62216 | tf_op jit(solution)/shard_map/ppermute | solution.py:524
  33.0 9.7 %collective-permute-start.40 = (f32[2,16,162]{2,1,0:T(8,128)S(1)}, f32[2,16,162]{2,1,0:T(8,128)S(1)}, u32[]{:S(2)}, u32[]{:S(2)}) collective-permute-start(f32[2,16,162]{2,1,0:T(8,128)S(1)} %get-tuple-element.111), channel_id=1, source_target_pairs={{0,8},{8,16},{16,24},{24,32},{32,40},{40,48},{48,56},{56,64},{64,7... | collective-permute-start | bytes 62216 | tf_op jit(solution)/shard_map/ppermute | solution.py:524
  35.0 7.8 %collective-permute-start.41 = (f32[2,16,162]{2,1,0:T(8,128)S(1)}, f32[2,16,162]{2,1,0:T(8,128)S(1)}, u32[]{:S(2)}, u32[]{:S(2)}) collective-permute-start(f32[2,16,162]{2,1,0:T(8,128)S(1)} %get-tuple-element.112), channel_id=1, source_target_pairs={{0,504},{8,0},{16,8},{24,16},{32,24},{40,32},{48,40},{56,48},{64,5... | collective-permute-start | bytes 62216 | tf_op jit(solution)/shard_map/ppermute | solution.py:524
  41.7 1.6 collective-permute-start.42
  42.2 3.6 %collective-permute-start.43 = (f32[2,16,162]{2,1,0:T(8,128)S(1)}, f32[2,16,162]{2,1,0:T(8,128)S(1)}, u32[]{:S(2)}, u32[]{:S(2)}) collective-permute-start(f32[2,16,162]{2,1,0:T(8,128)S(1)} %get-tuple-element.114), channel_id=1, source_target_pairs={{0,7},{1,0},{2,1},{3,2},{4,3},{5,4},{6,5},{7,6},{8,15},{9,8},{10,9... | collective-permute-start | bytes 62216 | tf_op jit(solution)/shard_map/ppermute | solution.py:524
  46.2 10.6 %collective-permute-start.44 = (f32[2,16,162]{2,1,0:T(8,128)S(1)}, f32[2,16,162]{2,1,0:T(8,128)S(1)}, u32[]{:S(2)}, u32[]{:S(2)}) collective-permute-start(f32[2,16,162]{2,1,0:T(8,128)S(1)} %get-tuple-element.118), channel_id=1, source_target_pairs={{0,8},{8,16},{16,24},{24,32},{32,40},{40,48},{48,56},{56,64},{64,7... | collective-permute-start | bytes 62216 | tf_op jit(solution)/shard_map/ppermute | solution.py:524
  48.1 8.7 %collective-permute-start.45 = (f32[2,16,162]{2,1,0:T(8,128)S(1)}, f32[2,16,162]{2,1,0:T(8,128)S(1)}, u32[]{:S(2)}, u32[]{:S(2)}) collective-permute-start(f32[2,16,162]{2,1,0:T(8,128)S(1)} %get-tuple-element.119), channel_id=1, source_target_pairs={{0,504},{8,0},{16,8},{24,16},{32,24},{40,32},{48,40},{56,48},{64,5... | collective-permute-start | bytes 62216 | tf_op jit(solution)/shard_map/ppermute | solution.py:524
  54.8 2.2 %collective-permute-start.46 = (f32[2,16,162]{2,1,0:T(8,128)S(1)}, f32[2,16,162]{2,1,0:T(8,128)S(1)}, u32[]{:S(2)}, u32[]{:S(2)}) collective-permute-start(f32[2,16,162]{2,1,0:T(8,128)S(1)} %get-tuple-element.120), channel_id=1, source_target_pairs={{0,1},{1,2},{2,3},{3,4},{4,5},{5,6},{6,7},{7,0},{8,9},{9,10},{10,1... | collective-permute-start | bytes 62216 | tf_op jit(solution)/shard_map/ppermute | solution.py:524
  55.1 3.3 %collective-permute-start.47 = (f32[2,16,162]{2,1,0:T(8,128)S(1)}, f32[2,16,162]{2,1,0:T(8,128)S(1)}, u32[]{:S(2)}, u32[]{:S(2)}) collective-permute-start(f32[2,16,162]{2,1,0:T(8,128)S(1)} %get-tuple-element.121), channel_id=1, source_target_pairs={{0,7},{1,0},{2,1},{3,2},{4,3},{5,4},{6,5},{7,6},{8,15},{9,8},{10,9... | collective-permute-start | bytes 62216 | tf_op jit(solution)/shard_map/ppermute | solution.py:524
  58.8 12.1 %collective-permute-start.48 = (f32[2,16,162]{2,1,0:T(8,128)S(1)}, f32[2,16,162]{2,1,0:T(8,128)S(1)}, u32[]{:S(2)}, u32[]{:S(2)}) collective-permute-start(f32[2,16,162]{2,1,0:T(8,128)S(1)} %get-tuple-element.125), channel_id=1, source_target_pairs={{0,8},{8,16},{16,24},{24,32},{32,40},{40,48},{48,56},{56,64},{64,7... | collective-permute-start | bytes 62216 | tf_op jit(solution)/shard_map/ppermute | solution.py:524
  60.7 10.2 %collective-permute-start.49 = (f32[2,16,162]{2,1,0:T(8,128)S(1)}, f32[2,16,162]{2,1,0:T(8,128)S(1)}, u32[]{:S(2)}, u32[]{:S(2)}) collective-permute-start(f32[2,16,162]{2,1,0:T(8,128)S(1)} %get-tuple-element.126), channel_id=1, source_target_pairs={{0,504},{8,0},{16,8},{24,16},{32,24},{40,32},{48,40},{56,48},{64,5... | collective-permute-start | bytes 62216 | tf_op jit(solution)/shard_map/ppermute | solution.py:524
  67.4 3.7 %collective-permute-start.50 = (f32[2,16,162]{2,1,0:T(8,128)S(1)}, f32[2,16,162]{2,1,0:T(8,128)S(1)}, u32[]{:S(2)}, u32[]{:S(2)}) collective-permute-start(f32[2,16,162]{2,1,0:T(8,128)S(1)} %get-tuple-element.127), channel_id=1, source_target_pairs={{0,1},{1,2},{2,3},{3,4},{4,5},{5,6},{6,7},{7,0},{8,9},{9,10},{10,1... | collective-permute-start | bytes 62216 | tf_op jit(solution)/shard_map/ppermute | solution.py:524
  67.9 3.3 %collective-permute-start.51 = (f32[2,16,162]{2,1,0:T(8,128)S(1)}, f32[2,16,162]{2,1,0:T(8,128)S(1)}, u32[]{:S(2)}, u32[]{:S(2)}) collective-permute-start(f32[2,16,162]{2,1,0:T(8,128)S(1)} %get-tuple-element.128), channel_id=1, source_target_pairs={{0,7},{1,0},{2,1},{3,2},{4,3},{5,4},{6,5},{7,6},{8,15},{9,8},{10,9... | collective-permute-start | bytes 62216 | tf_op jit(solution)/shard_map/ppermute | solution.py:524
  71.6 13.3 %collective-permute-start.52 = (f32[2,16,162]{2,1,0:T(8,128)S(1)}, f32[2,16,162]{2,1,0:T(8,128)S(1)}, u32[]{:S(2)}, u32[]{:S(2)}) collective-permute-start(f32[2,16,162]{2,1,0:T(8,128)S(1)} %get-tuple-element.132), channel_id=1, source_target_pairs={{0,8},{8,16},{16,24},{24,32},{32,40},{40,48},{48,56},{56,64},{64,7... | collective-permute-start | bytes 62216 | tf_op jit(solution)/shard_map/ppermute | solution.py:524
  73.5 11.4 %collective-permute-start.53 = (f32[2,16,162]{2,1,0:T(8,128)S(1)}, f32[2,16,162]{2,1,0:T(8,128)S(1)}, u32[]{:S(2)}, u32[]{:S(2)}) collective-permute-start(f32[2,16,162]{2,1,0:T(8,128)S(1)} %get-tuple-element.133), channel_id=1, source_target_pairs={{0,504},{8,0},{16,8},{24,16},{32,24},{40,32},{48,40},{56,48},{64,5... | collective-permute-start | bytes 62216 | tf_op jit(solution)/shard_map/ppermute | solution.py:524
  80.2 4.9 %collective-permute-start.54 = (f32[2,16,162]{2,1,0:T(8,128)S(1)}, f32[2,16,162]{2,1,0:T(8,128)S(1)}, u32[]{:S(2)}, u32[]{:S(2)}) collective-permute-start(f32[2,16,162]{2,1,0:T(8,128)S(1)} %get-tuple-element.134), channel_id=1, source_target_pairs={{0,1},{1,2},{2,3},{3,4},{4,5},{5,6},{6,7},{7,0},{8,9},{9,10},{10,1... | collective-permute-start | bytes 62216 | tf_op jit(solution)/shard_map/ppermute | solution.py:524
  80.8 4.6 %collective-permute-start.55 = (f32[2,16,162]{2,1,0:T(8,128)S(1)}, f32[2,16,162]{2,1,0:T(8,128)S(1)}, u32[]{:S(2)}, u32[]{:S(2)}) collective-permute-start(f32[2,16,162]{2,1,0:T(8,128)S(1)} %get-tuple-element.135), channel_id=1, source_target_pairs={{0,7},{1,0},{2,1},{3,2},{4,3},{5,4},{6,5},{7,6},{8,15},{9,8},{10,9... | collective-permute-start | bytes 62216 | tf_op jit(solution)/shard_map/ppermute | solution.py:524
  85.7 13.3 %collective-permute-start.56 = (f32[2,16,162]{2,1,0:T(8,128)S(1)}, f32[2,16,162]{2,1,0:T(8,128)S(1)}, u32[]{:S(2)}, u32[]{:S(2)}) collective-permute-start(f32[2,16,162]{2,1,0:T(8,128)S(1)} %get-tuple-element.139), channel_id=1, source_target_pairs={{0,8},{8,16},{16,24},{24,32},{32,40},{40,48},{48,56},{56,64},{64,7... | collective-permute-start | bytes 62216 | tf_op jit(solution)/shard_map/ppermute | solution.py:524
  87.6 11.4 %collective-permute-start.57 = (f32[2,16,162]{2,1,0:T(8,128)S(1)}, f32[2,16,162]{2,1,0:T(8,128)S(1)}, u32[]{:S(2)}, u32[]{:S(2)}) collective-permute-start(f32[2,16,162]{2,1,0:T(8,128)S(1)} %get-tuple-element.140), channel_id=1, source_target_pairs={{0,504},{8,0},{16,8},{24,16},{32,24},{40,32},{48,40},{56,48},{64,5... | collective-permute-start | bytes 62216 | tf_op jit(solution)/shard_map/ppermute | solution.py:524
  94.3 4.9 %collective-permute-start.58 = (f32[2,16,162]{2,1,0:T(8,128)S(1)}, f32[2,16,162]{2,1,0:T(8,128)S(1)}, u32[]{:S(2)}, u32[]{:S(2)}) collective-permute-start(f32[2,16,162]{2,1,0:T(8,128)S(1)} %get-tuple-element.141), channel_id=1, source_target_pairs={{0,1},{1,2},{2,3},{3,4},{4,5},{5,6},{6,7},{7,0},{8,9},{9,10},{10,1... | collective-permute-start | bytes 62216 | tf_op jit(solution)/shard_map/ppermute | solution.py:524
  94.3 5.1 %collective-permute-start.59 = (f32[2,16,162]{2,1,0:T(8,128)S(1)}, f32[2,16,162]{2,1,0:T(8,128)S(1)}, u32[]{:S(2)}, u32[]{:S(2)}) collective-permute-start(f32[2,16,162]{2,1,0:T(8,128)S(1)} %get-tuple-element.142), channel_id=1, source_target_pairs={{0,7},{1,0},{2,1},{3,2},{4,3},{5,4},{6,5},{7,6},{8,15},{9,8},{10,9... | collective-permute-start | bytes 62216 | tf_op jit(solution)/shard_map/ppermute | solution.py:524
  99.7 13.3 %collective-permute-start.60 = (f32[2,16,162]{2,1,0:T(8,128)S(1)}, f32[2,16,162]{2,1,0:T(8,128)S(1)}, u32[]{:S(2)}, u32[]{:S(2)}) collective-permute-start(f32[2,16,162]{2,1,0:T(8,128)S(1)} %get-tuple-element.146), channel_id=1, source_target_pairs={{0,8},{8,16},{16,24},{24,32},{32,40},{40,48},{48,56},{56,64},{64,7... | collective-permute-start | bytes 62216 | tf_op jit(solution)/shard_map/ppermute | solution.py:524
  101.7 11.4 %collective-permute-start.61 = (f32[2,16,162]{2,1,0:T(8,128)S(1)}, f32[2,16,162]{2,1,0:T(8,128)S(1)}, u32[]{:S(2)}, u32[]{:S(2)}) collective-permute-start(f32[2,16,162]{2,1,0:T(8,128)S(1)} %get-tuple-element.147), channel_id=1, source_target_pairs={{0,504},{8,0},{16,8},{24,16},{32,24},{40,32},{48,40},{56,48},{64,5... | collective-permute-start | bytes 62216 | tf_op jit(solution)/shard_map/ppermute | solution.py:524
  108.4 4.9 %collective-permute-start.62 = (f32[2,16,162]{2,1,0:T(8,128)S(1)}, f32[2,16,162]{2,1,0:T(8,128)S(1)}, u32[]{:S(2)}, u32[]{:S(2)}) collective-permute-start(f32[2,16,162]{2,1,0:T(8,128)S(1)} %get-tuple-element.148), channel_id=1, source_target_pairs={{0,1},{1,2},{2,3},{3,4},{4,5},{5,6},{6,7},{7,0},{8,9},{9,10},{10,1... | collective-permute-start | bytes 62216 | tf_op jit(solution)/shard_map/ppermute | solution.py:524
  108.4 5.1 %collective-permute-start.63 = (f32[2,16,162]{2,1,0:T(8,128)S(1)}, f32[2,16,162]{2,1,0:T(8,128)S(1)}, u32[]{:S(2)}, u32[]{:S(2)}) collective-permute-start(f32[2,16,162]{2,1,0:T(8,128)S(1)} %get-tuple-element.149), channel_id=1, source_target_pairs={{0,7},{1,0},{2,1},{3,2},{4,3},{5,4},{6,5},{7,6},{8,15},{9,8},{10,9... | collective-permute-start | bytes 62216 | tf_op jit(solution)/shard_map/ppermute | solution.py:524
  112.6 54.5 %copy-start.2 = (f32[4,162,162]{2,0,1:T(4,128)S(1)}, f32[4,162,162]{2,0,1:T(4,128)}, u32[]{:S(2)}) copy-start(f32[4,162,162]{2,0,1:T(4,128)} %param.14) | copy-start | bytes 1259716
  112.6 54.5 %copy-start.7 = (s32[4,6]{1,0:T(4,128)S(1)}, s32[4,6]{1,0:T(4,128)}, u32[]{:S(2)}) copy-start(s32[4,6]{1,0:T(4,128)} %param.17) | copy-start | bytes 292
  113.8 13.3 %collective-permute-start.64 = (f32[2,16,162]{2,1,0:T(8,128)S(1)}, f32[2,16,162]{2,1,0:T(8,128)S(1)}, u32[]{:S(2)}, u32[]{:S(2)}) collective-permute-start(f32[2,16,162]{2,1,0:T(8,128)S(1)} %get-tuple-element.153), channel_id=1, source_target_pairs={{0,8},{8,16},{16,24},{24,32},{32,40},{40,48},{48,56},{56,64},{64,7... | collective-permute-start | bytes 62216 | tf_op jit(solution)/shard_map/ppermute | solution.py:524
  115.7 11.4 %collective-permute-start.65 = (f32[2,16,162]{2,1,0:T(8,128)S(1)}, f32[2,16,162]{2,1,0:T(8,128)S(1)}, u32[]{:S(2)}, u32[]{:S(2)}) collective-permute-start(f32[2,16,162]{2,1,0:T(8,128)S(1)} %get-tuple-element.154), channel_id=1, source_target_pairs={{0,504},{8,0},{16,8},{24,16},{32,24},{40,32},{48,40},{56,48},{64,5... | collective-permute-start | bytes 62216 | tf_op jit(solution)/shard_map/ppermute | solution.py:524
  122.4 4.9 %collective-permute-start.66 = (f32[2,16,162]{2,1,0:T(8,128)S(1)}, f32[2,16,162]{2,1,0:T(8,128)S(1)}, u32[]{:S(2)}, u32[]{:S(2)}) collective-permute-start(f32[2,16,162]{2,1,0:T(8,128)S(1)} %get-tuple-element.155), channel_id=1, source_target_pairs={{0,1},{1,2},{2,3},{3,4},{4,5},{5,6},{6,7},{7,0},{8,9},{9,10},{10,1... | collective-permute-start | bytes 62216 | tf_op jit(solution)/shard_map/ppermute | solution.py:524
  122.5 5.1 %collective-permute-start.67 = (f32[2,16,162]{2,1,0:T(8,128)S(1)}, f32[2,16,162]{2,1,0:T(8,128)S(1)}, u32[]{:S(2)}, u32[]{:S(2)}) collective-permute-start(f32[2,16,162]{2,1,0:T(8,128)S(1)} %get-tuple-element.156), channel_id=1, source_target_pairs={{0,7},{1,0},{2,1},{3,2},{4,3},{5,4},{6,5},{7,6},{8,15},{9,8},{10,9... | collective-permute-start | bytes 62216 | tf_op jit(solution)/shard_map/ppermute | solution.py:524
  144.5 20.1 %all-to-all-start.1 = ((f32[16,8,128]{2,1,0:T(8,128)}), f32[16,8,128]{2,1,0:T(8,128)S(1)}, u32[]{:S(2)}, u32[]{:S(2)}) async-start(f32[16,8,128]{2,1,0:T(8,128)} %broadcast_in_dim.80), calls=%async_computation.1 | async-start | bytes 131072 | tf_op jit(solution)/shard_map/all_to_all | solution.py:502

commit v3 on v2

--- a/solution.py
+++ b/solution.py
@@ -227,24 +227,70 @@
     return both[:rows] + both[rows:] + dot32(high, block_low)
 
 
-def write_sends(halves, out_high_ref, out_low_ref, send_refs):
+FROM_X = CELLS
+FROM_Y = 2 * CELLS
+OUTWARD = 3 * CELLS
+BLOCKS = OUTWARD + 8
+RING_TARGETS = (0, 1, 2, 3, 0, 2, 1, 3)
+
+
+def local_products(halves, high_ref, low_ref):
+    results = []
+    for cell in range(CELLS):
+        total = None
+        for source, entry in (
+            (cell, cell), (cell ^ 2, FROM_X + (cell ^ 2)), (cell ^ 1, FROM_Y + (cell ^ 1))
+        ):
+            part = row_times(*halves[source], high_ref[entry], low_ref[entry])
+            total = part if total is None else total + part
+        results.append(total)
+    return results
+
+
+def outward_products(halves, high_ref, low_ref):
+    results = []
     for way in range(4):
         for place in range(2):
-            stacked, high = halves[OUT_CELLS[way][place]]
-            slot = 2 * way + place
-            send_refs[way][place] = row_times(
-                stacked, high, out_high_ref[slot], out_low_ref[slot]
+            entry = OUTWARD + 2 * way + place
+            results.append(
+                row_times(*halves[OUT_CELLS[way][place]], high_ref[entry], low_ref[entry])
             )
+    return results
+
+
+def padded(width):
+    return (width + 7) // 8 * 8
+
+
+def put_rows(ref, first, values):
+    rows = values[0].shape[0]
+    for place, value in enumerate(values):
+        ref[first + rows * place : first + rows * (place + 1), :] = value
+
+
+def get_rows(ref, first, rows, place):
+    return ref[first + rows * place : first + rows * (place + 1), :]
+
+
+def send_along_blk(local, outward, prev_ref, next_ref, first):
+    for ref, way, cells in ((prev_ref, 2, (0, 2)), (next_ref, 3, (1, 3))):
+        put_rows(
+            ref, first,
+            [
+                outward[2 * way], outward[2 * way + 1], local[cells[0]], local[cells[1]],
+                outward[cells[0] % 2], outward[2 + cells[0] % 2],
+            ],
+        )
 
 
 def setup_kernel(
     nbr_ref, flag_ref, src_ref, diag_ref, face_ref,
-    out_high_ref, out_low_ref, loc_high_ref, loc_low_ref, inv_high_ref, inv_low_ref,
-    base_ref, send0_ref, send1_ref, send2_ref, send3_ref, slot_ref,
-    center_ref, x_ref, y_ref, cell_ref, face_of_ref,
+    high_ref, low_ref, inv_high_ref, inv_low_ref, base_ref, local_ref, outward_ref,
+    blk_prev_ref, blk_next_ref, dom_prev_ref, dom_next_ref, slot_ref,
+    center_ref, x_ref, y_ref, product_ref, cell_ref, face_of_ref,
     *, dom_count, blk_count,
 ):
-    width = diag_ref.shape[-1]
+    width = diag_ref.shape[0]
     dom_here = lax.axis_index("dom")
     blk_here = lax.axis_index("blk")
     here = dom_here * blk_count + blk_here
@@ -289,76 +335,169 @@
 
             @pl.when(inside)
             def _():
-                face_of_ref[cell * 4 + way] = face
+                face_of_ref[slot * 4 + way] = face
 
     rows = lax.broadcasted_iota(jnp.int32, (width, width), 0)
     cols = lax.broadcasted_iota(jnp.int32, (width, width), 1)
     on_diag = rows == cols
-    for cell in range(CELLS):
-        slot = slot_ref[cell]
-        center = diag_ref[slot]
+    for slot in range(CELLS):
+        base_ref[cell_ref[slot]] = src_ref[:, slot, :]
+        center = diag_ref[:, slot, :]
         for face in range(6):
             wall = jnp.where(flag_ref[slot, face] == 1, 1.0, 0.0).astype(F32)
-            center = center + wall * face_ref[slot, face]
-        center_ref[cell] = center
+            center = center + wall * face_ref[face, :, slot, :]
+        center_ref[slot] = center
         marked = jnp.where(on_diag, center, 0.0)
         inv_row = 1.0 / jnp.sum(marked, axis=0, keepdims=True)
         inv_col = 1.0 / jnp.sum(marked, axis=1, keepdims=True)
         first = jnp.where(on_diag, inv_col, 0.0)
-        x_ref[cell] = 2.0 * first - inv_col * (center * inv_row)
+        x_ref[slot] = 2.0 * first - inv_col * (center * inv_row)
     for sweep in range(SWEEPS - 1):
+        for slot in range(CELLS):
+            y_ref[slot] = dot_full(center_ref[slot], x_ref[slot])
+        for slot in range(CELLS):
+            x_ref[slot] = 2.0 * x_ref[slot] - dot_full(x_ref[slot], y_ref[slot])
+    for slot in range(CELLS):
+        cell = cell_ref[slot]
+        x_high, x_low = split_halves(x_ref[slot])
+        inv_high_ref[cell] = x_high
+        inv_low_ref[cell] = x_low
+        own = dot_full(x_ref[slot], center_ref[slot]) - jnp.where(on_diag, 1.0, 0.0)
+        high_ref[cell], low_ref[cell] = split_halves(own)
+        for way in range(4):
+            face = face_of_ref[slot * 4 + way]
+            keep = jnp.where(face >= 0, 1.0, 0.0).astype(F32)
+            block = face_ref[jnp.maximum(face, 0), :, slot, :] * keep
+            f_high, f_low = split_halves(block)
+            product = dot32(x_high, f_high) + dot32(x_low, f_high) + dot32(x_high, f_low)
+            if way < 2:
+                leaves = cell // 2 == way
+                inner = FROM_X + cell
+                place = cell % 2
+            else:
+                leaves = cell % 2 == way - 2
+                inner = FROM_Y + cell
+                place = cell // 2
+            entry = jnp.where(leaves, OUTWARD + 2 * way + place, inner)
+            high_ref[entry], low_ref[entry] = split_halves(product)
+            product_ref[entry] = product
+    tall = padded(width)
+    for way, ref in enumerate((dom_prev_ref, dom_next_ref, blk_prev_ref, blk_next_ref)):
+        for place in range(2):
+            ref[tall * place : tall * place + width, :] = product_ref[OUTWARD + 2 * way + place]
+    halves = [stack_halves(base_ref[cell]) for cell in range(CELLS)]
+    local = local_products(halves, high_ref, low_ref)
+    outward = outward_products(halves, high_ref, low_ref)
+    for cell in range(CELLS):
+        local_ref[cell] = local[cell]
+    for entry in range(8):
+        outward_ref[entry] = outward[entry]
+    send_along_blk(local, outward, blk_prev_ref, blk_next_ref, 2 * tall)
+
+
+def middle_kernel(first_pair, *refs):
+    local_ref, outward_ref, from_prev_ref, from_next_ref = refs[:4]
+    sum_ref, dom_prev_ref, dom_next_ref = refs[-3:]
+    rows = local_ref.shape[1]
+    first = 0
+    if first_pair:
+        blocks_prev_ref, blocks_next_ref = refs[4:6]
+        first = blocks_prev_ref.shape[0]
+        dom_prev_ref[:first, :] = blocks_prev_ref[...]
+        dom_next_ref[:first, :] = blocks_next_ref[...]
+    sums = []
+    for cell in range(CELLS):
+        given = from_prev_ref if cell % 2 == 0 else from_next_ref
+        sums.append(local_ref[cell] + get_rows(given, first, rows, cell // 2))
+        sum_ref[cell] = sums[cell]
+    for ref, way in ((dom_prev_ref, 0), (dom_next_ref, 1)):
+        put_rows(
+            ref, first,
+            [
+                outward_ref[2 * way], outward_ref[2 * way + 1],
+                sums[2 * way], sums[2 * way + 1],
+                get_rows(from_prev_ref, first, rows, 4 + way),
+                get_rows(from_next_ref, first, rows, 4 + way),
+            ],
+        )
+
+
+def pair_kernel(first_pair, last_pair, older_count, *refs):
+    sum_ref, outward_ref, blk_prev_ref, blk_next_ref, dom_prev_ref, dom_next_ref = refs[:6]
+    high_ref, low_ref = refs[6:8]
+    refs = refs[8:]
+    rows = sum_ref.shape[1]
+    width = sum_ref.shape[2]
+    first = 0
+    if first_pair:
+        tall = padded(width)
+        first = 2 * tall
+    else:
+        in_high_ref, in_low_ref = refs[:2]
+        refs = refs[2:]
+    older = refs[:older_count]
+    refs = refs[older_count:]
+    if last_pair:
+        gram_in_ref, gram_ref, odd_ref, even_ref = refs
+    else:
+        odd_ref, even_ref, local_out_ref, outward_out_ref, prev_ref, next_ref = refs[:6]
+    if first_pair:
+        in_high_ref, in_low_ref = refs[6:]
+        for way, ref in enumerate((dom_prev_ref, dom_next_ref, blk_prev_ref, blk_next_ref)):
+            for place in range(2):
+                high, low = split_halves(ref[tall * place : tall * place + width, :])
+                in_high_ref[2 * way + place] = high
+                in_low_ref[2 * way + place] = low
+
+    def got(ref, place):
+        return get_rows(ref, first, rows, place)
+
+    odd = [
+        sum_ref[cell] + got(dom_prev_ref if cell < 2 else dom_next_ref, cell % 2)
+        for cell in range(CELLS)
+    ]
+    ring = []
+    for way, ref in enumerate((dom_prev_ref, dom_next_ref)):
+        for place in range(2):
+            ring.append(got(ref, 2 + place) + outward_ref[2 * way + place])
+    for way, ref in enumerate((blk_prev_ref, blk_next_ref)):
+        for place, corner_ref in enumerate((dom_prev_ref, dom_next_ref)):
+            ring.append(
+                got(ref, 2 + place) + outward_ref[4 + 2 * way + place] + got(corner_ref, 4 + way)
+            )
+    for cell in range(CELLS):
+        odd_ref[cell] = odd[cell]
+    even = local_products([stack_halves(value) for value in odd], high_ref, low_ref)
+    for place, value in enumerate(ring):
+        cell = RING_TARGETS[place]
+        even[cell] = even[cell] + row_times(
+            *stack_halves(value), in_high_ref[place], in_low_ref[place]
+        )
+    for cell in range(CELLS):
+        even_ref[cell] = even[cell]
+    if last_pair:
+        bases = list(older) + [odd_ref, even_ref]
+        gram = gram_rows(ITERS - 1, bases, gram_in_ref[...])
+        gram = gram_rows(ITERS, bases, gram)
+        half = gram.shape[0] // 2
+        gram_ref[...] = gram[:half] + pltpu.roll(gram[half:], 64, 1)
+    else:
+        halves = [stack_halves(value) for value in even]
+        local = local_products(halves, high_ref, low_ref)
+        outward = outward_products(halves, high_ref, low_ref)
         for cell in range(CELLS):
-            y_ref[cell] = dot_full(center_ref[cell], x_ref[cell])
-        for cell in range(CELLS):
-            x_ref[cell] = 2.0 * x_ref[cell] - dot_full(x_ref[cell], y_ref[cell])
-    halves = []
-    for cell in range(CELLS):
-        base = jnp.zeros(base_ref.shape[1:], F32)
-        for slot in range(CELLS):
-            base = jnp.where(slot_ref[cell] == slot, src_ref[:, slot, :], base)
-        base_ref[cell] = base
-        halves.append(stack_halves(base))
-        high, low = split_halves(x_ref[cell])
-        inv_high_ref[cell] = high
-        inv_low_ref[cell] = low
-        own = dot_full(x_ref[cell], center_ref[cell]) - jnp.where(on_diag, 1.0, 0.0)
-        high, low = split_halves(own)
-        loc_high_ref[cell] = high
-        loc_low_ref[cell] = low
-        slot = slot_ref[cell]
-        for way in range(4):
-            face = face_of_ref[cell * 4 + way]
-            keep = jnp.where(face >= 0, 1.0, 0.0).astype(F32)
-            block = face_ref[slot, jnp.maximum(face, 0)] * keep
-            f_high, f_low = split_halves(block)
-            product = (
-                dot32(inv_high_ref[cell], f_high)
-                + dot32(inv_low_ref[cell], f_high)
-                + dot32(inv_high_ref[cell], f_low)
-            )
-            high, low = split_halves(product)
-            if cell in OUT_CELLS[way]:
-                entry = 2 * way + OUT_CELLS[way].index(cell)
-                out_high_ref[entry] = high
-                out_low_ref[entry] = low
-            else:
-                entry = (4 if way < 2 else 8) + cell
-                loc_high_ref[entry] = high
-                loc_low_ref[entry] = low
-    write_sends(halves, out_high_ref, out_low_ref, (send0_ref, send1_ref, send2_ref, send3_ref))
-
-
-def local_kernel(step, base_refs, loc_high_ref, loc_low_ref, gram_in_ref, acc_ref, gram_ref):
-    newest = base_refs[step]
-    halves = [stack_halves(newest[cell]) for cell in range(CELLS)]
-    for cell in range(CELLS):
-        total = None
-        for source, entry in ((cell, cell), (cell ^ 2, 4 + (cell ^ 2)), (cell ^ 1, 8 + (cell ^ 1))):
-            stacked, high = halves[source]
-            part = row_times(stacked, high, loc_high_ref[entry], loc_low_ref[entry])
-            total = part if total is None else total + part
-        acc_ref[cell] = total
-    gram_ref[...] = gram_rows(step, base_refs, None if gram_in_ref is None else gram_in_ref[...])
+            local_out_ref[cell] = local[cell]
+        for entry in range(8):
+            outward_out_ref[entry] = outward[entry]
+        send_along_blk(local, outward, prev_ref, next_ref, 0)
+
+
+def gram_kernel(newest, *refs):
+    base_refs = refs[: newest + 1]
+    gram = None
+    if newest > 0:
+        gram = gram_rows(newest - 1, base_refs, refs[newest + 1][...])
+    refs[-1][...] = gram_rows(newest, base_refs, gram)
 
 
 def gram_rows(step, base_refs, gram):
@@ -374,34 +513,6 @@
         value = jnp.sum(total, axis=1, keepdims=True)
         gram = jnp.where(lanes == pair_lane(step, col), value, gram)
     return gram
-
-
-def add_received(acc_ref, recv_refs, base_ref):
-    from_dom_prev, from_dom_next, from_blk_prev, from_blk_next = recv_refs
-    for cell in range(CELLS):
-        dom_part = from_dom_prev[cell % 2] if cell < 2 else from_dom_next[cell % 2]
-        blk_part = from_blk_prev[cell // 2] if cell % 2 == 0 else from_blk_next[cell // 2]
-        base_ref[cell] = acc_ref[cell] + dom_part + blk_part
-
-
-def border_kernel(
-    acc_ref, recv0_ref, recv1_ref, recv2_ref, recv3_ref, out_high_ref, out_low_ref,
-    base_ref, send0_ref, send1_ref, send2_ref, send3_ref,
-):
-    add_received(acc_ref, (recv0_ref, recv1_ref, recv2_ref, recv3_ref), base_ref)
-    halves = [stack_halves(base_ref[cell]) for cell in range(CELLS)]
-    write_sends(halves, out_high_ref, out_low_ref, (send0_ref, send1_ref, send2_ref, send3_ref))
-
-
-def last_kernel(*refs):
-    acc_ref, recv0_ref, recv1_ref, recv2_ref, recv3_ref = refs[:5]
-    gram_in_ref = refs[5]
-    older = refs[6 : 6 + ITERS]
-    gram_ref, base_ref = refs[6 + ITERS :]
-    add_received(acc_ref, (recv0_ref, recv1_ref, recv2_ref, recv3_ref), base_ref)
-    gram = gram_rows(ITERS, list(older) + [base_ref], gram_in_ref[...])
-    half = gram.shape[0] // 2
-    gram_ref[...] = gram[:half] + pltpu.roll(gram[half:], 64, 1)
 
 
 def finish_kernel(*refs):
@@ -526,34 +637,32 @@
     )
 
 
-def exchange(sends):
-    to_dom_prev, to_dom_next, to_blk_prev, to_blk_next = sends
-    return (
-        rotated(to_dom_next, "dom", 1),
-        rotated(to_dom_prev, "dom", -1),
-        rotated(to_blk_next, "blk", 1),
-        rotated(to_blk_prev, "blk", -1),
-    )
+def both_ways(to_prev, to_next, axis):
+    return rotated(to_next, axis, 1), rotated(to_prev, axis, -1)
 
 
 def shards(adjoint_source, diag_blocks, face_blocks, neighbors, partner, flags):
     nrhs, elements, width = adjoint_source.shape
     block = (width, width)
+    tall = padded(width)
     field = struct(CELLS, nrhs, width)
-    edge = struct(2, nrhs, width)
+    ring = struct(8, nrhs, width)
+    edge = struct(6 * nrhs, width)
+    edge_blocks = struct(2 * tall + 6 * nrhs, width)
     cost = lambda flops, data: pl.CostEstimate(
         flops=flops, bytes_accessed=data, transcendentals=0
     )
     products = 2 * nrhs * width * width * 3
-    setup = pl.pallas_call(
+    outs = pl.pallas_call(
         functools.partial(
             setup_kernel, dom_count=lax.axis_size("dom"), blk_count=lax.axis_size("blk")
         ),
         out_shape=(
-            struct(8, *block, kind=BF16), struct(8, *block, kind=BF16),
-            struct(12, *block, kind=BF16), struct(12, *block, kind=BF16),
+            struct(BLOCKS, *block, kind=BF16), struct(BLOCKS, *block, kind=BF16),
             struct(CELLS, *block, kind=BF16), struct(CELLS, *block, kind=BF16),
-            field, edge, edge, edge, edge, struct(CELLS, kind=jnp.int32),
+            field, field, ring, edge_blocks, edge_blocks,
+            struct(2 * tall, width), struct(2 * tall, width),
+            struct(CELLS, kind=jnp.int32),
         ),
         in_specs=smem(2) + vmem(3),
         out_specs=tuple(vmem(11) + smem(1)),
@@ -561,60 +670,76 @@
             pltpu.VMEM((CELLS,) + block, F32),
             pltpu.VMEM((CELLS,) + block, F32),
             pltpu.VMEM((CELLS,) + block, F32),
+            pltpu.VMEM((BLOCKS,) + block, F32),
             pltpu.SMEM((CELLS,), jnp.int32),
             pltpu.SMEM((CELLS * 4,), jnp.int32),
         ],
         compiler_params=PARAMS,
         name="setup_blocks",
-    )
-    outs = setup(neighbors, flags, adjoint_source, diag_blocks, face_blocks)
-    out_high, out_low, loc_high, loc_low, inv_high, inv_low = outs[:6]
-    bases = [outs[6]]
-    sends = outs[7:11]
+    )(
+        neighbors, flags, adjoint_source,
+        jnp.transpose(diag_blocks, (1, 0, 2)), jnp.transpose(face_blocks, (1, 2, 0, 3)),
+    )
+    high, low, inv_high, inv_low, base, local, outward = outs[:7]
+    blk_sends = outs[7:9]
+    dom_blocks = outs[9:11]
     slots = outs[11]
+    bases = [base]
     gram = None
-    for step in range(ITERS):
-        received = exchange(sends)
-
-        def local_body(*refs, step=step):
-            has_gram = step > 0
-            base_refs = refs[: step + 1]
-            loc_refs = refs[step + 1 : step + 3]
-            gram_in = refs[step + 3] if has_gram else None
-            local_kernel(step, base_refs, *loc_refs, gram_in, *refs[-2:])
-
-        given = bases + [loc_high, loc_low] + ([gram] if step > 0 else [])
-        acc, gram = pl.pallas_call(
-            local_body,
-            out_shape=(field, struct(nrhs, 128)),
+    inward = ()
+    for pair in range(ITERS // 2):
+        first_pair = pair == 0
+        last_pair = pair == ITERS // 2 - 1
+        from_blk = both_ways(*blk_sends, "blk")
+        given = [local, outward, *from_blk] + (list(dom_blocks) if first_pair else [])
+        kind = edge_blocks if first_pair else edge
+        sums, *dom_sends = pl.pallas_call(
+            functools.partial(middle_kernel, first_pair),
+            out_shape=(field, kind, kind),
             in_specs=vmem(len(given)),
-            out_specs=tuple(vmem(2)),
+            out_specs=tuple(vmem(3)),
             compiler_params=PARAMS,
-            cost_estimate=cost(12 * products, 3000000),
-            name=f"local_part_{step}",
+            name=f"middle_part_{pair}",
         )(*given)
-        if step < ITERS - 1:
-            outs = pl.pallas_call(
-                border_kernel,
-                out_shape=(field, edge, edge, edge, edge),
-                in_specs=vmem(7),
-                out_specs=tuple(vmem(5)),
-                compiler_params=PARAMS,
-                cost_estimate=cost(8 * products, 2000000),
-                name=f"border_part_{step}",
-            )(acc, *received, out_high, out_low)
-            bases.append(outs[0])
-            sends = outs[1:]
+        from_dom = both_ways(*dom_sends, "dom")
+        newest = len(bases) - 1
+        given = bases + ([gram] if newest > 0 else [])
+        gram = pl.pallas_call(
+            functools.partial(gram_kernel, newest),
+            out_shape=struct(nrhs, 128),
+            in_specs=vmem(len(given)),
+            out_specs=vmem(1)[0],
+            compiler_params=PARAMS,
+            cost_estimate=cost(100000 * (newest + 1), 2000000),
+            name=f"gram_part_{pair}",
+        )(*given)
+        older = bases if last_pair else []
+        given = [sums, outward, *from_blk, *from_dom, high, low, *inward, *older]
+        if last_pair:
+            given.append(gram)
+            shapes = (struct(nrhs // 2, 128), field, field)
         else:
-            given = [acc, *received, gram] + bases
-            gram, _ = pl.pallas_call(
-                last_kernel,
-                out_shape=(struct(nrhs // 2, 128), field),
-                in_specs=vmem(len(given)),
-                out_specs=tuple(vmem(2)),
-                compiler_params=PARAMS,
-                name="last_part",
-            )(*given)
+            shapes = (field, field, field, ring, edge, edge)
+        if first_pair:
+            shapes += (struct(8, *block, kind=BF16), struct(8, *block, kind=BF16))
+        outs = pl.pallas_call(
+            functools.partial(pair_kernel, first_pair, last_pair, len(older)),
+            out_shape=shapes,
+            in_specs=vmem(len(given)),
+            out_specs=tuple(vmem(len(shapes))),
+            compiler_params=PARAMS,
+            cost_estimate=cost(40 * products, 6000000),
+            name=f"pair_part_{pair}",
+        )(*given)
+        if last_pair:
+            gram = outs[0]
+            bases.append(outs[1])
+        else:
+            bases += outs[:2]
+            local, outward = outs[2:4]
+            blk_sends = outs[4:6]
+        if first_pair:
+            inward = outs[6:]
     gram = sum_devices(gram)
     given = [gram] + bases + [inv_high, inv_low, slots]
     adjoint, rel, fine = pl.pallas_call(

time: 168 us -> 149 us (0.89)
  starting transfers between devices: 109 us -> 66.9 us
  waiting for transfers between devices: 21.4 us -> 37.7 us
  Pallas kernels: 14.4 us -> 25.8 us
  local copies, waits for them, and re-layouts: 4.83 us -> 0.68 us
    ppermute x32 -> x16, starting transfers between devices: 101 us -> 55.9 us  [rotated(): lax.ppermute(value, axis, [(source, (source + steps) % count) for source...]
    ppermute x32 -> x16, waiting for transfers between devices: 9.81 us -> 26.1 us  [rotated(): lax.ppermute(value, axis, [(source, (source + steps) % count) for source...]
    pallas_call x17 -> x13, Pallas kernels: 12.6 us -> 24 us  [the longest x1 18.4 us: shards(): pl.pallas_call(functools.partial(setup_kernel, dom_count=lax.axis_size('d...]
    unnamed x12 -> x10, local copies, waits for them, and re-layouts: 4.19 us -> 0.03 us
    all_to_all x1, starting transfers between devices: 8.53 us -> 11.1 us  [sum_groups(): lax.all_to_all(copies, axes, 0, 0, axis_index_groups=groups if len(groups...]
  transfers between devices with their start and end apart: 33 -> 17, of which waited for: 17 -> 16; matrix products, arithmetic and copies ran while one was open for 0% -> 0% of each run, Pallas kernels for 2% -> 0%
where the time goes in v3:
time: 149 us
  starting transfers between devices  66.9 us (45%)
  waiting for transfers between devices  37.7 us (25%)
  Pallas kernels  25.8 us (17%)
  blocking collectives  15.7 us (11%)
  between operations  1.71 us (1%)
    ppermute x16, starting transfers between devices, rotated(): lax.ppermute(value, axis, [(source, (source + steps) % count) for source...  55.9 us
    ppermute x16, waiting for transfers between devices, rotated(): lax.ppermute(value, axis, [(source, (source + steps) % count) for source...  26.1 us
    pallas_call x1, Pallas kernels, shards(): pl.pallas_call(functools.partial(setup_kernel, dom_count=lax.axis_size('d...  18.4 us
    all_to_all x1, blocking collectives, sum_groups(): lax.all_to_all(copies, axes, 0, 0, axis_index_groups=groups if len(groups...  15.7 us
    all_to_all x1, waiting for transfers between devices, sum_groups(): lax.all_to_all(copies, axes, 0, 0, axis_index_groups=groups if len(groups...  11.6 us
    all_to_all x1, starting transfers between devices, sum_groups(): lax.all_to_all(copies, axes, 0, 0, axis_index_groups=groups if len(groups...  11.1 us
    pallas_call x4, Pallas kernels, shards(): pl.pallas_call(functools.partial(pair_kernel, first_pair, last_pair, len(...  4.98 us
  transfers between devices with their start and end apart: 17, of which 16 were waited for; matrix products, arithmetic and copies ran while one was open for 0% of the time, Pallas kernels for 0%

profile of v3, /device:TPU:1, one launch (start us, length us, event | category | flops | bytes accessed | tf_op | source)
XLA Modules:
  0.0 148.8 jit_solution(5723364373265990022)
XLA Ops:
  0.6 18.4 %setup_blocks.1 = (bf16[20,162,162]{2,1,0:T(8,128)(2,1)S(1)}, bf16[20,162,162]{2,1,0:T(8,128)(2,1)S(1)}, bf16[4,162,162]{2,1,0:T(8,128)(2,1)S(1)}, bf16[4,162,16...) custom-call(s32[4,6]{1,0:T(4,128)} %nbr_ref.1, ...), custom_call_target="tpu_custom_call" | custom-call | tf_op jit(solution)/shard_map/setup_blocks/pallas_call | solution.py:656
  19.1 2.7 %collective-permute-start.36 = (f32[432,162]{1,0:T(8,128)S(1)}, f32[432,162]{1,0:T(8,128)S(1)}, u32[]{:S(2)}, u32[]{:S(2)}) collective-permute-start(f32[432,162]{1,0:T(8,128)S(1)} %get-tuple-element.82), channel_id=1, source_target_pairs={{0,1},{1,2},{2,3},{3,4},{4,5},{5,6},{6,7},{7,0},{8,9},{9,10},{10,1... | collective-permute-start | bytes 839816 | tf_op jit(solution)/shard_map/ppermute | solution.py:635
  21.8 4.2 %collective-permute-start.37 = (f32[432,162]{1,0:T(8,128)S(1)}, f32[432,162]{1,0:T(8,128)S(1)}, u32[]{:S(2)}, u32[]{:S(2)}) collective-permute-start(f32[432,162]{1,0:T(8,128)S(1)} %get-tuple-element.83), channel_id=1, source_target_pairs={{0,7},{1,0},{2,1},{3,2},{4,3},{5,4},{6,5},{7,6},{8,15},{9,8},{10,9... | collective-permute-start | bytes 839816 | tf_op jit(solution)/shard_map/ppermute | solution.py:635
  26.0 1.3 collective-permute-done.36.refs_2_
  27.3 2.5 %collective-permute-done.37.refs_3_ = f32[432,162]{1,0:T(8,128)S(1)} collective-permute-done((f32[432,162]{1,0:T(8,128)S(1)}, f32[432,162]{1,0:T(8,128)S(1)}, u32[]{:S(2)}, u32[]{:S(2)}) %collective-permute-start.37) | collective-permute-done | bytes 279968 | tf_op jit(solution)/shard_map/ppermute | solution.py:635
  29.8 0.1 middle_part_0.1
  29.9 2.8 %collective-permute-start.38 = (f32[432,162]{1,0:T(8,128)S(1)}, f32[432,162]{1,0:T(8,128)S(1)}, u32[]{:S(2)}, u32[]{:S(2)}) collective-permute-start(f32[432,162]{1,0:T(8,128)S(1)} %get-tuple-element.87), channel_id=1, source_target_pairs={{0,8},{8,16},{16,24},{24,32},{32,40},{40,48},{48,56},{56,64},{64,7... | collective-permute-start | bytes 839816 | tf_op jit(solution)/shard_map/ppermute | solution.py:635
  32.7 12.1 %collective-permute-start.39 = (f32[432,162]{1,0:T(8,128)S(1)}, f32[432,162]{1,0:T(8,128)S(1)}, u32[]{:S(2)}, u32[]{:S(2)}) collective-permute-start(f32[432,162]{1,0:T(8,128)S(1)} %get-tuple-element.88), channel_id=1, source_target_pairs={{0,504},{8,0},{16,8},{24,16},{32,24},{40,32},{48,40},{56,48},{64,5... | collective-permute-start | bytes 839816 | tf_op jit(solution)/shard_map/ppermute | solution.py:635
  44.8 8.6 %collective-permute-done.38.refs_4_ = f32[432,162]{1,0:T(8,128)S(1)} collective-permute-done((f32[432,162]{1,0:T(8,128)S(1)}, f32[432,162]{1,0:T(8,128)S(1)}, u32[]{:S(2)}, u32[]{:S(2)}) %collective-permute-start.38) | collective-permute-done | bytes 279968 | tf_op jit(solution)/shard_map/ppermute | solution.py:635
  53.4 1.0 collective-permute-done.39.refs_5_
  54.4 1.3 pair_part_0.1
  55.7 0.6 collective-permute-start.40
  56.3 0.2 collective-permute-start.41
  56.5 1.4 collective-permute-done.40.refs_2_
  58.0 2.7 %collective-permute-done.41.refs_3_ = f32[96,162]{1,0:T(8,128)S(1)} collective-permute-done((f32[96,162]{1,0:T(8,128)S(1)}, f32[96,162]{1,0:T(8,128)S(1)}, u32[]{:S(2)}, u32[]{:S(2)}) %collective-permute-start.41) | collective-permute-done | bytes 62240 | tf_op jit(solution)/shard_map/ppermute | solution.py:635
  60.7 1.9 %collective-permute-start.42 = (f32[96,162]{1,0:T(8,128)S(1)}, f32[96,162]{1,0:T(8,128)S(1)}, u32[]{:S(2)}, u32[]{:S(2)}) collective-permute-start(f32[96,162]{1,0:T(8,128)S(1)} %get-tuple-element.96), channel_id=1, source_target_pairs={{0,8},{8,16},{16,24},{24,32},{32,40},{40,48},{48,56},{56,64},{64,7... | collective-permute-start | bytes 186632 | tf_op jit(solution)/shard_map/ppermute | solution.py:635
  62.6 7.4 %collective-permute-start.43 = (f32[96,162]{1,0:T(8,128)S(1)}, f32[96,162]{1,0:T(8,128)S(1)}, u32[]{:S(2)}, u32[]{:S(2)}) collective-permute-start(f32[96,162]{1,0:T(8,128)S(1)} %get-tuple-element.97), channel_id=1, source_target_pairs={{0,504},{8,0},{16,8},{24,16},{32,24},{40,32},{48,40},{56,48},{64,5... | collective-permute-start | bytes 186632 | tf_op jit(solution)/shard_map/ppermute | solution.py:635
  70.0 0.1 collective-permute-done.42.refs_4_
  70.1 1.6 %collective-permute-done.43.refs_5_ = f32[96,162]{1,0:T(8,128)S(1)} collective-permute-done((f32[96,162]{1,0:T(8,128)S(1)}, f32[96,162]{1,0:T(8,128)S(1)}, u32[]{:S(2)}, u32[]{:S(2)}) %collective-permute-start.43) | collective-permute-done | bytes 62240 | tf_op jit(solution)/shard_map/ppermute | solution.py:635
  71.7 1.2 pair_part_1.1
  72.9 0.6 collective-permute-start.44
  73.4 1.4 collective-permute-start.45
  74.9 0.8 collective-permute-done.44.refs_2_
  75.6 1.8 %collective-permute-done.45.refs_3_ = f32[96,162]{1,0:T(8,128)S(1)} collective-permute-done((f32[96,162]{1,0:T(8,128)S(1)}, f32[96,162]{1,0:T(8,128)S(1)}, u32[]{:S(2)}, u32[]{:S(2)}) %collective-permute-start.45) | collective-permute-done | bytes 62240 | tf_op jit(solution)/shard_map/ppermute | solution.py:635
  77.5 1.9 %collective-permute-start.46 = (f32[96,162]{1,0:T(8,128)S(1)}, f32[96,162]{1,0:T(8,128)S(1)}, u32[]{:S(2)}, u32[]{:S(2)}) collective-permute-start(f32[96,162]{1,0:T(8,128)S(1)} %get-tuple-element.105), channel_id=1, source_target_pairs={{0,8},{8,16},{16,24},{24,32},{32,40},{40,48},{48,56},{56,64},{64,7... | collective-permute-start | bytes 186632 | tf_op jit(solution)/shard_map/ppermute | solution.py:635
  79.4 7.4 %collective-permute-start.47 = (f32[96,162]{1,0:T(8,128)S(1)}, f32[96,162]{1,0:T(8,128)S(1)}, u32[]{:S(2)}, u32[]{:S(2)}) collective-permute-start(f32[96,162]{1,0:T(8,128)S(1)} %get-tuple-element.106), channel_id=1, source_target_pairs={{0,504},{8,0},{16,8},{24,16},{32,24},{40,32},{48,40},{56,48},{64,5... | collective-permute-start | bytes 186632 | tf_op jit(solution)/shard_map/ppermute | solution.py:635
  86.8 0.1 collective-permute-done.46.refs_4_
  86.8 1.6 %collective-permute-done.47.refs_5_ = f32[96,162]{1,0:T(8,128)S(1)} collective-permute-done((f32[96,162]{1,0:T(8,128)S(1)}, f32[96,162]{1,0:T(8,128)S(1)}, u32[]{:S(2)}, u32[]{:S(2)}) %collective-permute-start.47) | collective-permute-done | bytes 62240 | tf_op jit(solution)/shard_map/ppermute | solution.py:635
  88.4 1.2 pair_part_2.1
  89.6 0.9 collective-permute-start.48
  90.5 2.6 %collective-permute-start.49 = (f32[96,162]{1,0:T(8,128)S(1)}, f32[96,162]{1,0:T(8,128)S(1)}, u32[]{:S(2)}, u32[]{:S(2)}) collective-permute-start(f32[96,162]{1,0:T(8,128)S(1)} %get-tuple-element.110), channel_id=1, source_target_pairs={{0,7},{1,0},{2,1},{3,2},{4,3},{5,4},{6,5},{7,6},{8,15},{9,8},{10,9... | collective-permute-start | bytes 186632 | tf_op jit(solution)/shard_map/ppermute | solution.py:635
  93.1 0.8 collective-permute-done.48.refs_2_
  93.9 0.9 collective-permute-done.49.refs_3_
  94.8 1.9 %collective-permute-start.50 = (f32[96,162]{1,0:T(8,128)S(1)}, f32[96,162]{1,0:T(8,128)S(1)}, u32[]{:S(2)}, u32[]{:S(2)}) collective-permute-start(f32[96,162]{1,0:T(8,128)S(1)} %get-tuple-element.112), channel_id=1, source_target_pairs={{0,8},{8,16},{16,24},{24,32},{32,40},{40,48},{48,56},{56,64},{64,7... | collective-permute-start | bytes 186632 | tf_op jit(solution)/shard_map/ppermute | solution.py:635
  96.7 7.1 %collective-permute-start.51 = (f32[96,162]{1,0:T(8,128)S(1)}, f32[96,162]{1,0:T(8,128)S(1)}, u32[]{:S(2)}, u32[]{:S(2)}) collective-permute-start(f32[96,162]{1,0:T(8,128)S(1)} %get-tuple-element.113), channel_id=1, source_target_pairs={{0,504},{8,0},{16,8},{24,16},{32,24},{40,32},{48,40},{56,48},{64,5... | collective-permute-start | bytes 186632 | tf_op jit(solution)/shard_map/ppermute | solution.py:635
  103.8 0.1 gram_part_0.1.refs_3_
  103.9 0.1 gram_part_1.1.refs_5_
  104.0 0.1 gram_part_2.1.refs_7_
  104.1 0.0 copy-start.1
  104.1 0.0 copy-start.2
  104.2 0.0 copy-start.4
  104.2 0.0 copy-start.5
  104.2 0.0 copy-start.6
  104.2 0.1 gram_part_3.1.refs_17_
  104.3 0.0 collective-permute-done.50.refs_4_
  104.3 1.1 collective-permute-done.51.refs_5_
  105.4 1.3 pair_part_3.1
  106.8 15.7 %all_to_all.10 = f32[32,8,128]{2,1,0:T(8,128)S(1)} all-to-all(f32[32,8,128]{2,1,0:T(8,128)S(1)} %broadcast_in_dim.79), channel_id=1, replica_groups={{0,1,2,3,4,5,6,7,8,9,10,11,12,13,14,15,16,17,18,19,20,21,22,23,24,25,26..., dimensions={0} | all-to-all | bytes 262144 | tf_op jit(solution)/shard_map/all_to_all | solution.py:613
  122.5 0.6 broadcast_in_dim.80
  123.2 11.1 %all-to-all-start.1 = ((f32[16,8,128]{2,1,0:T(8,128)}), f32[16,8,128]{2,1,0:T(8,128)S(1)}, u32[]{:S(2)}, u32[]{:S(2)}) async-start(f32[16,8,128]{2,1,0:T(8,128)} %broadcast_in_dim.80), calls=%async_computation.1 | async-start | bytes 131072 | tf_op jit(solution)/shard_map/all_to_all | solution.py:613
  134.3 11.6 %all-to-all-done.1 = f32[16,8,128]{2,1,0:T(8,128)S(1)} async-done(((f32[16,8,128]{2,1,0:T(8,128)}), f32[16,8,128]{2,1,0:T(8,128)S(1)}, u32[]{:S(2)}, u32[]{:S(2)}) %all-to-all-start.1) | async-done | bytes 65568 | tf_op jit(solution)/shard_map/all_to_all | solution.py:613
  145.9 1.8 %finish_part.1 = (f32[16,4,162]{2,1,0:T(4,128)}, f32[1,16]{1,0:T(1,128)}, s32[1]{0:T(128)}) custom-call(f32[8,128]{1,0:T(8,128)S(1)} %reduce_sum.469.refs_0_, f32[4,16,162]{2,1,0:T(8,128)S(1)} %get-tuple-element.114.refs_0_.refs_10_.refs_1_, f32[4,16,162]{2,1,0:T(8,128)S(1)} %get-tuple-element.115.refs_1_.refs_11_.refs_2_, ...), custom_call_target="tpu_custom_call" | custom-call | tf_op jit(solution)/shard_map/finish_part/pallas_call | solution.py:745
  148.4 0.0 copy-done.1
  148.4 0.0 copy-done.2
  148.4 0.0 copy-done.4
  148.4 0.0 copy-done.5
  148.4 0.0 copy-done.6
  148.4 0.2 conditional.1
  (6 shorter events, 0.1 us)
Async XLA Ops:
  19.1 8.2 %collective-permute-start.36 = (f32[432,162]{1,0:T(8,128)S(1)}, f32[432,162]{1,0:T(8,128)S(1)}, u32[]{:S(2)}, u32[]{:S(2)}) collective-permute-start(f32[432,162]{1,0:T(8,128)S(1)} %get-tuple-element.82), channel_id=1, source_target_pairs={{0,1},{1,2},{2,3},{3,4},{4,5},{5,6},{6,7},{7,0},{8,9},{9,10},{10,1... | collective-permute-start | bytes 839816 | tf_op jit(solution)/shard_map/ppermute | solution.py:635
  21.8 8.0 %collective-permute-start.37 = (f32[432,162]{1,0:T(8,128)S(1)}, f32[432,162]{1,0:T(8,128)S(1)}, u32[]{:S(2)}, u32[]{:S(2)}) collective-permute-start(f32[432,162]{1,0:T(8,128)S(1)} %get-tuple-element.83), channel_id=1, source_target_pairs={{0,7},{1,0},{2,1},{3,2},{4,3},{5,4},{6,5},{7,6},{8,15},{9,8},{10,9... | collective-permute-start | bytes 839816 | tf_op jit(solution)/shard_map/ppermute | solution.py:635
  29.9 23.5 %collective-permute-start.38 = (f32[432,162]{1,0:T(8,128)S(1)}, f32[432,162]{1,0:T(8,128)S(1)}, u32[]{:S(2)}, u32[]{:S(2)}) collective-permute-start(f32[432,162]{1,0:T(8,128)S(1)} %get-tuple-element.87), channel_id=1, source_target_pairs={{0,8},{8,16},{16,24},{24,32},{32,40},{40,48},{48,56},{56,64},{64,7... | collective-permute-start | bytes 839816 | tf_op jit(solution)/shard_map/ppermute | solution.py:635
  32.7 21.7 %collective-permute-start.39 = (f32[432,162]{1,0:T(8,128)S(1)}, f32[432,162]{1,0:T(8,128)S(1)}, u32[]{:S(2)}, u32[]{:S(2)}) collective-permute-start(f32[432,162]{1,0:T(8,128)S(1)} %get-tuple-element.88), channel_id=1, source_target_pairs={{0,504},{8,0},{16,8},{24,16},{32,24},{40,32},{48,40},{56,48},{64,5... | collective-permute-start | bytes 839816 | tf_op jit(solution)/shard_map/ppermute | solution.py:635
  55.7 2.3 %collective-permute-start.40 = (f32[96,162]{1,0:T(8,128)S(1)}, f32[96,162]{1,0:T(8,128)S(1)}, u32[]{:S(2)}, u32[]{:S(2)}) collective-permute-start(f32[96,162]{1,0:T(8,128)S(1)} %get-tuple-element.93), channel_id=1, source_target_pairs={{0,1},{1,2},{2,3},{3,4},{4,5},{5,6},{6,7},{7,0},{8,9},{9,10},{10,1... | collective-permute-start | bytes 186632 | tf_op jit(solution)/shard_map/ppermute | solution.py:635
  56.3 4.3 %collective-permute-start.41 = (f32[96,162]{1,0:T(8,128)S(1)}, f32[96,162]{1,0:T(8,128)S(1)}, u32[]{:S(2)}, u32[]{:S(2)}) collective-permute-start(f32[96,162]{1,0:T(8,128)S(1)} %get-tuple-element.94), channel_id=1, source_target_pairs={{0,7},{1,0},{2,1},{3,2},{4,3},{5,4},{6,5},{7,6},{8,15},{9,8},{10,9... | collective-permute-start | bytes 186632 | tf_op jit(solution)/shard_map/ppermute | solution.py:635
  60.7 9.4 %collective-permute-start.42 = (f32[96,162]{1,0:T(8,128)S(1)}, f32[96,162]{1,0:T(8,128)S(1)}, u32[]{:S(2)}, u32[]{:S(2)}) collective-permute-start(f32[96,162]{1,0:T(8,128)S(1)} %get-tuple-element.96), channel_id=1, source_target_pairs={{0,8},{8,16},{16,24},{24,32},{32,40},{40,48},{48,56},{56,64},{64,7... | collective-permute-start | bytes 186632 | tf_op jit(solution)/shard_map/ppermute | solution.py:635
  62.6 9.1 %collective-permute-start.43 = (f32[96,162]{1,0:T(8,128)S(1)}, f32[96,162]{1,0:T(8,128)S(1)}, u32[]{:S(2)}, u32[]{:S(2)}) collective-permute-start(f32[96,162]{1,0:T(8,128)S(1)} %get-tuple-element.97), channel_id=1, source_target_pairs={{0,504},{8,0},{16,8},{24,16},{32,24},{40,32},{48,40},{56,48},{64,5... | collective-permute-start | bytes 186632 | tf_op jit(solution)/shard_map/ppermute | solution.py:635
  72.9 2.8 %collective-permute-start.44 = (f32[96,162]{1,0:T(8,128)S(1)}, f32[96,162]{1,0:T(8,128)S(1)}, u32[]{:S(2)}, u32[]{:S(2)}) collective-permute-start(f32[96,162]{1,0:T(8,128)S(1)} %get-tuple-element.102), channel_id=1, source_target_pairs={{0,1},{1,2},{2,3},{3,4},{4,5},{5,6},{6,7},{7,0},{8,9},{9,10},{10,1... | collective-permute-start | bytes 186632 | tf_op jit(solution)/shard_map/ppermute | solution.py:635
  73.4 4.0 %collective-permute-start.45 = (f32[96,162]{1,0:T(8,128)S(1)}, f32[96,162]{1,0:T(8,128)S(1)}, u32[]{:S(2)}, u32[]{:S(2)}) collective-permute-start(f32[96,162]{1,0:T(8,128)S(1)} %get-tuple-element.103), channel_id=1, source_target_pairs={{0,7},{1,0},{2,1},{3,2},{4,3},{5,4},{6,5},{7,6},{8,15},{9,8},{10,9... | collective-permute-start | bytes 186632 | tf_op jit(solution)/shard_map/ppermute | solution.py:635
  77.5 9.4 %collective-permute-start.46 = (f32[96,162]{1,0:T(8,128)S(1)}, f32[96,162]{1,0:T(8,128)S(1)}, u32[]{:S(2)}, u32[]{:S(2)}) collective-permute-start(f32[96,162]{1,0:T(8,128)S(1)} %get-tuple-element.105), channel_id=1, source_target_pairs={{0,8},{8,16},{16,24},{24,32},{32,40},{40,48},{48,56},{56,64},{64,7... | collective-permute-start | bytes 186632 | tf_op jit(solution)/shard_map/ppermute | solution.py:635
  79.4 9.0 %collective-permute-start.47 = (f32[96,162]{1,0:T(8,128)S(1)}, f32[96,162]{1,0:T(8,128)S(1)}, u32[]{:S(2)}, u32[]{:S(2)}) collective-permute-start(f32[96,162]{1,0:T(8,128)S(1)} %get-tuple-element.106), channel_id=1, source_target_pairs={{0,504},{8,0},{16,8},{24,16},{32,24},{40,32},{48,40},{56,48},{64,5... | collective-permute-start | bytes 186632 | tf_op jit(solution)/shard_map/ppermute | solution.py:635
  89.6 4.3 %collective-permute-start.48 = (f32[96,162]{1,0:T(8,128)S(1)}, f32[96,162]{1,0:T(8,128)S(1)}, u32[]{:S(2)}, u32[]{:S(2)}) collective-permute-start(f32[96,162]{1,0:T(8,128)S(1)} %get-tuple-element.109), channel_id=1, source_target_pairs={{0,1},{1,2},{2,3},{3,4},{4,5},{5,6},{6,7},{7,0},{8,9},{9,10},{10,1... | collective-permute-start | bytes 186632 | tf_op jit(solution)/shard_map/ppermute | solution.py:635
  90.5 4.3 %collective-permute-start.49 = (f32[96,162]{1,0:T(8,128)S(1)}, f32[96,162]{1,0:T(8,128)S(1)}, u32[]{:S(2)}, u32[]{:S(2)}) collective-permute-start(f32[96,162]{1,0:T(8,128)S(1)} %get-tuple-element.110), channel_id=1, source_target_pairs={{0,7},{1,0},{2,1},{3,2},{4,3},{5,4},{6,5},{7,6},{8,15},{9,8},{10,9... | collective-permute-start | bytes 186632 | tf_op jit(solution)/shard_map/ppermute | solution.py:635
  94.8 9.6 %collective-permute-start.50 = (f32[96,162]{1,0:T(8,128)S(1)}, f32[96,162]{1,0:T(8,128)S(1)}, u32[]{:S(2)}, u32[]{:S(2)}) collective-permute-start(f32[96,162]{1,0:T(8,128)S(1)} %get-tuple-element.112), channel_id=1, source_target_pairs={{0,8},{8,16},{16,24},{24,32},{32,40},{40,48},{48,56},{56,64},{64,7... | collective-permute-start | bytes 186632 | tf_op jit(solution)/shard_map/ppermute | solution.py:635
  96.7 8.7 %collective-permute-start.51 = (f32[96,162]{1,0:T(8,128)S(1)}, f32[96,162]{1,0:T(8,128)S(1)}, u32[]{:S(2)}, u32[]{:S(2)}) collective-permute-start(f32[96,162]{1,0:T(8,128)S(1)} %get-tuple-element.113), channel_id=1, source_target_pairs={{0,504},{8,0},{16,8},{24,16},{32,24},{40,32},{48,40},{56,48},{64,5... | collective-permute-start | bytes 186632 | tf_op jit(solution)/shard_map/ppermute | solution.py:635
  104.1 44.3 %copy-start.1 = (f32[16,4,162]{2,1,0:T(4,128)S(1)}, f32[16,4,162]{2,1,0:T(4,128)}, u32[]{:S(2)}) copy-start(f32[16,4,162]{2,1,0:T(4,128)} %src_ref.1) | copy-start | bytes 124420
  104.1 44.3 %copy-start.2 = (f32[4,162,162]{2,0,1:T(4,128)S(1)}, f32[4,162,162]{2,0,1:T(4,128)}, u32[]{:S(2)}) copy-start(f32[4,162,162]{2,0,1:T(4,128)} %param.14) | copy-start | bytes 1259716
  104.2 44.2 %copy-start.4 = (s32[4,6]{1,0:T(4,128)S(1)}, s32[4,6]{1,0:T(4,128)}, u32[]{:S(2)}) copy-start(s32[4,6]{1,0:T(4,128)} %nbr_ref.1) | copy-start | bytes 292
  104.2 44.2 %copy-start.5 = (s32[4,6]{1,0:T(4,128)S(1)}, s32[4,6]{1,0:T(4,128)}, u32[]{:S(2)}) copy-start(s32[4,6]{1,0:T(4,128)} %flag_ref.1) | copy-start | bytes 292
  104.2 44.2 %copy-start.6 = (s32[4,6]{1,0:T(4,128)S(1)}, s32[4,6]{1,0:T(4,128)}, u32[]{:S(2)}) copy-start(s32[4,6]{1,0:T(4,128)} %param.17) | copy-start | bytes 292
  123.2 22.7 %all-to-all-start.1 = ((f32[16,8,128]{2,1,0:T(8,128)}), f32[16,8,128]{2,1,0:T(8,128)S(1)}, u32[]{:S(2)}, u32[]{:S(2)}) async-start(f32[16,8,128]{2,1,0:T(8,128)} %broadcast_in_dim.80), calls=%async_computation.1 | async-start | bytes 131072 | tf_op jit(solution)/shard_map/all_to_all | solution.py:613

commit v4 on v3

--- a/solution.py
+++ b/solution.py
@@ -262,14 +262,35 @@
     return (width + 7) // 8 * 8
 
 
+def tails_of(values):
+    rows, width = values[0].shape
+    tail = width - 128
+    total = None
+    for place, value in enumerate(values):
+        tile = jnp.concatenate([value[:, 128:], jnp.zeros((rows, 128 - tail), F32)], axis=1)
+        tile = tile if place == 0 else pltpu.roll(tile, tail * place, 1)
+        total = tile if total is None else total + tile
+    return total
+
+
+def tail_at(tile, tail, place):
+    turned = tile if place == 0 else pltpu.roll(tile, 128 - tail * place, 1)
+    return turned[:, :tail]
+
+
 def put_rows(ref, first, values):
     rows = values[0].shape[0]
     for place, value in enumerate(values):
-        ref[first + rows * place : first + rows * (place + 1), :] = value
-
-
-def get_rows(ref, first, rows, place):
-    return ref[first + rows * place : first + rows * (place + 1), :]
+        ref[first + rows * place : first + rows * (place + 1), :] = value[:, :128]
+    for part in range(2):
+        start = first + rows * (6 + part)
+        ref[start : start + rows, :] = tails_of(values[3 * part : 3 * part + 3])
+
+
+def get_rows(ref, first, rows, tail, place):
+    main = ref[first + rows * place : first + rows * (place + 1), :]
+    start = first + rows * (6 + place // 3)
+    return jnp.concatenate([main, tail_at(ref[start : start + rows, :], tail, place % 3)], axis=1)
 
 
 def send_along_blk(local, outward, prev_ref, next_ref, first):
@@ -284,13 +305,36 @@
 
 
 def setup_kernel(
-    nbr_ref, flag_ref, src_ref, diag_ref, face_ref,
+    nbr_ref, flag_ref, src_ref, diag_hbm_ref, face_hbm_ref,
     high_ref, low_ref, inv_high_ref, inv_low_ref, base_ref, local_ref, outward_ref,
     blk_prev_ref, blk_next_ref, dom_prev_ref, dom_next_ref, slot_ref,
-    center_ref, x_ref, y_ref, product_ref, cell_ref, face_of_ref,
+    center_ref, x_ref, y_ref, product_ref, face_ref, cell_ref, face_of_ref, diag_sem, face_sem,
     *, dom_count, blk_count,
 ):
-    width = diag_ref.shape[0]
+    width = diag_hbm_ref.shape[0]
+    diag_copies = [
+        pltpu.make_async_copy(
+            diag_hbm_ref.at[:, slot, :], center_ref.at[slot], diag_sem.at[slot]
+        )
+        for slot in range(CELLS)
+    ]
+    face_copies = [
+        [
+            pltpu.make_async_copy(
+                face_hbm_ref.at[face, :, slot, :], face_ref.at[slot, face], face_sem.at[slot, face]
+            )
+            for face in range(6)
+        ]
+        for slot in range(CELLS)
+    ]
+    for slot in range(CELLS):
+        diag_copies[slot].start()
+    for slot in range(CELLS):
+        for face in range(6):
+            pl.when(flag_ref[slot, face] == 1)(face_copies[slot][face].start)
+    for slot in range(CELLS):
+        for face in range(6):
+            pl.when(nbr_ref[slot, face] >= 0)(face_copies[slot][face].start)
     dom_here = lax.axis_index("dom")
     blk_here = lax.axis_index("blk")
     here = dom_here * blk_count + blk_here
@@ -342,11 +386,17 @@
     on_diag = rows == cols
     for slot in range(CELLS):
         base_ref[cell_ref[slot]] = src_ref[:, slot, :]
-        center = diag_ref[:, slot, :]
+        diag_copies[slot].wait()
+    for slot in range(CELLS):
         for face in range(6):
-            wall = jnp.where(flag_ref[slot, face] == 1, 1.0, 0.0).astype(F32)
-            center = center + wall * face_ref[face, :, slot, :]
-        center_ref[slot] = center
+
+            @pl.when(flag_ref[slot, face] == 1)
+            def _():
+                face_copies[slot][face].wait()
+                center_ref[slot] = center_ref[slot] + face_ref[slot, face]
+
+    for slot in range(CELLS):
+        center = center_ref[slot]
         marked = jnp.where(on_diag, center, 0.0)
         inv_row = 1.0 / jnp.sum(marked, axis=0, keepdims=True)
         inv_col = 1.0 / jnp.sum(marked, axis=1, keepdims=True)
@@ -358,6 +408,9 @@
         for slot in range(CELLS):
             x_ref[slot] = 2.0 * x_ref[slot] - dot_full(x_ref[slot], y_ref[slot])
     for slot in range(CELLS):
+        for face in range(6):
+            pl.when(nbr_ref[slot, face] >= 0)(face_copies[slot][face].wait)
+    for slot in range(CELLS):
         cell = cell_ref[slot]
         x_high, x_low = split_halves(x_ref[slot])
         inv_high_ref[cell] = x_high
@@ -366,8 +419,7 @@
         high_ref[cell], low_ref[cell] = split_halves(own)
         for way in range(4):
             face = face_of_ref[slot * 4 + way]
-            keep = jnp.where(face >= 0, 1.0, 0.0).astype(F32)
-            block = face_ref[jnp.maximum(face, 0), :, slot, :] * keep
+            block = jnp.where(face >= 0, face_ref[slot, jnp.maximum(face, 0)], 0.0)
             f_high, f_low = split_halves(block)
             product = dot32(x_high, f_high) + dot32(x_low, f_high) + dot32(x_high, f_low)
             if way < 2:
@@ -383,8 +435,10 @@
             product_ref[entry] = product
     tall = padded(width)
     for way, ref in enumerate((dom_prev_ref, dom_next_ref, blk_prev_ref, blk_next_ref)):
+        pair = [product_ref[OUTWARD + 2 * way + place] for place in range(2)]
         for place in range(2):
-            ref[tall * place : tall * place + width, :] = product_ref[OUTWARD + 2 * way + place]
+            ref[tall * place : tall * place + width, :] = pair[place][:, :128]
+        ref[2 * tall : 2 * tall + width, :] = tails_of(pair)
     halves = [stack_halves(base_ref[cell]) for cell in range(CELLS)]
     local = local_products(halves, high_ref, low_ref)
     outward = outward_products(halves, high_ref, low_ref)
@@ -392,13 +446,14 @@
         local_ref[cell] = local[cell]
     for entry in range(8):
         outward_ref[entry] = outward[entry]
-    send_along_blk(local, outward, blk_prev_ref, blk_next_ref, 2 * tall)
+    send_along_blk(local, outward, blk_prev_ref, blk_next_ref, 3 * tall)
 
 
 def middle_kernel(first_pair, *refs):
     local_ref, outward_ref, from_prev_ref, from_next_ref = refs[:4]
     sum_ref, dom_prev_ref, dom_next_ref = refs[-3:]
     rows = local_ref.shape[1]
+    tail = local_ref.shape[2] - 128
     first = 0
     if first_pair:
         blocks_prev_ref, blocks_next_ref = refs[4:6]
@@ -408,7 +463,7 @@
     sums = []
     for cell in range(CELLS):
         given = from_prev_ref if cell % 2 == 0 else from_next_ref
-        sums.append(local_ref[cell] + get_rows(given, first, rows, cell // 2))
+        sums.append(local_ref[cell] + get_rows(given, first, rows, tail, cell // 2))
         sum_ref[cell] = sums[cell]
     for ref, way in ((dom_prev_ref, 0), (dom_next_ref, 1)):
         put_rows(
@@ -416,8 +471,8 @@
             [
                 outward_ref[2 * way], outward_ref[2 * way + 1],
                 sums[2 * way], sums[2 * way + 1],
-                get_rows(from_prev_ref, first, rows, 4 + way),
-                get_rows(from_next_ref, first, rows, 4 + way),
+                get_rows(from_prev_ref, first, rows, tail, 4 + way),
+                get_rows(from_next_ref, first, rows, tail, 4 + way),
             ],
         )
 
@@ -431,7 +486,7 @@
     first = 0
     if first_pair:
         tall = padded(width)
-        first = 2 * tall
+        first = 3 * tall
     else:
         in_high_ref, in_low_ref = refs[:2]
         refs = refs[2:]
@@ -445,12 +500,14 @@
         in_high_ref, in_low_ref = refs[6:]
         for way, ref in enumerate((dom_prev_ref, dom_next_ref, blk_prev_ref, blk_next_ref)):
             for place in range(2):
-                high, low = split_halves(ref[tall * place : tall * place + width, :])
+                main = ref[tall * place : tall * place + width, :]
+                tail = tail_at(ref[2 * tall : 2 * tall + width, :], width - 128, place)
+                high, low = split_halves(jnp.concatenate([main, tail], axis=1))
                 in_high_ref[2 * way + place] = high
                 in_low_ref[2 * way + place] = low
 
     def got(ref, place):
-        return get_rows(ref, first, rows, place)
+        return get_rows(ref, first, rows, width - 128, place)
 
     odd = [
         sum_ref[cell] + got(dom_prev_ref if cell < 2 else dom_next_ref, cell % 2)
@@ -480,7 +537,9 @@
         gram = gram_rows(ITERS - 1, bases, gram_in_ref[...])
         gram = gram_rows(ITERS, bases, gram)
         half = gram.shape[0] // 2
-        gram_ref[...] = gram[:half] + pltpu.roll(gram[half:], 64, 1)
+        gram = gram[:half] + pltpu.roll(gram[half:], 64, 1)
+        for place in range(gram_ref.shape[0]):
+            gram_ref[place] = gram
     else:
         halves = [stack_halves(value) for value in even]
         local = local_products(halves, high_ref, low_ref)
@@ -520,7 +579,7 @@
     base_refs = refs[1 : 1 + ITERS]
     inv_high_ref, inv_low_ref, slot_ref, adjoint_ref, rel_ref, fine_ref = refs[1 + ITERS :]
     count = ITERS + 1
-    packed = gram_ref[...]
+    packed = sum_parts(gram_ref)
     gram = jnp.concatenate([packed, pltpu.roll(packed, 64, 1)], axis=0)
 
     def lane(row, col):
@@ -607,27 +666,42 @@
     return jax.ShapeDtypeStruct(shape, kind)
 
 
-def sum_groups(value, axes, groups):
-    size = len(groups[0])
-    copies = jnp.broadcast_to(value[None], (size,) + value.shape)
-    parts = lax.all_to_all(
-        copies, axes, 0, 0, axis_index_groups=groups if len(groups) > 1 else None
-    )
-    return jnp.sum(parts, axis=0)
-
-
-def sum_devices(value):
+def spread_kernel(parts_ref, copies_ref):
+    total = sum_parts(parts_ref)
+    for place in range(copies_ref.shape[0]):
+        copies_ref[place] = total
+
+
+def sum_parts(parts_ref):
+    total = parts_ref[0]
+    for place in range(1, parts_ref.shape[0]):
+        total = total + parts_ref[place]
+    return total
+
+
+def near_size():
+    dom_count = lax.axis_size("dom")
+    return 4 if dom_count % 4 == 0 else dom_count
+
+
+def sum_devices(copies):
     dom_count, blk_count = (lax.axis_size("dom"), lax.axis_size("blk"))
-    inner = 4 if dom_count % 4 == 0 else dom_count
+    inner = near_size()
     size = inner * blk_count
     near = [
         [first + k for k in range(size)] for first in range(0, dom_count * blk_count, size)
     ]
-    value = sum_groups(value, ("dom", "blk"), near)
-    if inner < dom_count:
-        far = [[first + k for k in range(0, dom_count, inner)] for first in range(inner)]
-        value = sum_groups(value, "dom", far)
-    return value
+    far = [[first + k for k in range(0, dom_count, inner)] for first in range(inner)]
+    parts = lax.all_to_all(copies, ("dom", "blk"), 0, 0, axis_index_groups=near)
+    copies = pl.pallas_call(
+        spread_kernel,
+        out_shape=struct(dom_count // inner, *copies.shape[1:]),
+        in_specs=vmem(1),
+        out_specs=vmem(1)[0],
+        compiler_params=PARAMS,
+        name="sum_near",
+    )(parts)
+    return lax.all_to_all(copies, "dom", 0, 0, axis_index_groups=far)
 
 
 def rotated(value, axis, steps):
@@ -647,8 +721,8 @@
     tall = padded(width)
     field = struct(CELLS, nrhs, width)
     ring = struct(8, nrhs, width)
-    edge = struct(6 * nrhs, width)
-    edge_blocks = struct(2 * tall + 6 * nrhs, width)
+    edge = struct(8 * nrhs, 128)
+    edge_blocks = struct(3 * tall + 8 * nrhs, 128)
     cost = lambda flops, data: pl.CostEstimate(
         flops=flops, bytes_accessed=data, transcendentals=0
     )
@@ -661,18 +735,21 @@
             struct(BLOCKS, *block, kind=BF16), struct(BLOCKS, *block, kind=BF16),
             struct(CELLS, *block, kind=BF16), struct(CELLS, *block, kind=BF16),
             field, field, ring, edge_blocks, edge_blocks,
-            struct(2 * tall, width), struct(2 * tall, width),
+            struct(3 * tall, 128), struct(3 * tall, 128),
             struct(CELLS, kind=jnp.int32),
         ),
-        in_specs=smem(2) + vmem(3),
+        in_specs=smem(2) + vmem(1) + [pl.BlockSpec(memory_space=pl.ANY)] * 2,
         out_specs=tuple(vmem(11) + smem(1)),
         scratch_shapes=[
             pltpu.VMEM((CELLS,) + block, F32),
             pltpu.VMEM((CELLS,) + block, F32),
             pltpu.VMEM((CELLS,) + block, F32),
             pltpu.VMEM((BLOCKS,) + block, F32),
+            pltpu.VMEM((CELLS, 6) + block, F32),
             pltpu.SMEM((CELLS,), jnp.int32),
             pltpu.SMEM((CELLS * 4,), jnp.int32),
+            pltpu.SemaphoreType.DMA((CELLS,)),
+            pltpu.SemaphoreType.DMA((CELLS, 6)),
         ],
         compiler_params=PARAMS,
         name="setup_blocks",
@@ -717,7 +794,7 @@
         given = [sums, outward, *from_blk, *from_dom, high, low, *inward, *older]
         if last_pair:
             given.append(gram)
-            shapes = (struct(nrhs // 2, 128), field, field)
+            shapes = (struct(near_size() * lax.axis_size("blk"), nrhs // 2, 128), field, field)
         else:
             shapes = (field, field, field, ring, edge, edge)
         if first_pair:

time: 149 us -> 135 us (0.906)
  Pallas kernels: 25.8 us -> 17.8 us
  waiting for transfers between devices: 37.7 us -> 30.8 us
    pallas_call x1, Pallas kernels: 18.4 us -> 8.99 us  [shards(): pl.pallas_call(functools.partial(setup_kernel, dom_count=lax.axis_size('d...]
    ppermute x16, waiting for transfers between devices: 26.1 us -> 19.2 us  [rotated(): lax.ppermute(value, axis, [(source, (source + steps) % count) for source...]
  transfers between devices with their start and end apart: 17 -> 17, of which waited for: 16 -> 14; matrix products, arithmetic and copies ran while one was open for 0% -> 0% of each run, Pallas kernels for 0% -> 0%
where the time goes in v4:
time: 135 us; the launch traced here: 134 us
  starting transfers between devices  67.7 us (50%)
  waiting for transfers between devices  30.8 us (23%)
  Pallas kernels  17.8 us (13%)
  blocking collectives  15.8 us (12%)
  between operations  1.73 us (1%)
    ppermute x16, starting transfers between devices, rotated(): lax.ppermute(value, axis, [(source, (source + steps) % count) for source...  56.7 us
    ppermute x16, waiting for transfers between devices, rotated(): lax.ppermute(value, axis, [(source, (source + steps) % count) for source...  19.2 us
    all_to_all x1, blocking collectives, sum_devices(): parts = lax.all_to_all(copies, ('dom', 'blk'), 0, 0, axis_index_groups=near)  15.8 us
    all_to_all x1, waiting for transfers between devices, sum_devices(): return lax.all_to_all(copies, 'dom', 0, 0, axis_index_groups=far)  11.6 us
    all_to_all x1, starting transfers between devices, sum_devices(): return lax.all_to_all(copies, 'dom', 0, 0, axis_index_groups=far)  11 us
    pallas_call x1, Pallas kernels, shards(): pl.pallas_call(functools.partial(setup_kernel, dom_count=lax.axis_size('d...  8.99 us
    pallas_call x4, Pallas kernels, shards(): pl.pallas_call(functools.partial(pair_kernel, first_pair, last_pair, len(...  5.25 us
  transfers between devices with their start and end apart: 17, of which 14 were waited for; matrix products, arithmetic and copies ran while one was open for 0% of the time, Pallas kernels for 0%

profile of v4, /device:TPU:1, one launch (start us, length us, event | category | flops | bytes accessed | tf_op | source)
XLA Modules:
  0.0 134.1 jit_solution(8249762620412463154)
XLA Ops:
  0.6 9.0 %setup_blocks.1 = (bf16[20,162,162]{2,1,0:T(8,128)(2,1)S(1)}, bf16[20,162,162]{2,1,0:T(8,128)(2,1)S(1)}, bf16[4,162,162]{2,1,0:T(8,128)(2,1)S(1)}, bf16[4,162,16...) custom-call(s32[4,6]{1,0:T(4,128)} %nbr_ref.1, ...), custom_call_target="tpu_custom_call" | custom-call | tf_op jit(solution)/shard_map/setup_blocks/pallas_call | solution.py:730
  9.6 2.7 %collective-permute-start.36 = (f32[632,128]{1,0:T(8,128)S(1)}, f32[632,128]{1,0:T(8,128)S(1)}, u32[]{:S(2)}, u32[]{:S(2)}) collective-permute-start(f32[632,128]{1,0:T(8,128)S(1)} %get-tuple-element.82), channel_id=1, source_target_pairs={{0,1},{1,2},{2,3},{3,4},{4,5},{5,6},{6,7},{7,0},{8,9},{9,10},{10,1... | collective-permute-start | bytes 970760 | tf_op jit(solution)/shard_map/ppermute | solution.py:709
  12.4 4.2 %collective-permute-start.37 = (f32[632,128]{1,0:T(8,128)S(1)}, f32[632,128]{1,0:T(8,128)S(1)}, u32[]{:S(2)}, u32[]{:S(2)}) collective-permute-start(f32[632,128]{1,0:T(8,128)S(1)} %get-tuple-element.83), channel_id=1, source_target_pairs={{0,7},{1,0},{2,1},{3,2},{4,3},{5,4},{6,5},{7,6},{8,15},{9,8},{10,9... | collective-permute-start | bytes 970760 | tf_op jit(solution)/shard_map/ppermute | solution.py:709
  16.6 1.1 collective-permute-done.36.refs_2_
  17.7 1.1 collective-permute-done.37.refs_3_
  18.8 0.2 middle_part_0.1
  19.0 3.1 %collective-permute-start.38 = (f32[632,128]{1,0:T(8,128)S(1)}, f32[632,128]{1,0:T(8,128)S(1)}, u32[]{:S(2)}, u32[]{:S(2)}) collective-permute-start(f32[632,128]{1,0:T(8,128)S(1)} %get-tuple-element.87), channel_id=1, source_target_pairs={{0,8},{8,16},{16,24},{24,32},{32,40},{40,48},{48,56},{56,64},{64,7... | collective-permute-start | bytes 970760 | tf_op jit(solution)/shard_map/ppermute | solution.py:709
  22.1 12.1 %collective-permute-start.39 = (f32[632,128]{1,0:T(8,128)S(1)}, f32[632,128]{1,0:T(8,128)S(1)}, u32[]{:S(2)}, u32[]{:S(2)}) collective-permute-start(f32[632,128]{1,0:T(8,128)S(1)} %get-tuple-element.88), channel_id=1, source_target_pairs={{0,504},{8,0},{16,8},{24,16},{32,24},{40,32},{48,40},{56,48},{64,5... | collective-permute-start | bytes 970760 | tf_op jit(solution)/shard_map/ppermute | solution.py:709
  34.2 6.1 %collective-permute-done.38.refs_4_ = f32[632,128]{1,0:T(8,128)S(1)} collective-permute-done((f32[632,128]{1,0:T(8,128)S(1)}, f32[632,128]{1,0:T(8,128)S(1)}, u32[]{:S(2)}, u32[]{:S(2)}) %collective-permute-start.38) | collective-permute-done | bytes 323616 | tf_op jit(solution)/shard_map/ppermute | solution.py:709
  40.3 1.0 collective-permute-done.39.refs_5_
  41.3 1.4 %pair_part_0.1 = (f32[4,16,162]{2,1,0:T(8,128)S(1)}, f32[4,16,162]{2,1,0:T(8,128)S(1)}, f32[4,16,162]{2,1,0:T(8,128)S(1)}, f32[8,16,162]{2,1,0:T(8,128)S(1)}, f3...) custom-call(f32[4,16,162]{2,1,0:T(8,128)S(1)} %get-tuple-element.86., ...), custom_call_target="tpu_custom_call" | custom-call | flops 100776960 | bytes 6000000 | tf_op jit(solution)/shard_map/pair_part_0/pallas_call | solution.py:802
  42.6 0.5 collective-permute-start.40
  43.1 0.3 collective-permute-start.41
  43.4 1.0 collective-permute-done.40.refs_2_
  44.4 2.4 %collective-permute-done.41.refs_3_ = f32[128,128]{1,0:T(8,128)S(1)} collective-permute-done((f32[128,128]{1,0:T(8,128)S(1)}, f32[128,128]{1,0:T(8,128)S(1)}, u32[]{:S(2)}, u32[]{:S(2)}) %collective-permute-start.41) | collective-permute-done | bytes 65568 | tf_op jit(solution)/shard_map/ppermute | solution.py:709
  46.8 0.1 middle_part_1.1
  46.9 1.9 %collective-permute-start.42 = (f32[128,128]{1,0:T(8,128)S(1)}, f32[128,128]{1,0:T(8,128)S(1)}, u32[]{:S(2)}, u32[]{:S(2)}) collective-permute-start(f32[128,128]{1,0:T(8,128)S(1)} %get-tuple-element.96), channel_id=1, source_target_pairs={{0,8},{8,16},{16,24},{24,32},{32,40},{40,48},{48,56},{56,64},{64,7... | collective-permute-start | bytes 196616 | tf_op jit(solution)/shard_map/ppermute | solution.py:709
  48.9 7.4 %collective-permute-start.43 = (f32[128,128]{1,0:T(8,128)S(1)}, f32[128,128]{1,0:T(8,128)S(1)}, u32[]{:S(2)}, u32[]{:S(2)}) collective-permute-start(f32[128,128]{1,0:T(8,128)S(1)} %get-tuple-element.97), channel_id=1, source_target_pairs={{0,504},{8,0},{16,8},{24,16},{32,24},{40,32},{48,40},{56,48},{64,5... | collective-permute-start | bytes 196616 | tf_op jit(solution)/shard_map/ppermute | solution.py:709
  56.3 0.0 collective-permute-done.42.refs_4_
  56.3 1.3 collective-permute-done.43.refs_5_
  57.6 1.3 pair_part_1.1
  58.9 0.9 collective-permute-start.44
  59.8 1.5 %collective-permute-start.45 = (f32[128,128]{1,0:T(8,128)S(1)}, f32[128,128]{1,0:T(8,128)S(1)}, u32[]{:S(2)}, u32[]{:S(2)}) collective-permute-start(f32[128,128]{1,0:T(8,128)S(1)} %get-tuple-element.103), channel_id=1, source_target_pairs={{0,7},{1,0},{2,1},{3,2},{4,3},{5,4},{6,5},{7,6},{8,15},{9,8},{10,9... | collective-permute-start | bytes 196616 | tf_op jit(solution)/shard_map/ppermute | solution.py:709
  61.3 0.7 collective-permute-done.44.refs_2_
  62.0 1.4 %collective-permute-done.45.refs_3_ = f32[128,128]{1,0:T(8,128)S(1)} collective-permute-done((f32[128,128]{1,0:T(8,128)S(1)}, f32[128,128]{1,0:T(8,128)S(1)}, u32[]{:S(2)}, u32[]{:S(2)}) %collective-permute-start.45) | collective-permute-done | bytes 65568 | tf_op jit(solution)/shard_map/ppermute | solution.py:709
  63.5 0.1 middle_part_2.1
  63.6 1.9 %collective-permute-start.46 = (f32[128,128]{1,0:T(8,128)S(1)}, f32[128,128]{1,0:T(8,128)S(1)}, u32[]{:S(2)}, u32[]{:S(2)}) collective-permute-start(f32[128,128]{1,0:T(8,128)S(1)} %get-tuple-element.105), channel_id=1, source_target_pairs={{0,8},{8,16},{16,24},{24,32},{32,40},{40,48},{48,56},{56,64},{64,7... | collective-permute-start | bytes 196616 | tf_op jit(solution)/shard_map/ppermute | solution.py:709
  65.5 7.3 %collective-permute-start.47 = (f32[128,128]{1,0:T(8,128)S(1)}, f32[128,128]{1,0:T(8,128)S(1)}, u32[]{:S(2)}, u32[]{:S(2)}) collective-permute-start(f32[128,128]{1,0:T(8,128)S(1)} %get-tuple-element.106), channel_id=1, source_target_pairs={{0,504},{8,0},{16,8},{24,16},{32,24},{40,32},{48,40},{56,48},{64,5... | collective-permute-start | bytes 196616 | tf_op jit(solution)/shard_map/ppermute | solution.py:709
  72.8 0.0 collective-permute-done.46.refs_4_
  72.9 1.3 collective-permute-done.47.refs_5_
  74.2 1.3 pair_part_2.1
  75.4 0.9 collective-permute-start.48
  76.3 2.7 %collective-permute-start.49 = (f32[128,128]{1,0:T(8,128)S(1)}, f32[128,128]{1,0:T(8,128)S(1)}, u32[]{:S(2)}, u32[]{:S(2)}) collective-permute-start(f32[128,128]{1,0:T(8,128)S(1)} %get-tuple-element.110), channel_id=1, source_target_pairs={{0,7},{1,0},{2,1},{3,2},{4,3},{5,4},{6,5},{7,6},{8,15},{9,8},{10,9... | collective-permute-start | bytes 196616 | tf_op jit(solution)/shard_map/ppermute | solution.py:709
  79.0 0.7 collective-permute-done.48.refs_2_
  79.8 0.4 collective-permute-done.49.refs_3_
  80.2 0.1 middle_part_3.1
  80.3 1.9 %collective-permute-start.50 = (f32[128,128]{1,0:T(8,128)S(1)}, f32[128,128]{1,0:T(8,128)S(1)}, u32[]{:S(2)}, u32[]{:S(2)}) collective-permute-start(f32[128,128]{1,0:T(8,128)S(1)} %get-tuple-element.112), channel_id=1, source_target_pairs={{0,8},{8,16},{16,24},{24,32},{32,40},{40,48},{48,56},{56,64},{64,7... | collective-permute-start | bytes 196616 | tf_op jit(solution)/shard_map/ppermute | solution.py:709
  82.2 7.3 %collective-permute-start.51 = (f32[128,128]{1,0:T(8,128)S(1)}, f32[128,128]{1,0:T(8,128)S(1)}, u32[]{:S(2)}, u32[]{:S(2)}) collective-permute-start(f32[128,128]{1,0:T(8,128)S(1)} %get-tuple-element.113), channel_id=1, source_target_pairs={{0,504},{8,0},{16,8},{24,16},{32,24},{40,32},{48,40},{56,48},{64,5... | collective-permute-start | bytes 196616 | tf_op jit(solution)/shard_map/ppermute | solution.py:709
  89.6 0.1 gram_part_0.1.refs_3_
  89.6 0.1 gram_part_1.1.refs_5_
  89.8 0.1 gram_part_2.1.refs_7_
  89.9 0.0 copy-start.1
  89.9 0.0 copy-start.2
  89.9 0.0 copy-start.4
  89.9 0.0 copy-start.5
  89.9 0.0 copy-start.6
  89.9 0.1 gram_part_3.1.refs_17_
  90.1 0.0 collective-permute-done.50.refs_4_
  90.1 0.6 collective-permute-done.51.refs_5_
  90.7 1.3 pair_part_3.1
  92.0 15.8 %all_to_all.10.parts_ref = f32[32,8,128]{2,1,0:T(8,128)S(1)} all-to-all(f32[32,8,128]{2,1,0:T(8,128)S(1)} %get-tuple-element.121), channel_id=1, replica_groups={{0,1,2,3,4,5,6,7,8,9,10,11,12,13,14,15,16,17,18,19,20,21,22,23,24,25,26..., dimensions={0} | all-to-all | bytes 262144 | tf_op jit(solution)/shard_map/all_to_all | solution.py:695
  107.8 0.7 sum_near.1
  108.5 11.0 %all-to-all-start.1 = ((f32[16,8,128]{2,1,0:T(8,128)}), f32[16,8,128]{2,1,0:T(8,128)S(1)}, u32[]{:S(2)}, u32[]{:S(2)}) async-start(f32[16,8,128]{2,1,0:T(8,128)} %sum_near.1), calls=%async_computation.1 | async-start | bytes 131072 | tf_op jit(solution)/shard_map/all_to_all | solution.py:704
  119.5 11.6 %all-to-all-done.1.refs_0_ = f32[16,8,128]{2,1,0:T(8,128)S(1)} async-done(((f32[16,8,128]{2,1,0:T(8,128)}), f32[16,8,128]{2,1,0:T(8,128)S(1)}, u32[]{:S(2)}, u32[]{:S(2)}) %all-to-all-start.1) | async-done | bytes 65568 | tf_op jit(solution)/shard_map/all_to_all | solution.py:704
  131.1 1.8 %finish_part.1 = (f32[16,4,162]{2,1,0:T(4,128)}, f32[1,16]{1,0:T(1,128)}, s32[1]{0:T(128)}) custom-call(f32[16,8,128]{2,1,0:T(8,128)S(1)} %all-to-all-done.1.refs_0_, f32[4,16,162]{2,1,0:T(8,128)S(1)} %get-tuple-element.114.refs_0_.refs_10_.refs_1_, f32[4,16,162]{2,1,0:T(8,128)S(1)} %get-tuple-element.115.refs_1_.refs_11_.refs_2_, ...), custom_call_target="tpu_custom_call" | custom-call | tf_op jit(solution)/shard_map/finish_part/pallas_call | solution.py:822
  133.6 0.0 copy-done.1
  133.6 0.0 copy-done.2
  133.6 0.0 copy-done.4
  133.6 0.0 copy-done.5
  133.6 0.0 copy-done.6
  133.6 0.3 conditional.1
Async XLA Ops:
  9.6 8.1 %collective-permute-start.36 = (f32[632,128]{1,0:T(8,128)S(1)}, f32[632,128]{1,0:T(8,128)S(1)}, u32[]{:S(2)}, u32[]{:S(2)}) collective-permute-start(f32[632,128]{1,0:T(8,128)S(1)} %get-tuple-element.82), channel_id=1, source_target_pairs={{0,1},{1,2},{2,3},{3,4},{4,5},{5,6},{6,7},{7,0},{8,9},{9,10},{10,1... | collective-permute-start | bytes 970760 | tf_op jit(solution)/shard_map/ppermute | solution.py:709
  12.4 6.5 %collective-permute-start.37 = (f32[632,128]{1,0:T(8,128)S(1)}, f32[632,128]{1,0:T(8,128)S(1)}, u32[]{:S(2)}, u32[]{:S(2)}) collective-permute-start(f32[632,128]{1,0:T(8,128)S(1)} %get-tuple-element.83), channel_id=1, source_target_pairs={{0,7},{1,0},{2,1},{3,2},{4,3},{5,4},{6,5},{7,6},{8,15},{9,8},{10,9... | collective-permute-start | bytes 970760 | tf_op jit(solution)/shard_map/ppermute | solution.py:709
  19.0 21.3 %collective-permute-start.38 = (f32[632,128]{1,0:T(8,128)S(1)}, f32[632,128]{1,0:T(8,128)S(1)}, u32[]{:S(2)}, u32[]{:S(2)}) collective-permute-start(f32[632,128]{1,0:T(8,128)S(1)} %get-tuple-element.87), channel_id=1, source_target_pairs={{0,8},{8,16},{16,24},{24,32},{32,40},{40,48},{48,56},{56,64},{64,7... | collective-permute-start | bytes 970760 | tf_op jit(solution)/shard_map/ppermute | solution.py:709
  22.1 19.2 %collective-permute-start.39 = (f32[632,128]{1,0:T(8,128)S(1)}, f32[632,128]{1,0:T(8,128)S(1)}, u32[]{:S(2)}, u32[]{:S(2)}) collective-permute-start(f32[632,128]{1,0:T(8,128)S(1)} %get-tuple-element.88), channel_id=1, source_target_pairs={{0,504},{8,0},{16,8},{24,16},{32,24},{40,32},{48,40},{56,48},{64,5... | collective-permute-start | bytes 970760 | tf_op jit(solution)/shard_map/ppermute | solution.py:709
  42.6 1.8 %collective-permute-start.40 = (f32[128,128]{1,0:T(8,128)S(1)}, f32[128,128]{1,0:T(8,128)S(1)}, u32[]{:S(2)}, u32[]{:S(2)}) collective-permute-start(f32[128,128]{1,0:T(8,128)S(1)} %get-tuple-element.93), channel_id=1, source_target_pairs={{0,1},{1,2},{2,3},{3,4},{4,5},{5,6},{6,7},{7,0},{8,9},{9,10},{10,1... | collective-permute-start | bytes 196616 | tf_op jit(solution)/shard_map/ppermute | solution.py:709
  43.1 3.7 %collective-permute-start.41 = (f32[128,128]{1,0:T(8,128)S(1)}, f32[128,128]{1,0:T(8,128)S(1)}, u32[]{:S(2)}, u32[]{:S(2)}) collective-permute-start(f32[128,128]{1,0:T(8,128)S(1)} %get-tuple-element.94), channel_id=1, source_target_pairs={{0,7},{1,0},{2,1},{3,2},{4,3},{5,4},{6,5},{7,6},{8,15},{9,8},{10,9... | collective-permute-start | bytes 196616 | tf_op jit(solution)/shard_map/ppermute | solution.py:709
  46.9 9.4 %collective-permute-start.42 = (f32[128,128]{1,0:T(8,128)S(1)}, f32[128,128]{1,0:T(8,128)S(1)}, u32[]{:S(2)}, u32[]{:S(2)}) collective-permute-start(f32[128,128]{1,0:T(8,128)S(1)} %get-tuple-element.96), channel_id=1, source_target_pairs={{0,8},{8,16},{16,24},{24,32},{32,40},{40,48},{48,56},{56,64},{64,7... | collective-permute-start | bytes 196616 | tf_op jit(solution)/shard_map/ppermute | solution.py:709
  48.9 8.7 %collective-permute-start.43 = (f32[128,128]{1,0:T(8,128)S(1)}, f32[128,128]{1,0:T(8,128)S(1)}, u32[]{:S(2)}, u32[]{:S(2)}) collective-permute-start(f32[128,128]{1,0:T(8,128)S(1)} %get-tuple-element.97), channel_id=1, source_target_pairs={{0,504},{8,0},{16,8},{24,16},{32,24},{40,32},{48,40},{56,48},{64,5... | collective-permute-start | bytes 196616 | tf_op jit(solution)/shard_map/ppermute | solution.py:709
  58.9 3.1 %collective-permute-start.44 = (f32[128,128]{1,0:T(8,128)S(1)}, f32[128,128]{1,0:T(8,128)S(1)}, u32[]{:S(2)}, u32[]{:S(2)}) collective-permute-start(f32[128,128]{1,0:T(8,128)S(1)} %get-tuple-element.102), channel_id=1, source_target_pairs={{0,1},{1,2},{2,3},{3,4},{4,5},{5,6},{6,7},{7,0},{8,9},{9,10},{10,1... | collective-permute-start | bytes 196616 | tf_op jit(solution)/shard_map/ppermute | solution.py:709
  59.8 3.7 %collective-permute-start.45 = (f32[128,128]{1,0:T(8,128)S(1)}, f32[128,128]{1,0:T(8,128)S(1)}, u32[]{:S(2)}, u32[]{:S(2)}) collective-permute-start(f32[128,128]{1,0:T(8,128)S(1)} %get-tuple-element.103), channel_id=1, source_target_pairs={{0,7},{1,0},{2,1},{3,2},{4,3},{5,4},{6,5},{7,6},{8,15},{9,8},{10,9... | collective-permute-start | bytes 196616 | tf_op jit(solution)/shard_map/ppermute | solution.py:709
  63.6 9.2 %collective-permute-start.46 = (f32[128,128]{1,0:T(8,128)S(1)}, f32[128,128]{1,0:T(8,128)S(1)}, u32[]{:S(2)}, u32[]{:S(2)}) collective-permute-start(f32[128,128]{1,0:T(8,128)S(1)} %get-tuple-element.105), channel_id=1, source_target_pairs={{0,8},{8,16},{16,24},{24,32},{32,40},{40,48},{48,56},{56,64},{64,7... | collective-permute-start | bytes 196616 | tf_op jit(solution)/shard_map/ppermute | solution.py:709
  65.5 8.6 %collective-permute-start.47 = (f32[128,128]{1,0:T(8,128)S(1)}, f32[128,128]{1,0:T(8,128)S(1)}, u32[]{:S(2)}, u32[]{:S(2)}) collective-permute-start(f32[128,128]{1,0:T(8,128)S(1)} %get-tuple-element.106), channel_id=1, source_target_pairs={{0,504},{8,0},{16,8},{24,16},{32,24},{40,32},{48,40},{56,48},{64,5... | collective-permute-start | bytes 196616 | tf_op jit(solution)/shard_map/ppermute | solution.py:709
  75.4 4.3 %collective-permute-start.48 = (f32[128,128]{1,0:T(8,128)S(1)}, f32[128,128]{1,0:T(8,128)S(1)}, u32[]{:S(2)}, u32[]{:S(2)}) collective-permute-start(f32[128,128]{1,0:T(8,128)S(1)} %get-tuple-element.109), channel_id=1, source_target_pairs={{0,1},{1,2},{2,3},{3,4},{4,5},{5,6},{6,7},{7,0},{8,9},{9,10},{10,1... | collective-permute-start | bytes 196616 | tf_op jit(solution)/shard_map/ppermute | solution.py:709
  76.3 3.8 %collective-permute-start.49 = (f32[128,128]{1,0:T(8,128)S(1)}, f32[128,128]{1,0:T(8,128)S(1)}, u32[]{:S(2)}, u32[]{:S(2)}) collective-permute-start(f32[128,128]{1,0:T(8,128)S(1)} %get-tuple-element.110), channel_id=1, source_target_pairs={{0,7},{1,0},{2,1},{3,2},{4,3},{5,4},{6,5},{7,6},{8,15},{9,8},{10,9... | collective-permute-start | bytes 196616 | tf_op jit(solution)/shard_map/ppermute | solution.py:709
  80.3 9.8 %collective-permute-start.50 = (f32[128,128]{1,0:T(8,128)S(1)}, f32[128,128]{1,0:T(8,128)S(1)}, u32[]{:S(2)}, u32[]{:S(2)}) collective-permute-start(f32[128,128]{1,0:T(8,128)S(1)} %get-tuple-element.112), channel_id=1, source_target_pairs={{0,8},{8,16},{16,24},{24,32},{32,40},{40,48},{48,56},{56,64},{64,7... | collective-permute-start | bytes 196616 | tf_op jit(solution)/shard_map/ppermute | solution.py:709
  82.2 8.5 %collective-permute-start.51 = (f32[128,128]{1,0:T(8,128)S(1)}, f32[128,128]{1,0:T(8,128)S(1)}, u32[]{:S(2)}, u32[]{:S(2)}) collective-permute-start(f32[128,128]{1,0:T(8,128)S(1)} %get-tuple-element.113), channel_id=1, source_target_pairs={{0,504},{8,0},{16,8},{24,16},{32,24},{40,32},{48,40},{56,48},{64,5... | collective-permute-start | bytes 196616 | tf_op jit(solution)/shard_map/ppermute | solution.py:709
  89.9 43.7 %copy-start.1 = (f32[16,4,162]{2,1,0:T(4,128)S(1)}, f32[16,4,162]{2,1,0:T(4,128)}, u32[]{:S(2)}) copy-start(f32[16,4,162]{2,1,0:T(4,128)} %src_ref.1) | copy-start | bytes 124420
  89.9 43.7 %copy-start.2 = (f32[4,162,162]{2,0,1:T(4,128)S(1)}, f32[4,162,162]{2,0,1:T(4,128)}, u32[]{:S(2)}) copy-start(f32[4,162,162]{2,0,1:T(4,128)} %param.14) | copy-start | bytes 1259716
  89.9 43.7 %copy-start.4 = (s32[4,6]{1,0:T(4,128)S(1)}, s32[4,6]{1,0:T(4,128)}, u32[]{:S(2)}) copy-start(s32[4,6]{1,0:T(4,128)} %nbr_ref.1) | copy-start | bytes 292
  89.9 43.7 %copy-start.5 = (s32[4,6]{1,0:T(4,128)S(1)}, s32[4,6]{1,0:T(4,128)}, u32[]{:S(2)}) copy-start(s32[4,6]{1,0:T(4,128)} %flag_ref.1) | copy-start | bytes 292
  89.9 43.7 %copy-start.6 = (s32[4,6]{1,0:T(4,128)S(1)}, s32[4,6]{1,0:T(4,128)}, u32[]{:S(2)}) copy-start(s32[4,6]{1,0:T(4,128)} %param.17) | copy-start | bytes 292
  108.5 22.6 %all-to-all-start.1 = ((f32[16,8,128]{2,1,0:T(8,128)}), f32[16,8,128]{2,1,0:T(8,128)S(1)}, u32[]{:S(2)}, u32[]{:S(2)}) async-start(f32[16,8,128]{2,1,0:T(8,128)} %sum_near.1), calls=%async_computation.1 | async-start | bytes 131072 | tf_op jit(solution)/shard_map/all_to_all | solution.py:704

commit v5 on v4

--- a/solution.py
+++ b/solution.py
@@ -282,14 +282,14 @@
     rows = values[0].shape[0]
     for place, value in enumerate(values):
         ref[first + rows * place : first + rows * (place + 1), :] = value[:, :128]
-    for part in range(2):
-        start = first + rows * (6 + part)
-        ref[start : start + rows, :] = tails_of(values[3 * part : 3 * part + 3])
-
-
-def get_rows(ref, first, rows, tail, place):
+    for part in range(0, len(values), 3):
+        start = first + rows * (len(values) + part // 3)
+        ref[start : start + rows, :] = tails_of(values[part : part + 3])
+
+
+def get_rows(ref, first, rows, tail, count, place):
     main = ref[first + rows * place : first + rows * (place + 1), :]
-    start = first + rows * (6 + place // 3)
+    start = first + rows * (count + place // 3)
     return jnp.concatenate([main, tail_at(ref[start : start + rows, :], tail, place % 3)], axis=1)
 
 
@@ -299,9 +299,16 @@
             ref, first,
             [
                 outward[2 * way], outward[2 * way + 1], local[cells[0]], local[cells[1]],
-                outward[cells[0] % 2], outward[2 + cells[0] % 2],
+                outward[2 + cells[0] % 2],
             ],
         )
+
+
+def send_to_dom_prev(local, outward, prev_ref, first):
+    put_rows(
+        prev_ref, first,
+        [outward[0], outward[1], local[0], local[1], outward[4], outward[6]],
+    )
 
 
 def setup_kernel(
@@ -447,46 +454,54 @@
     for entry in range(8):
         outward_ref[entry] = outward[entry]
     send_along_blk(local, outward, blk_prev_ref, blk_next_ref, 3 * tall)
-
-
-def middle_kernel(first_pair, *refs):
-    local_ref, outward_ref, from_prev_ref, from_next_ref = refs[:4]
-    sum_ref, dom_prev_ref, dom_next_ref = refs[-3:]
+    send_to_dom_prev(local, outward, dom_prev_ref, 3 * tall)
+
+
+FROM_BLK = 5
+FROM_DOM = 6
+RELAYED = 2
+
+
+def middle_kernel(first, local_ref, outward_ref, prev_ref, next_ref, sum_ref, dom_next_ref):
     rows = local_ref.shape[1]
     tail = local_ref.shape[2] - 128
-    first = 0
-    if first_pair:
-        blocks_prev_ref, blocks_next_ref = refs[4:6]
-        first = blocks_prev_ref.shape[0]
-        dom_prev_ref[:first, :] = blocks_prev_ref[...]
-        dom_next_ref[:first, :] = blocks_next_ref[...]
+
+    def got(ref, place):
+        return get_rows(ref, first, rows, tail, FROM_BLK, place)
+
     sums = []
     for cell in range(CELLS):
-        given = from_prev_ref if cell % 2 == 0 else from_next_ref
-        sums.append(local_ref[cell] + get_rows(given, first, rows, tail, cell // 2))
+        given = prev_ref if cell % 2 == 0 else next_ref
+        sums.append(local_ref[cell] + got(given, cell // 2))
         sum_ref[cell] = sums[cell]
-    for ref, way in ((dom_prev_ref, 0), (dom_next_ref, 1)):
-        put_rows(
-            ref, first,
-            [
-                outward_ref[2 * way], outward_ref[2 * way + 1],
-                sums[2 * way], sums[2 * way + 1],
-                get_rows(from_prev_ref, first, rows, tail, 4 + way),
-                get_rows(from_next_ref, first, rows, tail, 4 + way),
-            ],
-        )
+    put_rows(
+        dom_next_ref, 0,
+        [outward_ref[2], outward_ref[3], sums[2], sums[3], got(prev_ref, 4), got(next_ref, 4)],
+    )
+
+
+def relay_kernel(first, tail, sum_ref, dom_ref, prev_ref, next_ref):
+    rows = sum_ref.shape[1]
+
+    def got(place):
+        return get_rows(dom_ref, first, rows, tail, FROM_DOM, place)
+
+    put_rows(prev_ref, 0, [got(4), got(0)])
+    put_rows(next_ref, 0, [got(5), got(1)])
 
 
 def pair_kernel(first_pair, last_pair, older_count, *refs):
     sum_ref, outward_ref, blk_prev_ref, blk_next_ref, dom_prev_ref, dom_next_ref = refs[:6]
-    high_ref, low_ref = refs[6:8]
-    refs = refs[8:]
+    turn_prev_ref, turn_next_ref, high_ref, low_ref = refs[6:10]
+    refs = refs[10:]
     rows = sum_ref.shape[1]
     width = sum_ref.shape[2]
     first = 0
     if first_pair:
         tall = padded(width)
         first = 3 * tall
+        dom_blocks_ref = refs[0]
+        refs = refs[1:]
     else:
         in_high_ref, in_low_ref = refs[:2]
         refs = refs[2:]
@@ -495,10 +510,10 @@
     if last_pair:
         gram_in_ref, gram_ref, odd_ref, even_ref = refs
     else:
-        odd_ref, even_ref, local_out_ref, outward_out_ref, prev_ref, next_ref = refs[:6]
+        odd_ref, even_ref, local_out_ref, outward_out_ref, prev_ref, next_ref, dom_out_ref = refs[:7]
     if first_pair:
-        in_high_ref, in_low_ref = refs[6:]
-        for way, ref in enumerate((dom_prev_ref, dom_next_ref, blk_prev_ref, blk_next_ref)):
+        in_high_ref, in_low_ref = refs[7:]
+        for way, ref in enumerate((dom_blocks_ref, dom_next_ref, blk_prev_ref, blk_next_ref)):
             for place in range(2):
                 main = ref[tall * place : tall * place + width, :]
                 tail = tail_at(ref[2 * tall : 2 * tall + width, :], width - 128, place)
@@ -506,22 +521,34 @@
                 in_high_ref[2 * way + place] = high
                 in_low_ref[2 * way + place] = low
 
-    def got(ref, place):
-        return get_rows(ref, first, rows, width - 128, place)
+    tail = width - 128
+
+    def from_blk(ref, place):
+        return get_rows(ref, first, rows, tail, FROM_BLK, place)
+
+    def from_dom_prev(place):
+        return get_rows(dom_prev_ref, 0, rows, tail, FROM_DOM, place)
+
+    def from_dom_next(place):
+        return get_rows(dom_next_ref, first, rows, tail, FROM_DOM, place)
+
+    def turned(ref, place):
+        return get_rows(ref, 0, rows, tail, RELAYED, place)
 
     odd = [
-        sum_ref[cell] + got(dom_prev_ref if cell < 2 else dom_next_ref, cell % 2)
+        sum_ref[cell] + (from_dom_prev if cell < 2 else from_dom_next)(cell % 2)
         for cell in range(CELLS)
     ]
-    ring = []
-    for way, ref in enumerate((dom_prev_ref, dom_next_ref)):
-        for place in range(2):
-            ring.append(got(ref, 2 + place) + outward_ref[2 * way + place])
-    for way, ref in enumerate((blk_prev_ref, blk_next_ref)):
-        for place, corner_ref in enumerate((dom_prev_ref, dom_next_ref)):
-            ring.append(
-                got(ref, 2 + place) + outward_ref[4 + 2 * way + place] + got(corner_ref, 4 + way)
-            )
+    ring = [
+        from_dom_prev(2) + outward_ref[0],
+        from_dom_prev(3) + outward_ref[1],
+        from_dom_next(2) + outward_ref[2] + turned(turn_prev_ref, 0),
+        from_dom_next(3) + outward_ref[3] + turned(turn_next_ref, 0),
+        from_blk(blk_prev_ref, 2) + outward_ref[4] + from_dom_prev(4),
+        from_blk(blk_prev_ref, 3) + outward_ref[5] + turned(turn_prev_ref, 1),
+        from_blk(blk_next_ref, 2) + outward_ref[6] + from_dom_prev(5),
+        from_blk(blk_next_ref, 3) + outward_ref[7] + turned(turn_next_ref, 1),
+    ]
     for cell in range(CELLS):
         odd_ref[cell] = odd[cell]
     even = local_products([stack_halves(value) for value in odd], high_ref, low_ref)
@@ -549,6 +576,7 @@
         for entry in range(8):
             outward_out_ref[entry] = outward[entry]
         send_along_blk(local, outward, prev_ref, next_ref, 0)
+        send_to_dom_prev(local, outward, dom_out_ref, 0)
 
 
 def gram_kernel(newest, *refs):
@@ -721,8 +749,10 @@
     tall = padded(width)
     field = struct(CELLS, nrhs, width)
     ring = struct(8, nrhs, width)
-    edge = struct(8 * nrhs, 128)
-    edge_blocks = struct(3 * tall + 8 * nrhs, 128)
+    blk_edge = struct(7 * nrhs, 128)
+    dom_edge = struct(8 * nrhs, 128)
+    turn_edge = struct(3 * nrhs, 128)
+    with_blocks = lambda edge: struct(3 * tall + edge.shape[0], 128)
     cost = lambda flops, data: pl.CostEstimate(
         flops=flops, bytes_accessed=data, transcendentals=0
     )
@@ -734,8 +764,8 @@
         out_shape=(
             struct(BLOCKS, *block, kind=BF16), struct(BLOCKS, *block, kind=BF16),
             struct(CELLS, *block, kind=BF16), struct(CELLS, *block, kind=BF16),
-            field, field, ring, edge_blocks, edge_blocks,
-            struct(3 * tall, 128), struct(3 * tall, 128),
+            field, field, ring, with_blocks(blk_edge), with_blocks(blk_edge),
+            with_blocks(dom_edge), struct(3 * tall, 128),
             struct(CELLS, kind=jnp.int32),
         ),
         in_specs=smem(2) + vmem(1) + [pl.BlockSpec(memory_space=pl.ANY)] * 2,
@@ -759,7 +789,7 @@
     )
     high, low, inv_high, inv_low, base, local, outward = outs[:7]
     blk_sends = outs[7:9]
-    dom_blocks = outs[9:11]
+    dom_send, dom_blocks = outs[9:11]
     slots = outs[11]
     bases = [base]
     gram = None
@@ -767,18 +797,29 @@
     for pair in range(ITERS // 2):
         first_pair = pair == 0
         last_pair = pair == ITERS // 2 - 1
+        first = 3 * tall if first_pair else 0
         from_blk = both_ways(*blk_sends, "blk")
-        given = [local, outward, *from_blk] + (list(dom_blocks) if first_pair else [])
-        kind = edge_blocks if first_pair else edge
-        sums, *dom_sends = pl.pallas_call(
-            functools.partial(middle_kernel, first_pair),
-            out_shape=(field, kind, kind),
-            in_specs=vmem(len(given)),
-            out_specs=tuple(vmem(3)),
+        from_dom_next = rotated(dom_send, "dom", -1)
+        if first_pair:
+            inward = (rotated(dom_blocks, "dom", 1),)
+        sums, dom_send = pl.pallas_call(
+            functools.partial(middle_kernel, first),
+            out_shape=(field, dom_edge),
+            in_specs=vmem(4),
+            out_specs=tuple(vmem(2)),
             compiler_params=PARAMS,
             name=f"middle_part_{pair}",
-        )(*given)
-        from_dom = both_ways(*dom_sends, "dom")
+        )(local, outward, *from_blk)
+        from_dom_prev = rotated(dom_send, "dom", 1)
+        turns = pl.pallas_call(
+            functools.partial(relay_kernel, first, width - 128),
+            out_shape=(turn_edge, turn_edge),
+            in_specs=vmem(2),
+            out_specs=tuple(vmem(2)),
+            compiler_params=PARAMS,
+            name=f"relay_part_{pair}",
+        )(sums, from_dom_next)
+        turns = both_ways(*turns, "blk")
         newest = len(bases) - 1
         given = bases + ([gram] if newest > 0 else [])
         gram = pl.pallas_call(
@@ -791,12 +832,15 @@
             name=f"gram_part_{pair}",
         )(*given)
         older = bases if last_pair else []
-        given = [sums, outward, *from_blk, *from_dom, high, low, *inward, *older]
+        given = [
+            sums, outward, *from_blk, from_dom_prev, from_dom_next, *turns, high, low,
+            *inward, *older,
+        ]
         if last_pair:
             given.append(gram)
             shapes = (struct(near_size() * lax.axis_size("blk"), nrhs // 2, 128), field, field)
         else:
-            shapes = (field, field, field, ring, edge, edge)
+            shapes = (field, field, field, ring, blk_edge, blk_edge, dom_edge)
         if first_pair:
             shapes += (struct(8, *block, kind=BF16), struct(8, *block, kind=BF16))
         outs = pl.pallas_call(
@@ -815,8 +859,9 @@
             bases += outs[:2]
             local, outward = outs[2:4]
             blk_sends = outs[4:6]
+            dom_send = outs[6]
         if first_pair:
-            inward = outs[6:]
+            inward = outs[7:]
     gram = sum_devices(gram)
     given = [gram] + bases + [inv_high, inv_low, slots]
     adjoint, rel, fine = pl.pallas_call(

time: 135 us -> 132 us (0.978)
  waiting for transfers between devices: 30.8 us -> 25.1 us
  starting transfers between devices: 67.7 us -> 71.3 us
    ppermute x16 -> x25, starting transfers between devices: 56.7 us -> 63.2 us  [rotated(): lax.ppermute(value, axis, [(source, (source + steps) % count) for source...]
    ppermute x16 -> x25, waiting for transfers between devices: 19.2 us -> 13.5 us  [rotated(): lax.ppermute(value, axis, [(source, (source + steps) % count) for source...]
    all_to_all x1, starting transfers between devices: 11 us -> 8.09 us  [sum_devices(): return lax.all_to_all(copies, 'dom', 0, 0, axis_index_groups=far)]
  transfers between devices with their start and end apart: 17 -> 26, of which waited for: 14 -> 13; matrix products, arithmetic and copies ran while one was open for 0% -> 0% of each run, Pallas kernels for 0% -> 1%
where the time goes in v5:
time: 132 us; the launch traced here: 131 us
  starting transfers between devices  71.3 us (54%)
  waiting for transfers between devices  25.1 us (19%)
  Pallas kernels  17.8 us (13%)
  blocking collectives  14.8 us (11%)
  between operations  1.81 us (1%)
    ppermute x25, starting transfers between devices, rotated(): lax.ppermute(value, axis, [(source, (source + steps) % count) for source...  63.2 us
    all_to_all x1, blocking collectives, sum_devices(): parts = lax.all_to_all(copies, ('dom', 'blk'), 0, 0, axis_index_groups=near)  14.8 us
    ppermute x25, waiting for transfers between devices, rotated(): lax.ppermute(value, axis, [(source, (source + steps) % count) for source...  13.5 us
    all_to_all x1, waiting for transfers between devices, sum_devices(): return lax.all_to_all(copies, 'dom', 0, 0, axis_index_groups=far)  11.6 us
    pallas_call x1, Pallas kernels, shards(): pl.pallas_call(functools.partial(setup_kernel, dom_count=lax.axis_size('d...  8.49 us
    all_to_all x1, starting transfers between devices, sum_devices(): return lax.all_to_all(copies, 'dom', 0, 0, axis_index_groups=far)  8.09 us
    pallas_call x4, Pallas kernels, shards(): pl.pallas_call(functools.partial(pair_kernel, first_pair, last_pair, len(...  5.24 us
  transfers between devices with their start and end apart: 26, of which 13 were waited for; matrix products, arithmetic and copies ran while one was open for 0% of the time, Pallas kernels for 1%

profile of v5, /device:TPU:1, one launch (start us, length us, event | category | flops | bytes accessed | tf_op | source)
XLA Modules:
  0.0 131.1 jit_solution(10662865945581649344)
XLA Ops:
  0.6 8.5 %setup_blocks.1 = (bf16[20,162,162]{2,1,0:T(8,128)(2,1)S(1)}, bf16[20,162,162]{2,1,0:T(8,128)(2,1)S(1)}, bf16[4,162,162]{2,1,0:T(8,128)(2,1)S(1)}, bf16[4,162,16...) custom-call(s32[4,6]{1,0:T(4,128)} %nbr_ref.1, ...), custom_call_target="tpu_custom_call" | custom-call | tf_op jit(solution)/shard_map/setup_blocks/pallas_call | solution.py:760
  9.1 2.7 %collective-permute-start.36 = (f32[616,128]{1,0:T(8,128)S(1)}, f32[616,128]{1,0:T(8,128)S(1)}, u32[]{:S(2)}, u32[]{:S(2)}) collective-permute-start(f32[616,128]{1,0:T(8,128)S(1)} %get-tuple-element.89), channel_id=1, source_target_pairs={{0,1},{1,2},{2,3},{3,4},{4,5},{5,6},{6,7},{7,0},{8,9},{9,10},{10,1... | collective-permute-start | bytes 946184 | tf_op jit(solution)/shard_map/ppermute | solution.py:737
  11.8 4.3 %collective-permute-start.37 = (f32[616,128]{1,0:T(8,128)S(1)}, f32[616,128]{1,0:T(8,128)S(1)}, u32[]{:S(2)}, u32[]{:S(2)}) collective-permute-start(f32[616,128]{1,0:T(8,128)S(1)} %get-tuple-element.90), channel_id=1, source_target_pairs={{0,7},{1,0},{2,1},{3,2},{4,3},{5,4},{6,5},{7,6},{8,15},{9,8},{10,9... | collective-permute-start | bytes 946184 | tf_op jit(solution)/shard_map/ppermute | solution.py:737
  16.1 9.0 %collective-permute-start.39 = (f32[632,128]{1,0:T(8,128)S(1)}, f32[632,128]{1,0:T(8,128)S(1)}, u32[]{:S(2)}, u32[]{:S(2)}) collective-permute-start(f32[632,128]{1,0:T(8,128)S(1)} %get-tuple-element.93), channel_id=1, source_target_pairs={{0,504},{8,0},{16,8},{24,16},{32,24},{40,32},{48,40},{56,48},{64,5... | collective-permute-start | bytes 970760 | tf_op jit(solution)/shard_map/ppermute | solution.py:737
  25.1 1.9 %collective-permute-start.42 = (f32[504,128]{1,0:T(8,128)S(1)}, f32[504,128]{1,0:T(8,128)S(1)}, u32[]{:S(2)}, u32[]{:S(2)}) collective-permute-start(f32[504,128]{1,0:T(8,128)S(1)} %get-tuple-element.98), channel_id=1, source_target_pairs={{0,8},{8,16},{16,24},{24,32},{32,40},{40,48},{48,56},{56,64},{64,7... | collective-permute-start | bytes 774152 | tf_op jit(solution)/shard_map/ppermute | solution.py:737
  27.0 0.0 collective-permute-done.36.prev_ref.refs_2_
  27.0 0.0 collective-permute-done.37.next_ref.refs_3_
  27.0 0.1 middle_part_0.1
  27.2 1.9 %collective-permute-start.38 = (f32[128,128]{1,0:T(8,128)S(1)}, f32[128,128]{1,0:T(8,128)S(1)}, u32[]{:S(2)}, u32[]{:S(2)}) collective-permute-start(f32[128,128]{1,0:T(8,128)S(1)} %get-tuple-element.92), channel_id=1, source_target_pairs={{0,8},{8,16},{16,24},{24,32},{32,40},{40,48},{48,56},{56,64},{64,7... | collective-permute-start | bytes 196616 | tf_op jit(solution)/shard_map/ppermute | solution.py:737
  29.1 1.1 collective-permute-done.39.dom_ref.refs_5_
  30.2 0.1 relay_part_0.1
  30.3 3.9 %collective-permute-start.40 = (f32[48,128]{1,0:T(8,128)S(1)}, f32[48,128]{1,0:T(8,128)S(1)}, u32[]{:S(2)}, u32[]{:S(2)}) collective-permute-start(f32[48,128]{1,0:T(8,128)S(1)} %get-tuple-element.94), channel_id=1, source_target_pairs={{0,1},{1,2},{2,3},{3,4},{4,5},{5,6},{6,7},{7,0},{8,9},{9,10},{10,1... | collective-permute-start | bytes 73736 | tf_op jit(solution)/shard_map/ppermute | solution.py:737
  34.2 1.7 %collective-permute-done.42.refs_10_ = f32[504,128]{1,0:T(8,128)S(1)} collective-permute-done((f32[504,128]{1,0:T(8,128)S(1)}, f32[504,128]{1,0:T(8,128)S(1)}, u32[]{:S(2)}, u32[]{:S(2)}) %collective-permute-start.42) | collective-permute-done | bytes 258080 | tf_op jit(solution)/shard_map/ppermute | solution.py:737
  35.9 1.8 %collective-permute-done.41.refs_7_ = f32[48,128]{1,0:T(8,128)S(1)} collective-permute-done((f32[48,128]{1,0:T(8,128)S(1)}, f32[48,128]{1,0:T(8,128)S(1)}, u32[]{:S(2)}, u32[]{:S(2)}) %collective-permute-start.41) | collective-permute-done | bytes 24608 | tf_op jit(solution)/shard_map/ppermute | solution.py:737
  37.8 1.3 %pair_part_0.1 = (f32[4,16,162]{2,1,0:T(8,128)S(1)}, f32[4,16,162]{2,1,0:T(8,128)S(1)}, f32[4,16,162]{2,1,0:T(8,128)S(1)}, f32[8,16,162]{2,1,0:T(8,128)S(1)}, f3...) custom-call(f32[4,16,162]{2,1,0:T(8,128)S(1)} %get-tuple-element.91., ...), custom_call_target="tpu_custom_call" | custom-call | flops 100776960 | bytes 6000000 | tf_op jit(solution)/shard_map/pair_part_0/pallas_call | solution.py:846
  39.1 3.8 %collective-permute-start.43 = (f32[112,128]{1,0:T(8,128)S(1)}, f32[112,128]{1,0:T(8,128)S(1)}, u32[]{:S(2)}, u32[]{:S(2)}) collective-permute-start(f32[112,128]{1,0:T(8,128)S(1)} %get-tuple-element.101), channel_id=1, source_target_pairs={{0,1},{1,2},{2,3},{3,4},{4,5},{5,6},{6,7},{7,0},{8,9},{9,10},{10,1... | collective-permute-start | bytes 172040 | tf_op jit(solution)/shard_map/ppermute | solution.py:737
  42.9 3.9 %collective-permute-start.46 = (f32[128,128]{1,0:T(8,128)S(1)}, f32[128,128]{1,0:T(8,128)S(1)}, u32[]{:S(2)}, u32[]{:S(2)}) collective-permute-start(f32[128,128]{1,0:T(8,128)S(1)} %get-tuple-element.105), channel_id=1, source_target_pairs={{0,504},{8,0},{16,8},{24,16},{32,24},{40,32},{48,40},{56,48},{64,5... | collective-permute-start | bytes 196616 | tf_op jit(solution)/shard_map/ppermute | solution.py:737
  46.8 0.1 middle_part_1.1
  46.9 1.9 %collective-permute-start.45 = (f32[128,128]{1,0:T(8,128)S(1)}, f32[128,128]{1,0:T(8,128)S(1)}, u32[]{:S(2)}, u32[]{:S(2)}) collective-permute-start(f32[128,128]{1,0:T(8,128)S(1)} %get-tuple-element.104), channel_id=1, source_target_pairs={{0,8},{8,16},{16,24},{24,32},{32,40},{40,48},{48,56},{56,64},{64,7... | collective-permute-start | bytes 196616 | tf_op jit(solution)/shard_map/ppermute | solution.py:737
  48.9 0.1 relay_part_1.1
  49.0 1.9 %collective-permute-start.47 = (f32[48,128]{1,0:T(8,128)S(1)}, f32[48,128]{1,0:T(8,128)S(1)}, u32[]{:S(2)}, u32[]{:S(2)}) collective-permute-start(f32[48,128]{1,0:T(8,128)S(1)} %get-tuple-element.106), channel_id=1, source_target_pairs={{0,1},{1,2},{2,3},{3,4},{4,5},{5,6},{6,7},{7,0},{8,9},{9,10},{10,1... | collective-permute-start | bytes 73736 | tf_op jit(solution)/shard_map/ppermute | solution.py:737
  50.9 0.9 collective-permute-start.48
  51.8 0.7 collective-permute-done.47.refs_6_
  52.5 1.7 %collective-permute-done.48.refs_7_ = f32[48,128]{1,0:T(8,128)S(1)} collective-permute-done((f32[48,128]{1,0:T(8,128)S(1)}, f32[48,128]{1,0:T(8,128)S(1)}, u32[]{:S(2)}, u32[]{:S(2)}) %collective-permute-start.48) | collective-permute-done | bytes 24608 | tf_op jit(solution)/shard_map/ppermute | solution.py:737
  54.2 1.1 collective-permute-done.45.refs_4_
  55.3 1.3 pair_part_1.1
  56.5 2.7 %collective-permute-start.49 = (f32[112,128]{1,0:T(8,128)S(1)}, f32[112,128]{1,0:T(8,128)S(1)}, u32[]{:S(2)}, u32[]{:S(2)}) collective-permute-start(f32[112,128]{1,0:T(8,128)S(1)} %get-tuple-element.112), channel_id=1, source_target_pairs={{0,1},{1,2},{2,3},{3,4},{4,5},{5,6},{6,7},{7,0},{8,9},{9,10},{10,1... | collective-permute-start | bytes 172040 | tf_op jit(solution)/shard_map/ppermute | solution.py:737
  59.2 1.2 collective-permute-start.50
  60.5 4.2 %collective-permute-start.52 = (f32[128,128]{1,0:T(8,128)S(1)}, f32[128,128]{1,0:T(8,128)S(1)}, u32[]{:S(2)}, u32[]{:S(2)}) collective-permute-start(f32[128,128]{1,0:T(8,128)S(1)} %get-tuple-element.116), channel_id=1, source_target_pairs={{0,504},{8,0},{16,8},{24,16},{32,24},{40,32},{48,40},{56,48},{64,5... | collective-permute-start | bytes 196616 | tf_op jit(solution)/shard_map/ppermute | solution.py:737
  64.7 0.1 middle_part_2.1
  64.8 1.9 %collective-permute-start.51 = (f32[128,128]{1,0:T(8,128)S(1)}, f32[128,128]{1,0:T(8,128)S(1)}, u32[]{:S(2)}, u32[]{:S(2)}) collective-permute-start(f32[128,128]{1,0:T(8,128)S(1)} %get-tuple-element.115), channel_id=1, source_target_pairs={{0,8},{8,16},{16,24},{24,32},{32,40},{40,48},{48,56},{56,64},{64,7... | collective-permute-start | bytes 196616 | tf_op jit(solution)/shard_map/ppermute | solution.py:737
  66.8 0.1 relay_part_2.1
  66.9 0.4 collective-permute-start.53
  67.3 2.9 %collective-permute-start.54 = (f32[48,128]{1,0:T(8,128)S(1)}, f32[48,128]{1,0:T(8,128)S(1)}, u32[]{:S(2)}, u32[]{:S(2)}) collective-permute-start(f32[48,128]{1,0:T(8,128)S(1)} %get-tuple-element.118), channel_id=1, source_target_pairs={{0,7},{1,0},{2,1},{3,2},{4,3},{5,4},{6,5},{7,6},{8,15},{9,8},{10,9... | collective-permute-start | bytes 73736 | tf_op jit(solution)/shard_map/ppermute | solution.py:737
  70.1 0.7 collective-permute-done.53.refs_6_
  70.8 0.2 collective-permute-done.54.refs_7_
  71.0 2.2 %collective-permute-done.51.refs_4_ = f32[128,128]{1,0:T(8,128)S(1)} collective-permute-done((f32[128,128]{1,0:T(8,128)S(1)}, f32[128,128]{1,0:T(8,128)S(1)}, u32[]{:S(2)}, u32[]{:S(2)}) %collective-permute-start.51) | collective-permute-done | bytes 65568 | tf_op jit(solution)/shard_map/ppermute | solution.py:737
  73.2 1.3 pair_part_2.1
  74.5 0.7 collective-permute-start.55
  75.2 3.7 %collective-permute-start.56 = (f32[112,128]{1,0:T(8,128)S(1)}, f32[112,128]{1,0:T(8,128)S(1)}, u32[]{:S(2)}, u32[]{:S(2)}) collective-permute-start(f32[112,128]{1,0:T(8,128)S(1)} %get-tuple-element.122), channel_id=1, source_target_pairs={{0,7},{1,0},{2,1},{3,2},{4,3},{5,4},{6,5},{7,6},{8,15},{9,8},{10,9... | collective-permute-start | bytes 172040 | tf_op jit(solution)/shard_map/ppermute | solution.py:737
  78.9 4.2 %collective-permute-start.58 = (f32[128,128]{1,0:T(8,128)S(1)}, f32[128,128]{1,0:T(8,128)S(1)}, u32[]{:S(2)}, u32[]{:S(2)}) collective-permute-start(f32[128,128]{1,0:T(8,128)S(1)} %get-tuple-element.125), channel_id=1, source_target_pairs={{0,504},{8,0},{16,8},{24,16},{32,24},{40,32},{48,40},{56,48},{64,5... | collective-permute-start | bytes 196616 | tf_op jit(solution)/shard_map/ppermute | solution.py:737
  83.0 0.1 middle_part_3.1
  83.2 2.1 %collective-permute-start.57 = (f32[128,128]{1,0:T(8,128)S(1)}, f32[128,128]{1,0:T(8,128)S(1)}, u32[]{:S(2)}, u32[]{:S(2)}) collective-permute-start(f32[128,128]{1,0:T(8,128)S(1)} %get-tuple-element.124), channel_id=1, source_target_pairs={{0,8},{8,16},{16,24},{24,32},{32,40},{40,48},{48,56},{56,64},{64,7... | collective-permute-start | bytes 196616 | tf_op jit(solution)/shard_map/ppermute | solution.py:737
  85.3 0.1 relay_part_3.1
  85.4 3.2 %collective-permute-start.60 = (f32[48,128]{1,0:T(8,128)S(1)}, f32[48,128]{1,0:T(8,128)S(1)}, u32[]{:S(2)}, u32[]{:S(2)}) collective-permute-start(f32[48,128]{1,0:T(8,128)S(1)} %get-tuple-element.127), channel_id=1, source_target_pairs={{0,7},{1,0},{2,1},{3,2},{4,3},{5,4},{6,5},{7,6},{8,15},{9,8},{10,9... | collective-permute-start | bytes 73736 | tf_op jit(solution)/shard_map/ppermute | solution.py:737
  88.7 0.1 gram_part_0.1.refs_3_
  88.8 0.1 gram_part_1.1.refs_5_
  88.9 0.1 gram_part_2.1.refs_7_
  89.0 0.0 copy-start.1
  89.0 0.0 copy-start.2
  89.0 0.0 copy-start.4
  89.0 0.0 copy-start.5
  89.0 0.0 copy-start.6
  89.1 0.1 gram_part_3.1.refs_19_
  89.2 0.2 collective-permute-done.59.refs_6_
  89.4 0.2 collective-permute-done.60.refs_7_
  89.5 2.0 %collective-permute-done.57.refs_4_ = f32[128,128]{1,0:T(8,128)S(1)} collective-permute-done((f32[128,128]{1,0:T(8,128)S(1)}, f32[128,128]{1,0:T(8,128)S(1)}, u32[]{:S(2)}, u32[]{:S(2)}) %collective-permute-start.57) | collective-permute-done | bytes 65568 | tf_op jit(solution)/shard_map/ppermute | solution.py:737
  91.5 1.3 %pair_part_3.1 = (f32[32,8,128]{2,1,0:T(8,128)S(1)}, f32[4,16,162]{2,1,0:T(8,128)S(1)}, f32[4,16,162]{2,1,0:T(8,128)}) custom-call(f32[4,16,162]{2,1,0:T(8,128)S(1)} %get-tuple-element.123.sum_ref.refs_0_, f32[8,16,162]{2,1,0:T(8,128)S(1)} %get-tuple-element.120.outward_ref.refs_1_, f32[112,128]{1,0:T(8,128)S(1)} %collective-permute-done.55.prev_ref.refs_2_, ...), custom_call_target="tpu_custom_call" | custom-call | flops 100776960 | bytes 6000000 | tf_op jit(solution)/shard_map/pair_part_3/pallas_call | solution.py:846
  92.8 14.8 %all_to_all.10.parts_ref = f32[32,8,128]{2,1,0:T(8,128)S(1)} all-to-all(f32[32,8,128]{2,1,0:T(8,128)S(1)} %get-tuple-element.135), channel_id=1, replica_groups={{0,1,2,3,4,5,6,7,8,9,10,11,12,13,14,15,16,17,18,19,20,21,22,23,24,25,26..., dimensions={0} | all-to-all | bytes 262144 | tf_op jit(solution)/shard_map/all_to_all | solution.py:723
  107.6 0.7 sum_near.1
  108.3 8.1 %all-to-all-start.1 = ((f32[16,8,128]{2,1,0:T(8,128)}), f32[16,8,128]{2,1,0:T(8,128)S(1)}, u32[]{:S(2)}, u32[]{:S(2)}) async-start(f32[16,8,128]{2,1,0:T(8,128)} %sum_near.1), calls=%async_computation.1 | async-start | bytes 131072 | tf_op jit(solution)/shard_map/all_to_all | solution.py:732
  116.4 11.6 %all-to-all-done.1.refs_0_ = f32[16,8,128]{2,1,0:T(8,128)S(1)} async-done(((f32[16,8,128]{2,1,0:T(8,128)}), f32[16,8,128]{2,1,0:T(8,128)S(1)}, u32[]{:S(2)}, u32[]{:S(2)}) %all-to-all-start.1) | async-done | bytes 65568 | tf_op jit(solution)/shard_map/all_to_all | solution.py:732
  128.0 1.8 %finish_part.1 = (f32[16,4,162]{2,1,0:T(4,128)}, f32[1,16]{1,0:T(1,128)}, s32[1]{0:T(128)}) custom-call(f32[16,8,128]{2,1,0:T(8,128)S(1)} %all-to-all-done.1.refs_0_, f32[4,16,162]{2,1,0:T(8,128)S(1)} %get-tuple-element.128.refs_0_.refs_12_.refs_1_, f32[4,16,162]{2,1,0:T(8,128)S(1)} %get-tuple-element.129.refs_1_.refs_13_.refs_2_, ...), custom_call_target="tpu_custom_call" | custom-call | tf_op jit(solution)/shard_map/finish_part/pallas_call | solution.py:867
  130.6 0.3 conditional.1
  (19 shorter events, 0.0 us)
Async XLA Ops:
  9.1 17.9 %collective-permute-start.36 = (f32[616,128]{1,0:T(8,128)S(1)}, f32[616,128]{1,0:T(8,128)S(1)}, u32[]{:S(2)}, u32[]{:S(2)}) collective-permute-start(f32[616,128]{1,0:T(8,128)S(1)} %get-tuple-element.89), channel_id=1, source_target_pairs={{0,1},{1,2},{2,3},{3,4},{4,5},{5,6},{6,7},{7,0},{8,9},{9,10},{10,1... | collective-permute-start | bytes 946184 | tf_op jit(solution)/shard_map/ppermute | solution.py:737
  11.8 15.2 %collective-permute-start.37 = (f32[616,128]{1,0:T(8,128)S(1)}, f32[616,128]{1,0:T(8,128)S(1)}, u32[]{:S(2)}, u32[]{:S(2)}) collective-permute-start(f32[616,128]{1,0:T(8,128)S(1)} %get-tuple-element.90), channel_id=1, source_target_pairs={{0,7},{1,0},{2,1},{3,2},{4,3},{5,4},{6,5},{7,6},{8,15},{9,8},{10,9... | collective-permute-start | bytes 946184 | tf_op jit(solution)/shard_map/ppermute | solution.py:737
  16.1 14.1 %collective-permute-start.39 = (f32[632,128]{1,0:T(8,128)S(1)}, f32[632,128]{1,0:T(8,128)S(1)}, u32[]{:S(2)}, u32[]{:S(2)}) collective-permute-start(f32[632,128]{1,0:T(8,128)S(1)} %get-tuple-element.93), channel_id=1, source_target_pairs={{0,504},{8,0},{16,8},{24,16},{32,24},{40,32},{48,40},{56,48},{64,5... | collective-permute-start | bytes 970760 | tf_op jit(solution)/shard_map/ppermute | solution.py:737
  25.1 10.8 %collective-permute-start.42 = (f32[504,128]{1,0:T(8,128)S(1)}, f32[504,128]{1,0:T(8,128)S(1)}, u32[]{:S(2)}, u32[]{:S(2)}) collective-permute-start(f32[504,128]{1,0:T(8,128)S(1)} %get-tuple-element.98), channel_id=1, source_target_pairs={{0,8},{8,16},{16,24},{24,32},{32,40},{40,48},{48,56},{56,64},{64,7... | collective-permute-start | bytes 774152 | tf_op jit(solution)/shard_map/ppermute | solution.py:737
  27.2 10.6 %collective-permute-start.38 = (f32[128,128]{1,0:T(8,128)S(1)}, f32[128,128]{1,0:T(8,128)S(1)}, u32[]{:S(2)}, u32[]{:S(2)}) collective-permute-start(f32[128,128]{1,0:T(8,128)S(1)} %get-tuple-element.92), channel_id=1, source_target_pairs={{0,8},{8,16},{16,24},{24,32},{32,40},{40,48},{48,56},{56,64},{64,7... | collective-permute-start | bytes 196616 | tf_op jit(solution)/shard_map/ppermute | solution.py:737
  30.3 5.6 %collective-permute-start.40 = (f32[48,128]{1,0:T(8,128)S(1)}, f32[48,128]{1,0:T(8,128)S(1)}, u32[]{:S(2)}, u32[]{:S(2)}) collective-permute-start(f32[48,128]{1,0:T(8,128)S(1)} %get-tuple-element.94), channel_id=1, source_target_pairs={{0,1},{1,2},{2,3},{3,4},{4,5},{5,6},{6,7},{7,0},{8,9},{9,10},{10,1... | collective-permute-start | bytes 73736 | tf_op jit(solution)/shard_map/ppermute | solution.py:737
  34.2 3.5 %collective-permute-start.41 = (f32[48,128]{1,0:T(8,128)S(1)}, f32[48,128]{1,0:T(8,128)S(1)}, u32[]{:S(2)}, u32[]{:S(2)}) collective-permute-start(f32[48,128]{1,0:T(8,128)S(1)} %get-tuple-element.95), channel_id=1, source_target_pairs={{0,7},{1,0},{2,1},{3,2},{4,3},{5,4},{6,5},{7,6},{8,15},{9,8},{10,9... | collective-permute-start | bytes 73736 | tf_op jit(solution)/shard_map/ppermute | solution.py:737
  39.1 7.7 %collective-permute-start.43 = (f32[112,128]{1,0:T(8,128)S(1)}, f32[112,128]{1,0:T(8,128)S(1)}, u32[]{:S(2)}, u32[]{:S(2)}) collective-permute-start(f32[112,128]{1,0:T(8,128)S(1)} %get-tuple-element.101), channel_id=1, source_target_pairs={{0,1},{1,2},{2,3},{3,4},{4,5},{5,6},{6,7},{7,0},{8,9},{9,10},{10,1... | collective-permute-start | bytes 172040 | tf_op jit(solution)/shard_map/ppermute | solution.py:737
  42.9 3.9 %collective-permute-start.44 = (f32[112,128]{1,0:T(8,128)S(1)}, f32[112,128]{1,0:T(8,128)S(1)}, u32[]{:S(2)}, u32[]{:S(2)}) collective-permute-start(f32[112,128]{1,0:T(8,128)S(1)} %get-tuple-element.102), channel_id=1, source_target_pairs={{0,7},{1,0},{2,1},{3,2},{4,3},{5,4},{6,5},{7,6},{8,15},{9,8},{10,9... | collective-permute-start | bytes 172040 | tf_op jit(solution)/shard_map/ppermute | solution.py:737
  42.9 6.0 %collective-permute-start.46 = (f32[128,128]{1,0:T(8,128)S(1)}, f32[128,128]{1,0:T(8,128)S(1)}, u32[]{:S(2)}, u32[]{:S(2)}) collective-permute-start(f32[128,128]{1,0:T(8,128)S(1)} %get-tuple-element.105), channel_id=1, source_target_pairs={{0,504},{8,0},{16,8},{24,16},{32,24},{40,32},{48,40},{56,48},{64,5... | collective-permute-start | bytes 196616 | tf_op jit(solution)/shard_map/ppermute | solution.py:737
  46.9 8.3 %collective-permute-start.45 = (f32[128,128]{1,0:T(8,128)S(1)}, f32[128,128]{1,0:T(8,128)S(1)}, u32[]{:S(2)}, u32[]{:S(2)}) collective-permute-start(f32[128,128]{1,0:T(8,128)S(1)} %get-tuple-element.104), channel_id=1, source_target_pairs={{0,8},{8,16},{16,24},{24,32},{32,40},{40,48},{48,56},{56,64},{64,7... | collective-permute-start | bytes 196616 | tf_op jit(solution)/shard_map/ppermute | solution.py:737
  49.0 3.5 %collective-permute-start.47 = (f32[48,128]{1,0:T(8,128)S(1)}, f32[48,128]{1,0:T(8,128)S(1)}, u32[]{:S(2)}, u32[]{:S(2)}) collective-permute-start(f32[48,128]{1,0:T(8,128)S(1)} %get-tuple-element.106), channel_id=1, source_target_pairs={{0,1},{1,2},{2,3},{3,4},{4,5},{5,6},{6,7},{7,0},{8,9},{9,10},{10,1... | collective-permute-start | bytes 73736 | tf_op jit(solution)/shard_map/ppermute | solution.py:737
  50.9 3.3 %collective-permute-start.48 = (f32[48,128]{1,0:T(8,128)S(1)}, f32[48,128]{1,0:T(8,128)S(1)}, u32[]{:S(2)}, u32[]{:S(2)}) collective-permute-start(f32[48,128]{1,0:T(8,128)S(1)} %get-tuple-element.107), channel_id=1, source_target_pairs={{0,7},{1,0},{2,1},{3,2},{4,3},{5,4},{6,5},{7,6},{8,15},{9,8},{10,9... | collective-permute-start | bytes 73736 | tf_op jit(solution)/shard_map/ppermute | solution.py:737
  56.5 8.1 %collective-permute-start.49 = (f32[112,128]{1,0:T(8,128)S(1)}, f32[112,128]{1,0:T(8,128)S(1)}, u32[]{:S(2)}, u32[]{:S(2)}) collective-permute-start(f32[112,128]{1,0:T(8,128)S(1)} %get-tuple-element.112), channel_id=1, source_target_pairs={{0,1},{1,2},{2,3},{3,4},{4,5},{5,6},{6,7},{7,0},{8,9},{9,10},{10,1... | collective-permute-start | bytes 172040 | tf_op jit(solution)/shard_map/ppermute | solution.py:737
  59.2 5.4 %collective-permute-start.50 = (f32[112,128]{1,0:T(8,128)S(1)}, f32[112,128]{1,0:T(8,128)S(1)}, u32[]{:S(2)}, u32[]{:S(2)}) collective-permute-start(f32[112,128]{1,0:T(8,128)S(1)} %get-tuple-element.113), channel_id=1, source_target_pairs={{0,7},{1,0},{2,1},{3,2},{4,3},{5,4},{6,5},{7,6},{8,15},{9,8},{10,9... | collective-permute-start | bytes 172040 | tf_op jit(solution)/shard_map/ppermute | solution.py:737
  60.5 6.3 %collective-permute-start.52 = (f32[128,128]{1,0:T(8,128)S(1)}, f32[128,128]{1,0:T(8,128)S(1)}, u32[]{:S(2)}, u32[]{:S(2)}) collective-permute-start(f32[128,128]{1,0:T(8,128)S(1)} %get-tuple-element.116), channel_id=1, source_target_pairs={{0,504},{8,0},{16,8},{24,16},{32,24},{40,32},{48,40},{56,48},{64,5... | collective-permute-start | bytes 196616 | tf_op jit(solution)/shard_map/ppermute | solution.py:737
  64.8 8.3 %collective-permute-start.51 = (f32[128,128]{1,0:T(8,128)S(1)}, f32[128,128]{1,0:T(8,128)S(1)}, u32[]{:S(2)}, u32[]{:S(2)}) collective-permute-start(f32[128,128]{1,0:T(8,128)S(1)} %get-tuple-element.115), channel_id=1, source_target_pairs={{0,8},{8,16},{16,24},{24,32},{32,40},{40,48},{48,56},{56,64},{64,7... | collective-permute-start | bytes 196616 | tf_op jit(solution)/shard_map/ppermute | solution.py:737
  66.9 3.9 %collective-permute-start.53 = (f32[48,128]{1,0:T(8,128)S(1)}, f32[48,128]{1,0:T(8,128)S(1)}, u32[]{:S(2)}, u32[]{:S(2)}) collective-permute-start(f32[48,128]{1,0:T(8,128)S(1)} %get-tuple-element.117), channel_id=1, source_target_pairs={{0,1},{1,2},{2,3},{3,4},{4,5},{5,6},{6,7},{7,0},{8,9},{9,10},{10,1... | collective-permute-start | bytes 73736 | tf_op jit(solution)/shard_map/ppermute | solution.py:737
  67.3 3.7 %collective-permute-start.54 = (f32[48,128]{1,0:T(8,128)S(1)}, f32[48,128]{1,0:T(8,128)S(1)}, u32[]{:S(2)}, u32[]{:S(2)}) collective-permute-start(f32[48,128]{1,0:T(8,128)S(1)} %get-tuple-element.118), channel_id=1, source_target_pairs={{0,7},{1,0},{2,1},{3,2},{4,3},{5,4},{6,5},{7,6},{8,15},{9,8},{10,9... | collective-permute-start | bytes 73736 | tf_op jit(solution)/shard_map/ppermute | solution.py:737
  74.5 8.6 %collective-permute-start.55 = (f32[112,128]{1,0:T(8,128)S(1)}, f32[112,128]{1,0:T(8,128)S(1)}, u32[]{:S(2)}, u32[]{:S(2)}) collective-permute-start(f32[112,128]{1,0:T(8,128)S(1)} %get-tuple-element.121), channel_id=1, source_target_pairs={{0,1},{1,2},{2,3},{3,4},{4,5},{5,6},{6,7},{7,0},{8,9},{9,10},{10,1... | collective-permute-start | bytes 172040 | tf_op jit(solution)/shard_map/ppermute | solution.py:737
  75.2 7.9 %collective-permute-start.56 = (f32[112,128]{1,0:T(8,128)S(1)}, f32[112,128]{1,0:T(8,128)S(1)}, u32[]{:S(2)}, u32[]{:S(2)}) collective-permute-start(f32[112,128]{1,0:T(8,128)S(1)} %get-tuple-element.122), channel_id=1, source_target_pairs={{0,7},{1,0},{2,1},{3,2},{4,3},{5,4},{6,5},{7,6},{8,15},{9,8},{10,9... | collective-permute-start | bytes 172040 | tf_op jit(solution)/shard_map/ppermute | solution.py:737
  78.9 6.4 %collective-permute-start.58 = (f32[128,128]{1,0:T(8,128)S(1)}, f32[128,128]{1,0:T(8,128)S(1)}, u32[]{:S(2)}, u32[]{:S(2)}) collective-permute-start(f32[128,128]{1,0:T(8,128)S(1)} %get-tuple-element.125), channel_id=1, source_target_pairs={{0,504},{8,0},{16,8},{24,16},{32,24},{40,32},{48,40},{56,48},{64,5... | collective-permute-start | bytes 196616 | tf_op jit(solution)/shard_map/ppermute | solution.py:737
  83.2 8.3 %collective-permute-start.57 = (f32[128,128]{1,0:T(8,128)S(1)}, f32[128,128]{1,0:T(8,128)S(1)}, u32[]{:S(2)}, u32[]{:S(2)}) collective-permute-start(f32[128,128]{1,0:T(8,128)S(1)} %get-tuple-element.124), channel_id=1, source_target_pairs={{0,8},{8,16},{16,24},{24,32},{32,40},{40,48},{48,56},{56,64},{64,7... | collective-permute-start | bytes 196616 | tf_op jit(solution)/shard_map/ppermute | solution.py:737
  85.4 3.9 %collective-permute-start.59 = (f32[48,128]{1,0:T(8,128)S(1)}, f32[48,128]{1,0:T(8,128)S(1)}, u32[]{:S(2)}, u32[]{:S(2)}) collective-permute-start(f32[48,128]{1,0:T(8,128)S(1)} %get-tuple-element.126), channel_id=1, source_target_pairs={{0,1},{1,2},{2,3},{3,4},{4,5},{5,6},{6,7},{7,0},{8,9},{9,10},{10,1... | collective-permute-start | bytes 73736 | tf_op jit(solution)/shard_map/ppermute | solution.py:737
  85.4 4.1 %collective-permute-start.60 = (f32[48,128]{1,0:T(8,128)S(1)}, f32[48,128]{1,0:T(8,128)S(1)}, u32[]{:S(2)}, u32[]{:S(2)}) collective-permute-start(f32[48,128]{1,0:T(8,128)S(1)} %get-tuple-element.127), channel_id=1, source_target_pairs={{0,7},{1,0},{2,1},{3,2},{4,3},{5,4},{6,5},{7,6},{8,15},{9,8},{10,9... | collective-permute-start | bytes 73736 | tf_op jit(solution)/shard_map/ppermute | solution.py:737
  89.0 41.5 %copy-start.1 = (f32[16,4,162]{2,1,0:T(4,128)S(1)}, f32[16,4,162]{2,1,0:T(4,128)}, u32[]{:S(2)}) copy-start(f32[16,4,162]{2,1,0:T(4,128)} %src_ref.1) | copy-start | bytes 124420
  89.0 41.5 %copy-start.2 = (f32[4,162,162]{2,0,1:T(4,128)S(1)}, f32[4,162,162]{2,0,1:T(4,128)}, u32[]{:S(2)}) copy-start(f32[4,162,162]{2,0,1:T(4,128)} %param.14) | copy-start | bytes 1259716
  89.0 41.5 %copy-start.4 = (s32[4,6]{1,0:T(4,128)S(1)}, s32[4,6]{1,0:T(4,128)}, u32[]{:S(2)}) copy-start(s32[4,6]{1,0:T(4,128)} %nbr_ref.1) | copy-start | bytes 292
  89.0 41.5 %copy-start.5 = (s32[4,6]{1,0:T(4,128)S(1)}, s32[4,6]{1,0:T(4,128)}, u32[]{:S(2)}) copy-start(s32[4,6]{1,0:T(4,128)} %flag_ref.1) | copy-start | bytes 292
  89.0 41.5 %copy-start.6 = (s32[4,6]{1,0:T(4,128)S(1)}, s32[4,6]{1,0:T(4,128)}, u32[]{:S(2)}) copy-start(s32[4,6]{1,0:T(4,128)} %param.17) | copy-start | bytes 292
  108.3 19.7 %all-to-all-start.1 = ((f32[16,8,128]{2,1,0:T(8,128)}), f32[16,8,128]{2,1,0:T(8,128)S(1)}, u32[]{:S(2)}, u32[]{:S(2)}) async-start(f32[16,8,128]{2,1,0:T(8,128)} %sum_near.1), calls=%async_computation.1 | async-start | bytes 131072 | tf_op jit(solution)/shard_map/all_to_all | solution.py:732

commit v6 on v5

--- a/solution.py
+++ b/solution.py
@@ -339,9 +339,6 @@
     for slot in range(CELLS):
         for face in range(6):
             pl.when(flag_ref[slot, face] == 1)(face_copies[slot][face].start)
-    for slot in range(CELLS):
-        for face in range(6):
-            pl.when(nbr_ref[slot, face] >= 0)(face_copies[slot][face].start)
     dom_here = lax.axis_index("dom")
     blk_here = lax.axis_index("blk")
     here = dom_here * blk_count + blk_here
@@ -394,6 +391,9 @@
     for slot in range(CELLS):
         base_ref[cell_ref[slot]] = src_ref[:, slot, :]
         diag_copies[slot].wait()
+    for slot in range(CELLS):
+        for face in range(6):
+            pl.when(nbr_ref[slot, face] >= 0)(face_copies[slot][face].start)
     for slot in range(CELLS):
         for face in range(6):
 
@@ -490,38 +490,27 @@
     put_rows(next_ref, 0, [got(5), got(1)])
 
 
-def pair_kernel(first_pair, last_pair, older_count, *refs):
+def odd_kernel(first_pair, *refs):
     sum_ref, outward_ref, blk_prev_ref, blk_next_ref, dom_prev_ref, dom_next_ref = refs[:6]
-    turn_prev_ref, turn_next_ref, high_ref, low_ref = refs[6:10]
-    refs = refs[10:]
+    high_ref, low_ref = refs[6:8]
     rows = sum_ref.shape[1]
     width = sum_ref.shape[2]
+    tail = width - 128
     first = 0
     if first_pair:
         tall = padded(width)
         first = 3 * tall
-        dom_blocks_ref = refs[0]
-        refs = refs[1:]
-    else:
-        in_high_ref, in_low_ref = refs[:2]
-        refs = refs[2:]
-    older = refs[:older_count]
-    refs = refs[older_count:]
-    if last_pair:
-        gram_in_ref, gram_ref, odd_ref, even_ref = refs
-    else:
-        odd_ref, even_ref, local_out_ref, outward_out_ref, prev_ref, next_ref, dom_out_ref = refs[:7]
-    if first_pair:
-        in_high_ref, in_low_ref = refs[7:]
+        dom_blocks_ref = refs[8]
+        odd_ref, even_ref, in_high_ref, in_low_ref = refs[9:]
         for way, ref in enumerate((dom_blocks_ref, dom_next_ref, blk_prev_ref, blk_next_ref)):
             for place in range(2):
                 main = ref[tall * place : tall * place + width, :]
-                tail = tail_at(ref[2 * tall : 2 * tall + width, :], width - 128, place)
-                high, low = split_halves(jnp.concatenate([main, tail], axis=1))
+                rest = tail_at(ref[2 * tall : 2 * tall + width, :], tail, place)
+                high, low = split_halves(jnp.concatenate([main, rest], axis=1))
                 in_high_ref[2 * way + place] = high
                 in_low_ref[2 * way + place] = low
-
-    tail = width - 128
+    else:
+        in_high_ref, in_low_ref, odd_ref, even_ref = refs[8:]
 
     def from_blk(ref, place):
         return get_rows(ref, first, rows, tail, FROM_BLK, place)
@@ -531,9 +520,6 @@
 
     def from_dom_next(place):
         return get_rows(dom_next_ref, first, rows, tail, FROM_DOM, place)
-
-    def turned(ref, place):
-        return get_rows(ref, 0, rows, tail, RELAYED, place)
 
     odd = [
         sum_ref[cell] + (from_dom_prev if cell < 2 else from_dom_next)(cell % 2)
@@ -542,15 +528,13 @@
     ring = [
         from_dom_prev(2) + outward_ref[0],
         from_dom_prev(3) + outward_ref[1],
-        from_dom_next(2) + outward_ref[2] + turned(turn_prev_ref, 0),
-        from_dom_next(3) + outward_ref[3] + turned(turn_next_ref, 0),
+        from_dom_next(2) + outward_ref[2],
+        from_dom_next(3) + outward_ref[3],
         from_blk(blk_prev_ref, 2) + outward_ref[4] + from_dom_prev(4),
-        from_blk(blk_prev_ref, 3) + outward_ref[5] + turned(turn_prev_ref, 1),
+        from_blk(blk_prev_ref, 3) + outward_ref[5],
         from_blk(blk_next_ref, 2) + outward_ref[6] + from_dom_prev(5),
-        from_blk(blk_next_ref, 3) + outward_ref[7] + turned(turn_next_ref, 1),
+        from_blk(blk_next_ref, 3) + outward_ref[7],
     ]
-    for cell in range(CELLS):
-        odd_ref[cell] = odd[cell]
     even = local_products([stack_halves(value) for value in odd], high_ref, low_ref)
     for place, value in enumerate(ring):
         cell = RING_TARGETS[place]
@@ -558,11 +542,35 @@
             *stack_halves(value), in_high_ref[place], in_low_ref[place]
         )
     for cell in range(CELLS):
+        odd_ref[cell] = odd[cell]
+        even_ref[cell] = even[cell]
+
+
+TURNED = ((2, 0, 0), (3, 1, 0), (5, 0, 1), (7, 1, 1))
+
+
+def even_kernel(last_pair, older_count, *refs):
+    part_ref, turn_prev_ref, turn_next_ref, in_high_ref, in_low_ref = refs[:5]
+    refs = refs[5:]
+    rows = part_ref.shape[1]
+    tail = part_ref.shape[2] - 128
+    even = [part_ref[cell] for cell in range(CELLS)]
+    for place, side, item in TURNED:
+        value = get_rows((turn_prev_ref, turn_next_ref)[side], 0, rows, tail, RELAYED, item)
+        cell = RING_TARGETS[place]
+        even[cell] = even[cell] + row_times(
+            *stack_halves(value), in_high_ref[place], in_low_ref[place]
+        )
+    if last_pair:
+        older = refs[:older_count]
+        gram_in_ref, gram_ref, even_ref = refs[older_count:]
+    else:
+        high_ref, low_ref = refs[:2]
+        even_ref, local_out_ref, outward_out_ref, prev_ref, next_ref, dom_out_ref = refs[2:]
+    for cell in range(CELLS):
         even_ref[cell] = even[cell]
     if last_pair:
-        bases = list(older) + [odd_ref, even_ref]
-        gram = gram_rows(ITERS - 1, bases, gram_in_ref[...])
-        gram = gram_rows(ITERS, bases, gram)
+        gram = gram_rows(ITERS, list(older) + [even_ref], gram_in_ref[...])
         half = gram.shape[0] // 2
         gram = gram[:half] + pltpu.roll(gram[half:], 64, 1)
         for place in range(gram_ref.shape[0]):
@@ -581,9 +589,8 @@
 
 def gram_kernel(newest, *refs):
     base_refs = refs[: newest + 1]
-    gram = None
-    if newest > 0:
-        gram = gram_rows(newest - 1, base_refs, refs[newest + 1][...])
+    gram = None if newest == 1 else refs[newest + 1][...]
+    gram = gram_rows(newest - 1, base_refs, gram)
     refs[-1][...] = gram_rows(newest, base_refs, gram)
 
 
@@ -615,8 +622,8 @@
         return jnp.broadcast_to(gram[:, place : place + 1], gram.shape)
 
     diag = [lane(j, j) for j in range(count)]
-    scale = [1.0 / jnp.sqrt(value) for value in diag]
-    start = jnp.sqrt(diag[0])
+    scale = [lax.rsqrt(value) for value in diag]
+    start = diag[0] * scale[0]
     lower = [[None] * count for j in range(count)]
     solved = []
     ratio = [scale[j] * start for j in range(count)]
@@ -627,7 +634,7 @@
         for k in range(col):
             pivot = pivot - lower[col][k] * lower[col][k]
         smallest = jnp.minimum(smallest, pivot)
-        inv_root = 1.0 / jnp.sqrt(pivot)
+        inv_root = lax.rsqrt(pivot)
         inv_pivot.append(inv_root)
         for row in range(col + 1, count):
             value = lane(row, col) * scale[row] * scale[col]
@@ -641,7 +648,7 @@
     squares = solved[0] * solved[0]
     for j in range(1, count):
         squares = squares + solved[j] * solved[j]
-    rel = 1.0 / jnp.sqrt(squares)
+    rel = lax.rsqrt(squares)
     back = [None] * count
     for j in reversed(range(count)):
         value = solved[j]
@@ -820,8 +827,24 @@
             name=f"relay_part_{pair}",
         )(sums, from_dom_next)
         turns = both_ways(*turns, "blk")
+        given = [sums, outward, *from_blk, from_dom_prev, from_dom_next, high, low, *inward]
+        shapes = (field, field)
+        if first_pair:
+            shapes += (struct(8, *block, kind=BF16), struct(8, *block, kind=BF16))
+        odd, part, *made = pl.pallas_call(
+            functools.partial(odd_kernel, first_pair),
+            out_shape=shapes,
+            in_specs=vmem(len(given)),
+            out_specs=tuple(vmem(len(shapes))),
+            compiler_params=PARAMS,
+            cost_estimate=cost(20 * products, 6000000),
+            name=f"odd_part_{pair}",
+        )(*given)
+        if first_pair:
+            inward = made
+        bases.append(odd)
         newest = len(bases) - 1
-        given = bases + ([gram] if newest > 0 else [])
+        given = bases + ([gram] if newest > 1 else [])
         gram = pl.pallas_call(
             functools.partial(gram_kernel, newest),
             out_shape=struct(nrhs, 128),
@@ -831,37 +854,29 @@
             cost_estimate=cost(100000 * (newest + 1), 2000000),
             name=f"gram_part_{pair}",
         )(*given)
-        older = bases if last_pair else []
-        given = [
-            sums, outward, *from_blk, from_dom_prev, from_dom_next, *turns, high, low,
-            *inward, *older,
-        ]
+        given = [part, *turns, *inward]
         if last_pair:
-            given.append(gram)
-            shapes = (struct(near_size() * lax.axis_size("blk"), nrhs // 2, 128), field, field)
+            given += [*bases, gram]
+            shapes = (struct(near_size() * lax.axis_size("blk"), nrhs // 2, 128), field)
         else:
-            shapes = (field, field, field, ring, blk_edge, blk_edge, dom_edge)
-        if first_pair:
-            shapes += (struct(8, *block, kind=BF16), struct(8, *block, kind=BF16))
+            given += [high, low]
+            shapes = (field, field, ring, blk_edge, blk_edge, dom_edge)
         outs = pl.pallas_call(
-            functools.partial(pair_kernel, first_pair, last_pair, len(older)),
+            functools.partial(even_kernel, last_pair, len(bases)),
             out_shape=shapes,
             in_specs=vmem(len(given)),
             out_specs=tuple(vmem(len(shapes))),
             compiler_params=PARAMS,
-            cost_estimate=cost(40 * products, 6000000),
-            name=f"pair_part_{pair}",
+            cost_estimate=cost(24 * products, 6000000),
+            name=f"even_part_{pair}",
         )(*given)
         if last_pair:
             gram = outs[0]
-            bases.append(outs[1])
         else:
-            bases += outs[:2]
-            local, outward = outs[2:4]
-            blk_sends = outs[4:6]
-            dom_send = outs[6]
-        if first_pair:
-            inward = outs[7:]
+            bases.append(outs[0])
+            local, outward = outs[1:3]
+            blk_sends = outs[3:5]
+            dom_send = outs[5]
     gram = sum_devices(gram)
     given = [gram] + bases + [inv_high, inv_low, slots]
     adjoint, rel, fine = pl.pallas_call(

time: 132 us -> 130 us (0.985)
  starting transfers between devices: 71.3 us -> 68.3 us
    ppermute x25, starting transfers between devices: 63.2 us -> 61 us  [rotated(): lax.ppermute(value, axis, [(source, (source + steps) % count) for source...]
    pallas_call x4 -> x8, Pallas kernels: 5.24 us -> 6.18 us  [the longest x4 3.47 us: shards(): pl.pallas_call(functools.partial(even_kernel, last_pair, len(bases)), out...]
  transfers between devices with their start and end apart: 26 -> 26, of which waited for: 13 -> 8; matrix products, arithmetic and copies ran while one was open for 0% -> 0% of each run, Pallas kernels for 1% -> 3%
where the time goes in v6:
time: 130 us; the launch traced here: 129 us
  starting transfers between devices  68.3 us (53%)
  waiting for transfers between devices  25.3 us (19%)
  Pallas kernels  18.9 us (15%)
  blocking collectives  14.8 us (11%)
  between operations  1.82 us (1%)
    ppermute x25, starting transfers between devices, rotated(): lax.ppermute(value, axis, [(source, (source + steps) % count) for source...  61 us
    all_to_all x1, blocking collectives, sum_devices(): parts = lax.all_to_all(copies, ('dom', 'blk'), 0, 0, axis_index_groups=near)  14.8 us
    ppermute x25, waiting for transfers between devices, rotated(): lax.ppermute(value, axis, [(source, (source + steps) % count) for source...  13.7 us
    all_to_all x1, waiting for transfers between devices, sum_devices(): return lax.all_to_all(copies, 'dom', 0, 0, axis_index_groups=far)  11.6 us
    pallas_call x1, Pallas kernels, shards(): pl.pallas_call(functools.partial(setup_kernel, dom_count=lax.axis_size('d...  8.65 us
    all_to_all x1, starting transfers between devices, sum_devices(): return lax.all_to_all(copies, 'dom', 0, 0, axis_index_groups=far)  7.25 us
    pallas_call x4, Pallas kernels, shards(): pl.pallas_call(functools.partial(even_kernel, last_pair, len(bases)), out...  3.47 us
    pallas_call x4, Pallas kernels, shards(): pl.pallas_call(functools.partial(odd_kernel, first_pair), out_shape=shape...  2.71 us
  transfers between devices with their start and end apart: 26, of which 8 were waited for; matrix products, arithmetic and copies ran while one was open for 0% of the time, Pallas kernels for 3%

profile of v6, /device:TPU:1, one launch (start us, length us, event | category | flops | bytes accessed | tf_op | source)
XLA Modules:
  0.0 129.4 jit_solution(12582577937491278163)
XLA Ops:
  0.6 8.7 %setup_blocks.1 = (bf16[20,162,162]{2,1,0:T(8,128)(2,1)S(1)}, bf16[20,162,162]{2,1,0:T(8,128)(2,1)S(1)}, bf16[4,162,162]{2,1,0:T(8,128)(2,1)S(1)}, bf16[4,162,16...) custom-call(s32[4,6]{1,0:T(4,128)} %nbr_ref.1, ...), custom_call_target="tpu_custom_call" | custom-call | tf_op jit(solution)/shard_map/setup_blocks/pallas_call | solution.py:767
  9.3 2.7 %collective-permute-start.36 = (f32[616,128]{1,0:T(8,128)S(1)}, f32[616,128]{1,0:T(8,128)S(1)}, u32[]{:S(2)}, u32[]{:S(2)}) collective-permute-start(f32[616,128]{1,0:T(8,128)S(1)} %get-tuple-element.93), channel_id=1, source_target_pairs={{0,1},{1,2},{2,3},{3,4},{4,5},{5,6},{6,7},{7,0},{8,9},{9,10},{10,1... | collective-permute-start | bytes 946184 | tf_op jit(solution)/shard_map/ppermute | solution.py:744
  12.0 4.2 %collective-permute-start.37 = (f32[616,128]{1,0:T(8,128)S(1)}, f32[616,128]{1,0:T(8,128)S(1)}, u32[]{:S(2)}, u32[]{:S(2)}) collective-permute-start(f32[616,128]{1,0:T(8,128)S(1)} %get-tuple-element.94), channel_id=1, source_target_pairs={{0,7},{1,0},{2,1},{3,2},{4,3},{5,4},{6,5},{7,6},{8,15},{9,8},{10,9... | collective-permute-start | bytes 946184 | tf_op jit(solution)/shard_map/ppermute | solution.py:744
  16.2 9.1 %collective-permute-start.39 = (f32[632,128]{1,0:T(8,128)S(1)}, f32[632,128]{1,0:T(8,128)S(1)}, u32[]{:S(2)}, u32[]{:S(2)}) collective-permute-start(f32[632,128]{1,0:T(8,128)S(1)} %get-tuple-element.97), channel_id=1, source_target_pairs={{0,504},{8,0},{16,8},{24,16},{32,24},{40,32},{48,40},{56,48},{64,5... | collective-permute-start | bytes 970760 | tf_op jit(solution)/shard_map/ppermute | solution.py:744
  25.3 1.9 %collective-permute-start.40 = (f32[504,128]{1,0:T(8,128)S(1)}, f32[504,128]{1,0:T(8,128)S(1)}, u32[]{:S(2)}, u32[]{:S(2)}) collective-permute-start(f32[504,128]{1,0:T(8,128)S(1)} %get-tuple-element.100), channel_id=1, source_target_pairs={{0,8},{8,16},{16,24},{24,32},{32,40},{40,48},{48,56},{56,64},{64,7... | collective-permute-start | bytes 774152 | tf_op jit(solution)/shard_map/ppermute | solution.py:744
  27.2 0.0 collective-permute-done.36.prev_ref.refs_2_
  27.2 0.1 middle_part_0.1
  27.4 1.9 %collective-permute-start.38 = (f32[128,128]{1,0:T(8,128)S(1)}, f32[128,128]{1,0:T(8,128)S(1)}, u32[]{:S(2)}, u32[]{:S(2)}) collective-permute-start(f32[128,128]{1,0:T(8,128)S(1)} %get-tuple-element.96), channel_id=1, source_target_pairs={{0,8},{8,16},{16,24},{24,32},{32,40},{40,48},{48,56},{56,64},{64,7... | collective-permute-start | bytes 196616 | tf_op jit(solution)/shard_map/ppermute | solution.py:744
  29.3 1.1 collective-permute-done.39.refs_5_.dom_ref
  30.4 0.1 relay_part_0.1
  30.6 3.8 %collective-permute-start.41 = (f32[48,128]{1,0:T(8,128)S(1)}, f32[48,128]{1,0:T(8,128)S(1)}, u32[]{:S(2)}, u32[]{:S(2)}) collective-permute-start(f32[48,128]{1,0:T(8,128)S(1)} %get-tuple-element.102), channel_id=1, source_target_pairs={{0,1},{1,2},{2,3},{3,4},{4,5},{5,6},{6,7},{7,0},{8,9},{9,10},{10,1... | collective-permute-start | bytes 73736 | tf_op jit(solution)/shard_map/ppermute | solution.py:744
  34.4 1.8 %collective-permute-done.40.refs_8_ = f32[504,128]{1,0:T(8,128)S(1)} collective-permute-done((f32[504,128]{1,0:T(8,128)S(1)}, f32[504,128]{1,0:T(8,128)S(1)}, u32[]{:S(2)}, u32[]{:S(2)}) %collective-permute-start.40) | collective-permute-done | bytes 258080 | tf_op jit(solution)/shard_map/ppermute | solution.py:744
  36.2 1.4 %collective-permute-done.38.refs_4_ = f32[128,128]{1,0:T(8,128)S(1)} collective-permute-done((f32[128,128]{1,0:T(8,128)S(1)}, f32[128,128]{1,0:T(8,128)S(1)}, u32[]{:S(2)}, u32[]{:S(2)}) %collective-permute-start.38) | collective-permute-done | bytes 65568 | tf_op jit(solution)/shard_map/ppermute | solution.py:744
  37.6 0.7 odd_part_0.1
  38.3 0.0 collective-permute-done.41.refs_1_
  38.3 0.9 even_part_0.1
  39.2 4.1 %collective-permute-start.43 = (f32[112,128]{1,0:T(8,128)S(1)}, f32[112,128]{1,0:T(8,128)S(1)}, u32[]{:S(2)}, u32[]{:S(2)}) collective-permute-start(f32[112,128]{1,0:T(8,128)S(1)} %get-tuple-element.108), channel_id=1, source_target_pairs={{0,1},{1,2},{2,3},{3,4},{4,5},{5,6},{6,7},{7,0},{8,9},{9,10},{10,1... | collective-permute-start | bytes 172040 | tf_op jit(solution)/shard_map/ppermute | solution.py:744
  43.3 3.1 %collective-permute-start.46 = (f32[128,128]{1,0:T(8,128)S(1)}, f32[128,128]{1,0:T(8,128)S(1)}, u32[]{:S(2)}, u32[]{:S(2)}) collective-permute-start(f32[128,128]{1,0:T(8,128)S(1)} %get-tuple-element.112), channel_id=1, source_target_pairs={{0,504},{8,0},{16,8},{24,16},{32,24},{40,32},{48,40},{56,48},{64,5... | collective-permute-start | bytes 196616 | tf_op jit(solution)/shard_map/ppermute | solution.py:744
  46.5 0.4 collective-permute-done.44.next_ref.refs_3_
  46.9 0.1 middle_part_1.1
  47.0 1.9 %collective-permute-start.45 = (f32[128,128]{1,0:T(8,128)S(1)}, f32[128,128]{1,0:T(8,128)S(1)}, u32[]{:S(2)}, u32[]{:S(2)}) collective-permute-start(f32[128,128]{1,0:T(8,128)S(1)} %get-tuple-element.111), channel_id=1, source_target_pairs={{0,8},{8,16},{16,24},{24,32},{32,40},{40,48},{48,56},{56,64},{64,7... | collective-permute-start | bytes 196616 | tf_op jit(solution)/shard_map/ppermute | solution.py:744
  49.0 0.1 relay_part_1.1
  49.1 2.2 %collective-permute-start.47 = (f32[48,128]{1,0:T(8,128)S(1)}, f32[48,128]{1,0:T(8,128)S(1)}, u32[]{:S(2)}, u32[]{:S(2)}) collective-permute-start(f32[48,128]{1,0:T(8,128)S(1)} %get-tuple-element.114), channel_id=1, source_target_pairs={{0,1},{1,2},{2,3},{3,4},{4,5},{5,6},{6,7},{7,0},{8,9},{9,10},{10,1... | collective-permute-start | bytes 73736 | tf_op jit(solution)/shard_map/ppermute | solution.py:744
  51.3 0.2 collective-permute-start.48
  51.5 3.9 %collective-permute-done.45.refs_4_ = f32[128,128]{1,0:T(8,128)S(1)} collective-permute-done((f32[128,128]{1,0:T(8,128)S(1)}, f32[128,128]{1,0:T(8,128)S(1)}, u32[]{:S(2)}, u32[]{:S(2)}) %collective-permute-start.45) | collective-permute-done | bytes 65568 | tf_op jit(solution)/shard_map/ppermute | solution.py:744
  55.4 0.7 odd_part_1.1
  56.0 0.9 even_part_1.1
  56.9 2.3 %collective-permute-start.49 = (f32[112,128]{1,0:T(8,128)S(1)}, f32[112,128]{1,0:T(8,128)S(1)}, u32[]{:S(2)}, u32[]{:S(2)}) collective-permute-start(f32[112,128]{1,0:T(8,128)S(1)} %get-tuple-element.118), channel_id=1, source_target_pairs={{0,1},{1,2},{2,3},{3,4},{4,5},{5,6},{6,7},{7,0},{8,9},{9,10},{10,1... | collective-permute-start | bytes 172040 | tf_op jit(solution)/shard_map/ppermute | solution.py:744
  59.2 1.2 collective-permute-start.50
  60.4 3.5 %collective-permute-start.52 = (f32[128,128]{1,0:T(8,128)S(1)}, f32[128,128]{1,0:T(8,128)S(1)}, u32[]{:S(2)}, u32[]{:S(2)}) collective-permute-start(f32[128,128]{1,0:T(8,128)S(1)} %get-tuple-element.122), channel_id=1, source_target_pairs={{0,504},{8,0},{16,8},{24,16},{32,24},{40,32},{48,40},{56,48},{64,5... | collective-permute-start | bytes 196616 | tf_op jit(solution)/shard_map/ppermute | solution.py:744
  63.9 0.0 collective-permute-done.50.next_ref.refs_3_
  63.9 0.1 middle_part_2.1
  64.1 1.9 %collective-permute-start.51 = (f32[128,128]{1,0:T(8,128)S(1)}, f32[128,128]{1,0:T(8,128)S(1)}, u32[]{:S(2)}, u32[]{:S(2)}) collective-permute-start(f32[128,128]{1,0:T(8,128)S(1)} %get-tuple-element.121), channel_id=1, source_target_pairs={{0,8},{8,16},{16,24},{24,32},{32,40},{40,48},{48,56},{56,64},{64,7... | collective-permute-start | bytes 196616 | tf_op jit(solution)/shard_map/ppermute | solution.py:744
  66.0 0.1 relay_part_2.1
  66.2 1.1 collective-permute-start.53
  67.3 2.4 %collective-permute-start.54 = (f32[48,128]{1,0:T(8,128)S(1)}, f32[48,128]{1,0:T(8,128)S(1)}, u32[]{:S(2)}, u32[]{:S(2)}) collective-permute-start(f32[48,128]{1,0:T(8,128)S(1)} %get-tuple-element.125), channel_id=1, source_target_pairs={{0,7},{1,0},{2,1},{3,2},{4,3},{5,4},{6,5},{7,6},{8,15},{9,8},{10,9... | collective-permute-start | bytes 73736 | tf_op jit(solution)/shard_map/ppermute | solution.py:744
  69.7 2.7 %collective-permute-done.51.refs_4_ = f32[128,128]{1,0:T(8,128)S(1)} collective-permute-done((f32[128,128]{1,0:T(8,128)S(1)}, f32[128,128]{1,0:T(8,128)S(1)}, u32[]{:S(2)}, u32[]{:S(2)}) %collective-permute-start.51) | collective-permute-done | bytes 65568 | tf_op jit(solution)/shard_map/ppermute | solution.py:744
  72.4 0.7 odd_part_2.1
  73.1 0.9 even_part_2.1
  73.9 1.1 collective-permute-start.55
  75.1 3.3 %collective-permute-start.56 = (f32[112,128]{1,0:T(8,128)S(1)}, f32[112,128]{1,0:T(8,128)S(1)}, u32[]{:S(2)}, u32[]{:S(2)}) collective-permute-start(f32[112,128]{1,0:T(8,128)S(1)} %get-tuple-element.129), channel_id=1, source_target_pairs={{0,7},{1,0},{2,1},{3,2},{4,3},{5,4},{6,5},{7,6},{8,15},{9,8},{10,9... | collective-permute-start | bytes 172040 | tf_op jit(solution)/shard_map/ppermute | solution.py:744
  78.3 3.5 %collective-permute-start.58 = (f32[128,128]{1,0:T(8,128)S(1)}, f32[128,128]{1,0:T(8,128)S(1)}, u32[]{:S(2)}, u32[]{:S(2)}) collective-permute-start(f32[128,128]{1,0:T(8,128)S(1)} %get-tuple-element.132), channel_id=1, source_target_pairs={{0,504},{8,0},{16,8},{24,16},{32,24},{40,32},{48,40},{56,48},{64,5... | collective-permute-start | bytes 196616 | tf_op jit(solution)/shard_map/ppermute | solution.py:744
  81.8 0.1 middle_part_3.1
  82.0 2.1 %collective-permute-start.57 = (f32[128,128]{1,0:T(8,128)S(1)}, f32[128,128]{1,0:T(8,128)S(1)}, u32[]{:S(2)}, u32[]{:S(2)}) collective-permute-start(f32[128,128]{1,0:T(8,128)S(1)} %get-tuple-element.131), channel_id=1, source_target_pairs={{0,8},{8,16},{16,24},{24,32},{32,40},{40,48},{48,56},{56,64},{64,7... | collective-permute-start | bytes 196616 | tf_op jit(solution)/shard_map/ppermute | solution.py:744
  84.1 0.1 relay_part_3.1
  84.2 3.4 %collective-permute-start.60 = (f32[48,128]{1,0:T(8,128)S(1)}, f32[48,128]{1,0:T(8,128)S(1)}, u32[]{:S(2)}, u32[]{:S(2)}) collective-permute-start(f32[48,128]{1,0:T(8,128)S(1)} %get-tuple-element.135), channel_id=1, source_target_pairs={{0,7},{1,0},{2,1},{3,2},{4,3},{5,4},{6,5},{7,6},{8,15},{9,8},{10,9... | collective-permute-start | bytes 73736 | tf_op jit(solution)/shard_map/ppermute | solution.py:744
  87.6 0.1 gram_part_0.1.refs_4_
  87.7 0.1 gram_part_1.1.refs_6_
  87.8 0.1 gram_part_2.1.refs_8_
  88.0 0.0 copy-start.1
  88.0 0.0 copy-start.2
  88.0 0.0 copy-start.3
  88.0 0.0 copy-start.6
  88.0 0.0 copy-start.7
  88.0 2.3 %collective-permute-done.57.refs_4_ = f32[128,128]{1,0:T(8,128)S(1)} collective-permute-done((f32[128,128]{1,0:T(8,128)S(1)}, f32[128,128]{1,0:T(8,128)S(1)}, u32[]{:S(2)}, u32[]{:S(2)}) %collective-permute-start.57) | collective-permute-done | bytes 65568 | tf_op jit(solution)/shard_map/ppermute | solution.py:744
  90.3 0.7 odd_part_3.1
  91.0 0.2 gram_part_3.1.refs_13_
  91.2 0.9 even_part_3.1
  92.0 14.8 %all_to_all.10.parts_ref = f32[32,8,128]{2,1,0:T(8,128)S(1)} all-to-all(f32[32,8,128]{2,1,0:T(8,128)S(1)} %get-tuple-element.144), channel_id=1, replica_groups={{0,1,2,3,4,5,6,7,8,9,10,11,12,13,14,15,16,17,18,19,20,21,22,23,24,25,26..., dimensions={0} | all-to-all | bytes 262144 | tf_op jit(solution)/shard_map/all_to_all | solution.py:730
  106.9 0.7 sum_near.1
  107.5 7.3 %all-to-all-start.1 = ((f32[16,8,128]{2,1,0:T(8,128)}), f32[16,8,128]{2,1,0:T(8,128)S(1)}, u32[]{:S(2)}, u32[]{:S(2)}) async-start(f32[16,8,128]{2,1,0:T(8,128)} %sum_near.1), calls=%async_computation.1 | async-start | bytes 131072 | tf_op jit(solution)/shard_map/all_to_all | solution.py:739
  114.8 11.6 %all-to-all-done.1.refs_0_ = f32[16,8,128]{2,1,0:T(8,128)S(1)} async-done(((f32[16,8,128]{2,1,0:T(8,128)}), f32[16,8,128]{2,1,0:T(8,128)S(1)}, u32[]{:S(2)}, u32[]{:S(2)}) %all-to-all-start.1) | async-done | bytes 65568 | tf_op jit(solution)/shard_map/all_to_all | solution.py:739
  126.4 1.8 %finish_part.1 = (f32[16,4,162]{2,1,0:T(4,128)}, f32[1,16]{1,0:T(1,128)}, s32[1]{0:T(128)}) custom-call(f32[16,8,128]{2,1,0:T(8,128)S(1)} %all-to-all-done.1.refs_0_, f32[4,16,162]{2,1,0:T(8,128)S(1)} %get-tuple-element.136.refs_0_.refs_5_.refs_1_, f32[4,16,162]{2,1,0:T(8,128)S(1)} %get-tuple-element.137.refs_1_.refs_6_.refs_2_, ...), custom_call_target="tpu_custom_call" | custom-call | tf_op jit(solution)/shard_map/finish_part/pallas_call | solution.py:882
  128.9 0.3 conditional.1
  (23 shorter events, 0.1 us)
Async XLA Ops:
  9.3 17.9 %collective-permute-start.36 = (f32[616,128]{1,0:T(8,128)S(1)}, f32[616,128]{1,0:T(8,128)S(1)}, u32[]{:S(2)}, u32[]{:S(2)}) collective-permute-start(f32[616,128]{1,0:T(8,128)S(1)} %get-tuple-element.93), channel_id=1, source_target_pairs={{0,1},{1,2},{2,3},{3,4},{4,5},{5,6},{6,7},{7,0},{8,9},{9,10},{10,1... | collective-permute-start | bytes 946184 | tf_op jit(solution)/shard_map/ppermute | solution.py:744
  12.0 15.3 %collective-permute-start.37 = (f32[616,128]{1,0:T(8,128)S(1)}, f32[616,128]{1,0:T(8,128)S(1)}, u32[]{:S(2)}, u32[]{:S(2)}) collective-permute-start(f32[616,128]{1,0:T(8,128)S(1)} %get-tuple-element.94), channel_id=1, source_target_pairs={{0,7},{1,0},{2,1},{3,2},{4,3},{5,4},{6,5},{7,6},{8,15},{9,8},{10,9... | collective-permute-start | bytes 946184 | tf_op jit(solution)/shard_map/ppermute | solution.py:744
  16.2 14.2 %collective-permute-start.39 = (f32[632,128]{1,0:T(8,128)S(1)}, f32[632,128]{1,0:T(8,128)S(1)}, u32[]{:S(2)}, u32[]{:S(2)}) collective-permute-start(f32[632,128]{1,0:T(8,128)S(1)} %get-tuple-element.97), channel_id=1, source_target_pairs={{0,504},{8,0},{16,8},{24,16},{32,24},{40,32},{48,40},{56,48},{64,5... | collective-permute-start | bytes 970760 | tf_op jit(solution)/shard_map/ppermute | solution.py:744
  25.3 10.9 %collective-permute-start.40 = (f32[504,128]{1,0:T(8,128)S(1)}, f32[504,128]{1,0:T(8,128)S(1)}, u32[]{:S(2)}, u32[]{:S(2)}) collective-permute-start(f32[504,128]{1,0:T(8,128)S(1)} %get-tuple-element.100), channel_id=1, source_target_pairs={{0,8},{8,16},{16,24},{24,32},{32,40},{40,48},{48,56},{56,64},{64,7... | collective-permute-start | bytes 774152 | tf_op jit(solution)/shard_map/ppermute | solution.py:744
  27.4 10.2 %collective-permute-start.38 = (f32[128,128]{1,0:T(8,128)S(1)}, f32[128,128]{1,0:T(8,128)S(1)}, u32[]{:S(2)}, u32[]{:S(2)}) collective-permute-start(f32[128,128]{1,0:T(8,128)S(1)} %get-tuple-element.96), channel_id=1, source_target_pairs={{0,8},{8,16},{16,24},{24,32},{32,40},{40,48},{48,56},{56,64},{64,7... | collective-permute-start | bytes 196616 | tf_op jit(solution)/shard_map/ppermute | solution.py:744
  30.6 7.7 %collective-permute-start.41 = (f32[48,128]{1,0:T(8,128)S(1)}, f32[48,128]{1,0:T(8,128)S(1)}, u32[]{:S(2)}, u32[]{:S(2)}) collective-permute-start(f32[48,128]{1,0:T(8,128)S(1)} %get-tuple-element.102), channel_id=1, source_target_pairs={{0,1},{1,2},{2,3},{3,4},{4,5},{5,6},{6,7},{7,0},{8,9},{9,10},{10,1... | collective-permute-start | bytes 73736 | tf_op jit(solution)/shard_map/ppermute | solution.py:744
  34.4 3.9 %collective-permute-start.42 = (f32[48,128]{1,0:T(8,128)S(1)}, f32[48,128]{1,0:T(8,128)S(1)}, u32[]{:S(2)}, u32[]{:S(2)}) collective-permute-start(f32[48,128]{1,0:T(8,128)S(1)} %get-tuple-element.103), channel_id=1, source_target_pairs={{0,7},{1,0},{2,1},{3,2},{4,3},{5,4},{6,5},{7,6},{8,15},{9,8},{10,9... | collective-permute-start | bytes 73736 | tf_op jit(solution)/shard_map/ppermute | solution.py:744
  39.2 7.3 %collective-permute-start.43 = (f32[112,128]{1,0:T(8,128)S(1)}, f32[112,128]{1,0:T(8,128)S(1)}, u32[]{:S(2)}, u32[]{:S(2)}) collective-permute-start(f32[112,128]{1,0:T(8,128)S(1)} %get-tuple-element.108), channel_id=1, source_target_pairs={{0,1},{1,2},{2,3},{3,4},{4,5},{5,6},{6,7},{7,0},{8,9},{9,10},{10,1... | collective-permute-start | bytes 172040 | tf_op jit(solution)/shard_map/ppermute | solution.py:744
  43.3 3.6 %collective-permute-start.44 = (f32[112,128]{1,0:T(8,128)S(1)}, f32[112,128]{1,0:T(8,128)S(1)}, u32[]{:S(2)}, u32[]{:S(2)}) collective-permute-start(f32[112,128]{1,0:T(8,128)S(1)} %get-tuple-element.109), channel_id=1, source_target_pairs={{0,7},{1,0},{2,1},{3,2},{4,3},{5,4},{6,5},{7,6},{8,15},{9,8},{10,9... | collective-permute-start | bytes 172040 | tf_op jit(solution)/shard_map/ppermute | solution.py:744
  43.3 5.7 %collective-permute-start.46 = (f32[128,128]{1,0:T(8,128)S(1)}, f32[128,128]{1,0:T(8,128)S(1)}, u32[]{:S(2)}, u32[]{:S(2)}) collective-permute-start(f32[128,128]{1,0:T(8,128)S(1)} %get-tuple-element.112), channel_id=1, source_target_pairs={{0,504},{8,0},{16,8},{24,16},{32,24},{40,32},{48,40},{56,48},{64,5... | collective-permute-start | bytes 196616 | tf_op jit(solution)/shard_map/ppermute | solution.py:744
  47.0 8.3 %collective-permute-start.45 = (f32[128,128]{1,0:T(8,128)S(1)}, f32[128,128]{1,0:T(8,128)S(1)}, u32[]{:S(2)}, u32[]{:S(2)}) collective-permute-start(f32[128,128]{1,0:T(8,128)S(1)} %get-tuple-element.111), channel_id=1, source_target_pairs={{0,8},{8,16},{16,24},{24,32},{32,40},{40,48},{48,56},{56,64},{64,7... | collective-permute-start | bytes 196616 | tf_op jit(solution)/shard_map/ppermute | solution.py:744
  49.1 6.9 %collective-permute-start.47 = (f32[48,128]{1,0:T(8,128)S(1)}, f32[48,128]{1,0:T(8,128)S(1)}, u32[]{:S(2)}, u32[]{:S(2)}) collective-permute-start(f32[48,128]{1,0:T(8,128)S(1)} %get-tuple-element.114), channel_id=1, source_target_pairs={{0,1},{1,2},{2,3},{3,4},{4,5},{5,6},{6,7},{7,0},{8,9},{9,10},{10,1... | collective-permute-start | bytes 73736 | tf_op jit(solution)/shard_map/ppermute | solution.py:744
  51.3 4.7 %collective-permute-start.48 = (f32[48,128]{1,0:T(8,128)S(1)}, f32[48,128]{1,0:T(8,128)S(1)}, u32[]{:S(2)}, u32[]{:S(2)}) collective-permute-start(f32[48,128]{1,0:T(8,128)S(1)} %get-tuple-element.115), channel_id=1, source_target_pairs={{0,7},{1,0},{2,1},{3,2},{4,3},{5,4},{6,5},{7,6},{8,15},{9,8},{10,9... | collective-permute-start | bytes 73736 | tf_op jit(solution)/shard_map/ppermute | solution.py:744
  56.9 7.0 %collective-permute-start.49 = (f32[112,128]{1,0:T(8,128)S(1)}, f32[112,128]{1,0:T(8,128)S(1)}, u32[]{:S(2)}, u32[]{:S(2)}) collective-permute-start(f32[112,128]{1,0:T(8,128)S(1)} %get-tuple-element.118), channel_id=1, source_target_pairs={{0,1},{1,2},{2,3},{3,4},{4,5},{5,6},{6,7},{7,0},{8,9},{9,10},{10,1... | collective-permute-start | bytes 172040 | tf_op jit(solution)/shard_map/ppermute | solution.py:744
  59.2 4.7 %collective-permute-start.50 = (f32[112,128]{1,0:T(8,128)S(1)}, f32[112,128]{1,0:T(8,128)S(1)}, u32[]{:S(2)}, u32[]{:S(2)}) collective-permute-start(f32[112,128]{1,0:T(8,128)S(1)} %get-tuple-element.119), channel_id=1, source_target_pairs={{0,7},{1,0},{2,1},{3,2},{4,3},{5,4},{6,5},{7,6},{8,15},{9,8},{10,9... | collective-permute-start | bytes 172040 | tf_op jit(solution)/shard_map/ppermute | solution.py:744
  60.4 5.6 %collective-permute-start.52 = (f32[128,128]{1,0:T(8,128)S(1)}, f32[128,128]{1,0:T(8,128)S(1)}, u32[]{:S(2)}, u32[]{:S(2)}) collective-permute-start(f32[128,128]{1,0:T(8,128)S(1)} %get-tuple-element.122), channel_id=1, source_target_pairs={{0,504},{8,0},{16,8},{24,16},{32,24},{40,32},{48,40},{56,48},{64,5... | collective-permute-start | bytes 196616 | tf_op jit(solution)/shard_map/ppermute | solution.py:744
  64.1 8.3 %collective-permute-start.51 = (f32[128,128]{1,0:T(8,128)S(1)}, f32[128,128]{1,0:T(8,128)S(1)}, u32[]{:S(2)}, u32[]{:S(2)}) collective-permute-start(f32[128,128]{1,0:T(8,128)S(1)} %get-tuple-element.121), channel_id=1, source_target_pairs={{0,8},{8,16},{16,24},{24,32},{32,40},{40,48},{48,56},{56,64},{64,7... | collective-permute-start | bytes 196616 | tf_op jit(solution)/shard_map/ppermute | solution.py:744
  66.2 6.9 %collective-permute-start.53 = (f32[48,128]{1,0:T(8,128)S(1)}, f32[48,128]{1,0:T(8,128)S(1)}, u32[]{:S(2)}, u32[]{:S(2)}) collective-permute-start(f32[48,128]{1,0:T(8,128)S(1)} %get-tuple-element.124), channel_id=1, source_target_pairs={{0,1},{1,2},{2,3},{3,4},{4,5},{5,6},{6,7},{7,0},{8,9},{9,10},{10,1... | collective-permute-start | bytes 73736 | tf_op jit(solution)/shard_map/ppermute | solution.py:744
  67.3 5.8 %collective-permute-start.54 = (f32[48,128]{1,0:T(8,128)S(1)}, f32[48,128]{1,0:T(8,128)S(1)}, u32[]{:S(2)}, u32[]{:S(2)}) collective-permute-start(f32[48,128]{1,0:T(8,128)S(1)} %get-tuple-element.125), channel_id=1, source_target_pairs={{0,7},{1,0},{2,1},{3,2},{4,3},{5,4},{6,5},{7,6},{8,15},{9,8},{10,9... | collective-permute-start | bytes 73736 | tf_op jit(solution)/shard_map/ppermute | solution.py:744
  73.9 7.9 %collective-permute-start.55 = (f32[112,128]{1,0:T(8,128)S(1)}, f32[112,128]{1,0:T(8,128)S(1)}, u32[]{:S(2)}, u32[]{:S(2)}) collective-permute-start(f32[112,128]{1,0:T(8,128)S(1)} %get-tuple-element.128), channel_id=1, source_target_pairs={{0,1},{1,2},{2,3},{3,4},{4,5},{5,6},{6,7},{7,0},{8,9},{9,10},{10,1... | collective-permute-start | bytes 172040 | tf_op jit(solution)/shard_map/ppermute | solution.py:744
  75.1 6.8 %collective-permute-start.56 = (f32[112,128]{1,0:T(8,128)S(1)}, f32[112,128]{1,0:T(8,128)S(1)}, u32[]{:S(2)}, u32[]{:S(2)}) collective-permute-start(f32[112,128]{1,0:T(8,128)S(1)} %get-tuple-element.129), channel_id=1, source_target_pairs={{0,7},{1,0},{2,1},{3,2},{4,3},{5,4},{6,5},{7,6},{8,15},{9,8},{10,9... | collective-permute-start | bytes 172040 | tf_op jit(solution)/shard_map/ppermute | solution.py:744
  78.3 5.8 %collective-permute-start.58 = (f32[128,128]{1,0:T(8,128)S(1)}, f32[128,128]{1,0:T(8,128)S(1)}, u32[]{:S(2)}, u32[]{:S(2)}) collective-permute-start(f32[128,128]{1,0:T(8,128)S(1)} %get-tuple-element.132), channel_id=1, source_target_pairs={{0,504},{8,0},{16,8},{24,16},{32,24},{40,32},{48,40},{56,48},{64,5... | collective-permute-start | bytes 196616 | tf_op jit(solution)/shard_map/ppermute | solution.py:744
  82.0 8.3 %collective-permute-start.57 = (f32[128,128]{1,0:T(8,128)S(1)}, f32[128,128]{1,0:T(8,128)S(1)}, u32[]{:S(2)}, u32[]{:S(2)}) collective-permute-start(f32[128,128]{1,0:T(8,128)S(1)} %get-tuple-element.131), channel_id=1, source_target_pairs={{0,8},{8,16},{16,24},{24,32},{32,40},{40,48},{48,56},{56,64},{64,7... | collective-permute-start | bytes 196616 | tf_op jit(solution)/shard_map/ppermute | solution.py:744
  84.2 6.9 %collective-permute-start.59 = (f32[48,128]{1,0:T(8,128)S(1)}, f32[48,128]{1,0:T(8,128)S(1)}, u32[]{:S(2)}, u32[]{:S(2)}) collective-permute-start(f32[48,128]{1,0:T(8,128)S(1)} %get-tuple-element.134), channel_id=1, source_target_pairs={{0,1},{1,2},{2,3},{3,4},{4,5},{5,6},{6,7},{7,0},{8,9},{9,10},{10,1... | collective-permute-start | bytes 73736 | tf_op jit(solution)/shard_map/ppermute | solution.py:744
  84.2 6.9 %collective-permute-start.60 = (f32[48,128]{1,0:T(8,128)S(1)}, f32[48,128]{1,0:T(8,128)S(1)}, u32[]{:S(2)}, u32[]{:S(2)}) collective-permute-start(f32[48,128]{1,0:T(8,128)S(1)} %get-tuple-element.135), channel_id=1, source_target_pairs={{0,7},{1,0},{2,1},{3,2},{4,3},{5,4},{6,5},{7,6},{8,15},{9,8},{10,9... | collective-permute-start | bytes 73736 | tf_op jit(solution)/shard_map/ppermute | solution.py:744
  88.0 40.9 %copy-start.1 = (f32[16,4,162]{2,1,0:T(4,128)S(1)}, f32[16,4,162]{2,1,0:T(4,128)}, u32[]{:S(2)}) copy-start(f32[16,4,162]{2,1,0:T(4,128)} %src_ref.1) | copy-start | bytes 124420
  88.0 40.9 %copy-start.2 = (f32[4,162,162]{2,0,1:T(4,128)S(1)}, f32[4,162,162]{2,0,1:T(4,128)}, u32[]{:S(2)}) copy-start(f32[4,162,162]{2,0,1:T(4,128)} %param.14) | copy-start | bytes 1259716
  88.0 40.9 %copy-start.3 = (s32[4,6]{1,0:T(4,128)S(1)}, s32[4,6]{1,0:T(4,128)}, u32[]{:S(2)}) copy-start(s32[4,6]{1,0:T(4,128)} %nbr_ref.1) | copy-start | bytes 292
  88.0 40.9 %copy-start.6 = (s32[4,6]{1,0:T(4,128)S(1)}, s32[4,6]{1,0:T(4,128)}, u32[]{:S(2)}) copy-start(s32[4,6]{1,0:T(4,128)} %flag_ref.1) | copy-start | bytes 292
  88.0 40.9 %copy-start.7 = (s32[4,6]{1,0:T(4,128)S(1)}, s32[4,6]{1,0:T(4,128)}, u32[]{:S(2)}) copy-start(s32[4,6]{1,0:T(4,128)} %param.17) | copy-start | bytes 292
  107.5 18.9 %all-to-all-start.1 = ((f32[16,8,128]{2,1,0:T(8,128)}), f32[16,8,128]{2,1,0:T(8,128)S(1)}, u32[]{:S(2)}, u32[]{:S(2)}) async-start(f32[16,8,128]{2,1,0:T(8,128)} %sum_near.1), calls=%async_computation.1 | async-start | bytes 131072 | tf_op jit(solution)/shard_map/all_to_all | solution.py:739

commit v7 on v6

--- a/solution.py
+++ b/solution.py
@@ -212,8 +212,9 @@
     return jnp.dot(left, right, preferred_element_type=F32)
 
 
-def dot_full(left, right):
-    return jnp.dot(left, right, preferred_element_type=F32, precision=HIGH)
+def dot_halves(left_high, left_low, right_high, right_low):
+    small = dot32(left_low, right_high) + dot32(left_high, right_low)
+    return dot32(left_high, right_high) + small
 
 
 def stack_halves(vector):
@@ -315,7 +316,7 @@
     nbr_ref, flag_ref, src_ref, diag_hbm_ref, face_hbm_ref,
     high_ref, low_ref, inv_high_ref, inv_low_ref, base_ref, local_ref, outward_ref,
     blk_prev_ref, blk_next_ref, dom_prev_ref, dom_next_ref, slot_ref,
-    center_ref, x_ref, y_ref, product_ref, face_ref, cell_ref, face_of_ref, diag_sem, face_sem,
+    center_ref, x_ref, d_high_ref, d_low_ref, product_ref, face_ref, cell_ref, face_of_ref, diag_sem, face_sem,
     *, dom_count, blk_count,
 ):
     width = diag_hbm_ref.shape[0]
@@ -339,6 +340,9 @@
     for slot in range(CELLS):
         for face in range(6):
             pl.when(flag_ref[slot, face] == 1)(face_copies[slot][face].start)
+    for slot in range(CELLS):
+        for face in range(6):
+            pl.when(nbr_ref[slot, face] >= 0)(face_copies[slot][face].start)
     dom_here = lax.axis_index("dom")
     blk_here = lax.axis_index("blk")
     here = dom_here * blk_count + blk_here
@@ -393,9 +397,6 @@
         diag_copies[slot].wait()
     for slot in range(CELLS):
         for face in range(6):
-            pl.when(nbr_ref[slot, face] >= 0)(face_copies[slot][face].start)
-    for slot in range(CELLS):
-        for face in range(6):
 
             @pl.when(flag_ref[slot, face] == 1)
             def _():
@@ -407,13 +408,21 @@
         marked = jnp.where(on_diag, center, 0.0)
         inv_row = 1.0 / jnp.sum(marked, axis=0, keepdims=True)
         inv_col = 1.0 / jnp.sum(marked, axis=1, keepdims=True)
-        first = jnp.where(on_diag, inv_col, 0.0)
-        x_ref[slot] = 2.0 * first - inv_col * (center * inv_row)
-    for sweep in range(SWEEPS - 1):
+        defect = jnp.where(on_diag, 0.0, -inv_col * center)
+        x_ref[slot] = jnp.where(on_diag, inv_col, defect * inv_row)
+        d_high_ref[slot], d_low_ref[slot] = split_halves(defect)
+    for sweep in range(1, SWEEPS):
+        squares = [
+            dot_halves(d_high_ref[slot], d_low_ref[slot], d_high_ref[slot], d_low_ref[slot])
+            for slot in range(CELLS)
+        ]
         for slot in range(CELLS):
-            y_ref[slot] = dot_full(center_ref[slot], x_ref[slot])
+            d_high_ref[slot], d_low_ref[slot] = split_halves(squares[slot])
         for slot in range(CELLS):
-            x_ref[slot] = 2.0 * x_ref[slot] - dot_full(x_ref[slot], y_ref[slot])
+            x_high, x_low = split_halves(x_ref[slot])
+            x_ref[slot] = x_ref[slot] + dot_halves(
+                d_high_ref[slot], d_low_ref[slot], x_high, x_low
+            )
     for slot in range(CELLS):
         for face in range(6):
             pl.when(nbr_ref[slot, face] >= 0)(face_copies[slot][face].wait)
@@ -422,13 +431,13 @@
         x_high, x_low = split_halves(x_ref[slot])
         inv_high_ref[cell] = x_high
         inv_low_ref[cell] = x_low
-        own = dot_full(x_ref[slot], center_ref[slot]) - jnp.where(on_diag, 1.0, 0.0)
+        own = -dot_halves(d_high_ref[slot], d_low_ref[slot], d_high_ref[slot], d_low_ref[slot])
         high_ref[cell], low_ref[cell] = split_halves(own)
         for way in range(4):
             face = face_of_ref[slot * 4 + way]
             block = jnp.where(face >= 0, face_ref[slot, jnp.maximum(face, 0)], 0.0)
             f_high, f_low = split_halves(block)
-            product = dot32(x_high, f_high) + dot32(x_low, f_high) + dot32(x_high, f_low)
+            product = dot_halves(x_high, x_low, f_high, f_low)
             if way < 2:
                 leaves = cell // 2 == way
                 inner = FROM_X + cell
@@ -780,7 +789,8 @@
         scratch_shapes=[
             pltpu.VMEM((CELLS,) + block, F32),
             pltpu.VMEM((CELLS,) + block, F32),
-            pltpu.VMEM((CELLS,) + block, F32),
+            pltpu.VMEM((CELLS,) + block, BF16),
+            pltpu.VMEM((CELLS,) + block, BF16),
             pltpu.VMEM((BLOCKS,) + block, F32),
             pltpu.VMEM((CELLS, 6) + block, F32),
             pltpu.SMEM((CELLS,), jnp.int32),

time: 130 us -> 128 us (0.985)
  Pallas kernels: 18.9 us -> 17 us
    pallas_call x1, Pallas kernels: 8.65 us -> 6.76 us  [shards(): pl.pallas_call(functools.partial(setup_kernel, dom_count=lax.axis_size('d...]
where the time goes in v7:
time: 128 us; the launch traced here: 127 us
  starting transfers between devices  68.3 us (53%)
  waiting for transfers between devices  25.1 us (20%)
  Pallas kernels  17 us (13%)
  blocking collectives  14.8 us (12%)
  between operations  1.8 us (1%)
    ppermute x25, starting transfers between devices, rotated(): lax.ppermute(value, axis, [(source, (source + steps) % count) for source...  61.1 us
    all_to_all x1, blocking collectives, sum_devices(): parts = lax.all_to_all(copies, ('dom', 'blk'), 0, 0, axis_index_groups=near)  14.8 us
    ppermute x25, waiting for transfers between devices, rotated(): lax.ppermute(value, axis, [(source, (source + steps) % count) for source...  13.5 us
    all_to_all x1, waiting for transfers between devices, sum_devices(): return lax.all_to_all(copies, 'dom', 0, 0, axis_index_groups=far)  11.6 us
    all_to_all x1, starting transfers between devices, sum_devices(): return lax.all_to_all(copies, 'dom', 0, 0, axis_index_groups=far)  7.24 us
    pallas_call x1, Pallas kernels, shards(): pl.pallas_call(functools.partial(setup_kernel, dom_count=lax.axis_size('d...  6.76 us
    pallas_call x4, Pallas kernels, shards(): pl.pallas_call(functools.partial(even_kernel, last_pair, len(bases)), out...  3.47 us
    pallas_call x4, Pallas kernels, shards(): pl.pallas_call(functools.partial(odd_kernel, first_pair), out_shape=shape...  2.71 us
  transfers between devices with their start and end apart: 26, of which 8 were waited for; matrix products, arithmetic and copies ran while one was open for 0% of the time, Pallas kernels for 3%

profile of v7, /device:TPU:1, one launch (start us, length us, event | category | flops | bytes accessed | tf_op | source)
XLA Modules:
  0.0 127.4 jit_solution(12860595625147209261)
XLA Ops:
  0.6 6.8 %setup_blocks.1 = (bf16[20,162,162]{2,1,0:T(8,128)(2,1)S(1)}, bf16[20,162,162]{2,1,0:T(8,128)(2,1)S(1)}, bf16[4,162,162]{2,1,0:T(8,128)(2,1)S(1)}, bf16[4,162,16...) custom-call(s32[4,6]{1,0:T(4,128)} %nbr_ref.1, ...), custom_call_target="tpu_custom_call" | custom-call | tf_op jit(solution)/shard_map/setup_blocks/pallas_call | solution.py:776
  7.4 2.7 %collective-permute-start.36 = (f32[616,128]{1,0:T(8,128)S(1)}, f32[616,128]{1,0:T(8,128)S(1)}, u32[]{:S(2)}, u32[]{:S(2)}) collective-permute-start(f32[616,128]{1,0:T(8,128)S(1)} %get-tuple-element.93), channel_id=1, source_target_pairs={{0,1},{1,2},{2,3},{3,4},{4,5},{5,6},{6,7},{7,0},{8,9},{9,10},{10,1... | collective-permute-start | bytes 946184 | tf_op jit(solution)/shard_map/ppermute | solution.py:753
  10.1 4.2 %collective-permute-start.37 = (f32[616,128]{1,0:T(8,128)S(1)}, f32[616,128]{1,0:T(8,128)S(1)}, u32[]{:S(2)}, u32[]{:S(2)}) collective-permute-start(f32[616,128]{1,0:T(8,128)S(1)} %get-tuple-element.94), channel_id=1, source_target_pairs={{0,7},{1,0},{2,1},{3,2},{4,3},{5,4},{6,5},{7,6},{8,15},{9,8},{10,9... | collective-permute-start | bytes 946184 | tf_op jit(solution)/shard_map/ppermute | solution.py:753
  14.3 9.0 %collective-permute-start.39 = (f32[632,128]{1,0:T(8,128)S(1)}, f32[632,128]{1,0:T(8,128)S(1)}, u32[]{:S(2)}, u32[]{:S(2)}) collective-permute-start(f32[632,128]{1,0:T(8,128)S(1)} %get-tuple-element.97), channel_id=1, source_target_pairs={{0,504},{8,0},{16,8},{24,16},{32,24},{40,32},{48,40},{56,48},{64,5... | collective-permute-start | bytes 970760 | tf_op jit(solution)/shard_map/ppermute | solution.py:753
  23.4 1.9 %collective-permute-start.40 = (f32[504,128]{1,0:T(8,128)S(1)}, f32[504,128]{1,0:T(8,128)S(1)}, u32[]{:S(2)}, u32[]{:S(2)}) collective-permute-start(f32[504,128]{1,0:T(8,128)S(1)} %get-tuple-element.100), channel_id=1, source_target_pairs={{0,8},{8,16},{16,24},{24,32},{32,40},{40,48},{48,56},{56,64},{64,7... | collective-permute-start | bytes 774152 | tf_op jit(solution)/shard_map/ppermute | solution.py:753
  25.3 0.0 collective-permute-done.37.next_ref.refs_3_
  25.3 0.1 middle_part_0.1
  25.5 1.9 %collective-permute-start.38 = (f32[128,128]{1,0:T(8,128)S(1)}, f32[128,128]{1,0:T(8,128)S(1)}, u32[]{:S(2)}, u32[]{:S(2)}) collective-permute-start(f32[128,128]{1,0:T(8,128)S(1)} %get-tuple-element.96), channel_id=1, source_target_pairs={{0,8},{8,16},{16,24},{24,32},{32,40},{40,48},{48,56},{56,64},{64,7... | collective-permute-start | bytes 196616 | tf_op jit(solution)/shard_map/ppermute | solution.py:753
  27.4 1.0 collective-permute-done.39.refs_5_.dom_ref
  28.4 0.1 relay_part_0.1
  28.5 4.0 %collective-permute-start.41 = (f32[48,128]{1,0:T(8,128)S(1)}, f32[48,128]{1,0:T(8,128)S(1)}, u32[]{:S(2)}, u32[]{:S(2)}) collective-permute-start(f32[48,128]{1,0:T(8,128)S(1)} %get-tuple-element.102), channel_id=1, source_target_pairs={{0,1},{1,2},{2,3},{3,4},{4,5},{5,6},{6,7},{7,0},{8,9},{9,10},{10,1... | collective-permute-start | bytes 73736 | tf_op jit(solution)/shard_map/ppermute | solution.py:753
  32.6 0.0 collective-permute-start.42
  32.6 1.6 %collective-permute-done.40.refs_8_ = f32[504,128]{1,0:T(8,128)S(1)} collective-permute-done((f32[504,128]{1,0:T(8,128)S(1)}, f32[504,128]{1,0:T(8,128)S(1)}, u32[]{:S(2)}, u32[]{:S(2)}) %collective-permute-start.40) | collective-permute-done | bytes 258080 | tf_op jit(solution)/shard_map/ppermute | solution.py:753
  34.2 1.4 %collective-permute-done.38.refs_4_ = f32[128,128]{1,0:T(8,128)S(1)} collective-permute-done((f32[128,128]{1,0:T(8,128)S(1)}, f32[128,128]{1,0:T(8,128)S(1)}, u32[]{:S(2)}, u32[]{:S(2)}) %collective-permute-start.38) | collective-permute-done | bytes 65568 | tf_op jit(solution)/shard_map/ppermute | solution.py:753
  35.6 0.7 odd_part_0.1
  36.3 0.0 collective-permute-done.41.refs_1_
  36.3 0.9 even_part_0.1
  37.2 4.3 %collective-permute-start.43 = (f32[112,128]{1,0:T(8,128)S(1)}, f32[112,128]{1,0:T(8,128)S(1)}, u32[]{:S(2)}, u32[]{:S(2)}) collective-permute-start(f32[112,128]{1,0:T(8,128)S(1)} %get-tuple-element.108), channel_id=1, source_target_pairs={{0,1},{1,2},{2,3},{3,4},{4,5},{5,6},{6,7},{7,0},{8,9},{9,10},{10,1... | collective-permute-start | bytes 172040 | tf_op jit(solution)/shard_map/ppermute | solution.py:753
  41.5 3.1 %collective-permute-start.46 = (f32[128,128]{1,0:T(8,128)S(1)}, f32[128,128]{1,0:T(8,128)S(1)}, u32[]{:S(2)}, u32[]{:S(2)}) collective-permute-start(f32[128,128]{1,0:T(8,128)S(1)} %get-tuple-element.112), channel_id=1, source_target_pairs={{0,504},{8,0},{16,8},{24,16},{32,24},{40,32},{48,40},{56,48},{64,5... | collective-permute-start | bytes 196616 | tf_op jit(solution)/shard_map/ppermute | solution.py:753
  44.6 0.4 collective-permute-done.44.next_ref.refs_3_
  45.1 0.1 middle_part_1.1
  45.2 1.9 %collective-permute-start.45 = (f32[128,128]{1,0:T(8,128)S(1)}, f32[128,128]{1,0:T(8,128)S(1)}, u32[]{:S(2)}, u32[]{:S(2)}) collective-permute-start(f32[128,128]{1,0:T(8,128)S(1)} %get-tuple-element.111), channel_id=1, source_target_pairs={{0,8},{8,16},{16,24},{24,32},{32,40},{40,48},{48,56},{56,64},{64,7... | collective-permute-start | bytes 196616 | tf_op jit(solution)/shard_map/ppermute | solution.py:753
  47.1 0.1 relay_part_1.1
  47.3 2.2 %collective-permute-start.47 = (f32[48,128]{1,0:T(8,128)S(1)}, f32[48,128]{1,0:T(8,128)S(1)}, u32[]{:S(2)}, u32[]{:S(2)}) collective-permute-start(f32[48,128]{1,0:T(8,128)S(1)} %get-tuple-element.114), channel_id=1, source_target_pairs={{0,1},{1,2},{2,3},{3,4},{4,5},{5,6},{6,7},{7,0},{8,9},{9,10},{10,1... | collective-permute-start | bytes 73736 | tf_op jit(solution)/shard_map/ppermute | solution.py:753
  49.5 0.1 collective-permute-start.48
  49.6 4.0 %collective-permute-done.45.refs_4_ = f32[128,128]{1,0:T(8,128)S(1)} collective-permute-done((f32[128,128]{1,0:T(8,128)S(1)}, f32[128,128]{1,0:T(8,128)S(1)}, u32[]{:S(2)}, u32[]{:S(2)}) %collective-permute-start.45) | collective-permute-done | bytes 65568 | tf_op jit(solution)/shard_map/ppermute | solution.py:753
  53.5 0.7 odd_part_1.1
  54.2 0.9 even_part_1.1
  55.1 2.3 %collective-permute-start.49 = (f32[112,128]{1,0:T(8,128)S(1)}, f32[112,128]{1,0:T(8,128)S(1)}, u32[]{:S(2)}, u32[]{:S(2)}) collective-permute-start(f32[112,128]{1,0:T(8,128)S(1)} %get-tuple-element.118), channel_id=1, source_target_pairs={{0,1},{1,2},{2,3},{3,4},{4,5},{5,6},{6,7},{7,0},{8,9},{9,10},{10,1... | collective-permute-start | bytes 172040 | tf_op jit(solution)/shard_map/ppermute | solution.py:753
  57.4 1.1 collective-permute-start.50
  58.5 3.5 %collective-permute-start.52 = (f32[128,128]{1,0:T(8,128)S(1)}, f32[128,128]{1,0:T(8,128)S(1)}, u32[]{:S(2)}, u32[]{:S(2)}) collective-permute-start(f32[128,128]{1,0:T(8,128)S(1)} %get-tuple-element.122), channel_id=1, source_target_pairs={{0,504},{8,0},{16,8},{24,16},{32,24},{40,32},{48,40},{56,48},{64,5... | collective-permute-start | bytes 196616 | tf_op jit(solution)/shard_map/ppermute | solution.py:753
  62.0 0.1 middle_part_2.1
  62.2 1.9 %collective-permute-start.51 = (f32[128,128]{1,0:T(8,128)S(1)}, f32[128,128]{1,0:T(8,128)S(1)}, u32[]{:S(2)}, u32[]{:S(2)}) collective-permute-start(f32[128,128]{1,0:T(8,128)S(1)} %get-tuple-element.121), channel_id=1, source_target_pairs={{0,8},{8,16},{16,24},{24,32},{32,40},{40,48},{48,56},{56,64},{64,7... | collective-permute-start | bytes 196616 | tf_op jit(solution)/shard_map/ppermute | solution.py:753
  64.1 0.1 relay_part_2.1
  64.2 1.2 collective-permute-start.53
  65.4 2.3 %collective-permute-start.54 = (f32[48,128]{1,0:T(8,128)S(1)}, f32[48,128]{1,0:T(8,128)S(1)}, u32[]{:S(2)}, u32[]{:S(2)}) collective-permute-start(f32[48,128]{1,0:T(8,128)S(1)} %get-tuple-element.125), channel_id=1, source_target_pairs={{0,7},{1,0},{2,1},{3,2},{4,3},{5,4},{6,5},{7,6},{8,15},{9,8},{10,9... | collective-permute-start | bytes 73736 | tf_op jit(solution)/shard_map/ppermute | solution.py:753
  67.8 2.7 %collective-permute-done.51.refs_4_ = f32[128,128]{1,0:T(8,128)S(1)} collective-permute-done((f32[128,128]{1,0:T(8,128)S(1)}, f32[128,128]{1,0:T(8,128)S(1)}, u32[]{:S(2)}, u32[]{:S(2)}) %collective-permute-start.51) | collective-permute-done | bytes 65568 | tf_op jit(solution)/shard_map/ppermute | solution.py:753
  70.5 0.7 odd_part_2.1
  71.1 0.9 even_part_2.1
  72.0 1.2 collective-permute-start.55
  73.2 3.2 %collective-permute-start.56 = (f32[112,128]{1,0:T(8,128)S(1)}, f32[112,128]{1,0:T(8,128)S(1)}, u32[]{:S(2)}, u32[]{:S(2)}) collective-permute-start(f32[112,128]{1,0:T(8,128)S(1)} %get-tuple-element.129), channel_id=1, source_target_pairs={{0,7},{1,0},{2,1},{3,2},{4,3},{5,4},{6,5},{7,6},{8,15},{9,8},{10,9... | collective-permute-start | bytes 172040 | tf_op jit(solution)/shard_map/ppermute | solution.py:753
  76.4 3.5 %collective-permute-start.58 = (f32[128,128]{1,0:T(8,128)S(1)}, f32[128,128]{1,0:T(8,128)S(1)}, u32[]{:S(2)}, u32[]{:S(2)}) collective-permute-start(f32[128,128]{1,0:T(8,128)S(1)} %get-tuple-element.132), channel_id=1, source_target_pairs={{0,504},{8,0},{16,8},{24,16},{32,24},{40,32},{48,40},{56,48},{64,5... | collective-permute-start | bytes 196616 | tf_op jit(solution)/shard_map/ppermute | solution.py:753
  79.9 0.1 middle_part_3.1
  80.1 1.9 %collective-permute-start.57 = (f32[128,128]{1,0:T(8,128)S(1)}, f32[128,128]{1,0:T(8,128)S(1)}, u32[]{:S(2)}, u32[]{:S(2)}) collective-permute-start(f32[128,128]{1,0:T(8,128)S(1)} %get-tuple-element.131), channel_id=1, source_target_pairs={{0,8},{8,16},{16,24},{24,32},{32,40},{40,48},{48,56},{56,64},{64,7... | collective-permute-start | bytes 196616 | tf_op jit(solution)/shard_map/ppermute | solution.py:753
  82.0 0.1 relay_part_3.1
  82.1 3.5 %collective-permute-start.60 = (f32[48,128]{1,0:T(8,128)S(1)}, f32[48,128]{1,0:T(8,128)S(1)}, u32[]{:S(2)}, u32[]{:S(2)}) collective-permute-start(f32[48,128]{1,0:T(8,128)S(1)} %get-tuple-element.135), channel_id=1, source_target_pairs={{0,7},{1,0},{2,1},{3,2},{4,3},{5,4},{6,5},{7,6},{8,15},{9,8},{10,9... | collective-permute-start | bytes 73736 | tf_op jit(solution)/shard_map/ppermute | solution.py:753
  85.7 0.1 gram_part_0.1.refs_4_
  85.7 0.1 gram_part_1.1.refs_6_
  85.9 0.1 gram_part_2.1.refs_8_
  86.0 0.0 copy-start.1
  86.0 0.0 copy-start.2
  86.0 0.0 copy-start.3
  86.0 0.0 copy-start.6
  86.0 0.0 copy-start.7
  86.1 2.3 %collective-permute-done.57.refs_4_ = f32[128,128]{1,0:T(8,128)S(1)} collective-permute-done((f32[128,128]{1,0:T(8,128)S(1)}, f32[128,128]{1,0:T(8,128)S(1)}, u32[]{:S(2)}, u32[]{:S(2)}) %collective-permute-start.57) | collective-permute-done | bytes 65568 | tf_op jit(solution)/shard_map/ppermute | solution.py:753
  88.4 0.7 odd_part_3.1
  89.0 0.2 gram_part_3.1.refs_13_
  89.2 0.9 even_part_3.1
  90.1 14.8 %all_to_all.10.parts_ref = f32[32,8,128]{2,1,0:T(8,128)S(1)} all-to-all(f32[32,8,128]{2,1,0:T(8,128)S(1)} %get-tuple-element.144), channel_id=1, replica_groups={{0,1,2,3,4,5,6,7,8,9,10,11,12,13,14,15,16,17,18,19,20,21,22,23,24,25,26..., dimensions={0} | all-to-all | bytes 262144 | tf_op jit(solution)/shard_map/all_to_all | solution.py:739
  104.9 0.7 sum_near.1
  105.6 7.2 %all-to-all-start.1 = ((f32[16,8,128]{2,1,0:T(8,128)}), f32[16,8,128]{2,1,0:T(8,128)S(1)}, u32[]{:S(2)}, u32[]{:S(2)}) async-start(f32[16,8,128]{2,1,0:T(8,128)} %sum_near.1), calls=%async_computation.1 | async-start | bytes 131072 | tf_op jit(solution)/shard_map/all_to_all | solution.py:748
  112.8 11.6 %all-to-all-done.1.refs_0_ = f32[16,8,128]{2,1,0:T(8,128)S(1)} async-done(((f32[16,8,128]{2,1,0:T(8,128)}), f32[16,8,128]{2,1,0:T(8,128)S(1)}, u32[]{:S(2)}, u32[]{:S(2)}) %all-to-all-start.1) | async-done | bytes 65568 | tf_op jit(solution)/shard_map/all_to_all | solution.py:748
  124.4 1.8 %finish_part.1 = (f32[16,4,162]{2,1,0:T(4,128)}, f32[1,16]{1,0:T(1,128)}, s32[1]{0:T(128)}) custom-call(f32[16,8,128]{2,1,0:T(8,128)S(1)} %all-to-all-done.1.refs_0_, f32[4,16,162]{2,1,0:T(8,128)S(1)} %get-tuple-element.136.refs_0_.refs_5_.refs_1_, f32[4,16,162]{2,1,0:T(8,128)S(1)} %get-tuple-element.137.refs_1_.refs_6_.refs_2_, ...), custom_call_target="tpu_custom_call" | custom-call | tf_op jit(solution)/shard_map/finish_part/pallas_call | solution.py:892
  127.0 0.2 conditional.1
  (23 shorter events, 0.1 us)
Async XLA Ops:
  7.4 17.9 %collective-permute-start.36 = (f32[616,128]{1,0:T(8,128)S(1)}, f32[616,128]{1,0:T(8,128)S(1)}, u32[]{:S(2)}, u32[]{:S(2)}) collective-permute-start(f32[616,128]{1,0:T(8,128)S(1)} %get-tuple-element.93), channel_id=1, source_target_pairs={{0,1},{1,2},{2,3},{3,4},{4,5},{5,6},{6,7},{7,0},{8,9},{9,10},{10,1... | collective-permute-start | bytes 946184 | tf_op jit(solution)/shard_map/ppermute | solution.py:753
  10.1 15.2 %collective-permute-start.37 = (f32[616,128]{1,0:T(8,128)S(1)}, f32[616,128]{1,0:T(8,128)S(1)}, u32[]{:S(2)}, u32[]{:S(2)}) collective-permute-start(f32[616,128]{1,0:T(8,128)S(1)} %get-tuple-element.94), channel_id=1, source_target_pairs={{0,7},{1,0},{2,1},{3,2},{4,3},{5,4},{6,5},{7,6},{8,15},{9,8},{10,9... | collective-permute-start | bytes 946184 | tf_op jit(solution)/shard_map/ppermute | solution.py:753
  14.3 14.1 %collective-permute-start.39 = (f32[632,128]{1,0:T(8,128)S(1)}, f32[632,128]{1,0:T(8,128)S(1)}, u32[]{:S(2)}, u32[]{:S(2)}) collective-permute-start(f32[632,128]{1,0:T(8,128)S(1)} %get-tuple-element.97), channel_id=1, source_target_pairs={{0,504},{8,0},{16,8},{24,16},{32,24},{40,32},{48,40},{56,48},{64,5... | collective-permute-start | bytes 970760 | tf_op jit(solution)/shard_map/ppermute | solution.py:753
  23.4 10.8 %collective-permute-start.40 = (f32[504,128]{1,0:T(8,128)S(1)}, f32[504,128]{1,0:T(8,128)S(1)}, u32[]{:S(2)}, u32[]{:S(2)}) collective-permute-start(f32[504,128]{1,0:T(8,128)S(1)} %get-tuple-element.100), channel_id=1, source_target_pairs={{0,8},{8,16},{16,24},{24,32},{32,40},{40,48},{48,56},{56,64},{64,7... | collective-permute-start | bytes 774152 | tf_op jit(solution)/shard_map/ppermute | solution.py:753
  25.5 10.1 %collective-permute-start.38 = (f32[128,128]{1,0:T(8,128)S(1)}, f32[128,128]{1,0:T(8,128)S(1)}, u32[]{:S(2)}, u32[]{:S(2)}) collective-permute-start(f32[128,128]{1,0:T(8,128)S(1)} %get-tuple-element.96), channel_id=1, source_target_pairs={{0,8},{8,16},{16,24},{24,32},{32,40},{40,48},{48,56},{56,64},{64,7... | collective-permute-start | bytes 196616 | tf_op jit(solution)/shard_map/ppermute | solution.py:753
  28.5 7.7 %collective-permute-start.41 = (f32[48,128]{1,0:T(8,128)S(1)}, f32[48,128]{1,0:T(8,128)S(1)}, u32[]{:S(2)}, u32[]{:S(2)}) collective-permute-start(f32[48,128]{1,0:T(8,128)S(1)} %get-tuple-element.102), channel_id=1, source_target_pairs={{0,1},{1,2},{2,3},{3,4},{4,5},{5,6},{6,7},{7,0},{8,9},{9,10},{10,1... | collective-permute-start | bytes 73736 | tf_op jit(solution)/shard_map/ppermute | solution.py:753
  32.6 3.7 %collective-permute-start.42 = (f32[48,128]{1,0:T(8,128)S(1)}, f32[48,128]{1,0:T(8,128)S(1)}, u32[]{:S(2)}, u32[]{:S(2)}) collective-permute-start(f32[48,128]{1,0:T(8,128)S(1)} %get-tuple-element.103), channel_id=1, source_target_pairs={{0,7},{1,0},{2,1},{3,2},{4,3},{5,4},{6,5},{7,6},{8,15},{9,8},{10,9... | collective-permute-start | bytes 73736 | tf_op jit(solution)/shard_map/ppermute | solution.py:753
  37.2 7.5 %collective-permute-start.43 = (f32[112,128]{1,0:T(8,128)S(1)}, f32[112,128]{1,0:T(8,128)S(1)}, u32[]{:S(2)}, u32[]{:S(2)}) collective-permute-start(f32[112,128]{1,0:T(8,128)S(1)} %get-tuple-element.108), channel_id=1, source_target_pairs={{0,1},{1,2},{2,3},{3,4},{4,5},{5,6},{6,7},{7,0},{8,9},{9,10},{10,1... | collective-permute-start | bytes 172040 | tf_op jit(solution)/shard_map/ppermute | solution.py:753
  41.5 3.6 %collective-permute-start.44 = (f32[112,128]{1,0:T(8,128)S(1)}, f32[112,128]{1,0:T(8,128)S(1)}, u32[]{:S(2)}, u32[]{:S(2)}) collective-permute-start(f32[112,128]{1,0:T(8,128)S(1)} %get-tuple-element.109), channel_id=1, source_target_pairs={{0,7},{1,0},{2,1},{3,2},{4,3},{5,4},{6,5},{7,6},{8,15},{9,8},{10,9... | collective-permute-start | bytes 172040 | tf_op jit(solution)/shard_map/ppermute | solution.py:753
  41.5 5.7 %collective-permute-start.46 = (f32[128,128]{1,0:T(8,128)S(1)}, f32[128,128]{1,0:T(8,128)S(1)}, u32[]{:S(2)}, u32[]{:S(2)}) collective-permute-start(f32[128,128]{1,0:T(8,128)S(1)} %get-tuple-element.112), channel_id=1, source_target_pairs={{0,504},{8,0},{16,8},{24,16},{32,24},{40,32},{48,40},{56,48},{64,5... | collective-permute-start | bytes 196616 | tf_op jit(solution)/shard_map/ppermute | solution.py:753
  45.2 8.3 %collective-permute-start.45 = (f32[128,128]{1,0:T(8,128)S(1)}, f32[128,128]{1,0:T(8,128)S(1)}, u32[]{:S(2)}, u32[]{:S(2)}) collective-permute-start(f32[128,128]{1,0:T(8,128)S(1)} %get-tuple-element.111), channel_id=1, source_target_pairs={{0,8},{8,16},{16,24},{24,32},{32,40},{40,48},{48,56},{56,64},{64,7... | collective-permute-start | bytes 196616 | tf_op jit(solution)/shard_map/ppermute | solution.py:753
  47.3 6.9 %collective-permute-start.47 = (f32[48,128]{1,0:T(8,128)S(1)}, f32[48,128]{1,0:T(8,128)S(1)}, u32[]{:S(2)}, u32[]{:S(2)}) collective-permute-start(f32[48,128]{1,0:T(8,128)S(1)} %get-tuple-element.114), channel_id=1, source_target_pairs={{0,1},{1,2},{2,3},{3,4},{4,5},{5,6},{6,7},{7,0},{8,9},{9,10},{10,1... | collective-permute-start | bytes 73736 | tf_op jit(solution)/shard_map/ppermute | solution.py:753
  49.5 4.7 %collective-permute-start.48 = (f32[48,128]{1,0:T(8,128)S(1)}, f32[48,128]{1,0:T(8,128)S(1)}, u32[]{:S(2)}, u32[]{:S(2)}) collective-permute-start(f32[48,128]{1,0:T(8,128)S(1)} %get-tuple-element.115), channel_id=1, source_target_pairs={{0,7},{1,0},{2,1},{3,2},{4,3},{5,4},{6,5},{7,6},{8,15},{9,8},{10,9... | collective-permute-start | bytes 73736 | tf_op jit(solution)/shard_map/ppermute | solution.py:753
  55.1 6.9 %collective-permute-start.49 = (f32[112,128]{1,0:T(8,128)S(1)}, f32[112,128]{1,0:T(8,128)S(1)}, u32[]{:S(2)}, u32[]{:S(2)}) collective-permute-start(f32[112,128]{1,0:T(8,128)S(1)} %get-tuple-element.118), channel_id=1, source_target_pairs={{0,1},{1,2},{2,3},{3,4},{4,5},{5,6},{6,7},{7,0},{8,9},{9,10},{10,1... | collective-permute-start | bytes 172040 | tf_op jit(solution)/shard_map/ppermute | solution.py:753
  57.4 4.6 %collective-permute-start.50 = (f32[112,128]{1,0:T(8,128)S(1)}, f32[112,128]{1,0:T(8,128)S(1)}, u32[]{:S(2)}, u32[]{:S(2)}) collective-permute-start(f32[112,128]{1,0:T(8,128)S(1)} %get-tuple-element.119), channel_id=1, source_target_pairs={{0,7},{1,0},{2,1},{3,2},{4,3},{5,4},{6,5},{7,6},{8,15},{9,8},{10,9... | collective-permute-start | bytes 172040 | tf_op jit(solution)/shard_map/ppermute | solution.py:753
  58.5 5.6 %collective-permute-start.52 = (f32[128,128]{1,0:T(8,128)S(1)}, f32[128,128]{1,0:T(8,128)S(1)}, u32[]{:S(2)}, u32[]{:S(2)}) collective-permute-start(f32[128,128]{1,0:T(8,128)S(1)} %get-tuple-element.122), channel_id=1, source_target_pairs={{0,504},{8,0},{16,8},{24,16},{32,24},{40,32},{48,40},{56,48},{64,5... | collective-permute-start | bytes 196616 | tf_op jit(solution)/shard_map/ppermute | solution.py:753
  62.2 8.3 %collective-permute-start.51 = (f32[128,128]{1,0:T(8,128)S(1)}, f32[128,128]{1,0:T(8,128)S(1)}, u32[]{:S(2)}, u32[]{:S(2)}) collective-permute-start(f32[128,128]{1,0:T(8,128)S(1)} %get-tuple-element.121), channel_id=1, source_target_pairs={{0,8},{8,16},{16,24},{24,32},{32,40},{40,48},{48,56},{56,64},{64,7... | collective-permute-start | bytes 196616 | tf_op jit(solution)/shard_map/ppermute | solution.py:753
  64.2 6.9 %collective-permute-start.53 = (f32[48,128]{1,0:T(8,128)S(1)}, f32[48,128]{1,0:T(8,128)S(1)}, u32[]{:S(2)}, u32[]{:S(2)}) collective-permute-start(f32[48,128]{1,0:T(8,128)S(1)} %get-tuple-element.124), channel_id=1, source_target_pairs={{0,1},{1,2},{2,3},{3,4},{4,5},{5,6},{6,7},{7,0},{8,9},{9,10},{10,1... | collective-permute-start | bytes 73736 | tf_op jit(solution)/shard_map/ppermute | solution.py:753
  65.4 5.7 %collective-permute-start.54 = (f32[48,128]{1,0:T(8,128)S(1)}, f32[48,128]{1,0:T(8,128)S(1)}, u32[]{:S(2)}, u32[]{:S(2)}) collective-permute-start(f32[48,128]{1,0:T(8,128)S(1)} %get-tuple-element.125), channel_id=1, source_target_pairs={{0,7},{1,0},{2,1},{3,2},{4,3},{5,4},{6,5},{7,6},{8,15},{9,8},{10,9... | collective-permute-start | bytes 73736 | tf_op jit(solution)/shard_map/ppermute | solution.py:753
  72.0 7.9 %collective-permute-start.55 = (f32[112,128]{1,0:T(8,128)S(1)}, f32[112,128]{1,0:T(8,128)S(1)}, u32[]{:S(2)}, u32[]{:S(2)}) collective-permute-start(f32[112,128]{1,0:T(8,128)S(1)} %get-tuple-element.128), channel_id=1, source_target_pairs={{0,1},{1,2},{2,3},{3,4},{4,5},{5,6},{6,7},{7,0},{8,9},{9,10},{10,1... | collective-permute-start | bytes 172040 | tf_op jit(solution)/shard_map/ppermute | solution.py:753
  73.2 6.7 %collective-permute-start.56 = (f32[112,128]{1,0:T(8,128)S(1)}, f32[112,128]{1,0:T(8,128)S(1)}, u32[]{:S(2)}, u32[]{:S(2)}) collective-permute-start(f32[112,128]{1,0:T(8,128)S(1)} %get-tuple-element.129), channel_id=1, source_target_pairs={{0,7},{1,0},{2,1},{3,2},{4,3},{5,4},{6,5},{7,6},{8,15},{9,8},{10,9... | collective-permute-start | bytes 172040 | tf_op jit(solution)/shard_map/ppermute | solution.py:753
  76.4 5.6 %collective-permute-start.58 = (f32[128,128]{1,0:T(8,128)S(1)}, f32[128,128]{1,0:T(8,128)S(1)}, u32[]{:S(2)}, u32[]{:S(2)}) collective-permute-start(f32[128,128]{1,0:T(8,128)S(1)} %get-tuple-element.132), channel_id=1, source_target_pairs={{0,504},{8,0},{16,8},{24,16},{32,24},{40,32},{48,40},{56,48},{64,5... | collective-permute-start | bytes 196616 | tf_op jit(solution)/shard_map/ppermute | solution.py:753
  80.1 8.3 %collective-permute-start.57 = (f32[128,128]{1,0:T(8,128)S(1)}, f32[128,128]{1,0:T(8,128)S(1)}, u32[]{:S(2)}, u32[]{:S(2)}) collective-permute-start(f32[128,128]{1,0:T(8,128)S(1)} %get-tuple-element.131), channel_id=1, source_target_pairs={{0,8},{8,16},{16,24},{24,32},{32,40},{40,48},{48,56},{56,64},{64,7... | collective-permute-start | bytes 196616 | tf_op jit(solution)/shard_map/ppermute | solution.py:753
  82.1 7.1 %collective-permute-start.59 = (f32[48,128]{1,0:T(8,128)S(1)}, f32[48,128]{1,0:T(8,128)S(1)}, u32[]{:S(2)}, u32[]{:S(2)}) collective-permute-start(f32[48,128]{1,0:T(8,128)S(1)} %get-tuple-element.134), channel_id=1, source_target_pairs={{0,1},{1,2},{2,3},{3,4},{4,5},{5,6},{6,7},{7,0},{8,9},{9,10},{10,1... | collective-permute-start | bytes 73736 | tf_op jit(solution)/shard_map/ppermute | solution.py:753
  82.1 7.1 %collective-permute-start.60 = (f32[48,128]{1,0:T(8,128)S(1)}, f32[48,128]{1,0:T(8,128)S(1)}, u32[]{:S(2)}, u32[]{:S(2)}) collective-permute-start(f32[48,128]{1,0:T(8,128)S(1)} %get-tuple-element.135), channel_id=1, source_target_pairs={{0,7},{1,0},{2,1},{3,2},{4,3},{5,4},{6,5},{7,6},{8,15},{9,8},{10,9... | collective-permute-start | bytes 73736 | tf_op jit(solution)/shard_map/ppermute | solution.py:753
  86.0 40.9 %copy-start.1 = (f32[16,4,162]{2,1,0:T(4,128)S(1)}, f32[16,4,162]{2,1,0:T(4,128)}, u32[]{:S(2)}) copy-start(f32[16,4,162]{2,1,0:T(4,128)} %src_ref.1) | copy-start | bytes 124420
  86.0 40.9 %copy-start.2 = (f32[4,162,162]{2,0,1:T(4,128)S(1)}, f32[4,162,162]{2,0,1:T(4,128)}, u32[]{:S(2)}) copy-start(f32[4,162,162]{2,0,1:T(4,128)} %param.14) | copy-start | bytes 1259716
  86.0 40.9 %copy-start.3 = (s32[4,6]{1,0:T(4,128)S(1)}, s32[4,6]{1,0:T(4,128)}, u32[]{:S(2)}) copy-start(s32[4,6]{1,0:T(4,128)} %nbr_ref.1) | copy-start | bytes 292
  86.0 40.9 %copy-start.6 = (s32[4,6]{1,0:T(4,128)S(1)}, s32[4,6]{1,0:T(4,128)}, u32[]{:S(2)}) copy-start(s32[4,6]{1,0:T(4,128)} %flag_ref.1) | copy-start | bytes 292
  86.0 40.9 %copy-start.7 = (s32[4,6]{1,0:T(4,128)S(1)}, s32[4,6]{1,0:T(4,128)}, u32[]{:S(2)}) copy-start(s32[4,6]{1,0:T(4,128)} %param.17) | copy-start | bytes 292
  105.6 18.8 %all-to-all-start.1 = ((f32[16,8,128]{2,1,0:T(8,128)}), f32[16,8,128]{2,1,0:T(8,128)S(1)}, u32[]{:S(2)}, u32[]{:S(2)}) async-start(f32[16,8,128]{2,1,0:T(8,128)} %sum_near.1), calls=%async_computation.1 | async-start | bytes 131072 | tf_op jit(solution)/shard_map/all_to_all | solution.py:748

commit v8 on v7

--- a/solution.py
+++ b/solution.py
@@ -471,7 +471,7 @@
 RELAYED = 2
 
 
-def middle_kernel(first, local_ref, outward_ref, prev_ref, next_ref, sum_ref, dom_next_ref):
+def middle_kernel(first, local_ref, outward_ref, next_ref, prev_ref, sum_ref, dom_next_ref):
     rows = local_ref.shape[1]
     tail = local_ref.shape[2] - 128
 
@@ -500,7 +500,7 @@
 
 
 def odd_kernel(first_pair, *refs):
-    sum_ref, outward_ref, blk_prev_ref, blk_next_ref, dom_prev_ref, dom_next_ref = refs[:6]
+    sum_ref, outward_ref, blk_next_ref, blk_prev_ref, dom_prev_ref, dom_next_ref = refs[:6]
     high_ref, low_ref = refs[6:8]
     rows = sum_ref.shape[1]
     width = sum_ref.shape[2]
@@ -559,7 +559,7 @@
 
 
 def even_kernel(last_pair, older_count, *refs):
-    part_ref, turn_prev_ref, turn_next_ref, in_high_ref, in_low_ref = refs[:5]
+    part_ref, turn_next_ref, turn_prev_ref, in_high_ref, in_low_ref = refs[:5]
     refs = refs[5:]
     rows = part_ref.shape[1]
     tail = part_ref.shape[2] - 128
@@ -756,7 +756,9 @@
 
 
 def both_ways(to_prev, to_next, axis):
-    return rotated(to_next, axis, 1), rotated(to_prev, axis, -1)
+    from_next = rotated(to_prev, axis, -1)
+    from_prev = rotated(to_next, axis, 1)
+    return from_next, from_prev
 
 
 def shards(adjoint_source, diag_blocks, face_blocks, neighbors, partner, flags):

time: 128 us -> 126 us (0.984)
  waiting for transfers between devices: 25.1 us -> 30.3 us
  starting transfers between devices: 68.3 us -> 63.4 us
  blocking collectives: 14.8 us -> 12.4 us
    ppermute x25, waiting for transfers between devices: 13.5 us -> 18.7 us  [rotated(): lax.ppermute(value, axis, [(source, (source + steps) % count) for source...]
    ppermute x25, starting transfers between devices: 61.1 us -> 56.8 us  [rotated(): lax.ppermute(value, axis, [(source, (source + steps) % count) for source...]
    all_to_all x1, blocking collectives: 14.8 us -> 12.4 us  [sum_devices(): parts = lax.all_to_all(copies, ('dom', 'blk'), 0, 0, axis_index_groups=near)]
  transfers between devices with their start and end apart: 26 -> 26, of which waited for: 8 -> 7; matrix products, arithmetic and copies ran while one was open for 0% -> 0% of each run, Pallas kernels for 3% -> 3%
where the time goes in v8:
time: 126 us; the launch traced here: 125 us
  starting transfers between devices  63.4 us (50%)
  waiting for transfers between devices  30.3 us (24%)
  Pallas kernels  16.9 us (13%)
  blocking collectives  12.4 us (10%)
  between operations  1.83 us (1%)
    ppermute x25, starting transfers between devices, rotated(): lax.ppermute(value, axis, [(source, (source + steps) % count) for source...  56.8 us
    ppermute x25, waiting for transfers between devices, rotated(): lax.ppermute(value, axis, [(source, (source + steps) % count) for source...  18.7 us
    all_to_all x1, blocking collectives, sum_devices(): parts = lax.all_to_all(copies, ('dom', 'blk'), 0, 0, axis_index_groups=near)  12.4 us
    all_to_all x1, waiting for transfers between devices, sum_devices(): return lax.all_to_all(copies, 'dom', 0, 0, axis_index_groups=far)  11.6 us
    pallas_call x1, Pallas kernels, shards(): pl.pallas_call(functools.partial(setup_kernel, dom_count=lax.axis_size('d...  6.71 us
    all_to_all x1, starting transfers between devices, sum_devices(): return lax.all_to_all(copies, 'dom', 0, 0, axis_index_groups=far)  6.59 us
    pallas_call x4, Pallas kernels, shards(): pl.pallas_call(functools.partial(even_kernel, last_pair, len(bases)), out...  3.47 us
    pallas_call x4, Pallas kernels, shards(): pl.pallas_call(functools.partial(odd_kernel, first_pair), out_shape=shape...  2.71 us
  transfers between devices with their start and end apart: 26, of which 7 were waited for; matrix products, arithmetic and copies ran while one was open for 0% of the time, Pallas kernels for 3%

profile of v8, /device:TPU:1, one launch (start us, length us, event | category | flops | bytes accessed | tf_op | source)
XLA Modules:
  0.0 125.1 jit_solution(16165561516321768684)
XLA Ops:
  0.6 6.7 %setup_blocks.1 = (bf16[20,162,162]{2,1,0:T(8,128)(2,1)S(1)}, bf16[20,162,162]{2,1,0:T(8,128)(2,1)S(1)}, bf16[4,162,162]{2,1,0:T(8,128)(2,1)S(1)}, bf16[4,162,16...) custom-call(s32[4,6]{1,0:T(4,128)} %nbr_ref.1, ...), custom_call_target="tpu_custom_call" | custom-call | tf_op jit(solution)/shard_map/setup_blocks/pallas_call | solution.py:778
  7.3 7.1 %collective-permute-start.36 = (f32[616,128]{1,0:T(8,128)S(1)}, f32[616,128]{1,0:T(8,128)S(1)}, u32[]{:S(2)}, u32[]{:S(2)}) collective-permute-start(f32[616,128]{1,0:T(8,128)S(1)} %get-tuple-element.93), channel_id=1, source_target_pairs={{0,7},{1,0},{2,1},{3,2},{4,3},{5,4},{6,5},{7,6},{8,15},{9,8},{10,9... | collective-permute-start | bytes 946184 | tf_op jit(solution)/shard_map/ppermute | solution.py:753
  14.4 0.0 collective-permute-start.37
  14.4 9.0 %collective-permute-start.39 = (f32[632,128]{1,0:T(8,128)S(1)}, f32[632,128]{1,0:T(8,128)S(1)}, u32[]{:S(2)}, u32[]{:S(2)}) collective-permute-start(f32[632,128]{1,0:T(8,128)S(1)} %get-tuple-element.97), channel_id=1, source_target_pairs={{0,504},{8,0},{16,8},{24,16},{32,24},{40,32},{48,40},{56,48},{64,5... | collective-permute-start | bytes 970760 | tf_op jit(solution)/shard_map/ppermute | solution.py:753
  23.4 1.9 %collective-permute-start.40 = (f32[504,128]{1,0:T(8,128)S(1)}, f32[504,128]{1,0:T(8,128)S(1)}, u32[]{:S(2)}, u32[]{:S(2)}) collective-permute-start(f32[504,128]{1,0:T(8,128)S(1)} %get-tuple-element.100), channel_id=1, source_target_pairs={{0,8},{8,16},{16,24},{24,32},{32,40},{40,48},{48,56},{56,64},{64,7... | collective-permute-start | bytes 774152 | tf_op jit(solution)/shard_map/ppermute | solution.py:753
  25.4 0.1 middle_part_0.1
  25.5 1.9 %collective-permute-start.38 = (f32[128,128]{1,0:T(8,128)S(1)}, f32[128,128]{1,0:T(8,128)S(1)}, u32[]{:S(2)}, u32[]{:S(2)}) collective-permute-start(f32[128,128]{1,0:T(8,128)S(1)} %get-tuple-element.96), channel_id=1, source_target_pairs={{0,8},{8,16},{16,24},{24,32},{32,40},{40,48},{48,56},{56,64},{64,7... | collective-permute-start | bytes 196616 | tf_op jit(solution)/shard_map/ppermute | solution.py:753
  27.4 1.6 %collective-permute-done.39.refs_5_.dom_ref = f32[632,128]{1,0:T(8,128)S(1)} collective-permute-done((f32[632,128]{1,0:T(8,128)S(1)}, f32[632,128]{1,0:T(8,128)S(1)}, u32[]{:S(2)}, u32[]{:S(2)}) %collective-permute-start.39) | collective-permute-done | bytes 323616 | tf_op jit(solution)/shard_map/ppermute | solution.py:753
  29.0 0.1 relay_part_0.1
  29.1 2.2 %collective-permute-start.41 = (f32[48,128]{1,0:T(8,128)S(1)}, f32[48,128]{1,0:T(8,128)S(1)}, u32[]{:S(2)}, u32[]{:S(2)}) collective-permute-start(f32[48,128]{1,0:T(8,128)S(1)} %get-tuple-element.102), channel_id=1, source_target_pairs={{0,7},{1,0},{2,1},{3,2},{4,3},{5,4},{6,5},{7,6},{8,15},{9,8},{10,9... | collective-permute-start | bytes 73736 | tf_op jit(solution)/shard_map/ppermute | solution.py:753
  31.4 0.8 collective-permute-start.42
  32.1 2.6 %collective-permute-done.40.refs_8_ = f32[504,128]{1,0:T(8,128)S(1)} collective-permute-done((f32[504,128]{1,0:T(8,128)S(1)}, f32[504,128]{1,0:T(8,128)S(1)}, u32[]{:S(2)}, u32[]{:S(2)}) %collective-permute-start.40) | collective-permute-done | bytes 258080 | tf_op jit(solution)/shard_map/ppermute | solution.py:753
  34.8 1.4 %collective-permute-done.38.refs_4_ = f32[128,128]{1,0:T(8,128)S(1)} collective-permute-done((f32[128,128]{1,0:T(8,128)S(1)}, f32[128,128]{1,0:T(8,128)S(1)}, u32[]{:S(2)}, u32[]{:S(2)}) %collective-permute-start.38) | collective-permute-done | bytes 65568 | tf_op jit(solution)/shard_map/ppermute | solution.py:753
  36.2 0.7 odd_part_0.1
  36.9 0.9 even_part_0.1
  37.7 2.5 %collective-permute-start.43 = (f32[112,128]{1,0:T(8,128)S(1)}, f32[112,128]{1,0:T(8,128)S(1)}, u32[]{:S(2)}, u32[]{:S(2)}) collective-permute-start(f32[112,128]{1,0:T(8,128)S(1)} %get-tuple-element.108), channel_id=1, source_target_pairs={{0,7},{1,0},{2,1},{3,2},{4,3},{5,4},{6,5},{7,6},{8,15},{9,8},{10,9... | collective-permute-start | bytes 172040 | tf_op jit(solution)/shard_map/ppermute | solution.py:753
  40.3 1.1 collective-permute-start.44
  41.4 4.9 %collective-permute-start.46 = (f32[128,128]{1,0:T(8,128)S(1)}, f32[128,128]{1,0:T(8,128)S(1)}, u32[]{:S(2)}, u32[]{:S(2)}) collective-permute-start(f32[128,128]{1,0:T(8,128)S(1)} %get-tuple-element.112), channel_id=1, source_target_pairs={{0,504},{8,0},{16,8},{24,16},{32,24},{40,32},{48,40},{56,48},{64,5... | collective-permute-start | bytes 196616 | tf_op jit(solution)/shard_map/ppermute | solution.py:753
  46.3 0.0 collective-permute-done.43.next_ref.refs_2_
  46.3 0.0 collective-permute-done.44.prev_ref.refs_3_
  46.3 0.1 middle_part_1.1
  46.5 1.9 %collective-permute-start.45 = (f32[128,128]{1,0:T(8,128)S(1)}, f32[128,128]{1,0:T(8,128)S(1)}, u32[]{:S(2)}, u32[]{:S(2)}) collective-permute-start(f32[128,128]{1,0:T(8,128)S(1)} %get-tuple-element.111), channel_id=1, source_target_pairs={{0,8},{8,16},{16,24},{24,32},{32,40},{40,48},{48,56},{56,64},{64,7... | collective-permute-start | bytes 196616 | tf_op jit(solution)/shard_map/ppermute | solution.py:753
  48.4 0.0 collective-permute-done.46.refs_5_.dom_ref
  48.4 0.1 relay_part_1.1
  48.6 1.2 collective-permute-start.47
  49.8 0.5 collective-permute-start.48
  50.3 4.5 %collective-permute-done.45.refs_4_ = f32[128,128]{1,0:T(8,128)S(1)} collective-permute-done((f32[128,128]{1,0:T(8,128)S(1)}, f32[128,128]{1,0:T(8,128)S(1)}, u32[]{:S(2)}, u32[]{:S(2)}) %collective-permute-start.45) | collective-permute-done | bytes 65568 | tf_op jit(solution)/shard_map/ppermute | solution.py:753
  54.8 0.7 odd_part_1.1
  55.5 0.9 even_part_1.1
  56.3 2.4 %collective-permute-start.49 = (f32[112,128]{1,0:T(8,128)S(1)}, f32[112,128]{1,0:T(8,128)S(1)}, u32[]{:S(2)}, u32[]{:S(2)}) collective-permute-start(f32[112,128]{1,0:T(8,128)S(1)} %get-tuple-element.118), channel_id=1, source_target_pairs={{0,7},{1,0},{2,1},{3,2},{4,3},{5,4},{6,5},{7,6},{8,15},{9,8},{10,9... | collective-permute-start | bytes 172040 | tf_op jit(solution)/shard_map/ppermute | solution.py:753
  58.7 4.8 %collective-permute-start.52 = (f32[128,128]{1,0:T(8,128)S(1)}, f32[128,128]{1,0:T(8,128)S(1)}, u32[]{:S(2)}, u32[]{:S(2)}) collective-permute-start(f32[128,128]{1,0:T(8,128)S(1)} %get-tuple-element.122), channel_id=1, source_target_pairs={{0,504},{8,0},{16,8},{24,16},{32,24},{40,32},{48,40},{56,48},{64,5... | collective-permute-start | bytes 196616 | tf_op jit(solution)/shard_map/ppermute | solution.py:753
  63.5 0.1 middle_part_2.1
  63.7 1.9 %collective-permute-start.51 = (f32[128,128]{1,0:T(8,128)S(1)}, f32[128,128]{1,0:T(8,128)S(1)}, u32[]{:S(2)}, u32[]{:S(2)}) collective-permute-start(f32[128,128]{1,0:T(8,128)S(1)} %get-tuple-element.121), channel_id=1, source_target_pairs={{0,8},{8,16},{16,24},{24,32},{32,40},{40,48},{48,56},{56,64},{64,7... | collective-permute-start | bytes 196616 | tf_op jit(solution)/shard_map/ppermute | solution.py:753
  65.6 0.1 relay_part_2.1
  65.8 0.8 collective-permute-start.53
  66.5 1.0 collective-permute-start.54
  67.5 4.5 %collective-permute-done.51.refs_4_ = f32[128,128]{1,0:T(8,128)S(1)} collective-permute-done((f32[128,128]{1,0:T(8,128)S(1)}, f32[128,128]{1,0:T(8,128)S(1)}, u32[]{:S(2)}, u32[]{:S(2)}) %collective-permute-start.51) | collective-permute-done | bytes 65568 | tf_op jit(solution)/shard_map/ppermute | solution.py:753
  72.0 0.7 odd_part_2.1
  72.7 0.9 even_part_2.1
  73.5 1.9 %collective-permute-start.55 = (f32[112,128]{1,0:T(8,128)S(1)}, f32[112,128]{1,0:T(8,128)S(1)}, u32[]{:S(2)}, u32[]{:S(2)}) collective-permute-start(f32[112,128]{1,0:T(8,128)S(1)} %get-tuple-element.128), channel_id=1, source_target_pairs={{0,7},{1,0},{2,1},{3,2},{4,3},{5,4},{6,5},{7,6},{8,15},{9,8},{10,9... | collective-permute-start | bytes 172040 | tf_op jit(solution)/shard_map/ppermute | solution.py:753
  75.5 5.2 %collective-permute-start.58 = (f32[128,128]{1,0:T(8,128)S(1)}, f32[128,128]{1,0:T(8,128)S(1)}, u32[]{:S(2)}, u32[]{:S(2)}) collective-permute-start(f32[128,128]{1,0:T(8,128)S(1)} %get-tuple-element.132), channel_id=1, source_target_pairs={{0,504},{8,0},{16,8},{24,16},{32,24},{40,32},{48,40},{56,48},{64,5... | collective-permute-start | bytes 196616 | tf_op jit(solution)/shard_map/ppermute | solution.py:753
  80.7 0.1 middle_part_3.1
  80.9 1.9 %collective-permute-start.57 = (f32[128,128]{1,0:T(8,128)S(1)}, f32[128,128]{1,0:T(8,128)S(1)}, u32[]{:S(2)}, u32[]{:S(2)}) collective-permute-start(f32[128,128]{1,0:T(8,128)S(1)} %get-tuple-element.131), channel_id=1, source_target_pairs={{0,8},{8,16},{16,24},{24,32},{32,40},{40,48},{48,56},{56,64},{64,7... | collective-permute-start | bytes 196616 | tf_op jit(solution)/shard_map/ppermute | solution.py:753
  82.8 0.1 relay_part_3.1
  83.0 0.8 collective-permute-start.59
  83.7 1.0 collective-permute-start.60
  84.7 0.1 gram_part_0.1.refs_4_
  84.8 0.1 gram_part_1.1.refs_6_
  84.9 0.1 gram_part_2.1.refs_8_
  85.0 0.0 copy-start.1
  85.1 0.0 copy-start.2
  85.1 0.0 copy-start.3
  85.1 0.0 copy-start.6
  85.1 0.0 copy-start.7
  85.1 4.1 %collective-permute-done.57.refs_4_ = f32[128,128]{1,0:T(8,128)S(1)} collective-permute-done((f32[128,128]{1,0:T(8,128)S(1)}, f32[128,128]{1,0:T(8,128)S(1)}, u32[]{:S(2)}, u32[]{:S(2)}) %collective-permute-start.57) | collective-permute-done | bytes 65568 | tf_op jit(solution)/shard_map/ppermute | solution.py:753
  89.2 0.7 odd_part_3.1
  89.9 0.2 gram_part_3.1.refs_13_
  90.1 0.9 even_part_3.1
  90.9 12.4 %all_to_all.10.parts_ref = f32[32,8,128]{2,1,0:T(8,128)S(1)} all-to-all(f32[32,8,128]{2,1,0:T(8,128)S(1)} %get-tuple-element.144), channel_id=1, replica_groups={{0,1,2,3,4,5,6,7,8,9,10,11,12,13,14,15,16,17,18,19,20,21,22,23,24,25,26..., dimensions={0} | all-to-all | bytes 262144 | tf_op jit(solution)/shard_map/all_to_all | solution.py:739
  103.3 0.7 sum_near.1
  104.0 6.6 %all-to-all-start.1 = ((f32[16,8,128]{2,1,0:T(8,128)}), f32[16,8,128]{2,1,0:T(8,128)S(1)}, u32[]{:S(2)}, u32[]{:S(2)}) async-start(f32[16,8,128]{2,1,0:T(8,128)} %sum_near.1), calls=%async_computation.1 | async-start | bytes 131072 | tf_op jit(solution)/shard_map/all_to_all | solution.py:748
  110.6 11.6 %all-to-all-done.1.refs_0_ = f32[16,8,128]{2,1,0:T(8,128)S(1)} async-done(((f32[16,8,128]{2,1,0:T(8,128)}), f32[16,8,128]{2,1,0:T(8,128)S(1)}, u32[]{:S(2)}, u32[]{:S(2)}) %all-to-all-start.1) | async-done | bytes 65568 | tf_op jit(solution)/shard_map/all_to_all | solution.py:748
  122.2 1.8 %finish_part.1 = (f32[16,4,162]{2,1,0:T(4,128)}, f32[1,16]{1,0:T(1,128)}, s32[1]{0:T(128)}) custom-call(f32[16,8,128]{2,1,0:T(8,128)S(1)} %all-to-all-done.1.refs_0_, f32[4,16,162]{2,1,0:T(8,128)S(1)} %get-tuple-element.136.refs_0_.refs_5_.refs_1_, f32[4,16,162]{2,1,0:T(8,128)S(1)} %get-tuple-element.137.refs_1_.refs_6_.refs_2_, ...), custom_call_target="tpu_custom_call" | custom-call | tf_op jit(solution)/shard_map/finish_part/pallas_call | solution.py:894
  124.7 0.3 conditional.1
  (23 shorter events, 0.1 us)
Async XLA Ops:
  7.3 18.0 %collective-permute-start.36 = (f32[616,128]{1,0:T(8,128)S(1)}, f32[616,128]{1,0:T(8,128)S(1)}, u32[]{:S(2)}, u32[]{:S(2)}) collective-permute-start(f32[616,128]{1,0:T(8,128)S(1)} %get-tuple-element.93), channel_id=1, source_target_pairs={{0,7},{1,0},{2,1},{3,2},{4,3},{5,4},{6,5},{7,6},{8,15},{9,8},{10,9... | collective-permute-start | bytes 946184 | tf_op jit(solution)/shard_map/ppermute | solution.py:753
  14.4 11.0 %collective-permute-start.37 = (f32[616,128]{1,0:T(8,128)S(1)}, f32[616,128]{1,0:T(8,128)S(1)}, u32[]{:S(2)}, u32[]{:S(2)}) collective-permute-start(f32[616,128]{1,0:T(8,128)S(1)} %get-tuple-element.94), channel_id=1, source_target_pairs={{0,1},{1,2},{2,3},{3,4},{4,5},{5,6},{6,7},{7,0},{8,9},{9,10},{10,1... | collective-permute-start | bytes 946184 | tf_op jit(solution)/shard_map/ppermute | solution.py:753
  14.4 14.6 %collective-permute-start.39 = (f32[632,128]{1,0:T(8,128)S(1)}, f32[632,128]{1,0:T(8,128)S(1)}, u32[]{:S(2)}, u32[]{:S(2)}) collective-permute-start(f32[632,128]{1,0:T(8,128)S(1)} %get-tuple-element.97), channel_id=1, source_target_pairs={{0,504},{8,0},{16,8},{24,16},{32,24},{40,32},{48,40},{56,48},{64,5... | collective-permute-start | bytes 970760 | tf_op jit(solution)/shard_map/ppermute | solution.py:753
  23.4 11.3 %collective-permute-start.40 = (f32[504,128]{1,0:T(8,128)S(1)}, f32[504,128]{1,0:T(8,128)S(1)}, u32[]{:S(2)}, u32[]{:S(2)}) collective-permute-start(f32[504,128]{1,0:T(8,128)S(1)} %get-tuple-element.100), channel_id=1, source_target_pairs={{0,8},{8,16},{16,24},{24,32},{32,40},{40,48},{48,56},{56,64},{64,7... | collective-permute-start | bytes 774152 | tf_op jit(solution)/shard_map/ppermute | solution.py:753
  25.5 10.6 %collective-permute-start.38 = (f32[128,128]{1,0:T(8,128)S(1)}, f32[128,128]{1,0:T(8,128)S(1)}, u32[]{:S(2)}, u32[]{:S(2)}) collective-permute-start(f32[128,128]{1,0:T(8,128)S(1)} %get-tuple-element.96), channel_id=1, source_target_pairs={{0,8},{8,16},{16,24},{24,32},{32,40},{40,48},{48,56},{56,64},{64,7... | collective-permute-start | bytes 196616 | tf_op jit(solution)/shard_map/ppermute | solution.py:753
  29.1 7.7 %collective-permute-start.41 = (f32[48,128]{1,0:T(8,128)S(1)}, f32[48,128]{1,0:T(8,128)S(1)}, u32[]{:S(2)}, u32[]{:S(2)}) collective-permute-start(f32[48,128]{1,0:T(8,128)S(1)} %get-tuple-element.102), channel_id=1, source_target_pairs={{0,7},{1,0},{2,1},{3,2},{4,3},{5,4},{6,5},{7,6},{8,15},{9,8},{10,9... | collective-permute-start | bytes 73736 | tf_op jit(solution)/shard_map/ppermute | solution.py:753
  31.4 5.5 %collective-permute-start.42 = (f32[48,128]{1,0:T(8,128)S(1)}, f32[48,128]{1,0:T(8,128)S(1)}, u32[]{:S(2)}, u32[]{:S(2)}) collective-permute-start(f32[48,128]{1,0:T(8,128)S(1)} %get-tuple-element.103), channel_id=1, source_target_pairs={{0,1},{1,2},{2,3},{3,4},{4,5},{5,6},{6,7},{7,0},{8,9},{9,10},{10,1... | collective-permute-start | bytes 73736 | tf_op jit(solution)/shard_map/ppermute | solution.py:753
  37.7 8.6 %collective-permute-start.43 = (f32[112,128]{1,0:T(8,128)S(1)}, f32[112,128]{1,0:T(8,128)S(1)}, u32[]{:S(2)}, u32[]{:S(2)}) collective-permute-start(f32[112,128]{1,0:T(8,128)S(1)} %get-tuple-element.108), channel_id=1, source_target_pairs={{0,7},{1,0},{2,1},{3,2},{4,3},{5,4},{6,5},{7,6},{8,15},{9,8},{10,9... | collective-permute-start | bytes 172040 | tf_op jit(solution)/shard_map/ppermute | solution.py:753
  40.3 6.0 %collective-permute-start.44 = (f32[112,128]{1,0:T(8,128)S(1)}, f32[112,128]{1,0:T(8,128)S(1)}, u32[]{:S(2)}, u32[]{:S(2)}) collective-permute-start(f32[112,128]{1,0:T(8,128)S(1)} %get-tuple-element.109), channel_id=1, source_target_pairs={{0,1},{1,2},{2,3},{3,4},{4,5},{5,6},{6,7},{7,0},{8,9},{9,10},{10,1... | collective-permute-start | bytes 172040 | tf_op jit(solution)/shard_map/ppermute | solution.py:753
  41.4 7.0 %collective-permute-start.46 = (f32[128,128]{1,0:T(8,128)S(1)}, f32[128,128]{1,0:T(8,128)S(1)}, u32[]{:S(2)}, u32[]{:S(2)}) collective-permute-start(f32[128,128]{1,0:T(8,128)S(1)} %get-tuple-element.112), channel_id=1, source_target_pairs={{0,504},{8,0},{16,8},{24,16},{32,24},{40,32},{48,40},{56,48},{64,5... | collective-permute-start | bytes 196616 | tf_op jit(solution)/shard_map/ppermute | solution.py:753
  46.5 8.3 %collective-permute-start.45 = (f32[128,128]{1,0:T(8,128)S(1)}, f32[128,128]{1,0:T(8,128)S(1)}, u32[]{:S(2)}, u32[]{:S(2)}) collective-permute-start(f32[128,128]{1,0:T(8,128)S(1)} %get-tuple-element.111), channel_id=1, source_target_pairs={{0,8},{8,16},{16,24},{24,32},{32,40},{40,48},{48,56},{56,64},{64,7... | collective-permute-start | bytes 196616 | tf_op jit(solution)/shard_map/ppermute | solution.py:753
  48.6 6.9 %collective-permute-start.47 = (f32[48,128]{1,0:T(8,128)S(1)}, f32[48,128]{1,0:T(8,128)S(1)}, u32[]{:S(2)}, u32[]{:S(2)}) collective-permute-start(f32[48,128]{1,0:T(8,128)S(1)} %get-tuple-element.114), channel_id=1, source_target_pairs={{0,7},{1,0},{2,1},{3,2},{4,3},{5,4},{6,5},{7,6},{8,15},{9,8},{10,9... | collective-permute-start | bytes 73736 | tf_op jit(solution)/shard_map/ppermute | solution.py:753
  49.8 5.7 %collective-permute-start.48 = (f32[48,128]{1,0:T(8,128)S(1)}, f32[48,128]{1,0:T(8,128)S(1)}, u32[]{:S(2)}, u32[]{:S(2)}) collective-permute-start(f32[48,128]{1,0:T(8,128)S(1)} %get-tuple-element.115), channel_id=1, source_target_pairs={{0,1},{1,2},{2,3},{3,4},{4,5},{5,6},{6,7},{7,0},{8,9},{9,10},{10,1... | collective-permute-start | bytes 73736 | tf_op jit(solution)/shard_map/ppermute | solution.py:753
  56.3 7.2 %collective-permute-start.49 = (f32[112,128]{1,0:T(8,128)S(1)}, f32[112,128]{1,0:T(8,128)S(1)}, u32[]{:S(2)}, u32[]{:S(2)}) collective-permute-start(f32[112,128]{1,0:T(8,128)S(1)} %get-tuple-element.118), channel_id=1, source_target_pairs={{0,7},{1,0},{2,1},{3,2},{4,3},{5,4},{6,5},{7,6},{8,15},{9,8},{10,9... | collective-permute-start | bytes 172040 | tf_op jit(solution)/shard_map/ppermute | solution.py:753
  58.7 4.8 %collective-permute-start.50 = (f32[112,128]{1,0:T(8,128)S(1)}, f32[112,128]{1,0:T(8,128)S(1)}, u32[]{:S(2)}, u32[]{:S(2)}) collective-permute-start(f32[112,128]{1,0:T(8,128)S(1)} %get-tuple-element.119), channel_id=1, source_target_pairs={{0,1},{1,2},{2,3},{3,4},{4,5},{5,6},{6,7},{7,0},{8,9},{9,10},{10,1... | collective-permute-start | bytes 172040 | tf_op jit(solution)/shard_map/ppermute | solution.py:753
  58.7 6.9 %collective-permute-start.52 = (f32[128,128]{1,0:T(8,128)S(1)}, f32[128,128]{1,0:T(8,128)S(1)}, u32[]{:S(2)}, u32[]{:S(2)}) collective-permute-start(f32[128,128]{1,0:T(8,128)S(1)} %get-tuple-element.122), channel_id=1, source_target_pairs={{0,504},{8,0},{16,8},{24,16},{32,24},{40,32},{48,40},{56,48},{64,5... | collective-permute-start | bytes 196616 | tf_op jit(solution)/shard_map/ppermute | solution.py:753
  63.7 8.3 %collective-permute-start.51 = (f32[128,128]{1,0:T(8,128)S(1)}, f32[128,128]{1,0:T(8,128)S(1)}, u32[]{:S(2)}, u32[]{:S(2)}) collective-permute-start(f32[128,128]{1,0:T(8,128)S(1)} %get-tuple-element.121), channel_id=1, source_target_pairs={{0,8},{8,16},{16,24},{24,32},{32,40},{40,48},{48,56},{56,64},{64,7... | collective-permute-start | bytes 196616 | tf_op jit(solution)/shard_map/ppermute | solution.py:753
  65.8 6.9 %collective-permute-start.53 = (f32[48,128]{1,0:T(8,128)S(1)}, f32[48,128]{1,0:T(8,128)S(1)}, u32[]{:S(2)}, u32[]{:S(2)}) collective-permute-start(f32[48,128]{1,0:T(8,128)S(1)} %get-tuple-element.124), channel_id=1, source_target_pairs={{0,7},{1,0},{2,1},{3,2},{4,3},{5,4},{6,5},{7,6},{8,15},{9,8},{10,9... | collective-permute-start | bytes 73736 | tf_op jit(solution)/shard_map/ppermute | solution.py:753
  66.5 6.1 %collective-permute-start.54 = (f32[48,128]{1,0:T(8,128)S(1)}, f32[48,128]{1,0:T(8,128)S(1)}, u32[]{:S(2)}, u32[]{:S(2)}) collective-permute-start(f32[48,128]{1,0:T(8,128)S(1)} %get-tuple-element.125), channel_id=1, source_target_pairs={{0,1},{1,2},{2,3},{3,4},{4,5},{5,6},{6,7},{7,0},{8,9},{9,10},{10,1... | collective-permute-start | bytes 73736 | tf_op jit(solution)/shard_map/ppermute | solution.py:753
  73.5 7.2 %collective-permute-start.55 = (f32[112,128]{1,0:T(8,128)S(1)}, f32[112,128]{1,0:T(8,128)S(1)}, u32[]{:S(2)}, u32[]{:S(2)}) collective-permute-start(f32[112,128]{1,0:T(8,128)S(1)} %get-tuple-element.128), channel_id=1, source_target_pairs={{0,7},{1,0},{2,1},{3,2},{4,3},{5,4},{6,5},{7,6},{8,15},{9,8},{10,9... | collective-permute-start | bytes 172040 | tf_op jit(solution)/shard_map/ppermute | solution.py:753
  75.5 5.2 %collective-permute-start.56 = (f32[112,128]{1,0:T(8,128)S(1)}, f32[112,128]{1,0:T(8,128)S(1)}, u32[]{:S(2)}, u32[]{:S(2)}) collective-permute-start(f32[112,128]{1,0:T(8,128)S(1)} %get-tuple-element.129), channel_id=1, source_target_pairs={{0,1},{1,2},{2,3},{3,4},{4,5},{5,6},{6,7},{7,0},{8,9},{9,10},{10,1... | collective-permute-start | bytes 172040 | tf_op jit(solution)/shard_map/ppermute | solution.py:753
  75.5 7.3 %collective-permute-start.58 = (f32[128,128]{1,0:T(8,128)S(1)}, f32[128,128]{1,0:T(8,128)S(1)}, u32[]{:S(2)}, u32[]{:S(2)}) collective-permute-start(f32[128,128]{1,0:T(8,128)S(1)} %get-tuple-element.132), channel_id=1, source_target_pairs={{0,504},{8,0},{16,8},{24,16},{32,24},{40,32},{48,40},{56,48},{64,5... | collective-permute-start | bytes 196616 | tf_op jit(solution)/shard_map/ppermute | solution.py:753
  80.9 8.3 %collective-permute-start.57 = (f32[128,128]{1,0:T(8,128)S(1)}, f32[128,128]{1,0:T(8,128)S(1)}, u32[]{:S(2)}, u32[]{:S(2)}) collective-permute-start(f32[128,128]{1,0:T(8,128)S(1)} %get-tuple-element.131), channel_id=1, source_target_pairs={{0,8},{8,16},{16,24},{24,32},{32,40},{40,48},{48,56},{56,64},{64,7... | collective-permute-start | bytes 196616 | tf_op jit(solution)/shard_map/ppermute | solution.py:753
  83.0 7.1 %collective-permute-start.59 = (f32[48,128]{1,0:T(8,128)S(1)}, f32[48,128]{1,0:T(8,128)S(1)}, u32[]{:S(2)}, u32[]{:S(2)}) collective-permute-start(f32[48,128]{1,0:T(8,128)S(1)} %get-tuple-element.134), channel_id=1, source_target_pairs={{0,7},{1,0},{2,1},{3,2},{4,3},{5,4},{6,5},{7,6},{8,15},{9,8},{10,9... | collective-permute-start | bytes 73736 | tf_op jit(solution)/shard_map/ppermute | solution.py:753
  83.7 6.3 %collective-permute-start.60 = (f32[48,128]{1,0:T(8,128)S(1)}, f32[48,128]{1,0:T(8,128)S(1)}, u32[]{:S(2)}, u32[]{:S(2)}) collective-permute-start(f32[48,128]{1,0:T(8,128)S(1)} %get-tuple-element.135), channel_id=1, source_target_pairs={{0,1},{1,2},{2,3},{3,4},{4,5},{5,6},{6,7},{7,0},{8,9},{9,10},{10,1... | collective-permute-start | bytes 73736 | tf_op jit(solution)/shard_map/ppermute | solution.py:753
  85.0 39.6 %copy-start.1 = (f32[16,4,162]{2,1,0:T(4,128)S(1)}, f32[16,4,162]{2,1,0:T(4,128)}, u32[]{:S(2)}) copy-start(f32[16,4,162]{2,1,0:T(4,128)} %src_ref.1) | copy-start | bytes 124420
  85.1 39.6 %copy-start.2 = (f32[4,162,162]{2,0,1:T(4,128)S(1)}, f32[4,162,162]{2,0,1:T(4,128)}, u32[]{:S(2)}) copy-start(f32[4,162,162]{2,0,1:T(4,128)} %param.14) | copy-start | bytes 1259716
  85.1 39.6 %copy-start.3 = (s32[4,6]{1,0:T(4,128)S(1)}, s32[4,6]{1,0:T(4,128)}, u32[]{:S(2)}) copy-start(s32[4,6]{1,0:T(4,128)} %nbr_ref.1) | copy-start | bytes 292
  85.1 39.6 %copy-start.6 = (s32[4,6]{1,0:T(4,128)S(1)}, s32[4,6]{1,0:T(4,128)}, u32[]{:S(2)}) copy-start(s32[4,6]{1,0:T(4,128)} %flag_ref.1) | copy-start | bytes 292
  85.1 39.6 %copy-start.7 = (s32[4,6]{1,0:T(4,128)S(1)}, s32[4,6]{1,0:T(4,128)}, u32[]{:S(2)}) copy-start(s32[4,6]{1,0:T(4,128)} %param.17) | copy-start | bytes 292
  104.0 18.2 %all-to-all-start.1 = ((f32[16,8,128]{2,1,0:T(8,128)}), f32[16,8,128]{2,1,0:T(8,128)S(1)}, u32[]{:S(2)}, u32[]{:S(2)}) async-start(f32[16,8,128]{2,1,0:T(8,128)} %sum_near.1), calls=%async_computation.1 | async-start | bytes 131072 | tf_op jit(solution)/shard_map/all_to_all | solution.py:748

commit v9 on v8

--- a/solution.py
+++ b/solution.py
@@ -661,7 +661,7 @@
     back = [None] * count
     for j in reversed(range(count)):
         value = solved[j]
-        for k in range(j + 1, count):
+        for k in reversed(range(j + 1, count)):
             value = value - lower[k][j] * back[k]
         back[j] = value * inv_pivot[j]
     inv_squares = 1.0 / squares
@@ -901,10 +901,9 @@
         compiler_params=PARAMS,
         name="finish_part",
     )(*given)
-    return lax.cond(
-        fine[0] == 1,
-        lambda given: (adjoint, rel.reshape(nrhs)),
-        lambda given: direct_path(*given),
+    return lax.switch(
+        fine[0],
+        [lambda given: direct_path(*given), lambda given: (adjoint, rel.reshape(nrhs))],
         (adjoint_source, diag_blocks, face_blocks, neighbors, partner, flags),
     )
 

time: 126 us -> 126 us (level)
  no operation moved by 1% of the time
where the time goes in v9:
time: 126 us; the launch traced here: 125 us
  starting transfers between devices  63.2 us (50%)
  waiting for transfers between devices  30.5 us (24%)
  Pallas kernels  16.9 us (13%)
  blocking collectives  12.4 us (10%)
  between operations  1.83 us (1%)
    ppermute x25, starting transfers between devices, rotated(): lax.ppermute(value, axis, [(source, (source + steps) % count) for source...  56.7 us
    ppermute x25, waiting for transfers between devices, rotated(): lax.ppermute(value, axis, [(source, (source + steps) % count) for source...  18.9 us
    all_to_all x1, blocking collectives, sum_devices(): parts = lax.all_to_all(copies, ('dom', 'blk'), 0, 0, axis_index_groups=near)  12.4 us
    all_to_all x1, waiting for transfers between devices, sum_devices(): return lax.all_to_all(copies, 'dom', 0, 0, axis_index_groups=far)  11.6 us
    pallas_call x1, Pallas kernels, shards(): pl.pallas_call(functools.partial(setup_kernel, dom_count=lax.axis_size('d...  6.7 us
    all_to_all x1, starting transfers between devices, sum_devices(): return lax.all_to_all(copies, 'dom', 0, 0, axis_index_groups=far)  6.54 us
    pallas_call x4, Pallas kernels, shards(): pl.pallas_call(functools.partial(even_kernel, last_pair, len(bases)), out...  3.47 us
    pallas_call x4, Pallas kernels, shards(): pl.pallas_call(functools.partial(odd_kernel, first_pair), out_shape=shape...  2.71 us
  transfers between devices with their start and end apart: 26, of which 7 were waited for; matrix products, arithmetic and copies ran while one was open for 0% of the time, Pallas kernels for 3%

profile of v9, /device:TPU:1, one launch (start us, length us, event | category | flops | bytes accessed | tf_op | source)
XLA Modules:
  0.0 125.1 jit_solution(12621339527807736935)
XLA Ops:
  0.6 6.7 %setup_blocks.1 = (bf16[20,162,162]{2,1,0:T(8,128)(2,1)S(1)}, bf16[20,162,162]{2,1,0:T(8,128)(2,1)S(1)}, bf16[4,162,162]{2,1,0:T(8,128)(2,1)S(1)}, bf16[4,162,16...) custom-call(s32[4,6]{1,0:T(4,128)} %nbr_ref.1, ...), custom_call_target="tpu_custom_call" | custom-call | tf_op jit(solution)/shard_map/setup_blocks/pallas_call | solution.py:778
  7.3 7.0 %collective-permute-start.36 = (f32[616,128]{1,0:T(8,128)S(1)}, f32[616,128]{1,0:T(8,128)S(1)}, u32[]{:S(2)}, u32[]{:S(2)}) collective-permute-start(f32[616,128]{1,0:T(8,128)S(1)} %get-tuple-element.93), channel_id=1, source_target_pairs={{0,7},{1,0},{2,1},{3,2},{4,3},{5,4},{6,5},{7,6},{8,15},{9,8},{10,9... | collective-permute-start | bytes 946184 | tf_op jit(solution)/shard_map/ppermute | solution.py:753
  14.4 0.0 collective-permute-start.37
  14.4 9.1 %collective-permute-start.39 = (f32[632,128]{1,0:T(8,128)S(1)}, f32[632,128]{1,0:T(8,128)S(1)}, u32[]{:S(2)}, u32[]{:S(2)}) collective-permute-start(f32[632,128]{1,0:T(8,128)S(1)} %get-tuple-element.97), channel_id=1, source_target_pairs={{0,504},{8,0},{16,8},{24,16},{32,24},{40,32},{48,40},{56,48},{64,5... | collective-permute-start | bytes 970760 | tf_op jit(solution)/shard_map/ppermute | solution.py:753
  23.5 1.9 %collective-permute-start.40 = (f32[504,128]{1,0:T(8,128)S(1)}, f32[504,128]{1,0:T(8,128)S(1)}, u32[]{:S(2)}, u32[]{:S(2)}) collective-permute-start(f32[504,128]{1,0:T(8,128)S(1)} %get-tuple-element.100), channel_id=1, source_target_pairs={{0,8},{8,16},{16,24},{24,32},{32,40},{40,48},{48,56},{56,64},{64,7... | collective-permute-start | bytes 774152 | tf_op jit(solution)/shard_map/ppermute | solution.py:753
  25.4 0.0 collective-permute-done.37.prev_ref.refs_3_
  25.4 0.1 middle_part_0.1
  25.6 1.9 %collective-permute-start.38 = (f32[128,128]{1,0:T(8,128)S(1)}, f32[128,128]{1,0:T(8,128)S(1)}, u32[]{:S(2)}, u32[]{:S(2)}) collective-permute-start(f32[128,128]{1,0:T(8,128)S(1)} %get-tuple-element.96), channel_id=1, source_target_pairs={{0,8},{8,16},{16,24},{24,32},{32,40},{40,48},{48,56},{56,64},{64,7... | collective-permute-start | bytes 196616 | tf_op jit(solution)/shard_map/ppermute | solution.py:753
  27.5 1.7 %collective-permute-done.39.refs_5_.dom_ref = f32[632,128]{1,0:T(8,128)S(1)} collective-permute-done((f32[632,128]{1,0:T(8,128)S(1)}, f32[632,128]{1,0:T(8,128)S(1)}, u32[]{:S(2)}, u32[]{:S(2)}) %collective-permute-start.39) | collective-permute-done | bytes 323616 | tf_op jit(solution)/shard_map/ppermute | solution.py:753
  29.2 0.1 relay_part_0.1
  29.3 2.1 %collective-permute-start.41 = (f32[48,128]{1,0:T(8,128)S(1)}, f32[48,128]{1,0:T(8,128)S(1)}, u32[]{:S(2)}, u32[]{:S(2)}) collective-permute-start(f32[48,128]{1,0:T(8,128)S(1)} %get-tuple-element.102), channel_id=1, source_target_pairs={{0,7},{1,0},{2,1},{3,2},{4,3},{5,4},{6,5},{7,6},{8,15},{9,8},{10,9... | collective-permute-start | bytes 73736 | tf_op jit(solution)/shard_map/ppermute | solution.py:753
  31.4 0.8 collective-permute-start.42
  32.2 2.7 %collective-permute-done.40.refs_8_ = f32[504,128]{1,0:T(8,128)S(1)} collective-permute-done((f32[504,128]{1,0:T(8,128)S(1)}, f32[504,128]{1,0:T(8,128)S(1)}, u32[]{:S(2)}, u32[]{:S(2)}) %collective-permute-start.40) | collective-permute-done | bytes 258080 | tf_op jit(solution)/shard_map/ppermute | solution.py:753
  34.9 1.4 %collective-permute-done.38.refs_4_ = f32[128,128]{1,0:T(8,128)S(1)} collective-permute-done((f32[128,128]{1,0:T(8,128)S(1)}, f32[128,128]{1,0:T(8,128)S(1)}, u32[]{:S(2)}, u32[]{:S(2)}) %collective-permute-start.38) | collective-permute-done | bytes 65568 | tf_op jit(solution)/shard_map/ppermute | solution.py:753
  36.3 0.7 odd_part_0.1
  37.1 0.9 even_part_0.1
  37.9 2.4 %collective-permute-start.43 = (f32[112,128]{1,0:T(8,128)S(1)}, f32[112,128]{1,0:T(8,128)S(1)}, u32[]{:S(2)}, u32[]{:S(2)}) collective-permute-start(f32[112,128]{1,0:T(8,128)S(1)} %get-tuple-element.108), channel_id=1, source_target_pairs={{0,7},{1,0},{2,1},{3,2},{4,3},{5,4},{6,5},{7,6},{8,15},{9,8},{10,9... | collective-permute-start | bytes 172040 | tf_op jit(solution)/shard_map/ppermute | solution.py:753
  40.3 1.1 collective-permute-start.44
  41.5 4.9 %collective-permute-start.46 = (f32[128,128]{1,0:T(8,128)S(1)}, f32[128,128]{1,0:T(8,128)S(1)}, u32[]{:S(2)}, u32[]{:S(2)}) collective-permute-start(f32[128,128]{1,0:T(8,128)S(1)} %get-tuple-element.112), channel_id=1, source_target_pairs={{0,504},{8,0},{16,8},{24,16},{32,24},{40,32},{48,40},{56,48},{64,5... | collective-permute-start | bytes 196616 | tf_op jit(solution)/shard_map/ppermute | solution.py:753
  46.4 0.0 collective-permute-done.44.prev_ref.refs_3_
  46.4 0.1 middle_part_1.1
  46.5 1.9 %collective-permute-start.45 = (f32[128,128]{1,0:T(8,128)S(1)}, f32[128,128]{1,0:T(8,128)S(1)}, u32[]{:S(2)}, u32[]{:S(2)}) collective-permute-start(f32[128,128]{1,0:T(8,128)S(1)} %get-tuple-element.111), channel_id=1, source_target_pairs={{0,8},{8,16},{16,24},{24,32},{32,40},{40,48},{48,56},{56,64},{64,7... | collective-permute-start | bytes 196616 | tf_op jit(solution)/shard_map/ppermute | solution.py:753
  48.5 0.0 collective-permute-done.46.refs_5_.dom_ref
  48.5 0.1 relay_part_1.1
  48.6 1.2 collective-permute-start.47
  49.8 0.5 collective-permute-start.48
  50.4 4.5 %collective-permute-done.45.refs_4_ = f32[128,128]{1,0:T(8,128)S(1)} collective-permute-done((f32[128,128]{1,0:T(8,128)S(1)}, f32[128,128]{1,0:T(8,128)S(1)}, u32[]{:S(2)}, u32[]{:S(2)}) %collective-permute-start.45) | collective-permute-done | bytes 65568 | tf_op jit(solution)/shard_map/ppermute | solution.py:753
  54.9 0.7 odd_part_1.1
  55.5 0.9 even_part_1.1
  56.4 2.4 %collective-permute-start.49 = (f32[112,128]{1,0:T(8,128)S(1)}, f32[112,128]{1,0:T(8,128)S(1)}, u32[]{:S(2)}, u32[]{:S(2)}) collective-permute-start(f32[112,128]{1,0:T(8,128)S(1)} %get-tuple-element.118), channel_id=1, source_target_pairs={{0,7},{1,0},{2,1},{3,2},{4,3},{5,4},{6,5},{7,6},{8,15},{9,8},{10,9... | collective-permute-start | bytes 172040 | tf_op jit(solution)/shard_map/ppermute | solution.py:753
  58.8 4.8 %collective-permute-start.52 = (f32[128,128]{1,0:T(8,128)S(1)}, f32[128,128]{1,0:T(8,128)S(1)}, u32[]{:S(2)}, u32[]{:S(2)}) collective-permute-start(f32[128,128]{1,0:T(8,128)S(1)} %get-tuple-element.122), channel_id=1, source_target_pairs={{0,504},{8,0},{16,8},{24,16},{32,24},{40,32},{48,40},{56,48},{64,5... | collective-permute-start | bytes 196616 | tf_op jit(solution)/shard_map/ppermute | solution.py:753
  63.6 0.1 middle_part_2.1
  63.7 1.9 %collective-permute-start.51 = (f32[128,128]{1,0:T(8,128)S(1)}, f32[128,128]{1,0:T(8,128)S(1)}, u32[]{:S(2)}, u32[]{:S(2)}) collective-permute-start(f32[128,128]{1,0:T(8,128)S(1)} %get-tuple-element.121), channel_id=1, source_target_pairs={{0,8},{8,16},{16,24},{24,32},{32,40},{40,48},{48,56},{56,64},{64,7... | collective-permute-start | bytes 196616 | tf_op jit(solution)/shard_map/ppermute | solution.py:753
  65.7 0.1 relay_part_2.1
  65.8 0.8 collective-permute-start.53
  66.6 1.0 collective-permute-start.54
  67.6 4.5 %collective-permute-done.51.refs_4_ = f32[128,128]{1,0:T(8,128)S(1)} collective-permute-done((f32[128,128]{1,0:T(8,128)S(1)}, f32[128,128]{1,0:T(8,128)S(1)}, u32[]{:S(2)}, u32[]{:S(2)}) %collective-permute-start.51) | collective-permute-done | bytes 65568 | tf_op jit(solution)/shard_map/ppermute | solution.py:753
  72.1 0.7 odd_part_2.1
  72.7 0.9 even_part_2.1
  73.6 2.0 %collective-permute-start.55 = (f32[112,128]{1,0:T(8,128)S(1)}, f32[112,128]{1,0:T(8,128)S(1)}, u32[]{:S(2)}, u32[]{:S(2)}) collective-permute-start(f32[112,128]{1,0:T(8,128)S(1)} %get-tuple-element.128), channel_id=1, source_target_pairs={{0,7},{1,0},{2,1},{3,2},{4,3},{5,4},{6,5},{7,6},{8,15},{9,8},{10,9... | collective-permute-start | bytes 172040 | tf_op jit(solution)/shard_map/ppermute | solution.py:753
  75.5 5.2 %collective-permute-start.58 = (f32[128,128]{1,0:T(8,128)S(1)}, f32[128,128]{1,0:T(8,128)S(1)}, u32[]{:S(2)}, u32[]{:S(2)}) collective-permute-start(f32[128,128]{1,0:T(8,128)S(1)} %get-tuple-element.132), channel_id=1, source_target_pairs={{0,504},{8,0},{16,8},{24,16},{32,24},{40,32},{48,40},{56,48},{64,5... | collective-permute-start | bytes 196616 | tf_op jit(solution)/shard_map/ppermute | solution.py:753
  80.8 0.1 middle_part_3.1
  80.9 1.9 %collective-permute-start.57 = (f32[128,128]{1,0:T(8,128)S(1)}, f32[128,128]{1,0:T(8,128)S(1)}, u32[]{:S(2)}, u32[]{:S(2)}) collective-permute-start(f32[128,128]{1,0:T(8,128)S(1)} %get-tuple-element.131), channel_id=1, source_target_pairs={{0,8},{8,16},{16,24},{24,32},{32,40},{40,48},{48,56},{56,64},{64,7... | collective-permute-start | bytes 196616 | tf_op jit(solution)/shard_map/ppermute | solution.py:753
  82.9 0.1 relay_part_3.1
  83.0 0.8 collective-permute-start.59
  83.8 1.0 collective-permute-start.60
  84.8 0.1 gram_part_0.1.refs_4_
  84.9 0.1 gram_part_1.1.refs_6_
  85.0 0.1 gram_part_2.1.refs_8_
  85.1 0.0 copy-start.1
  85.1 0.0 copy-start.2
  85.1 0.0 copy-start.3
  85.1 0.0 copy-start.6
  85.1 0.0 copy-start.7
  85.2 4.1 %collective-permute-done.57.refs_4_ = f32[128,128]{1,0:T(8,128)S(1)} collective-permute-done((f32[128,128]{1,0:T(8,128)S(1)}, f32[128,128]{1,0:T(8,128)S(1)}, u32[]{:S(2)}, u32[]{:S(2)}) %collective-permute-start.57) | collective-permute-done | bytes 65568 | tf_op jit(solution)/shard_map/ppermute | solution.py:753
  89.3 0.7 odd_part_3.1
  89.9 0.2 gram_part_3.1.refs_13_
  90.1 0.9 even_part_3.1
  91.0 12.4 %all_to_all.10.parts_ref = f32[32,8,128]{2,1,0:T(8,128)S(1)} all-to-all(f32[32,8,128]{2,1,0:T(8,128)S(1)} %get-tuple-element.144), channel_id=1, replica_groups={{0,1,2,3,4,5,6,7,8,9,10,11,12,13,14,15,16,17,18,19,20,21,22,23,24,25,26..., dimensions={0} | all-to-all | bytes 262144 | tf_op jit(solution)/shard_map/all_to_all | solution.py:739
  103.4 0.7 sum_near.1
  104.0 6.5 %all-to-all-start.1 = ((f32[16,8,128]{2,1,0:T(8,128)}), f32[16,8,128]{2,1,0:T(8,128)S(1)}, u32[]{:S(2)}, u32[]{:S(2)}) async-start(f32[16,8,128]{2,1,0:T(8,128)} %sum_near.1), calls=%async_computation.1 | async-start | bytes 131072 | tf_op jit(solution)/shard_map/all_to_all | solution.py:748
  110.6 11.6 %all-to-all-done.1.refs_0_ = f32[16,8,128]{2,1,0:T(8,128)S(1)} async-done(((f32[16,8,128]{2,1,0:T(8,128)}), f32[16,8,128]{2,1,0:T(8,128)S(1)}, u32[]{:S(2)}, u32[]{:S(2)}) %all-to-all-start.1) | async-done | bytes 65568 | tf_op jit(solution)/shard_map/all_to_all | solution.py:748
  122.2 1.7 %finish_part.1 = (f32[16,4,162]{2,1,0:T(4,128)}, f32[1,16]{1,0:T(1,128)}, s32[1]{0:T(128)}) custom-call(f32[16,8,128]{2,1,0:T(8,128)S(1)} %all-to-all-done.1.refs_0_, f32[4,16,162]{2,1,0:T(8,128)S(1)} %get-tuple-element.136.refs_0_.refs_5_.refs_1_, f32[4,16,162]{2,1,0:T(8,128)S(1)} %get-tuple-element.137.refs_1_.refs_6_.refs_2_, ...), custom_call_target="tpu_custom_call" | custom-call | tf_op jit(solution)/shard_map/finish_part/pallas_call | solution.py:894
  124.6 0.3 conditional.1
  (23 shorter events, 0.1 us)
Async XLA Ops:
  7.3 18.1 %collective-permute-start.36 = (f32[616,128]{1,0:T(8,128)S(1)}, f32[616,128]{1,0:T(8,128)S(1)}, u32[]{:S(2)}, u32[]{:S(2)}) collective-permute-start(f32[616,128]{1,0:T(8,128)S(1)} %get-tuple-element.93), channel_id=1, source_target_pairs={{0,7},{1,0},{2,1},{3,2},{4,3},{5,4},{6,5},{7,6},{8,15},{9,8},{10,9... | collective-permute-start | bytes 946184 | tf_op jit(solution)/shard_map/ppermute | solution.py:753
  14.4 11.1 %collective-permute-start.37 = (f32[616,128]{1,0:T(8,128)S(1)}, f32[616,128]{1,0:T(8,128)S(1)}, u32[]{:S(2)}, u32[]{:S(2)}) collective-permute-start(f32[616,128]{1,0:T(8,128)S(1)} %get-tuple-element.94), channel_id=1, source_target_pairs={{0,1},{1,2},{2,3},{3,4},{4,5},{5,6},{6,7},{7,0},{8,9},{9,10},{10,1... | collective-permute-start | bytes 946184 | tf_op jit(solution)/shard_map/ppermute | solution.py:753
  14.4 14.8 %collective-permute-start.39 = (f32[632,128]{1,0:T(8,128)S(1)}, f32[632,128]{1,0:T(8,128)S(1)}, u32[]{:S(2)}, u32[]{:S(2)}) collective-permute-start(f32[632,128]{1,0:T(8,128)S(1)} %get-tuple-element.97), channel_id=1, source_target_pairs={{0,504},{8,0},{16,8},{24,16},{32,24},{40,32},{48,40},{56,48},{64,5... | collective-permute-start | bytes 970760 | tf_op jit(solution)/shard_map/ppermute | solution.py:753
  23.5 11.4 %collective-permute-start.40 = (f32[504,128]{1,0:T(8,128)S(1)}, f32[504,128]{1,0:T(8,128)S(1)}, u32[]{:S(2)}, u32[]{:S(2)}) collective-permute-start(f32[504,128]{1,0:T(8,128)S(1)} %get-tuple-element.100), channel_id=1, source_target_pairs={{0,8},{8,16},{16,24},{24,32},{32,40},{40,48},{48,56},{56,64},{64,7... | collective-permute-start | bytes 774152 | tf_op jit(solution)/shard_map/ppermute | solution.py:753
  25.6 10.7 %collective-permute-start.38 = (f32[128,128]{1,0:T(8,128)S(1)}, f32[128,128]{1,0:T(8,128)S(1)}, u32[]{:S(2)}, u32[]{:S(2)}) collective-permute-start(f32[128,128]{1,0:T(8,128)S(1)} %get-tuple-element.96), channel_id=1, source_target_pairs={{0,8},{8,16},{16,24},{24,32},{32,40},{40,48},{48,56},{56,64},{64,7... | collective-permute-start | bytes 196616 | tf_op jit(solution)/shard_map/ppermute | solution.py:753
  29.3 7.7 %collective-permute-start.41 = (f32[48,128]{1,0:T(8,128)S(1)}, f32[48,128]{1,0:T(8,128)S(1)}, u32[]{:S(2)}, u32[]{:S(2)}) collective-permute-start(f32[48,128]{1,0:T(8,128)S(1)} %get-tuple-element.102), channel_id=1, source_target_pairs={{0,7},{1,0},{2,1},{3,2},{4,3},{5,4},{6,5},{7,6},{8,15},{9,8},{10,9... | collective-permute-start | bytes 73736 | tf_op jit(solution)/shard_map/ppermute | solution.py:753
  31.4 5.6 %collective-permute-start.42 = (f32[48,128]{1,0:T(8,128)S(1)}, f32[48,128]{1,0:T(8,128)S(1)}, u32[]{:S(2)}, u32[]{:S(2)}) collective-permute-start(f32[48,128]{1,0:T(8,128)S(1)} %get-tuple-element.103), channel_id=1, source_target_pairs={{0,1},{1,2},{2,3},{3,4},{4,5},{5,6},{6,7},{7,0},{8,9},{9,10},{10,1... | collective-permute-start | bytes 73736 | tf_op jit(solution)/shard_map/ppermute | solution.py:753
  37.9 8.5 %collective-permute-start.43 = (f32[112,128]{1,0:T(8,128)S(1)}, f32[112,128]{1,0:T(8,128)S(1)}, u32[]{:S(2)}, u32[]{:S(2)}) collective-permute-start(f32[112,128]{1,0:T(8,128)S(1)} %get-tuple-element.108), channel_id=1, source_target_pairs={{0,7},{1,0},{2,1},{3,2},{4,3},{5,4},{6,5},{7,6},{8,15},{9,8},{10,9... | collective-permute-start | bytes 172040 | tf_op jit(solution)/shard_map/ppermute | solution.py:753
  40.3 6.0 %collective-permute-start.44 = (f32[112,128]{1,0:T(8,128)S(1)}, f32[112,128]{1,0:T(8,128)S(1)}, u32[]{:S(2)}, u32[]{:S(2)}) collective-permute-start(f32[112,128]{1,0:T(8,128)S(1)} %get-tuple-element.109), channel_id=1, source_target_pairs={{0,1},{1,2},{2,3},{3,4},{4,5},{5,6},{6,7},{7,0},{8,9},{9,10},{10,1... | collective-permute-start | bytes 172040 | tf_op jit(solution)/shard_map/ppermute | solution.py:753
  41.5 7.0 %collective-permute-start.46 = (f32[128,128]{1,0:T(8,128)S(1)}, f32[128,128]{1,0:T(8,128)S(1)}, u32[]{:S(2)}, u32[]{:S(2)}) collective-permute-start(f32[128,128]{1,0:T(8,128)S(1)} %get-tuple-element.112), channel_id=1, source_target_pairs={{0,504},{8,0},{16,8},{24,16},{32,24},{40,32},{48,40},{56,48},{64,5... | collective-permute-start | bytes 196616 | tf_op jit(solution)/shard_map/ppermute | solution.py:753
  46.5 8.3 %collective-permute-start.45 = (f32[128,128]{1,0:T(8,128)S(1)}, f32[128,128]{1,0:T(8,128)S(1)}, u32[]{:S(2)}, u32[]{:S(2)}) collective-permute-start(f32[128,128]{1,0:T(8,128)S(1)} %get-tuple-element.111), channel_id=1, source_target_pairs={{0,8},{8,16},{16,24},{24,32},{32,40},{40,48},{48,56},{56,64},{64,7... | collective-permute-start | bytes 196616 | tf_op jit(solution)/shard_map/ppermute | solution.py:753
  48.6 6.9 %collective-permute-start.47 = (f32[48,128]{1,0:T(8,128)S(1)}, f32[48,128]{1,0:T(8,128)S(1)}, u32[]{:S(2)}, u32[]{:S(2)}) collective-permute-start(f32[48,128]{1,0:T(8,128)S(1)} %get-tuple-element.114), channel_id=1, source_target_pairs={{0,7},{1,0},{2,1},{3,2},{4,3},{5,4},{6,5},{7,6},{8,15},{9,8},{10,9... | collective-permute-start | bytes 73736 | tf_op jit(solution)/shard_map/ppermute | solution.py:753
  49.8 5.7 %collective-permute-start.48 = (f32[48,128]{1,0:T(8,128)S(1)}, f32[48,128]{1,0:T(8,128)S(1)}, u32[]{:S(2)}, u32[]{:S(2)}) collective-permute-start(f32[48,128]{1,0:T(8,128)S(1)} %get-tuple-element.115), channel_id=1, source_target_pairs={{0,1},{1,2},{2,3},{3,4},{4,5},{5,6},{6,7},{7,0},{8,9},{9,10},{10,1... | collective-permute-start | bytes 73736 | tf_op jit(solution)/shard_map/ppermute | solution.py:753
  56.4 7.2 %collective-permute-start.49 = (f32[112,128]{1,0:T(8,128)S(1)}, f32[112,128]{1,0:T(8,128)S(1)}, u32[]{:S(2)}, u32[]{:S(2)}) collective-permute-start(f32[112,128]{1,0:T(8,128)S(1)} %get-tuple-element.118), channel_id=1, source_target_pairs={{0,7},{1,0},{2,1},{3,2},{4,3},{5,4},{6,5},{7,6},{8,15},{9,8},{10,9... | collective-permute-start | bytes 172040 | tf_op jit(solution)/shard_map/ppermute | solution.py:753
  58.8 4.8 %collective-permute-start.50 = (f32[112,128]{1,0:T(8,128)S(1)}, f32[112,128]{1,0:T(8,128)S(1)}, u32[]{:S(2)}, u32[]{:S(2)}) collective-permute-start(f32[112,128]{1,0:T(8,128)S(1)} %get-tuple-element.119), channel_id=1, source_target_pairs={{0,1},{1,2},{2,3},{3,4},{4,5},{5,6},{6,7},{7,0},{8,9},{9,10},{10,1... | collective-permute-start | bytes 172040 | tf_op jit(solution)/shard_map/ppermute | solution.py:753
  58.8 6.9 %collective-permute-start.52 = (f32[128,128]{1,0:T(8,128)S(1)}, f32[128,128]{1,0:T(8,128)S(1)}, u32[]{:S(2)}, u32[]{:S(2)}) collective-permute-start(f32[128,128]{1,0:T(8,128)S(1)} %get-tuple-element.122), channel_id=1, source_target_pairs={{0,504},{8,0},{16,8},{24,16},{32,24},{40,32},{48,40},{56,48},{64,5... | collective-permute-start | bytes 196616 | tf_op jit(solution)/shard_map/ppermute | solution.py:753
  63.7 8.3 %collective-permute-start.51 = (f32[128,128]{1,0:T(8,128)S(1)}, f32[128,128]{1,0:T(8,128)S(1)}, u32[]{:S(2)}, u32[]{:S(2)}) collective-permute-start(f32[128,128]{1,0:T(8,128)S(1)} %get-tuple-element.121), channel_id=1, source_target_pairs={{0,8},{8,16},{16,24},{24,32},{32,40},{40,48},{48,56},{56,64},{64,7... | collective-permute-start | bytes 196616 | tf_op jit(solution)/shard_map/ppermute | solution.py:753
  65.8 6.9 %collective-permute-start.53 = (f32[48,128]{1,0:T(8,128)S(1)}, f32[48,128]{1,0:T(8,128)S(1)}, u32[]{:S(2)}, u32[]{:S(2)}) collective-permute-start(f32[48,128]{1,0:T(8,128)S(1)} %get-tuple-element.124), channel_id=1, source_target_pairs={{0,7},{1,0},{2,1},{3,2},{4,3},{5,4},{6,5},{7,6},{8,15},{9,8},{10,9... | collective-permute-start | bytes 73736 | tf_op jit(solution)/shard_map/ppermute | solution.py:753
  66.6 6.1 %collective-permute-start.54 = (f32[48,128]{1,0:T(8,128)S(1)}, f32[48,128]{1,0:T(8,128)S(1)}, u32[]{:S(2)}, u32[]{:S(2)}) collective-permute-start(f32[48,128]{1,0:T(8,128)S(1)} %get-tuple-element.125), channel_id=1, source_target_pairs={{0,1},{1,2},{2,3},{3,4},{4,5},{5,6},{6,7},{7,0},{8,9},{9,10},{10,1... | collective-permute-start | bytes 73736 | tf_op jit(solution)/shard_map/ppermute | solution.py:753
  73.6 7.2 %collective-permute-start.55 = (f32[112,128]{1,0:T(8,128)S(1)}, f32[112,128]{1,0:T(8,128)S(1)}, u32[]{:S(2)}, u32[]{:S(2)}) collective-permute-start(f32[112,128]{1,0:T(8,128)S(1)} %get-tuple-element.128), channel_id=1, source_target_pairs={{0,7},{1,0},{2,1},{3,2},{4,3},{5,4},{6,5},{7,6},{8,15},{9,8},{10,9... | collective-permute-start | bytes 172040 | tf_op jit(solution)/shard_map/ppermute | solution.py:753
  75.5 5.2 %collective-permute-start.56 = (f32[112,128]{1,0:T(8,128)S(1)}, f32[112,128]{1,0:T(8,128)S(1)}, u32[]{:S(2)}, u32[]{:S(2)}) collective-permute-start(f32[112,128]{1,0:T(8,128)S(1)} %get-tuple-element.129), channel_id=1, source_target_pairs={{0,1},{1,2},{2,3},{3,4},{4,5},{5,6},{6,7},{7,0},{8,9},{9,10},{10,1... | collective-permute-start | bytes 172040 | tf_op jit(solution)/shard_map/ppermute | solution.py:753
  75.5 7.3 %collective-permute-start.58 = (f32[128,128]{1,0:T(8,128)S(1)}, f32[128,128]{1,0:T(8,128)S(1)}, u32[]{:S(2)}, u32[]{:S(2)}) collective-permute-start(f32[128,128]{1,0:T(8,128)S(1)} %get-tuple-element.132), channel_id=1, source_target_pairs={{0,504},{8,0},{16,8},{24,16},{32,24},{40,32},{48,40},{56,48},{64,5... | collective-permute-start | bytes 196616 | tf_op jit(solution)/shard_map/ppermute | solution.py:753
  80.9 8.3 %collective-permute-start.57 = (f32[128,128]{1,0:T(8,128)S(1)}, f32[128,128]{1,0:T(8,128)S(1)}, u32[]{:S(2)}, u32[]{:S(2)}) collective-permute-start(f32[128,128]{1,0:T(8,128)S(1)} %get-tuple-element.131), channel_id=1, source_target_pairs={{0,8},{8,16},{16,24},{24,32},{32,40},{40,48},{48,56},{56,64},{64,7... | collective-permute-start | bytes 196616 | tf_op jit(solution)/shard_map/ppermute | solution.py:753
  83.0 7.1 %collective-permute-start.59 = (f32[48,128]{1,0:T(8,128)S(1)}, f32[48,128]{1,0:T(8,128)S(1)}, u32[]{:S(2)}, u32[]{:S(2)}) collective-permute-start(f32[48,128]{1,0:T(8,128)S(1)} %get-tuple-element.134), channel_id=1, source_target_pairs={{0,7},{1,0},{2,1},{3,2},{4,3},{5,4},{6,5},{7,6},{8,15},{9,8},{10,9... | collective-permute-start | bytes 73736 | tf_op jit(solution)/shard_map/ppermute | solution.py:753
  83.8 6.3 %collective-permute-start.60 = (f32[48,128]{1,0:T(8,128)S(1)}, f32[48,128]{1,0:T(8,128)S(1)}, u32[]{:S(2)}, u32[]{:S(2)}) collective-permute-start(f32[48,128]{1,0:T(8,128)S(1)} %get-tuple-element.135), channel_id=1, source_target_pairs={{0,1},{1,2},{2,3},{3,4},{4,5},{5,6},{6,7},{7,0},{8,9},{9,10},{10,1... | collective-permute-start | bytes 73736 | tf_op jit(solution)/shard_map/ppermute | solution.py:753
  85.1 39.5 %copy-start.1 = (f32[16,4,162]{2,1,0:T(4,128)S(1)}, f32[16,4,162]{2,1,0:T(4,128)}, u32[]{:S(2)}) copy-start(f32[16,4,162]{2,1,0:T(4,128)} %src_ref.1) | copy-start | bytes 124420
  85.1 39.5 %copy-start.2 = (f32[4,162,162]{2,0,1:T(4,128)S(1)}, f32[4,162,162]{2,0,1:T(4,128)}, u32[]{:S(2)}) copy-start(f32[4,162,162]{2,0,1:T(4,128)} %param.14) | copy-start | bytes 1259716
  85.1 39.5 %copy-start.3 = (s32[4,6]{1,0:T(4,128)S(1)}, s32[4,6]{1,0:T(4,128)}, u32[]{:S(2)}) copy-start(s32[4,6]{1,0:T(4,128)} %nbr_ref.1) | copy-start | bytes 292
  85.1 39.5 %copy-start.6 = (s32[4,6]{1,0:T(4,128)S(1)}, s32[4,6]{1,0:T(4,128)}, u32[]{:S(2)}) copy-start(s32[4,6]{1,0:T(4,128)} %flag_ref.1) | copy-start | bytes 292
  85.1 39.5 %copy-start.7 = (s32[4,6]{1,0:T(4,128)S(1)}, s32[4,6]{1,0:T(4,128)}, u32[]{:S(2)}) copy-start(s32[4,6]{1,0:T(4,128)} %param.17) | copy-start | bytes 292
  104.0 18.1 %all-to-all-start.1 = ((f32[16,8,128]{2,1,0:T(8,128)}), f32[16,8,128]{2,1,0:T(8,128)S(1)}, u32[]{:S(2)}, u32[]{:S(2)}) async-start(f32[16,8,128]{2,1,0:T(8,128)} %sum_near.1), calls=%async_computation.1 | async-start | bytes 131072 | tf_op jit(solution)/shard_map/all_to_all | solution.py:748
